TPU v7x, 32 devices: a whole 2x2x4 slice. The times are simulated.
32 devices in a mesh: lon: 4 (over y, core), lat: 4 (over z), lev: 2 (over x).
Axes of the slice: x: 2, y: 2, z: 4, core: 2. Of those that a mesh axis runs over, the one named last changes fastest.
Arguments:
- fields: float32 [4, 8, 32, 7200], P(None, 'lev', 'lat', 'lon'), may hold values from -6 to 6
- surface: float32 [32, 7200], P('lat', 'lon'), may hold values from -3 to 3
- filter_rows: int32 [16], replicated, may hold values from 0 to 31, as said below
- keep_counts: int32 [16], replicated, may hold values from 1 to 128
Outputs:
- advanced: float32 [4, 8, 32, 7200], P(None, 'lev', 'lat', 'lon')
Inputs may be any that keep to these rules, and one draw needn't show every extreme that they name: `filter_rows`: 16 distinct rows in increasing order: exactly 4 of the 8 rows of each aligned block of 8 rows, row 0 and row 31 among them.
All inputs are finite; a program needn't handle non-finite values.
Results may differ from a plain program's by a relative error of at most 0.0001.
Values sent between devices are 32-bit elements; how exact they have to be, the bound alone decides.
No kernel may reach another device: no remote copies, remote signals or barrier semaphores. Data moves between devices by JAX's collectives and lax.ppermute only.
A program may use at most 64 MiB of HBM per device.

v0:
```python
import jax
import jax.numpy as jnp
from jax import lax
from jax.sharding import PartitionSpec as P

NLON = 7200
KMAX = 128
STEPS = 2


GRAVITY_SCALE = 0.05
BUOYANCY = 0.5
CORIOLIS = 0.3
ZONAL_COEF = 0.08
NORTH_COEF = 0.2
DAMPING = 0.25
FIRST_LAT = -70.0
ROW_STEP = 0.05
PRECISE = lax.Precision.HIGHEST


def carried_in(value, axis, combine, identity):
    devices, place = (lax.axis_size(axis), lax.axis_index(axis))
    everything = lax.all_gather(value, axis)
    start = jnp.broadcast_to(jnp.asarray(identity, value.dtype), value.shape)

    def step(k, before):
        at = devices - 1 - k
        reached = at > place
        new = combine(before, everything[at])
        return jnp.where(reached, new, before)

    return lax.fori_loop(0, devices, step, start)


def extended(block, sides, width, periodic):
    for axis, dim in sides:
        count = lax.axis_size(axis)
        forward = [(i, i + 1) for i in range(count - 1)]
        if periodic:
            forward.append((count - 1, 0))
        backward = [(target, source) for source, target in forward]
        low = lax.ppermute(
            lax.slice_in_dim(block, block.shape[dim] - width, None, axis=dim), axis, forward
        )
        high = lax.ppermute(lax.slice_in_dim(block, 0, width, axis=dim), axis, backward)
        block = jnp.concatenate([low, block, high], axis=dim)
    return block


def row_geometry(row_index):
    based = row_index.astype(jnp.float32)
    to_radian = jnp.pi / 180.0
    middle = (FIRST_LAT + (based + 0.5) * ROW_STEP) * to_radian
    northern = (FIRST_LAT + (based + 1.0) * ROW_STEP) * to_radian
    southern = (FIRST_LAT + based * ROW_STEP) * to_radian
    return (
        jnp.cos(middle),
        jnp.cos(northern),
        jnp.cos(southern),
        CORIOLIS * jnp.sin(middle),
        CORIOLIS * jnp.sin(northern),
    )


def layer_weight(values):
    return GRAVITY_SCALE * (1.0 + values[2]) * (1.0 + BUOYANCY * values[3])


def advance(padded, geometry):
    cos_mid, cos_north, cos_south, cor_mid, cor_north = [g[:, None] for g in geometry]
    height = padded.shape[-2] - 2
    width = padded.shape[-1] - 2

    def part(which, row_shift, col_shift):
        return padded[
            which,
            ...,
            1 + row_shift : 1 + row_shift + height,
            1 + col_shift : 1 + col_shift + width,
        ]

    zonal = ZONAL_COEF / cos_mid
    uwind_mid, uwind_west, uwind_north, uwind_corner = (
        part(0, 0, 0),
        part(0, 0, -1),
        part(0, 1, 0),
        part(0, 1, -1),
    )
    vwind_mid, vwind_east, vwind_south, vwind_corner = (
        part(1, 0, 0),
        part(1, 0, 1),
        part(1, -1, 0),
        part(1, -1, 1),
    )
    depth_mid, depth_east, depth_west = (part(2, 0, 0), part(2, 0, 1), part(2, 0, -1))
    depth_north, depth_south = (part(2, 1, 0), part(2, -1, 0))
    heat_mid, heat_east, heat_west = (part(3, 0, 0), part(3, 0, 1), part(3, 0, -1))
    heat_north, heat_south = (part(3, 1, 0), part(3, -1, 0))
    geopot_mid, geopot_east, geopot_north = (part(4, 0, 0), part(4, 0, 1), part(4, 1, 0))
    uwind_new = (
        uwind_mid
        + cor_mid * 0.25 * (vwind_mid + vwind_east + vwind_south + vwind_corner)
        - zonal * (geopot_east - geopot_mid)
    )
    vwind_new = (
        vwind_mid
        - cor_north * 0.25 * (uwind_mid + uwind_west + uwind_north + uwind_corner)
        - NORTH_COEF * (geopot_north - geopot_mid)
    )
    flux_east = uwind_mid * (2.0 + depth_mid + depth_east) * 0.5
    flux_west = uwind_west * (2.0 + depth_west + depth_mid) * 0.5
    flux_north = vwind_mid * (2.0 + depth_mid + depth_north) * 0.5
    flux_south = vwind_south * (2.0 + depth_south + depth_mid) * 0.5
    depth_new = (
        depth_mid
        - zonal * (flux_east - flux_west)
        - NORTH_COEF * (cos_north * flux_north - cos_south * flux_south) / cos_mid
    )
    heat_new = (
        heat_mid
        - 0.25 * (uwind_mid + uwind_west) * zonal * (heat_east - heat_west)
        - 0.25 * (vwind_mid + vwind_south) * NORTH_COEF * (heat_north - heat_south)
    )
    return jnp.stack([uwind_new, vwind_new, depth_new, heat_new])


def wave_table(lon_start, count, wave_count):
    longitude = lon_start + jnp.arange(count, dtype=jnp.int32)
    wavenumber = jnp.arange(wave_count, dtype=jnp.int32)
    angles = (longitude[:, None] * wavenumber[None, :] % NLON).astype(jnp.float32) * (
        2.0 * jnp.pi / NLON
    )
    return jnp.concatenate([jnp.cos(angles), jnp.sin(angles)], 1)


def mode_weights(keep, wave_count):
    wavenumber = jnp.arange(wave_count, dtype=jnp.int32)
    scaled = jnp.where(wavenumber == 0, 1.0, 2.0).astype(jnp.float32) / NLON
    kept = jnp.where(
        wavenumber[None, :] < keep[:, None], scaled[None, :], jnp.zeros((), jnp.float32)
    )
    return jnp.concatenate([kept, kept], 1)


def add_terms(earlier, later):
    return earlier + later


def slot_layout(filter_rows, keep_counts, band_rows):
    band_index = jnp.arange(band_rows, dtype=jnp.int32)
    rows_here = lax.axis_index("lat") * band_rows + band_index
    matches = rows_here[:, None] == filter_rows[None, :]
    flagged = jnp.any(matches, 1)
    keep_here = jnp.sum(jnp.where(matches, keep_counts[None, :], 0), 1)
    row_rank = jnp.cumsum(flagged.astype(jnp.int32)) - 1
    slot_count = band_rows // 2
    chosen = flagged[None, :] & (
        row_rank[None, :] == jnp.arange(slot_count, dtype=jnp.int32)[:, None]
    )
    slot_row = jnp.sum(jnp.where(chosen, band_index[None, :], 0), 1)
    slot_keep = jnp.sum(jnp.where(chosen, keep_here[None, :], 0), 1)
    slot_live = jnp.any(chosen, 1).astype(jnp.float32)
    return (slot_row, slot_keep, slot_live)


def one_step(fields, surface, geometry, slot_row, slot_keep, slot_live):
    lev_count, band_rows, columns = (fields.shape[1], fields.shape[2], fields.shape[3])
    weight = layer_weight(fields)
    below_here = jnp.flip(jnp.cumsum(jnp.flip(weight, 0), 0), 0) - weight
    column = jnp.sum(weight, 0)
    beneath = carried_in(column, "lev", add_terms, jnp.zeros_like(column))
    geopot = surface[None] + beneath[None] + below_here + 0.5 * weight
    stacked = jnp.concatenate([fields, geopot[None]], 0)
    widened = extended(stacked, (("lon", 3),), 1, True)
    padded = extended(widened, (("lat", 2),), 1, False)
    updated = advance(padded, geometry)
    slot_count = slot_row.shape[0]
    picked = jnp.take(updated, slot_row, axis=2).reshape(4 * lev_count, slot_count, columns)
    waves = wave_table(lax.axis_index("lon") * columns, columns, KMAX)
    spectra = jnp.einsum("vrn,nk->vrk", picked, waves, precision=PRECISE)
    spectra = lax.psum(spectra, "lon")
    smooth = jnp.einsum(
        "vrk,nk->vrn", spectra * mode_weights(slot_keep, KMAX), waves, precision=PRECISE
    )
    change = (DAMPING - 1.0) * (picked - smooth) * slot_live[:, None]
    change = change.reshape(4, lev_count, slot_count, columns)
    return updated.at[:, :, slot_row, :].add(change)


def local(fields, surface, filter_rows, keep_counts):
    band_rows = fields.shape[2]
    geometry = row_geometry(
        lax.axis_index("lat") * band_rows + jnp.arange(band_rows, dtype=jnp.int32)
    )
    slot_row, slot_keep, slot_live = slot_layout(filter_rows, keep_counts, band_rows)
    for count in range(STEPS):
        fields = one_step(fields, surface, geometry, slot_row, slot_keep, slot_live)
    return fields


def solution(mesh):
    in_specs = (P(None, "lev", "lat", "lon"), P("lat", "lon"), P(), P())
    out_specs = P(None, "lev", "lat", "lon")
    return jax.shard_map(local, mesh=mesh, in_specs=in_specs, out_specs=out_specs, check_vma=False)
```

profile of v0, /device:TPU:8, one launch (start us, length us, event | category | flops | bytes accessed | tf_op | source)
XLA Modules:
  0.0 164.6 jit_solution(12533228920907565269)
XLA Ops:
  6.5 1.5 copy.11
  8.3 4.9 %all-gather = f32[16,1800]{1,0:T(8,128)S(1)} all-gather(f32[8,1800]{1,0:T(8,128)S(1)} %get-tuple-element.280), channel_id=2, replica_groups=mesh['lon'=4,'lat'=4,'lev'=2] {'lev'}, dimensions={0}, use_global_device_ids=true | all-gather | bytes 172800 | tf_op jit(solution)/shard_map/all_gather | solution.py:24
  19.5 1.3 pad_maximum_fusion
  21.4 5.0 %fusion.7 = (f32[1800,128]{1,0:T(8,128)S(1)}, f32[1800,128]{1,0:T(8,128)}) fusion(s32[1800]{0:T(1024)S(1)} %iota_add_fusion), kind=kLoop, calls=%fused_computation.30 | loop fusion | flops 2073600 | bytes 1850400 | tf_op jit(solution)/shard_map/cos | solution.py:134
  27.0 3.2 %concatenate.72 = f32[5,4,8,1802]{3,1,2,0:T(4,128)S(1)} concatenate(f32[5,4,8,1]{3,1,2,0:T(4,128)S(1)} %collective-permute-done.1, f32[5,4,8,1800]{3,1,2,0:T(4,128)} %pad_maximum_fusion, f32[5,4,8,1]{3,1,2,0:T(4,128)S(1)} %collective-permute-done), dimensions={3} | concatenate | bytes 2306560 | tf_op jit(solution)/shard_map/concatenate | solution.py:47
  30.3 1.9 %collective-permute-start.3 = (f32[5,4,1,1802]{3,1,2,0:T(4,128)S(1)}, f32[5,4,1,1802]{3,1,2,0:T(4,128)S(1)}, u32[]{:S(2)}, u32[]{:S(2)}) collective-permute-start(f32[5,4,1,1802]{3,1,2,0:T(4,128)S(1)} %get-tuple-element.286), channel_id=1, source_target_pairs={{2,0},{4,2},{6,4},{3,1},{5,3},{7,5},{10,8},{12,10},{14,12},{11,9},... | collective-permute-start | bytes 432488 | tf_op jit(solution)/shard_map/ppermute | solution.py:46
  32.9 3.9 %collective-permute-start.2 = (f32[5,4,1,1802]{3,1,2,0:T(4,128)S(1)}, f32[5,4,1,1802]{3,1,2,0:T(4,128)S(1)}, u32[]{:S(2)}, u32[]{:S(2)}) collective-permute-start(f32[5,4,1,1802]{3,1,2,0:T(4,128)S(1)} %get-tuple-element.287), channel_id=1, source_target_pairs={{0,2},{2,4},{4,6},{1,3},{3,5},{5,7},{8,10},{10,12},{12,14},{9,11},... | collective-permute-start | bytes 432488 | tf_op jit(solution)/shard_map/ppermute | solution.py:43
  36.8 2.0 %collective-permute-done.3 = f32[5,4,1,1802]{3,1,2,0:T(4,128)S(1)} collective-permute-done((f32[5,4,1,1802]{3,1,2,0:T(4,128)S(1)}, f32[5,4,1,1802]{3,1,2,0:T(4,128)S(1)}, u32[]{:S(2)}, u32[]{:S(2)}) %collective-permute-start.3) | collective-permute-done | bytes 144192 | tf_op jit(solution)/shard_map/ppermute | solution.py:46
  39.9 1.4 collective-permute-done.2
  47.1 1.7 %fusion.10 = f32[16,4,256]{2,0,1:T(8,128)} fusion(f32[16,4,1800]{2,0,1:T(8,128)S(1)} %reshape.147, f32[1800,128]{1,0:T(8,128)S(1)} %copy-done, f32[1800,128]{1,0:T(8,128)S(1)} %get-tuple-element.290), kind=kOutput, calls=%fused_computation.33 | convolution fusion | flops 354355200 | bytes 2369536 | tf_op jit(solution)/shard_map/vrn,nk->vrk/dot_general | solution.py:181
  48.9 32.0 %all-reduce.3.cloned.1.call-done = f32[16,4,256]{2,0,1:T(8,128)} async-done(((f32[16,4,256]{2,0,1:T(8,128)}), f32[16,4,256]{2,0,1:T(8,128)}) %all-reduce.3.cloned.1.call-update) | async-done | bytes 65552 | tf_op jit(solution)/shard_map/psum | solution.py:182
  80.9 3.4 %fusion.1 = f32[16,4,1800]{2,0,1:T(8,128)} fusion(f32[16,4,1800]{2,0,1:T(8,128)S(1)} %reshape.147, f32[1800,128]{1,0:T(8,128)S(1)} %copy-done, f32[1800,128]{1,0:T(8,128)S(1)} %get-tuple-element.290, f32[4]{0:T(128)S(1)} %copy-done.8, f32[16,4,256]{2,0,1:T(8,128)} %all-reduce.3.cloned.1.call-done, f32[4,256]{1,0:T(4,128)S(1)} %pad_maximum_fusion.20), kind=kOutput, calls=%fused_computation.9 | convolution fusion | flops 354601984 | bytes 2834448 | tf_op jit(solution)/shard_map/vrk,nk->vrn/dot_general | solution.py:183
  87.0 5.1 %all-gather.1 = f32[16,1800]{1,0:T(8,128)S(1)} all-gather(f32[8,1800]{1,0:T(8,128)S(1)} %get-tuple-element.276), channel_id=3, replica_groups=mesh['lon'=4,'lat'=4,'lev'=2] {'lev'}, dimensions={0}, use_global_device_ids=true | all-gather | bytes 172800 | tf_op jit(solution)/shard_map/all_gather | solution.py:24
  94.7 1.3 pad_maximum_fusion.1
  98.1 3.2 %concatenate.80 = f32[5,4,8,1802]{3,1,2,0:T(4,128)S(1)} concatenate(f32[5,4,8,1]{3,1,2,0:T(4,128)S(1)} %collective-permute-done.5, f32[5,4,8,1800]{3,1,2,0:T(4,128)} %pad_maximum_fusion.1, f32[5,4,8,1]{3,1,2,0:T(4,128)S(1)} %collective-permute-done.4), dimensions={3} | concatenate | bytes 2306560 | tf_op jit(solution)/shard_map/concatenate | solution.py:47
  101.4 3.4 %collective-permute-start.6 = (f32[5,4,1,1802]{3,1,2,0:T(4,128)S(1)}, f32[5,4,1,1802]{3,1,2,0:T(4,128)S(1)}, u32[]{:S(2)}, u32[]{:S(2)}) collective-permute-start(f32[5,4,1,1802]{3,1,2,0:T(4,128)S(1)} %get-tuple-element.283), channel_id=1, source_target_pairs={{0,2},{2,4},{4,6},{1,3},{3,5},{5,7},{8,10},{10,12},{12,14},{9,11},... | collective-permute-start | bytes 432488 | tf_op jit(solution)/shard_map/ppermute | solution.py:43
  104.8 2.5 %collective-permute-start.7 = (f32[5,4,1,1802]{3,1,2,0:T(4,128)S(1)}, f32[5,4,1,1802]{3,1,2,0:T(4,128)S(1)}, u32[]{:S(2)}, u32[]{:S(2)}) collective-permute-start(f32[5,4,1,1802]{3,1,2,0:T(4,128)S(1)} %get-tuple-element.282), channel_id=1, source_target_pairs={{2,0},{4,2},{6,4},{3,1},{5,3},{7,5},{10,8},{12,10},{14,12},{11,9},... | collective-permute-start | bytes 432488 | tf_op jit(solution)/shard_map/ppermute | solution.py:46
  107.3 1.2 collective-permute-done.6
  108.5 1.3 fusion.47
  109.8 2.1 %collective-permute-done.7 = f32[5,4,1,1802]{3,1,2,0:T(4,128)S(1)} collective-permute-done((f32[5,4,1,1802]{3,1,2,0:T(4,128)S(1)}, f32[5,4,1,1802]{3,1,2,0:T(4,128)S(1)}, u32[]{:S(2)}, u32[]{:S(2)}) %collective-permute-start.7) | collective-permute-done | bytes 144192 | tf_op jit(solution)/shard_map/ppermute | solution.py:46
  117.6 1.7 %fusion.9 = f32[16,4,256]{2,0,1:T(8,128)} fusion(f32[16,4,1800]{2,0,1:T(8,128)S(1)} %reshape.149, f32[1800,128]{1,0:T(8,128)S(1)} %copy-done.1, f32[1800,128]{1,0:T(8,128)S(1)} %get-tuple-element.290), kind=kOutput, calls=%fused_computation.32 | convolution fusion | flops 354355200 | bytes 2369536 | tf_op jit(solution)/shard_map/vrn,nk->vrk/dot_general | solution.py:181
  119.3 31.6 %all-reduce.5.cloned.1.call-done = f32[16,4,256]{2,0,1:T(8,128)} async-done(((f32[16,4,256]{2,0,1:T(8,128)}), f32[16,4,256]{2,0,1:T(8,128)}) %all-reduce.5.cloned.1.call-update) | async-done | bytes 65552 | tf_op jit(solution)/shard_map/psum | solution.py:182
  151.0 3.4 %fusion = f32[16,4,1800]{2,0,1:T(8,128)} fusion(f32[16,4,1800]{2,0,1:T(8,128)S(1)} %reshape.149, f32[1800,128]{1,0:T(8,128)S(1)} %copy-done.1, f32[1800,128]{1,0:T(8,128)S(1)} %get-tuple-element.290, f32[4]{0:T(128)S(1)} %copy-done.9, f32[16,4,256]{2,0,1:T(8,128)} %all-reduce.5.cloned.1.call-done, f32[4,256]{1,0:T(4,128)S(1)} %pad_maximum_fusion.20), kind=kOutput, calls=%fused_computation.7 | convolution fusion | flops 354601984 | bytes 2834448 | tf_op jit(solution)/shard_map/vrk,nk->vrn/dot_general | solution.py:183
  155.6 1.2 scatter_fusion.1
  (120 shorter events, 30.5 us)
Async XLA Ops:
  6.5 74.4 %all-reduce.3.cloned.1.call-start = ((), (), s32[]{:S(2)}) async-start(), calls=%async_computation | async-start | bytes 131072 | tf_op jit(solution)/shard_map/psum | solution.py:182
  13.2 1.8 %copy-start.2 = (f32[8,1800]{1,0:T(8,128)S(1)}, f32[8,1800]{1,0:T(8,128)}, u32[]{:S(2)}) copy-start(f32[8,1800]{1,0:T(8,128)} %param.11) | copy-start | bytes 172804
  15.2 11.8 %collective-permute-start = (f32[5,4,8,1]{3,1,2,0:T(4,128)S(1)}, f32[5,4,8,1]{3,1,2,0:T(4,128)S(1)}, u32[]{:S(2)}, u32[]{:S(2)}) collective-permute-start(f32[5,4,8,1]{3,1,2,0:T(4,128)S(1)} %get-tuple-element.288), channel_id=1, source_target_pairs={{8,0},{16,8},{24,16},{0,24},{9,1},{17,9},{25,17},{1,25},{10,2},{18... | collective-permute-start | bytes 1928 | tf_op jit(solution)/shard_map/ppermute | solution.py:46
  15.3 11.7 %collective-permute-start.1 = (f32[5,4,8,1]{3,1,2,0:T(4,128)S(1)}, f32[5,4,8,1]{3,1,2,0:T(4,128)S(1)}, u32[]{:S(2)}, u32[]{:S(2)}) collective-permute-start(f32[5,4,8,1]{3,1,2,0:T(4,128)S(1)} %get-tuple-element.289), channel_id=1, source_target_pairs={{0,8},{8,16},{16,24},{24,0},{1,9},{9,17},{17,25},{25,1},{2,10},{10... | collective-permute-start | bytes 1928 | tf_op jit(solution)/shard_map/ppermute | solution.py:43
  30.3 8.5 %collective-permute-start.3 = (f32[5,4,1,1802]{3,1,2,0:T(4,128)S(1)}, f32[5,4,1,1802]{3,1,2,0:T(4,128)S(1)}, u32[]{:S(2)}, u32[]{:S(2)}) collective-permute-start(f32[5,4,1,1802]{3,1,2,0:T(4,128)S(1)} %get-tuple-element.286), channel_id=1, source_target_pairs={{2,0},{4,2},{6,4},{3,1},{5,3},{7,5},{10,8},{12,10},{14,12},{11,9},... | collective-permute-start | bytes 432488 | tf_op jit(solution)/shard_map/ppermute | solution.py:46
  32.3 10.6 %copy-start.18 = (f32[8]{0:T(128)}, f32[8]{0:T(128)S(1)}, u32[]{:S(2)}) copy-start(f32[8]{0:T(128)S(1)} %fusion.112) | copy-start | bytes 100
  32.9 11.2 %copy-start.4 = (s32[1024]{0:T(1024)}, s32[1024]{0:T(1024)S(1)}, u32[]{:S(2)}) copy-start(s32[1024]{0:T(1024)S(1)} %pad_clamp_fusion) | copy-start | bytes 12292
  32.9 8.4 %collective-permute-start.2 = (f32[5,4,1,1802]{3,1,2,0:T(4,128)S(1)}, f32[5,4,1,1802]{3,1,2,0:T(4,128)S(1)}, u32[]{:S(2)}, u32[]{:S(2)}) collective-permute-start(f32[5,4,1,1802]{3,1,2,0:T(4,128)S(1)} %get-tuple-element.287), channel_id=1, source_target_pairs={{0,2},{2,4},{4,6},{1,3},{3,5},{5,7},{8,10},{10,12},{12,14},{9,11},... | collective-permute-start | bytes 432488 | tf_op jit(solution)/shard_map/ppermute | solution.py:43
  38.8 2.5 %copy-start.16 = (f32[8]{0:T(128)S(1)}, f32[8]{0:T(128)}, u32[]{:S(2)}) copy-start(f32[8]{0:T(128)} %get-tuple-element.296) | copy-start | bytes 100
  45.0 2.2 %copy-start = (f32[1800,128]{1,0:T(8,128)S(1)}, f32[1800,128]{1,0:T(8,128)}, u32[]{:S(2)}) copy-start(f32[1800,128]{1,0:T(8,128)} %get-tuple-element.291) | copy-start | bytes 2764804
  47.1 33.8 %copy-start.8 = (f32[4]{0:T(128)S(1)}, f32[4]{0:T(128)}, u32[]{:S(2)}) copy-start(f32[4]{0:T(128)} %broadcast_select_fusion) | copy-start | bytes 52
  48.9 102.1 %all-reduce.5.cloned.1.call-start = ((), (), s32[]{:S(2)}) async-start(), calls=%async_computation.1 | async-start | bytes 131072 | tf_op jit(solution)/shard_map/psum | solution.py:182
  48.9 36.6 %copy-start.7 = (s32[4]{0:T(128)S(1)}, s32[4]{0:T(128)}, u32[]{:S(2)}) copy-start(s32[4]{0:T(128)} %fusion.107) | copy-start | bytes 52
  86.8 5.4 %copy-start.3 = (f32[8,1800]{1,0:T(8,128)S(1)}, f32[8,1800]{1,0:T(8,128)}, u32[]{:S(2)}) copy-start(f32[8,1800]{1,0:T(8,128)} %param.11) | copy-start | bytes 172804
  94.2 2.9 %collective-permute-start.4 = (f32[5,4,8,1]{3,1,2,0:T(4,128)S(1)}, f32[5,4,8,1]{3,1,2,0:T(4,128)S(1)}, u32[]{:S(2)}, u32[]{:S(2)}) collective-permute-start(f32[5,4,8,1]{3,1,2,0:T(4,128)S(1)} %get-tuple-element.284), channel_id=1, source_target_pairs={{8,0},{16,8},{24,16},{0,24},{9,1},{17,9},{25,17},{1,25},{10,2},{18... | collective-permute-start | bytes 1928 | tf_op jit(solution)/shard_map/ppermute | solution.py:46
  94.2 3.9 %collective-permute-start.5 = (f32[5,4,8,1]{3,1,2,0:T(4,128)S(1)}, f32[5,4,8,1]{3,1,2,0:T(4,128)S(1)}, u32[]{:S(2)}, u32[]{:S(2)}) collective-permute-start(f32[5,4,8,1]{3,1,2,0:T(4,128)S(1)} %get-tuple-element.285), channel_id=1, source_target_pairs={{0,8},{8,16},{16,24},{24,0},{1,9},{9,17},{17,25},{25,1},{2,10},{10... | collective-permute-start | bytes 1928 | tf_op jit(solution)/shard_map/ppermute | solution.py:43
  101.4 7.1 %collective-permute-start.6 = (f32[5,4,1,1802]{3,1,2,0:T(4,128)S(1)}, f32[5,4,1,1802]{3,1,2,0:T(4,128)S(1)}, u32[]{:S(2)}, u32[]{:S(2)}) collective-permute-start(f32[5,4,1,1802]{3,1,2,0:T(4,128)S(1)} %get-tuple-element.283), channel_id=1, source_target_pairs={{0,2},{2,4},{4,6},{1,3},{3,5},{5,7},{8,10},{10,12},{12,14},{9,11},... | collective-permute-start | bytes 432488 | tf_op jit(solution)/shard_map/ppermute | solution.py:43
  104.8 7.1 %copy-start.12 = (f32[8]{0:T(128)S(1)}, f32[8]{0:T(128)}, u32[]{:S(2)}) copy-start(f32[8]{0:T(128)} %get-tuple-element.292) | copy-start | bytes 100
  104.8 7.1 %copy-start.14 = (f32[8]{0:T(128)S(1)}, f32[8]{0:T(128)}, u32[]{:S(2)}) copy-start(f32[8]{0:T(128)} %get-tuple-element.293) | copy-start | bytes 100
  104.8 7.1 %copy-start.19 = (f32[8]{0:T(128)S(1)}, f32[8]{0:T(128)}, u32[]{:S(2)}) copy-start(f32[8]{0:T(128)} %copy-done.18) | copy-start | bytes 100
  104.8 7.1 %collective-permute-start.7 = (f32[5,4,1,1802]{3,1,2,0:T(4,128)S(1)}, f32[5,4,1,1802]{3,1,2,0:T(4,128)S(1)}, u32[]{:S(2)}, u32[]{:S(2)}) collective-permute-start(f32[5,4,1,1802]{3,1,2,0:T(4,128)S(1)} %get-tuple-element.282), channel_id=1, source_target_pairs={{2,0},{4,2},{6,4},{3,1},{5,3},{7,5},{10,8},{12,10},{14,12},{11,9},... | collective-permute-start | bytes 432488 | tf_op jit(solution)/shard_map/ppermute | solution.py:46
  109.8 3.1 %copy-start.17 = (f32[8]{0:T(128)S(1)}, f32[8]{0:T(128)}, u32[]{:S(2)}) copy-start(f32[8]{0:T(128)} %get-tuple-element.296) | copy-start | bytes 100
  115.4 2.2 %copy-start.1 = (f32[1800,128]{1,0:T(8,128)S(1)}, f32[1800,128]{1,0:T(8,128)}, u32[]{:S(2)}) copy-start(f32[1800,128]{1,0:T(8,128)} %get-tuple-element.291) | copy-start | bytes 2764804
  117.6 33.4 %copy-start.9 = (f32[4]{0:T(128)S(1)}, f32[4]{0:T(128)}, u32[]{:S(2)}) copy-start(f32[4]{0:T(128)} %broadcast_select_fusion) | copy-start | bytes 52
  (8 other events, 7.3 us)
Sparse Core Ops, SparseCore 0:
  49.0 31.9 all-reduce.2
  119.5 31.4 all-reduce.4
where the time goes:
time: 167 us; the launch traced here: 165 us
  waiting for transfers between devices  72.5 us (43%)
  other arithmetic  26.8 us (16%)
  local copies, waits for them, and re-layouts  18.3 us (11%)
  between operations  14 us (8%)
  starting transfers between devices  12.8 us (8%)
  matrix products  10.3 us (6%)
  blocking collectives  9.98 us (6%)
    psum x2, waiting for transfers between devices, one_step(): spectra = lax.psum(spectra, 'lon')  63.6 us
    all_gather x2, blocking collectives, carried_in(): everything = lax.all_gather(value, axis)  9.98 us
    ppermute x4, starting transfers between devices, extended(): lax.ppermute(lax.slice_in_dim(block, block.shape[dim] - width, None, axis...  8.3 us
    dot_general x2, matrix products, one_step(): jnp.einsum('vrk,nk->vrn', spectra * mode_weights(slot_keep, KMAX), waves,...  6.85 us
    concatenate x2, local copies, waits for them, and re-layouts, extended(): block = jnp.concatenate([low, block, high], axis=dim)  6.39 us
    ppermute x4, waiting for transfers between devices, extended(): lax.ppermute(lax.slice_in_dim(block, 0, width, axis=dim), axis, backward)  5.13 us
    cos x1, other arithmetic, wave_table(): return jnp.concatenate([jnp.cos(angles), jnp.sin(angles)], 1)  4.97 us
    ppermute x4, starting transfers between devices, extended(): lax.ppermute(lax.slice_in_dim(block, 0, width, axis=dim), axis, backward)  4.48 us
  transfers between devices with their start and end apart: 10, of which 8 were waited for; matrix products, arithmetic and copies ran while one was open for 9% of the time, Pallas kernels for 0%

commit v1 on v0

v1 whole, which is shorter than its diff:
```python
import functools

import jax
import jax.numpy as jnp
import ml_dtypes
import numpy as np
from jax import lax
from jax.experimental import pallas as pl
from jax.experimental.pallas import tpu as pltpu
from jax.sharding import PartitionSpec as P

KMAX = 128
GRAVITY_SCALE = 0.05
BUOYANCY = 0.5
CORIOLIS = 0.3
ZONAL_COEF = 0.08
NORTH_COEF = 0.2
DAMPING = 0.25
FIRST_LAT = -70.0
ROW_STEP = 0.05
LANES = 128
VMEM_LIMIT = 24 * 1024 * 1024


def layer_weight(h, t):
    return GRAVITY_SCALE * (1.0 + h) * (1.0 + BUOYANCY * t)


def east(x):
    return pltpu.roll(x, x.shape[1] - 1, 1)


def west(x):
    return pltpu.roll(x, 1, 1)


def rows_up(x):
    return pltpu.roll(x, x.shape[0] - 1, 0)


def rows_down(x):
    return pltpu.roll(x, 1, 0)


def row_iota(x):
    return lax.broadcasted_iota(jnp.int32, x.shape, 0)


def with_last(x, row):
    return jnp.where(row_iota(x) == x.shape[0] - 1, jnp.broadcast_to(row, x.shape), rows_up(x))


def with_first(x, row):
    return jnp.where(row_iota(x) == 0, jnp.broadcast_to(row, x.shape), rows_down(x))


def wide(geom, k, lo, hi, width):
    return jnp.concatenate([geom[k, lo:hi, :]] * (width // LANES), 1)


class Sizes:
    def __init__(self, mesh, fields_shape, filter_count):
        _, levels, rows, columns = fields_shape
        self.n_lon, self.n_lat, self.n_lev = (mesh.shape[a] for a in ("lon", "lat", "lev"))
        self.L = levels // self.n_lev
        self.R = rows // self.n_lat
        self.C = columns // self.n_lon
        self.N = columns
        self.W = -(-(self.C + 4) // LANES) * LANES
        self.slots = filter_count // self.n_lat
        self.filters = filter_count
        self.planes = 4 * self.L + 1
        self.base = (self.C - 1) // LANES * LANES
        self.tiles = self.W // LANES
        self.extra = -(-self.tiles // self.R)
        self.lat_rows = -(-(7 * self.L + 1) // 8) * 8
        assert self.R == 2 * self.L and self.n_lon % 2 == 0
        assert 2 <= self.C - self.base <= LANES - 2 and 2 * self.planes <= LANES


def pack_edges(z, fhead, ftail, shead, stail, m1, m2):
    lane = lax.broadcasted_iota(jnp.int32, (z.R, LANES), 1)
    left = jnp.zeros((z.R, LANES), jnp.float32)
    right = left
    first = z.C - 2 - z.base
    for p in range(z.planes):
        f, l = divmod(p, z.L)
        head = fhead[f, l] if p < 4 * z.L else shead[...]
        tail = ftail[f, l] if p < 4 * z.L else stail[...]
        here = (lane >= 2 * p) & (lane < 2 * p + 2)
        left = jnp.where(here, pltpu.roll(head, 2 * p, 1) if p else head, left)
        shift = (2 * p - first) % LANES
        right = jnp.where(here, pltpu.roll(tail, shift, 1) if shift else tail, right)
    even = lax.axis_index("lon") % 2 == 0

    @pl.when(even)
    def _():
        m1[...] = right
        m2[...] = left

    @pl.when(jnp.logical_not(even))
    def _():
        m1[...] = left
        m2[...] = right


def widen(z, fields, surface, r1, r2, x, m1, m2, sums, from_right, from_left):
    lon_even = lax.axis_index("lon") % 2 == 0

    @pl.when(lon_even)
    def _():
        from_right[...] = r1[...]
        from_left[...] = r2[...]

    @pl.when(jnp.logical_not(lon_even))
    def _():
        from_right[...] = r2[...]
        from_left[...] = r1[...]

    lane = lax.broadcasted_iota(jnp.int32, (z.R, LANES), 1)
    last = z.C - z.base
    fr, fl = from_right[...], from_left[...]
    for p in range(z.planes):
        f, l = divmod(p, z.L)
        if p < 4 * z.L:
            x[p, :, 0 : z.C] = fields[f, l]
        else:
            x[p, :, 0 : z.C] = surface[...]
        for start in range(z.base, z.W, LANES):
            if start == z.base:
                tile = jnp.where(lane < last, x[p, :, start : start + LANES], 0.0)
                shift = (last - 2 * p) % LANES
                moved = pltpu.roll(fr, shift, 1) if shift else fr
                tile = jnp.where((lane >= last) & (lane < last + 2), moved, tile)
            else:
                tile = jnp.zeros((z.R, LANES), jnp.float32)
            if start == z.W - LANES:
                moved = pltpu.roll(fl, LANES - 2 - 2 * p, 1)
                tile = jnp.where(lane >= LANES - 2, moved, tile)
            x[p, :, start : start + LANES] = tile

    lat_even = lax.axis_index("lat") % 2 == 0
    near1 = jnp.where(lat_even, z.R - 1, 0)
    far1 = jnp.where(lat_even, z.R - 2, 1)
    for msg, near, far in ((m1, near1, far1), (m2, z.R - 1 - near1, z.R - 1 - far1)):
        for p in range(4 * z.L):
            msg[p : p + 1, :] = x[p, pl.ds(near, 1), :]
        for p in range(z.L, 4 * z.L):
            to = 3 * z.L + p
            msg[to : to + 1, :] = x[p, pl.ds(far, 1), :]
        to = 7 * z.L
        msg[to : to + 1, :] = x[4 * z.L, pl.ds(near, 1), :]
        if z.lat_rows > to + 1:
            msg[to + 1 :, :] = jnp.zeros((z.lat_rows - to - 1, z.W), jnp.float32)
    total = layer_weight(x[2 * z.L], x[3 * z.L])
    for l in range(1, z.L):
        total = total + layer_weight(x[2 * z.L + l], x[3 * z.L + l])
    sums[...] = total


def put_column_sums(z, msg, total, south, north):
    if total is not None:
        msg[:, 0 : z.W] = total
    for d, row in enumerate((south, north)):
        for t in range(z.tiles):
            at = z.W + (d * z.extra + t // z.R) * LANES
            msg[t % z.R : t % z.R + 1, at : at + LANES] = row[:, t * LANES : (t + 1) * LANES]


def ring_sum(z, w):
    south = w[0:1]
    north = w[z.L : z.L + 1]
    for l in range(1, z.L):
        south = south + w[l : l + 1]
        north = north + w[z.L + l : z.L + l + 1]
    return south, north


def halo_rows(z, sums, r1, r2, ring, ring_surface, msg):
    lat_even = lax.axis_index("lat") % 2 == 0

    def place(d, source):
        for k in range(7):
            ring[k, d * z.L : (d + 1) * z.L, :] = source[k * z.L : (k + 1) * z.L, :]
        ring_surface[d * z.L : (d + 1) * z.L, :] = jnp.broadcast_to(
            source[7 * z.L : 7 * z.L + 1, :], (z.L, z.W)
        )

    @pl.when(lat_even)
    def _():
        place(0, r2)
        place(1, r1)

    @pl.when(jnp.logical_not(lat_even))
    def _():
        place(0, r1)
        place(1, r2)

    south, north = ring_sum(z, layer_weight(ring[2], ring[3]))
    put_column_sums(z, msg, sums[...], south, north)


def in_band(z, shape):
    lat = lax.axis_index("lat")
    row = lax.broadcasted_iota(jnp.int32, shape, 0)
    south = jnp.where(lat > 0, 1.0, 0.0)
    north = jnp.where(lat < z.n_lat - 1, 1.0, 0.0)
    return jnp.where(row < z.L, south, north)


def ring_geopot(z, h, t):
    w = layer_weight(h, t)
    row = row_iota(w)
    level = jnp.where(row < z.L, row, row - z.L)
    q = 0.5 * w
    for s in range(1, z.L):
        q = q + jnp.where(level < z.L - s, pltpu.roll(w, 2 * z.L - s, 0), 0.0)
    return q * in_band(z, w.shape)


def tendencies(coef, u, v, h, t, un, vs, hn, hs, tn, ts, q, qn, which="uvht"):
    zonal, cor, corn, north, south = coef
    out = {}
    if "u" in which:
        a = v + vs
        out["u"] = u + cor * (a + east(a)) - zonal * (east(q) - q)
    if "v" in which:
        b = u + un
        out["v"] = v - corn * (b + west(b)) - NORTH_COEF * (qn - q)
    if "h" in which:
        flux = u * (2.0 + h + east(h)) * 0.5
        out["h"] = (
            h
            - zonal * (flux - west(flux))
            - (north * (v * (2.0 + h + hn) * 0.5) - south * (vs * (2.0 + hs + h) * 0.5))
        )
    if "t" in which:
        out["t"] = (
            t
            - 0.25 * (u + west(u)) * zonal * (east(t) - west(t))
            - (0.25 * NORTH_COEF) * (v + vs) * (tn - ts)
        )
    return out


def advance_tile(z, geom, get, un_row, vs_row, h_ring, t_ring, q_ring, put, qput=None):
    coef = [wide(geom, k, 0, z.R, z.W) for k in range(5)]
    below = None
    for l in reversed(range(z.L)):
        u, v, h, t = (get(f, l) for f in range(4))
        w = layer_weight(h, t)
        q = 0.5 * w if below is None else below + 0.5 * w
        below = w if below is None else below + w
        s, n = l, z.L + l
        new = tendencies(
            coef, u, v, h, t,
            with_last(u, un_row(l)), with_first(v, vs_row(l)),
            with_last(h, h_ring[n : n + 1, :]), with_first(h, h_ring[s : s + 1, :]),
            with_last(t, t_ring[n : n + 1, :]), with_first(t, t_ring[s : s + 1, :]),
            q, with_last(q, q_ring[n : n + 1, :]),
        )
        for f, name in enumerate("uvht"):
            put(f, l, new[name])
        if qput is not None:
            qput(l, q)


def first_step(z, x, ring, geom, y, yring, inner, q_ring):
    L = z.L
    q_ring[...] = ring_geopot(z, ring[2], ring[3])

    def get(f, l):
        return x[f * L + l]

    def put(f, l, value):
        y[f * L + l] = value

    def qput(l, q):
        inner[3, l : l + 1, :] = q[0:1]

    inner[3, L:, :] = jnp.zeros((L, z.W), jnp.float32)
    advance_tile(
        z, geom, get,
        lambda l: ring[0, L + l : L + l + 1, :], lambda l: ring[1, l : l + 1, :],
        ring.at[2], ring.at[3], q_ring, put, qput,
    )
    for l in range(L):
        inner[0, l : l + 1, :] = x[l, 0:1, :]
        inner[0, L + l : L + l + 1, :] = x[L + l, z.R - 1 : z.R, :]
        for k, f in ((1, 2), (2, 3)):
            inner[k, l : l + 1, :] = x[f * L + l, 0:1, :]
            inner[k, L + l : L + l + 1, :] = x[f * L + l, z.R - 1 : z.R, :]
    south = lax.broadcasted_iota(jnp.int32, (2 * L, z.W), 0) < L
    coef = [wide(geom, k, z.R, z.R + 2 * L, z.W) for k in range(5)]
    u, v, h, t = (ring[k] for k in range(4))
    new = tendencies(
        coef, u, v, h, t,
        inner[0], jnp.where(south, ring[4], inner[0]),
        jnp.where(south, inner[1], ring[5]), jnp.where(south, ring[5], inner[1]),
        jnp.where(south, inner[2], ring[6]), jnp.where(south, ring[6], inner[2]),
        q_ring[...], inner[3],
    )
    mask = in_band(z, (2 * L, z.W))
    yring[0] = jnp.where(south, new["v"], new["u"]) * mask
    yring[1] = new["h"] * mask
    yring[2] = new["t"] * mask


def level_part(z, surface, ring_surface, got):
    live = jnp.where(lax.axis_index("lev") < z.n_lev - 1, 1.0, 0.0)
    lat = lax.axis_index("lat")
    tile = surface + live * got[:, 0 : z.W]
    rows = []
    for d in range(2):
        there = jnp.where(lat > 0, 1.0, 0.0) if d == 0 else jnp.where(lat < z.n_lat - 1, 1.0, 0.0)
        parts = []
        for t in range(z.tiles):
            at = z.W + (d * z.extra + t // z.R) * LANES
            parts.append(got[t % z.R : t % z.R + 1, at : at + LANES])
        sums = jnp.concatenate(parts, 1)
        rows.append(there * (ring_surface[d * z.L : d * z.L + 1, :] + live * sums))
    return tile, rows[0], rows[1]


def split(x):
    high = x.astype(jnp.bfloat16)
    return high, (x - high.astype(jnp.float32)).astype(jnp.bfloat16)


def dot(a, b, dims):
    return lax.dot_general(a, b, (dims, ((), ())), preferred_element_type=jnp.float32)


def product(x, wh, wl, dims):
    high, low = split(x)
    return dot(high, wh[...], dims) + dot(low, wh[...], dims) + dot(high, wl[...], dims)


def spectra(z, x, wh, wl, phase):
    lane = lax.broadcasted_iota(jnp.int32, (x.shape[0], z.W - z.base), 1)
    tail = jnp.where(lane < z.C - z.base, x[:, z.base :], 0.0)
    if z.base:
        x = jnp.concatenate([x[:, : z.base], tail], 1)
    else:
        x = tail
    s = product(x, wh, wl, ((1,), (0,)))
    a, b = s[:, :KMAX], s[:, KMAX:]
    c, d = phase[0:1, :], phase[1:2, :]
    return jnp.concatenate([a * c - b * d, a * d + b * c], 1)


def slot_row(z, rows, s):
    lat = lax.axis_index("lat")
    return rows[lat * z.slots + s] - lat * z.R


def pick_spectra(z, full, rows, out):
    for s in range(z.slots):
        at = slot_row(z, rows, s)
        for p in range(4 * z.L):
            to = p * z.slots + s
            out[to : to + 1, :] = full[pl.ds(p * z.R + at, 1), :]


def first_spectra(z, y, yring, surface, ring_surface, got, geom, wh, wl, phase, rows, state, sring, out, full):
    L = z.L
    g, gs, gn = level_part(z, surface[...], ring_surface, got)
    du = wide(geom, 0, 0, z.R, z.W) * (east(g) - g)
    dv = NORTH_COEF * (with_last(g, gn) - g)
    for l in range(L):
        state[l] = y[l] - du
        state[L + l] = y[L + l] - dv
    for p in range(2 * L, 4 * L):
        state[p] = y[p]
    south = lax.broadcasted_iota(jnp.int32, (2 * L, z.W), 0) < L
    shape = (2 * L, z.W)
    du_north = wide(geom, 0, z.R, z.R + 2 * L, z.W) * jnp.broadcast_to(east(jnp.broadcast_to(gn, shape)) - gn, shape)
    dv_south = NORTH_COEF * jnp.broadcast_to(g[0:1] - gs, shape)
    sring[0] = yring[0] - jnp.where(south, dv_south, du_north) * in_band(z, shape)
    sring[1] = yring[1]
    sring[2] = yring[2]
    m = 4 * L * z.R
    everything = jnp.concatenate(
        [state[...].reshape(m, z.W), sring[...].reshape(6 * L, z.W)], 0
    )
    full[...] = spectra(z, everything, wh, wl, phase)
    pick_spectra(z, full, rows, out)
    out[4 * L * z.slots :, :] = full[m:, :]


def second_spectra(z, y, surface, ring_surface, got, geom, wh, wl, phase, rows, state, out, full):
    L = z.L
    g, _, gn = level_part(z, surface[...], ring_surface, got)
    du = wide(geom, 0, 0, z.R, z.W) * (east(g) - g)
    dv = NORTH_COEF * (with_last(g, gn) - g)
    for l in range(L):
        state[l] = y[l] - du
        state[L + l] = y[L + l] - dv
    for p in range(2 * L, 4 * L):
        state[p] = y[p]
    full[...] = spectra(z, state[...].reshape(4 * L * z.R, z.W), wh, wl, phase)
    pick_spectra(z, full, rows, out)


def mode_weight(z, keep):
    k = lax.broadcasted_iota(jnp.int32, keep.shape, 1)
    k = jnp.where(k < KMAX, k, k - KMAX)
    scale = jnp.where(k == 0, 1.0 / z.N, 2.0 / z.N)
    return jnp.where(k < keep, scale, 0.0)


def tile_keep(z, rows, keeps, width):
    lat = lax.axis_index("lat")
    r = lax.broadcasted_iota(jnp.int32, (z.R, width), 0)
    keep = jnp.zeros((z.R, width), jnp.int32)
    for s in range(z.slots):
        keep = jnp.where(r == slot_row(z, rows, s), keeps[lat * z.slots + s], keep)
    return keep


def ring_keep(z, rows, keeps, width):
    lat = lax.axis_index("lat")
    before = jnp.maximum(lat * z.slots - 1, 0)
    after = jnp.minimum((lat + 1) * z.slots, z.filters - 1)
    south = jnp.where((lat > 0) & (rows[before] == lat * z.R - 1), keeps[before], 0)
    north = jnp.where((lat < z.n_lat - 1) & (rows[after] == (lat + 1) * z.R), keeps[after], 0)
    r = lax.broadcasted_iota(jnp.int32, (2 * z.L, width), 0)
    return jnp.where(r < z.L, south, north)


def damping(keep):
    return jnp.where(keep > 0, 1.0 - DAMPING, 0.0)


def local_modes(total, phase):
    a, b = total[:, :KMAX], total[:, KMAX:]
    c, d = phase[0:1, :], phase[1:2, :]
    return jnp.concatenate([a * c + b * d, b * c - a * d], 1)


def tile_modes(z, modes, rows, weight, planes):
    r = lax.broadcasted_iota(jnp.int32, (z.R, 2 * KMAX), 0)
    out = []
    for p in planes:
        tile = jnp.zeros((z.R, 2 * KMAX), jnp.float32)
        for s in range(z.slots):
            row = modes[p * z.slots + s : p * z.slots + s + 1, :]
            tile = jnp.where(r == slot_row(z, rows, s), jnp.broadcast_to(row, tile.shape), tile)
        out.append(tile * weight)
    return out


def smooth(modes, wh, wl):
    return product(modes, wh, wl, ((1,), (1,)))


def filter_mass(z, state, sring, part, got, wh, wl, phase, rows, keeps, ht, htring, uvmodes, msg):
    L, m = z.L, 4 * z.L * z.slots
    modes = local_modes(part[...] + got[...], phase)
    keep = tile_keep(z, rows, keeps, 2 * KMAX)
    rkeep = ring_keep(z, rows, keeps, 2 * KMAX)
    weight, rweight = mode_weight(z, keep), mode_weight(z, rkeep)
    ring = [modes[m + k * 2 * L : m + (k + 1) * 2 * L] * rweight for k in range(3)]
    tiles = tile_modes(z, modes, rows, weight, range(4 * L))
    uvmodes[...] = jnp.concatenate(tiles[: 2 * L] + [ring[0]], 0)
    s = smooth(jnp.concatenate(tiles[2 * L :] + ring[1:], 0), wh, wl)
    damp = jnp.broadcast_to(damping(keep[:, 0:1]), (z.R, z.W))
    rdamp = jnp.broadcast_to(damping(rkeep[:, 0:1]), (2 * L, z.W))
    for p in range(2 * L):
        x = state[2 * L + p]
        ht[p] = x + damp * (s[p * z.R : (p + 1) * z.R] - x)
    for k in range(2):
        x = sring[1 + k]
        at = 2 * L * z.R + k * 2 * L
        htring[k] = x + rdamp * (s[at : at + 2 * L] - x)
    total = layer_weight(ht[0], ht[L])
    for l in range(1, L):
        total = total + layer_weight(ht[l], ht[L + l])
    south, north = ring_sum(z, layer_weight(htring[0], htring[1]))
    put_column_sums(z, msg, total, south, north)


def second_step(z, state, sring, uvmodes, ht, htring, geom, wh, wl, rows, keeps, y, uv, uvring, q_ring):
    L = z.L
    s = smooth(uvmodes[...], wh, wl)
    damp = jnp.broadcast_to(damping(tile_keep(z, rows, keeps, LANES)[:, 0:1]), (z.R, z.W))
    rdamp = jnp.broadcast_to(damping(ring_keep(z, rows, keeps, LANES)[:, 0:1]), (2 * L, z.W))
    for p in range(2 * L):
        x = state[p]
        uv[p] = x + damp * (s[p * z.R : (p + 1) * z.R] - x)
    x = sring[0]
    uvring[...] = x + rdamp * (s[2 * L * z.R :] - x)
    q_ring[...] = ring_geopot(z, htring[0], htring[1])

    def get(f, l):
        return uv[f * L + l] if f < 2 else ht[(f - 2) * L + l]

    def put(f, l, value):
        y[f * L + l] = value

    advance_tile(
        z, geom, get,
        lambda l: uvring[L + l : L + l + 1, :], lambda l: uvring[l : l + 1, :],
        htring.at[0], htring.at[1], q_ring, put,
    )


def filter_all(z, state, part, got, wh, wl, phase, rows, keeps, out):
    L = z.L
    modes = local_modes(part[...] + got[...], phase)
    keep = tile_keep(z, rows, keeps, 2 * KMAX)
    tiles = tile_modes(z, modes, rows, mode_weight(z, keep), range(4 * L))
    s = smooth(jnp.concatenate(tiles, 0), wh, wl)
    damp = jnp.broadcast_to(damping(keep[:, 0:1]), (z.R, z.W))
    for p in range(4 * L):
        f, l = divmod(p, L)
        x = state[p]
        new = x + damp * (s[p * z.R : (p + 1) * z.R] - x)
        out[f, l] = new[:, : z.C]


def local(z, wave_high, wave_low, fields, surface, filter_rows, keep_counts):
    L, R, W = z.L, z.R, z.W
    f32 = jnp.float32
    vmem = pl.BlockSpec(memory_space=pltpu.VMEM)
    smem = pl.BlockSpec(memory_space=pltpu.SMEM)

    def call(kernel, outs, ins, scratch=(), flops=1_000_000):
        size = sum(int(np.prod(s)) for s in outs) * 4 + sum(i.size * i.dtype.itemsize for i in ins)
        return pl.pallas_call(
            functools.partial(kernel, z),
            out_shape=[jax.ShapeDtypeStruct(s, f32) for s in outs],
            in_specs=[smem if i.dtype == jnp.int32 else vmem for i in ins],
            out_specs=[vmem] * len(outs),
            scratch_shapes=[pltpu.VMEM(s, f32) for s in scratch],
            compiler_params=pltpu.CompilerParams(vmem_limit_bytes=VMEM_LIMIT),
            cost_estimate=pl.CostEstimate(flops=flops, bytes_accessed=size, transcendentals=0),
            name=kernel.__name__,
        )(*ins)

    lat, lon = lax.axis_index("lat"), lax.axis_index("lon")
    index = lax.broadcasted_iota(jnp.int32, (R + 2 * L, LANES), 0)
    index = jnp.where(index < R, index, jnp.where(index < R + L, -1, R))
    based = (lat * R + index).astype(f32)
    to_radian = jnp.pi / 180.0
    middle = (FIRST_LAT + (based + 0.5) * ROW_STEP) * to_radian
    northern = (FIRST_LAT + (based + 1.0) * ROW_STEP) * to_radian
    southern = (FIRST_LAT + based * ROW_STEP) * to_radian
    cos_mid = jnp.cos(middle)
    geom = jnp.stack(
        [
            ZONAL_COEF / cos_mid,
            (0.25 * CORIOLIS) * jnp.sin(middle),
            (0.25 * CORIOLIS) * jnp.sin(northern),
            NORTH_COEF * jnp.cos(northern) / cos_mid,
            NORTH_COEF * jnp.cos(southern) / cos_mid,
        ]
    )
    turn = (lon * z.C * jnp.arange(KMAX, dtype=jnp.int32)) % z.N
    angle = turn.astype(f32) * (2.0 * jnp.pi / z.N)
    phase = jnp.stack([jnp.cos(angle), jnp.sin(angle)])

    def swaps(n):
        one = [(i, i ^ 1) for i in range(n)]
        return one

    lon_one = [(i, i ^ 1) for i in range(z.n_lon)]
    lon_two = [(i, (((i + 1) % z.n_lon ^ 1) - 1) % z.n_lon) for i in range(z.n_lon)]
    lat_one = [(i, i ^ 1) for i in range(z.n_lat) if i ^ 1 < z.n_lat]
    lat_two = [(i, ((i + 1) ^ 1) - 1) for i in range(1, z.n_lat) if ((i + 1) ^ 1) - 1 < z.n_lat]

    def from_below(column):
        if z.n_lev == 2:
            return lax.ppermute(column, "lev", [(0, 1), (1, 0)])
        place = lax.axis_index("lev")
        total = jnp.zeros_like(column)
        for s in range(1, z.n_lev):
            got = lax.ppermute(column, "lev", [(i, i - s) for i in range(s, z.n_lev)])
            total = total + jnp.where(place + s < z.n_lev, got, 0.0)
        return total

    def over_lon(part):
        got, step = None, 1
        while step < z.n_lon:
            if got is not None:
                part = part + got
            got = lax.ppermute(part, "lon", [(i, i ^ step) for i in range(z.n_lon)])
            step *= 2
        return part, got

    head = lambda i: (0, 0, 0, 0)
    tail = lambda i: (0, 0, 0, z.base // LANES)
    edge = pl.BlockSpec((R, LANES), lambda i: (0, 0))
    e1, e2 = pl.pallas_call(
        functools.partial(pack_edges, z),
        grid=(1,),
        out_shape=[jax.ShapeDtypeStruct((R, LANES), f32)] * 2,
        in_specs=[
            pl.BlockSpec((4, L, R, LANES), head),
            pl.BlockSpec((4, L, R, LANES), tail),
            edge,
            pl.BlockSpec((R, LANES), lambda i: (0, z.base // LANES)),
        ],
        out_specs=[edge] * 2,
        name="pack_edges",
    )(fields, fields, surface, surface)
    e1 = lax.ppermute(e1, "lon", lon_one)
    e2 = lax.ppermute(e2, "lon", lon_two)

    x, m1, m2, sums = call(
        widen,
        [(z.planes, R, W), (z.lat_rows, W), (z.lat_rows, W), (R, W)],
        [fields, surface, e1, e2],
        [(R, LANES)] * 2,
    )
    m1 = lax.ppermute(m1, "lat", lat_one)
    m2 = lax.ppermute(m2, "lat", lat_two)

    sent = (R, W + 2 * z.extra * LANES)
    ring, ring_surface, msg = call(
        halo_rows, [(7, 2 * L, W), (2 * L, W), sent], [sums, m1, m2]
    )
    got = from_below(msg)
    y, yring = call(
        first_step,
        [(4 * L, R, W), (3, 2 * L, W)],
        [x, ring, geom],
        [(4, 2 * L, W), (2 * L, W)],
        flops=10_000_000,
    )
    m = 4 * L * R
    surface_tile = x[4 * L]
    state, sring, part = call(
        first_spectra,
        [(4 * L, R, W), (3, 2 * L, W), (4 * L * z.slots + 6 * L, 2 * KMAX)],
        [y, yring, surface_tile, ring_surface, got, geom, wave_high, wave_low, phase, filter_rows],
        [(m + 6 * L, 2 * KMAX)],
    )
    part, got = over_lon(part)
    ht, htring, uvmodes, msg = call(
        filter_mass,
        [(2 * L, R, W), (2, 2 * L, W), (2 * L * R + 2 * L, 2 * KMAX), sent],
        [state, sring, part, got, wave_high, wave_low, phase, filter_rows, keep_counts],
    )
    got = from_below(msg)
    (y,) = call(
        second_step,
        [(4 * L, R, W)],
        [state, sring, uvmodes, ht, htring, geom, wave_high, wave_low, filter_rows, keep_counts],
        [(2 * L, R, W), (2 * L, W), (2 * L, W)],
        flops=10_000_000,
    )
    state, part = call(
        second_spectra,
        [(4 * L, R, W), (4 * L * z.slots, 2 * KMAX)],
        [y, surface_tile, ring_surface, got, geom, wave_high, wave_low, phase, filter_rows],
        [(m, 2 * KMAX)],
    )
    part, got = over_lon(part)
    (out,) = call(
        filter_all,
        [(4, L, R, z.C)],
        [state, part, got, wave_high, wave_low, phase, filter_rows, keep_counts],
    )
    return out


def wave_tables(z):
    lane = np.arange(z.W)
    j = np.where(lane >= z.W - 2, lane - z.W, lane)
    angle = 2.0 * np.pi * ((j[:, None] * np.arange(KMAX)[None, :]) % z.N) / z.N
    table = np.concatenate([np.cos(angle), np.sin(angle)], 1).astype(np.float32)
    high = table.astype(ml_dtypes.bfloat16)
    low = (table - high.astype(np.float32)).astype(ml_dtypes.bfloat16)
    return high, low


def solution(mesh):
    def run(fields, surface, filter_rows, keep_counts):
        z = Sizes(mesh, fields.shape, filter_rows.shape[0])
        high, low = wave_tables(z)

        def body(fields, surface, filter_rows, keep_counts):
            return local(
                z, jnp.asarray(high), jnp.asarray(low), fields, surface, filter_rows, keep_counts
            )

        spec = P(None, "lev", "lat", "lon")
        return jax.shard_map(
            body,
            mesh=mesh,
            in_specs=(spec, P("lat", "lon"), P(), P()),
            out_specs=spec,
            check_vma=False,
        )(fields, surface, filter_rows, keep_counts)

    return run
```

time: 167 us -> 45.9 us (0.27); the launches traced: 165 us -> 45.6 us
  waiting for transfers between devices: 72.5 us -> 18.3 us
  other arithmetic: 26.8 us -> 0.77 us
  local copies, waits for them, and re-layouts: 18.3 us -> 1.33 us
  between operations: 14 us -> 0.14 us
  Pallas kernels: 0 us -> 11.9 us
  matrix products: 10.3 us -> 0 us
  blocking collectives: 9.98 us -> 0 us
    psum x2 -> x0, waiting for transfers between devices: 63.6 us -> none  [one_step(): spectra = lax.psum(spectra, 'lon')]
    pallas_call x0 -> x9, Pallas kernels: none -> 11.9 us  [the longest x8 10.3 us: call(): pl.pallas_call(functools.partial(kernel, z), out_shape=[jax.ShapeDtypeStr...]
    dot_general x4 -> x0, matrix products: 10.3 us -> none  [the longest x2 6.85 us: one_step(): jnp.einsum('vrk,nk->vrn', spectra * mode_weights(slot_keep, KMAX), waves,...]
    all_gather x2 -> x0, blocking collectives: 9.98 us -> none  [carried_in(): everything = lax.all_gather(value, axis)]
    ppermute x8 -> x10, waiting for transfers between devices: 8.85 us -> 18.3 us  [the longest x4 8.43 us: over_lon(): got = lax.ppermute(part, 'lon', [(i, i ^ step) for i in range(z.n_lon)])]
    concatenate x2 -> x0, local copies, waits for them, and re-layouts: 6.39 us -> none  [extended(): block = jnp.concatenate([low, block, high], axis=dim)]
    cos x2 -> x0, other arithmetic: 5.01 us -> none  [the longest x1 4.97 us: wave_table(): return jnp.concatenate([jnp.cos(angles), jnp.sin(angles)], 1)]
    reshape x4 -> x0, local copies, waits for them, and re-layouts: 4.73 us -> none  [the longest x2 2.4 us: one_step(): jnp.take(updated, slot_row, axis=2)]
  transfers between devices with their start and end apart: 10 -> 10, of which waited for: 8 -> 9; matrix products, arithmetic and copies ran while one was open for 9% -> 2% of each run, Pallas kernels for 0% -> 7%
where the time goes in v1:
time: 45.9 us; the launch traced here: 45.6 us
  waiting for transfers between devices  18.3 us (40%)
  starting transfers between devices  13.2 us (29%)
  Pallas kernels  11.9 us (26%)
  local copies, waits for them, and re-layouts  1.33 us (3%)
  other arithmetic  0.77 us (2%)
    pallas_call x8, Pallas kernels, call(): pl.pallas_call(functools.partial(kernel, z), out_shape=[jax.ShapeDtypeStr...  10.3 us
    ppermute x4, waiting for transfers between devices, over_lon(): got = lax.ppermute(part, 'lon', [(i, i ^ step) for i in range(z.n_lon)])  8.43 us
    ppermute x1, starting transfers between devices, local(): m2 = lax.ppermute(m2, 'lat', lat_two)  4.74 us
    ppermute x4, starting transfers between devices, over_lon(): got = lax.ppermute(part, 'lon', [(i, i ^ step) for i in range(z.n_lon)])  3.31 us
    ppermute x2, starting transfers between devices, from_below(): return lax.ppermute(column, 'lev', [(0, 1), (1, 0)])  3.11 us
    ppermute x1, waiting for transfers between devices, local(): m1 = lax.ppermute(m1, 'lat', lat_one)  3.08 us
    ppermute x1, waiting for transfers between devices, local(): m2 = lax.ppermute(m2, 'lat', lat_two)  3.02 us
    ppermute x2, waiting for transfers between devices, from_below(): return lax.ppermute(column, 'lev', [(0, 1), (1, 0)])  2.67 us
  transfers between devices with their start and end apart: 10, of which 9 were waited for; matrix products, arithmetic and copies ran while one was open for 2% of the time, Pallas kernels for 7%

profile of v1, /device:TPU:8, one launch (start us, length us, event | category | flops | bytes accessed | tf_op | source)
XLA Modules:
  0.0 45.6 jit_solution(12169759784153670236)
XLA Ops:
  0.0 1.7 %pack_edges.1 = (f32[8,128]{1,0:T(8,128)}, f32[8,128]{1,0:T(8,128)}) custom-call(f32[4,4,8,1800]{3,2,1,0:T(8,128)} %fields.1, f32[4,4,8,1800]{3,2,1,0:T(8,128)} %fields.1, f32[8,1800]{1,0:T(8,128)} %surface.1, f32[8,1800]{1,0:T(8,128)} %surface.1), custom_call_target="tpu_custom_call" | custom-call | tf_op jit(solution)/shard_map/pack_edges/pallas_call | solution.py:594
  1.7 1.6 %collective-permute-start.1 = (f32[8,128]{1,0:T(8,128)}, f32[8,128]{1,0:T(8,128)S(1)}, u32[]{:S(2)}, u32[]{:S(2)}) collective-permute-start(f32[8,128]{1,0:T(8,128)} %get-tuple-element.26), channel_id=1, source_target_pairs={{0,24},{8,16},{16,8},{24,0},{1,25},{9,17},{17,9},{25,1},{2,26},{10... | collective-permute-start | bytes 12296 | tf_op jit(solution)/shard_map/ppermute | solution.py:608
  3.9 1.1 %collective-permute-done.1.r2 = f32[8,128]{1,0:T(8,128)S(1)} collective-permute-done((f32[8,128]{1,0:T(8,128)}, f32[8,128]{1,0:T(8,128)S(1)}, u32[]{:S(2)}, u32[]{:S(2)}) %collective-permute-start.1) | collective-permute-done | bytes 4128 | tf_op jit(solution)/shard_map/ppermute | solution.py:608
  5.7 4.7 %collective-permute-start.3 = (f32[32,1920]{1,0:T(8,128)S(1)}, f32[32,1920]{1,0:T(8,128)S(1)}, u32[]{:S(2)}, u32[]{:S(2)}) collective-permute-start(f32[32,1920]{1,0:T(8,128)S(1)} %get-tuple-element.30), channel_id=1, source_target_pairs={{2,4},{4,2},{3,5},{5,3},{10,12},{12,10},{11,13},{13,11},{18,20},{2... | collective-permute-start | bytes 737288 | tf_op jit(solution)/shard_map/ppermute | solution.py:617
  10.6 3.1 %collective-permute-done.2.r1 = f32[32,1920]{1,0:T(8,128)S(1)} collective-permute-done((f32[32,1920]{1,0:T(8,128)S(1)}, f32[32,1920]{1,0:T(8,128)S(1)}, u32[]{:S(2)}, u32[]{:S(2)}) %collective-permute-start.2) | collective-permute-done | bytes 245792 | tf_op jit(solution)/shard_map/ppermute | solution.py:616
  13.7 3.0 %collective-permute-done.3.r2 = f32[32,1920]{1,0:T(8,128)S(1)} collective-permute-done((f32[32,1920]{1,0:T(8,128)S(1)}, f32[32,1920]{1,0:T(8,128)S(1)}, u32[]{:S(2)}, u32[]{:S(2)}) %collective-permute-start.3) | collective-permute-done | bytes 245792 | tf_op jit(solution)/shard_map/ppermute | solution.py:617
  16.8 1.6 %collective-permute-start.4 = (f32[8,2432]{1,0:T(8,128)S(1)}, f32[8,2432]{1,0:T(8,128)S(1)}, u32[]{:S(2)}, u32[]{:S(2)}) collective-permute-start(f32[8,2432]{1,0:T(8,128)S(1)} %get-tuple-element.35), channel_id=1, source_target_pairs={{0,1},{1,0},{2,3},{3,2},{4,5},{5,4},{6,7},{7,6},{8,9},{9,8},{10,11... | collective-permute-start | bytes 233480 | tf_op jit(solution)/shard_map/ppermute | solution.py:574
  18.4 1.1 %first_step.1 = (f32[16,8,1920]{2,1,0:T(8,128)S(1)}, f32[3,8,1920]{2,1,0:T(8,128)S(1)}) custom-call(f32[17,8,1920]{2,1,0:T(8,128)S(1)} %get-tuple-element.27.x, f32[7,8,1920]{2,1,0:T(8,128)S(1)} %get-tuple-element.31.ring, f32[5,16,128]{2,1,0:T(8,128)S(1)} %constant_dynamic-update-slice_fusion.geom), custom_call_target="tpu_custom_call" | custom-call | flops 10000000 | bytes 2682880 | tf_op jit(solution)/shard_map/first_step/pallas_call | solution.py:530
  19.5 1.8 %collective-permute-done.4.got = f32[8,2432]{1,0:T(8,128)S(1)} collective-permute-done((f32[8,2432]{1,0:T(8,128)S(1)}, f32[8,2432]{1,0:T(8,128)S(1)}, u32[]{:S(2)}, u32[]{:S(2)}) %collective-permute-start.4) | collective-permute-done | bytes 77856 | tf_op jit(solution)/shard_map/ppermute | solution.py:574
  21.3 0.6 %copy-done.4 = s32[16]{0:T(128)S(1)} copy-done((s32[16]{0:T(128)S(1)}, s32[16]{0:T(128)}, u32[]{:S(2)}) %copy-start.4) | copy-done | bytes 88
  21.9 1.4 %first_spectra.1 = (f32[16,8,1920]{2,1,0:T(8,128)S(1)}, f32[3,8,1920]{2,1,0:T(8,128)S(1)}, f32[88,256]{1,0:T(8,128)S(1)}) custom-call(f32[16,8,1920]{2,1,0:T(8,128)S(1)} %get-tuple-element.32.y, f32[3,8,1920]{2,1,0:T(8,128)S(1)} %get-tuple-element.33.yring, f32[8,1920]{1,0:T(8,128)S(1)} %slice_bitcast_fusion.surface, ...), custom_call_target="tpu_custom_call" | custom-call | flops 1000000 | bytes 4633664 | tf_op jit(solution)/shard_map/first_spectra/pallas_call | solution.py:530
  23.4 1.3 %collective-permute-done.5 = f32[88,256]{1,0:T(8,128)S(1)} collective-permute-done((f32[88,256]{1,0:T(8,128)S(1)}, f32[88,256]{1,0:T(8,128)S(1)}, u32[]{:S(2)}, u32[]{:S(2)}) %collective-permute-start.5) | collective-permute-done | bytes 90144 | tf_op jit(solution)/shard_map/ppermute | solution.py:587
  24.7 1.6 %collective-permute-start.6 = (f32[88,256]{1,0:T(8,128)S(1)}, f32[88,256]{1,0:T(8,128)S(1)}, u32[]{:S(2)}, u32[]{:S(2)}) collective-permute-start(f32[88,256]{1,0:T(8,128)S(1)} %add.150.part), channel_id=1, source_target_pairs={{0,16},{8,24},{16,0},{24,8},{1,17},{9,25},{17,1},{25,9},{2,18},{10... | collective-permute-start | bytes 270344 | tf_op jit(solution)/shard_map/ppermute | solution.py:587
  26.3 3.2 %collective-permute-done.6.got = f32[88,256]{1,0:T(8,128)S(1)} collective-permute-done((f32[88,256]{1,0:T(8,128)S(1)}, f32[88,256]{1,0:T(8,128)S(1)}, u32[]{:S(2)}, u32[]{:S(2)}) %collective-permute-start.6) | collective-permute-done | bytes 90144 | tf_op jit(solution)/shard_map/ppermute | solution.py:587
  29.4 0.7 %copy-done.5 = s32[16]{0:T(128)S(1)} copy-done((s32[16]{0:T(128)S(1)}, s32[16]{0:T(128)}, u32[]{:S(2)}) %copy-start.5) | copy-done | bytes 88
  30.1 1.5 %filter_mass.1 = (f32[8,8,1920]{2,1,0:T(8,128)S(1)}, f32[2,8,1920]{2,1,0:T(8,128)S(1)}, f32[72,256]{1,0:T(8,128)S(1)}, f32[8,2432]{1,0:T(8,128)S(1)}) custom-call(f32[16,8,1920]{2,1,0:T(8,128)S(1)} %get-tuple-element.36.state, f32[3,8,1920]{2,1,0:T(8,128)S(1)} %get-tuple-element.37.sring, f32[88,256]{1,0:T(8,128)S(1)} %add.150.part, ...), custom_call_target="tpu_custom_call" | custom-call | flops 1000000 | bytes 4080768 | tf_op jit(solution)/shard_map/filter_mass/pallas_call | solution.py:530
  31.6 1.6 %collective-permute-start.7 = (f32[8,2432]{1,0:T(8,128)S(1)}, f32[8,2432]{1,0:T(8,128)S(1)}, u32[]{:S(2)}, u32[]{:S(2)}) collective-permute-start(f32[8,2432]{1,0:T(8,128)S(1)} %get-tuple-element.42), channel_id=1, source_target_pairs={{0,1},{1,0},{2,3},{3,2},{4,5},{5,4},{6,7},{7,6},{8,9},{9,8},{10,11... | collective-permute-start | bytes 233480 | tf_op jit(solution)/shard_map/ppermute | solution.py:574
  33.2 2.0 %second_step.1.y = f32[16,8,1920]{2,1,0:T(8,128)S(1)} custom-call(f32[16,8,1920]{2,1,0:T(8,128)S(1)} %get-tuple-element.36.state, f32[3,8,1920]{2,1,0:T(8,128)S(1)} %get-tuple-element.37.sring, f32[72,256]{1,0:T(8,128)S(1)} %get-tuple-element.39.uvmodes, f32[8,8,1920]{2,1,0:T(8,128)S(1)} %get-tuple-element.40.ht, ...), custom_call_target="tpu_custom_call" | custom-call | flops 10000000 | bytes 4845696 | tf_op jit(solution)/shard_map/second_step/pallas_call | solution.py:530
  35.3 0.9 %collective-permute-done.7.got = f32[8,2432]{1,0:T(8,128)S(1)} collective-permute-done((f32[8,2432]{1,0:T(8,128)S(1)}, f32[8,2432]{1,0:T(8,128)S(1)}, u32[]{:S(2)}, u32[]{:S(2)}) %collective-permute-start.7) | collective-permute-done | bytes 77856 | tf_op jit(solution)/shard_map/ppermute | solution.py:574
  36.1 1.3 %second_spectra.1 = (f32[16,8,1920]{2,1,0:T(8,128)S(1)}, f32[64,256]{1,0:T(8,128)S(1)}) custom-call(f32[16,8,1920]{2,1,0:T(8,128)S(1)} %second_step.1.y, f32[8,1920]{1,0:T(8,128)S(1)} %slice_bitcast_fusion.surface, f32[8,1920]{1,0:T(8,128)S(1)} %get-tuple-element.34.ring_surface, f32[8,2432]{1,0:T(8,128)S(1)} %collective-permute-done.7.got, ...), custom_call_target="tpu_custom_call" | custom-call | flops 1000000 | bytes 4240448 | tf_op jit(solution)/shard_map/second_spectra/pallas_call | solution.py:530
  37.5 1.2 %collective-permute-done.8 = f32[64,256]{1,0:T(8,128)S(1)} collective-permute-done((f32[64,256]{1,0:T(8,128)S(1)}, f32[64,256]{1,0:T(8,128)S(1)}, u32[]{:S(2)}, u32[]{:S(2)}) %collective-permute-start.8) | collective-permute-done | bytes 65568 | tf_op jit(solution)/shard_map/ppermute | solution.py:587
  38.7 1.6 %collective-permute-start.9 = (f32[64,256]{1,0:T(8,128)S(1)}, f32[64,256]{1,0:T(8,128)S(1)}, u32[]{:S(2)}, u32[]{:S(2)}) collective-permute-start(f32[64,256]{1,0:T(8,128)S(1)} %add.151.part), channel_id=1, source_target_pairs={{0,16},{8,24},{16,0},{24,8},{1,17},{9,25},{17,1},{25,9},{2,18},{10... | collective-permute-start | bytes 196616 | tf_op jit(solution)/shard_map/ppermute | solution.py:587
  40.3 2.8 %collective-permute-done.9.got = f32[64,256]{1,0:T(8,128)S(1)} collective-permute-done((f32[64,256]{1,0:T(8,128)S(1)}, f32[64,256]{1,0:T(8,128)S(1)}, u32[]{:S(2)}, u32[]{:S(2)}) %collective-permute-start.9) | collective-permute-done | bytes 65568 | tf_op jit(solution)/shard_map/ppermute | solution.py:587
  43.1 2.5 %filter_all.1 = f32[4,4,8,1800]{3,2,1,0:T(8,128)} custom-call(f32[16,8,1920]{2,1,0:T(8,128)S(1)} %get-tuple-element.43.state, f32[64,256]{1,0:T(8,128)S(1)} %add.151.part, f32[64,256]{1,0:T(8,128)S(1)} %collective-permute-done.9.got, bf16[1920,256]{1,0:T(8,128)(2,1)S(1)} %copy-done.1, bf16[1920,256]{1,0:T(8,128)(2,1)S(1)} %copy-done, ...), custom_call_target="tpu_custom_call" | custom-call | flops 1000000 | bytes 4002944 | tf_op jit(solution)/shard_map/filter_all/pallas_call | solution.py:530
  (29 shorter events, 1.7 us)
Async XLA Ops:
  0.0 5.0 %copy-start.2 = (f32[4,4,8,1800]{3,2,1,0:T(8,128)S(1)}, f32[4,4,8,1800]{3,2,1,0:T(8,128)}, u32[]{:S(2)}) copy-start(f32[4,4,8,1800]{3,2,1,0:T(8,128)} %fields.1) | copy-start | bytes 2764804
  1.7 3.3 %copy-start.3 = (f32[8,1800]{1,0:T(8,128)S(1)}, f32[8,1800]{1,0:T(8,128)}, u32[]{:S(2)}) copy-start(f32[8,1800]{1,0:T(8,128)} %surface.1) | copy-start | bytes 172804
  1.7 2.3 %collective-permute-start = (f32[8,128]{1,0:T(8,128)}, f32[8,128]{1,0:T(8,128)S(1)}, u32[]{:S(2)}, u32[]{:S(2)}) collective-permute-start(f32[8,128]{1,0:T(8,128)} %get-tuple-element.25), channel_id=1, source_target_pairs={{0,8},{8,0},{16,24},{24,16},{1,9},{9,1},{17,25},{25,17},{2,10},{10... | collective-permute-start | bytes 12296 | tf_op jit(solution)/shard_map/ppermute | solution.py:607
  1.7 3.3 %collective-permute-start.1 = (f32[8,128]{1,0:T(8,128)}, f32[8,128]{1,0:T(8,128)S(1)}, u32[]{:S(2)}, u32[]{:S(2)}) collective-permute-start(f32[8,128]{1,0:T(8,128)} %get-tuple-element.26), channel_id=1, source_target_pairs={{0,24},{8,16},{16,8},{24,0},{1,25},{9,17},{17,9},{25,1},{2,26},{10... | collective-permute-start | bytes 12296 | tf_op jit(solution)/shard_map/ppermute | solution.py:608
  5.3 8.4 %collective-permute-start.2 = (f32[32,1920]{1,0:T(8,128)S(1)}, f32[32,1920]{1,0:T(8,128)S(1)}, u32[]{:S(2)}, u32[]{:S(2)}) collective-permute-start(f32[32,1920]{1,0:T(8,128)S(1)} %get-tuple-element.29), channel_id=1, source_target_pairs={{0,2},{2,0},{4,6},{6,4},{1,3},{3,1},{5,7},{7,5},{8,10},{10,8},{12,... | collective-permute-start | bytes 737288 | tf_op jit(solution)/shard_map/ppermute | solution.py:616
  5.7 11.0 %collective-permute-start.3 = (f32[32,1920]{1,0:T(8,128)S(1)}, f32[32,1920]{1,0:T(8,128)S(1)}, u32[]{:S(2)}, u32[]{:S(2)}) collective-permute-start(f32[32,1920]{1,0:T(8,128)S(1)} %get-tuple-element.30), channel_id=1, source_target_pairs={{2,4},{4,2},{3,5},{5,3},{10,12},{12,10},{11,13},{13,11},{18,20},{2... | collective-permute-start | bytes 737288 | tf_op jit(solution)/shard_map/ppermute | solution.py:617
  16.7 4.6 %copy-start = (bf16[1920,256]{1,0:T(8,128)(2,1)S(1)}, bf16[1920,256]{1,0:T(8,128)(2,1)}, u32[]{:S(2)}) copy-start(bf16[1920,256]{1,0:T(8,128)(2,1)} %constant.53.clone.wl) | copy-start | bytes 2949124
  16.7 4.6 %copy-start.1 = (bf16[1920,256]{1,0:T(8,128)(2,1)S(1)}, bf16[1920,256]{1,0:T(8,128)(2,1)}, u32[]{:S(2)}) copy-start(bf16[1920,256]{1,0:T(8,128)(2,1)} %constant.52.clone.wh) | copy-start | bytes 2949124
  16.8 4.5 %collective-permute-start.4 = (f32[8,2432]{1,0:T(8,128)S(1)}, f32[8,2432]{1,0:T(8,128)S(1)}, u32[]{:S(2)}, u32[]{:S(2)}) collective-permute-start(f32[8,2432]{1,0:T(8,128)S(1)} %get-tuple-element.35), channel_id=1, source_target_pairs={{0,1},{1,0},{2,3},{3,2},{4,5},{5,4},{6,7},{7,6},{8,9},{9,8},{10,11... | collective-permute-start | bytes 233480 | tf_op jit(solution)/shard_map/ppermute | solution.py:574
  21.3 0.7 %copy-start.4 = (s32[16]{0:T(128)S(1)}, s32[16]{0:T(128)}, u32[]{:S(2)}) copy-start(s32[16]{0:T(128)} %rows.9) | copy-start | bytes 196
  23.3 1.4 %collective-permute-start.5 = (f32[88,256]{1,0:T(8,128)S(1)}, f32[88,256]{1,0:T(8,128)S(1)}, u32[]{:S(2)}, u32[]{:S(2)}) collective-permute-start(f32[88,256]{1,0:T(8,128)S(1)} %get-tuple-element.38), channel_id=1, source_target_pairs={{0,8},{8,0},{16,24},{24,16},{1,9},{9,1},{17,25},{25,17},{2,10},{10... | collective-permute-start | bytes 270344 | tf_op jit(solution)/shard_map/ppermute | solution.py:587
  24.7 4.7 %collective-permute-start.6 = (f32[88,256]{1,0:T(8,128)S(1)}, f32[88,256]{1,0:T(8,128)S(1)}, u32[]{:S(2)}, u32[]{:S(2)}) collective-permute-start(f32[88,256]{1,0:T(8,128)S(1)} %add.150.part), channel_id=1, source_target_pairs={{0,16},{8,24},{16,0},{24,8},{1,17},{9,25},{17,1},{25,9},{2,18},{10... | collective-permute-start | bytes 270344 | tf_op jit(solution)/shard_map/ppermute | solution.py:587
  29.4 0.7 %copy-start.5 = (s32[16]{0:T(128)S(1)}, s32[16]{0:T(128)}, u32[]{:S(2)}) copy-start(s32[16]{0:T(128)} %keeps.5) | copy-start | bytes 196
  31.6 4.5 %collective-permute-start.7 = (f32[8,2432]{1,0:T(8,128)S(1)}, f32[8,2432]{1,0:T(8,128)S(1)}, u32[]{:S(2)}, u32[]{:S(2)}) collective-permute-start(f32[8,2432]{1,0:T(8,128)S(1)} %get-tuple-element.42), channel_id=1, source_target_pairs={{0,1},{1,0},{2,3},{3,2},{4,5},{5,4},{6,7},{7,6},{8,9},{9,8},{10,11... | collective-permute-start | bytes 233480 | tf_op jit(solution)/shard_map/ppermute | solution.py:574
  37.4 1.3 %collective-permute-start.8 = (f32[64,256]{1,0:T(8,128)S(1)}, f32[64,256]{1,0:T(8,128)S(1)}, u32[]{:S(2)}, u32[]{:S(2)}) collective-permute-start(f32[64,256]{1,0:T(8,128)S(1)} %get-tuple-element.44), channel_id=1, source_target_pairs={{0,8},{8,0},{16,24},{24,16},{1,9},{9,1},{17,25},{25,17},{2,10},{10... | collective-permute-start | bytes 196616 | tf_op jit(solution)/shard_map/ppermute | solution.py:587
  38.7 4.3 %collective-permute-start.9 = (f32[64,256]{1,0:T(8,128)S(1)}, f32[64,256]{1,0:T(8,128)S(1)}, u32[]{:S(2)}, u32[]{:S(2)}) collective-permute-start(f32[64,256]{1,0:T(8,128)S(1)} %add.151.part), channel_id=1, source_target_pairs={{0,16},{8,24},{16,0},{24,8},{1,17},{9,25},{17,1},{25,9},{2,18},{10... | collective-permute-start | bytes 196616 | tf_op jit(solution)/shard_map/ppermute | solution.py:587

commit v2 on v1

--- a/solution.py
+++ b/solution.py
@@ -74,6 +74,11 @@
         self.tiles = self.W // LANES
         self.extra = -(-self.tiles // self.R)
         self.lat_rows = -(-(7 * self.L + 1) // 8) * 8
+        width = -(-self.base // LANES // 3) * LANES if self.base else self.W
+        cuts = [c for c in range(0, self.base + 1, width)] if self.base else [0]
+        if self.C - cuts[-1] <= LANES and len(cuts) > 1:
+            cuts.pop()
+        self.chunks = list(zip(cuts, cuts[1:] + [self.C]))
         assert self.R == 2 * self.L and self.n_lon % 2 == 0
         assert 2 <= self.C - self.base <= LANES - 2 and 2 * self.planes <= LANES
 
@@ -104,7 +109,7 @@
         m2[...] = right
 
 
-def widen(z, fields, surface, r1, r2, x, m1, m2, sums, from_right, from_left):
+def widen(z, fields, surface, r1, r2, rows, keeps, x, m1, m2, sums, from_right, from_left):
     lon_even = lax.axis_index("lon") % 2 == 0
 
     @pl.when(lon_even)
@@ -505,18 +510,30 @@
     )
 
 
-def filter_all(z, state, part, got, wh, wl, phase, rows, keeps, out):
+def filter_all(z, state, part, got, wh, wl, phase, rows, keeps, out, held, sem):
     L = z.L
     modes = local_modes(part[...] + got[...], phase)
     keep = tile_keep(z, rows, keeps, 2 * KMAX)
     tiles = tile_modes(z, modes, rows, mode_weight(z, keep), range(4 * L))
-    s = smooth(jnp.concatenate(tiles, 0), wh, wl)
-    damp = jnp.broadcast_to(damping(keep[:, 0:1]), (z.R, z.W))
-    for p in range(4 * L):
-        f, l = divmod(p, L)
-        x = state[p]
-        new = x + damp * (s[p * z.R : (p + 1) * z.R] - x)
-        out[f, l] = new[:, : z.C]
+    high, low = split(jnp.concatenate(tiles, 0))
+    damp = damping(keep[:, 0:1])
+    across = ((1,), (1,))
+    copies = []
+    for i, (lo, hi) in enumerate(z.chunks):
+        top = min(-(-hi // LANES) * LANES, z.W)
+        w, v = wh[lo:top, :], wl[lo:top, :]
+        s = dot(high, w, across) + dot(low, w, across) + dot(high, v, across)
+        d = jnp.broadcast_to(damp, (z.R, top - lo))
+        for p in range(4 * L):
+            x = state[p, :, lo:top]
+            new = x + d * (s[p * z.R : (p + 1) * z.R] - x)
+            held[p // L, p % L, :, lo:hi] = new[:, : hi - lo]
+        copies.append(
+            pltpu.make_async_copy(held.at[:, :, :, lo:hi], out.at[:, :, :, lo:hi], sem.at[i])
+        )
+        copies[-1].start()
+    for copy in copies:
+        copy.wait()
 
 
 def local(z, wave_high, wave_low, fields, surface, filter_rows, keep_counts):
@@ -559,10 +576,6 @@
     turn = (lon * z.C * jnp.arange(KMAX, dtype=jnp.int32)) % z.N
     angle = turn.astype(f32) * (2.0 * jnp.pi / z.N)
     phase = jnp.stack([jnp.cos(angle), jnp.sin(angle)])
-
-    def swaps(n):
-        one = [(i, i ^ 1) for i in range(n)]
-        return one
 
     lon_one = [(i, i ^ 1) for i in range(z.n_lon)]
     lon_two = [(i, (((i + 1) % z.n_lon ^ 1) - 1) % z.n_lon) for i in range(z.n_lon)]
@@ -610,7 +623,7 @@
     x, m1, m2, sums = call(
         widen,
         [(z.planes, R, W), (z.lat_rows, W), (z.lat_rows, W), (R, W)],
-        [fields, surface, e1, e2],
+        [fields, surface, e1, e2, filter_rows, keep_counts],
         [(R, LANES)] * 2,
     )
     m1 = lax.ppermute(m1, "lat", lat_one)
@@ -657,12 +670,18 @@
         [(m, 2 * KMAX)],
     )
     part, got = over_lon(part)
-    (out,) = call(
-        filter_all,
-        [(4, L, R, z.C)],
-        [state, part, got, wave_high, wave_low, phase, filter_rows, keep_counts],
-    )
-    return out
+    return pl.pallas_call(
+        functools.partial(filter_all, z),
+        out_shape=jax.ShapeDtypeStruct((4, L, R, z.C), f32),
+        in_specs=[vmem] * 6 + [smem] * 2,
+        out_specs=pl.BlockSpec(memory_space=pl.ANY),
+        scratch_shapes=[
+            pltpu.VMEM((4, L, R, z.C), f32),
+            pltpu.SemaphoreType.DMA((len(z.chunks),)),
+        ],
+        compiler_params=pltpu.CompilerParams(vmem_limit_bytes=VMEM_LIMIT),
+        name="filter_all",
+    )(state, part, got, wave_high, wave_low, phase, filter_rows, keep_counts)
 
 
 def wave_tables(z):

time: 45.9 us -> 45 us (0.980)
  local copies, waits for them, and re-layouts: 1.33 us -> 0.03 us
    pallas_call x0 -> x1, Pallas kernels: none -> 2.35 us  [local(): pl.pallas_call(functools.partial(filter_all, z), out_shape=jax.ShapeDtype...]
    pallas_call x8 -> x7, Pallas kernels: 10.3 us -> 8.33 us  [call(): pl.pallas_call(functools.partial(kernel, z), out_shape=[jax.ShapeDtypeStr...]
    unnamed x12, local copies, waits for them, and re-layouts: 1.32 us -> 0.03 us
where the time goes in v2:
time: 45 us; the launch traced here: 44.7 us
  waiting for transfers between devices  18.2 us (40%)
  starting transfers between devices  13.2 us (29%)
  Pallas kernels  12.3 us (27%)
  other arithmetic  0.77 us (2%)
    ppermute x4, waiting for transfers between devices, over_lon(): got = lax.ppermute(part, 'lon', [(i, i ^ step) for i in range(z.n_lon)])  8.42 us
    pallas_call x7, Pallas kernels, call(): pl.pallas_call(functools.partial(kernel, z), out_shape=[jax.ShapeDtypeStr...  8.33 us
    ppermute x1, starting transfers between devices, local(): m2 = lax.ppermute(m2, 'lat', lat_two)  4.75 us
    ppermute x4, starting transfers between devices, over_lon(): got = lax.ppermute(part, 'lon', [(i, i ^ step) for i in range(z.n_lon)])  3.31 us
    ppermute x2, starting transfers between devices, from_below(): return lax.ppermute(column, 'lev', [(0, 1), (1, 0)])  3.11 us
    ppermute x1, waiting for transfers between devices, local(): m1 = lax.ppermute(m1, 'lat', lat_one)  3.08 us
    ppermute x1, waiting for transfers between devices, local(): m2 = lax.ppermute(m2, 'lat', lat_two)  3.02 us
    ppermute x2, waiting for transfers between devices, from_below(): return lax.ppermute(column, 'lev', [(0, 1), (1, 0)])  2.64 us
  transfers between devices with their start and end apart: 10, of which 9 were waited for; matrix products, arithmetic and copies ran while one was open for 2% of the time, Pallas kernels for 7%

profile of v2, /device:TPU:8, one launch (start us, length us, event | category | flops | bytes accessed | tf_op | source)
XLA Modules:
  0.0 44.7 jit_solution(11979004759952649879)
XLA Ops:
  0.0 1.7 %pack_edges.1 = (f32[8,128]{1,0:T(8,128)}, f32[8,128]{1,0:T(8,128)}) custom-call(f32[4,4,8,1800]{3,2,1,0:T(8,128)} %fields.1, f32[4,4,8,1800]{3,2,1,0:T(8,128)} %fields.1, f32[8,1800]{1,0:T(8,128)} %surface.1, f32[8,1800]{1,0:T(8,128)} %surface.1), custom_call_target="tpu_custom_call" | custom-call | tf_op jit(solution)/shard_map/pack_edges/pallas_call | solution.py:607
  1.7 1.6 %collective-permute-start.1 = (f32[8,128]{1,0:T(8,128)}, f32[8,128]{1,0:T(8,128)S(1)}, u32[]{:S(2)}, u32[]{:S(2)}) collective-permute-start(f32[8,128]{1,0:T(8,128)} %get-tuple-element.26), channel_id=1, source_target_pairs={{0,24},{8,16},{16,8},{24,0},{1,25},{9,17},{17,9},{25,1},{2,26},{10... | collective-permute-start | bytes 12296 | tf_op jit(solution)/shard_map/ppermute | solution.py:621
  3.9 1.0 %collective-permute-done.1.r2 = f32[8,128]{1,0:T(8,128)S(1)} collective-permute-done((f32[8,128]{1,0:T(8,128)}, f32[8,128]{1,0:T(8,128)S(1)}, u32[]{:S(2)}, u32[]{:S(2)}) %collective-permute-start.1) | collective-permute-done | bytes 4128 | tf_op jit(solution)/shard_map/ppermute | solution.py:621
  5.0 0.9 %widen.1 = (f32[17,8,1920]{2,1,0:T(8,128)S(1)}, f32[32,1920]{1,0:T(8,128)S(1)}, f32[32,1920]{1,0:T(8,128)S(1)}, f32[8,1920]{1,0:T(8,128)S(1)}) custom-call(f32[4,4,8,1800]{3,2,1,0:T(8,128)S(1)} %copy-done.2, f32[8,1800]{1,0:T(8,128)S(1)} %copy-done.3, f32[8,128]{1,0:T(8,128)S(1)} %collective-permute-done.r1, f32[8,128]{1,0:T(8,128)S(1)} %collective-permute-done.1.r2, ...), custom_call_target="tpu_custom_call" | custom-call | flops 1000000 | bytes 2584960 | tf_op jit(solution)/shard_map/widen/pallas_call | solution.py:547
  5.9 0.4 collective-permute-start.2
  6.2 4.7 %collective-permute-start.3 = (f32[32,1920]{1,0:T(8,128)S(1)}, f32[32,1920]{1,0:T(8,128)S(1)}, u32[]{:S(2)}, u32[]{:S(2)}) collective-permute-start(f32[32,1920]{1,0:T(8,128)S(1)} %get-tuple-element.30), channel_id=1, source_target_pairs={{2,4},{4,2},{3,5},{5,3},{10,12},{12,10},{11,13},{13,11},{18,20},{2... | collective-permute-start | bytes 737288 | tf_op jit(solution)/shard_map/ppermute | solution.py:630
  11.2 3.1 %collective-permute-done.2.r1 = f32[32,1920]{1,0:T(8,128)S(1)} collective-permute-done((f32[32,1920]{1,0:T(8,128)S(1)}, f32[32,1920]{1,0:T(8,128)S(1)}, u32[]{:S(2)}, u32[]{:S(2)}) %collective-permute-start.2) | collective-permute-done | bytes 245792 | tf_op jit(solution)/shard_map/ppermute | solution.py:629
  14.2 3.0 %collective-permute-done.3.r2 = f32[32,1920]{1,0:T(8,128)S(1)} collective-permute-done((f32[32,1920]{1,0:T(8,128)S(1)}, f32[32,1920]{1,0:T(8,128)S(1)}, u32[]{:S(2)}, u32[]{:S(2)}) %collective-permute-start.3) | collective-permute-done | bytes 245792 | tf_op jit(solution)/shard_map/ppermute | solution.py:630
  17.4 1.6 %collective-permute-start.4 = (f32[8,2432]{1,0:T(8,128)S(1)}, f32[8,2432]{1,0:T(8,128)S(1)}, u32[]{:S(2)}, u32[]{:S(2)}) collective-permute-start(f32[8,2432]{1,0:T(8,128)S(1)} %get-tuple-element.35), channel_id=1, source_target_pairs={{0,1},{1,0},{2,3},{3,2},{4,5},{5,4},{6,7},{7,6},{8,9},{9,8},{10,11... | collective-permute-start | bytes 233480 | tf_op jit(solution)/shard_map/ppermute | solution.py:587
  19.0 1.1 %first_step.1 = (f32[16,8,1920]{2,1,0:T(8,128)S(1)}, f32[3,8,1920]{2,1,0:T(8,128)S(1)}) custom-call(f32[17,8,1920]{2,1,0:T(8,128)S(1)} %get-tuple-element.27.x, f32[7,8,1920]{2,1,0:T(8,128)S(1)} %get-tuple-element.31.ring, f32[5,16,128]{2,1,0:T(8,128)S(1)} %constant_dynamic-update-slice_fusion.geom), custom_call_target="tpu_custom_call" | custom-call | flops 10000000 | bytes 2682880 | tf_op jit(solution)/shard_map/first_step/pallas_call | solution.py:547
  20.0 1.8 %collective-permute-done.4.got = f32[8,2432]{1,0:T(8,128)S(1)} collective-permute-done((f32[8,2432]{1,0:T(8,128)S(1)}, f32[8,2432]{1,0:T(8,128)S(1)}, u32[]{:S(2)}, u32[]{:S(2)}) %collective-permute-start.4) | collective-permute-done | bytes 77856 | tf_op jit(solution)/shard_map/ppermute | solution.py:587
  21.9 1.4 %first_spectra.1 = (f32[16,8,1920]{2,1,0:T(8,128)S(1)}, f32[3,8,1920]{2,1,0:T(8,128)S(1)}, f32[88,256]{1,0:T(8,128)S(1)}) custom-call(f32[16,8,1920]{2,1,0:T(8,128)S(1)} %get-tuple-element.32.y, f32[3,8,1920]{2,1,0:T(8,128)S(1)} %get-tuple-element.33.yring, f32[8,1920]{1,0:T(8,128)S(1)} %slice_bitcast_fusion.surface, ...), custom_call_target="tpu_custom_call" | custom-call | flops 1000000 | bytes 4633664 | tf_op jit(solution)/shard_map/first_spectra/pallas_call | solution.py:547
  23.3 1.3 %collective-permute-done.5 = f32[88,256]{1,0:T(8,128)S(1)} collective-permute-done((f32[88,256]{1,0:T(8,128)S(1)}, f32[88,256]{1,0:T(8,128)S(1)}, u32[]{:S(2)}, u32[]{:S(2)}) %collective-permute-start.5) | collective-permute-done | bytes 90144 | tf_op jit(solution)/shard_map/ppermute | solution.py:600
  24.6 1.6 %collective-permute-start.6 = (f32[88,256]{1,0:T(8,128)S(1)}, f32[88,256]{1,0:T(8,128)S(1)}, u32[]{:S(2)}, u32[]{:S(2)}) collective-permute-start(f32[88,256]{1,0:T(8,128)S(1)} %add.150.part), channel_id=1, source_target_pairs={{0,16},{8,24},{16,0},{24,8},{1,17},{9,25},{17,1},{25,9},{2,18},{10... | collective-permute-start | bytes 270344 | tf_op jit(solution)/shard_map/ppermute | solution.py:600
  26.2 3.2 %collective-permute-done.6.got = f32[88,256]{1,0:T(8,128)S(1)} collective-permute-done((f32[88,256]{1,0:T(8,128)S(1)}, f32[88,256]{1,0:T(8,128)S(1)}, u32[]{:S(2)}, u32[]{:S(2)}) %collective-permute-start.6) | collective-permute-done | bytes 90144 | tf_op jit(solution)/shard_map/ppermute | solution.py:600
  29.4 1.5 %filter_mass.1 = (f32[8,8,1920]{2,1,0:T(8,128)S(1)}, f32[2,8,1920]{2,1,0:T(8,128)S(1)}, f32[72,256]{1,0:T(8,128)S(1)}, f32[8,2432]{1,0:T(8,128)S(1)}) custom-call(f32[16,8,1920]{2,1,0:T(8,128)S(1)} %get-tuple-element.36.state, f32[3,8,1920]{2,1,0:T(8,128)S(1)} %get-tuple-element.37.sring, f32[88,256]{1,0:T(8,128)S(1)} %add.150.part, ...), custom_call_target="tpu_custom_call" | custom-call | flops 1000000 | bytes 4080768 | tf_op jit(solution)/shard_map/filter_mass/pallas_call | solution.py:547
  30.9 1.6 %collective-permute-start.7 = (f32[8,2432]{1,0:T(8,128)S(1)}, f32[8,2432]{1,0:T(8,128)S(1)}, u32[]{:S(2)}, u32[]{:S(2)}) collective-permute-start(f32[8,2432]{1,0:T(8,128)S(1)} %get-tuple-element.42), channel_id=1, source_target_pairs={{0,1},{1,0},{2,3},{3,2},{4,5},{5,4},{6,7},{7,6},{8,9},{9,8},{10,11... | collective-permute-start | bytes 233480 | tf_op jit(solution)/shard_map/ppermute | solution.py:587
  32.5 2.1 %second_step.1.y = f32[16,8,1920]{2,1,0:T(8,128)S(1)} custom-call(f32[16,8,1920]{2,1,0:T(8,128)S(1)} %get-tuple-element.36.state, f32[3,8,1920]{2,1,0:T(8,128)S(1)} %get-tuple-element.37.sring, f32[72,256]{1,0:T(8,128)S(1)} %get-tuple-element.39.uvmodes, f32[8,8,1920]{2,1,0:T(8,128)S(1)} %get-tuple-element.40.ht, ...), custom_call_target="tpu_custom_call" | custom-call | flops 10000000 | bytes 4845696 | tf_op jit(solution)/shard_map/second_step/pallas_call | solution.py:547
  34.6 0.8 %collective-permute-done.7.got = f32[8,2432]{1,0:T(8,128)S(1)} collective-permute-done((f32[8,2432]{1,0:T(8,128)S(1)}, f32[8,2432]{1,0:T(8,128)S(1)}, u32[]{:S(2)}, u32[]{:S(2)}) %collective-permute-start.7) | collective-permute-done | bytes 77856 | tf_op jit(solution)/shard_map/ppermute | solution.py:587
  35.4 1.3 %second_spectra.1 = (f32[16,8,1920]{2,1,0:T(8,128)S(1)}, f32[64,256]{1,0:T(8,128)S(1)}) custom-call(f32[16,8,1920]{2,1,0:T(8,128)S(1)} %second_step.1.y, f32[8,1920]{1,0:T(8,128)S(1)} %slice_bitcast_fusion.surface, f32[8,1920]{1,0:T(8,128)S(1)} %get-tuple-element.34.ring_surface, f32[8,2432]{1,0:T(8,128)S(1)} %collective-permute-done.7.got, ...), custom_call_target="tpu_custom_call" | custom-call | flops 1000000 | bytes 4240448 | tf_op jit(solution)/shard_map/second_spectra/pallas_call | solution.py:547
  36.7 1.2 %collective-permute-done.8 = f32[64,256]{1,0:T(8,128)S(1)} collective-permute-done((f32[64,256]{1,0:T(8,128)S(1)}, f32[64,256]{1,0:T(8,128)S(1)}, u32[]{:S(2)}, u32[]{:S(2)}) %collective-permute-start.8) | collective-permute-done | bytes 65568 | tf_op jit(solution)/shard_map/ppermute | solution.py:600
  38.0 1.6 %collective-permute-start.9 = (f32[64,256]{1,0:T(8,128)S(1)}, f32[64,256]{1,0:T(8,128)S(1)}, u32[]{:S(2)}, u32[]{:S(2)}) collective-permute-start(f32[64,256]{1,0:T(8,128)S(1)} %add.151.part), channel_id=1, source_target_pairs={{0,16},{8,24},{16,0},{24,8},{1,17},{9,25},{17,1},{25,9},{2,18},{10... | collective-permute-start | bytes 196616 | tf_op jit(solution)/shard_map/ppermute | solution.py:600
  39.6 2.7 %collective-permute-done.9.got = f32[64,256]{1,0:T(8,128)S(1)} collective-permute-done((f32[64,256]{1,0:T(8,128)S(1)}, f32[64,256]{1,0:T(8,128)S(1)}, u32[]{:S(2)}, u32[]{:S(2)}) %collective-permute-start.9) | collective-permute-done | bytes 65568 | tf_op jit(solution)/shard_map/ppermute | solution.py:600
  42.3 2.3 %filter_all.1 = f32[4,4,8,1800]{3,2,1,0:T(8,128)} custom-call(f32[16,8,1920]{2,1,0:T(8,128)S(1)} %get-tuple-element.43.state, f32[64,256]{1,0:T(8,128)S(1)} %add.151.part, f32[64,256]{1,0:T(8,128)S(1)} %collective-permute-done.9.got, bf16[1920,256]{1,0:T(8,128)(2,1)S(1)} %copy-done.1, bf16[1920,256]{1,0:T(8,128)(2,1)S(1)} %copy-done, ...), custom_call_target="tpu_custom_call" | custom-call | tf_op jit(solution)/shard_map/filter_all/pallas_call | solution.py:673
  (29 shorter events, 1.1 us)
Async XLA Ops:
  0.0 5.0 %copy-start.2 = (f32[4,4,8,1800]{3,2,1,0:T(8,128)S(1)}, f32[4,4,8,1800]{3,2,1,0:T(8,128)}, u32[]{:S(2)}) copy-start(f32[4,4,8,1800]{3,2,1,0:T(8,128)} %fields.1) | copy-start | bytes 2764804
  1.7 3.3 %copy-start.3 = (f32[8,1800]{1,0:T(8,128)S(1)}, f32[8,1800]{1,0:T(8,128)}, u32[]{:S(2)}) copy-start(f32[8,1800]{1,0:T(8,128)} %surface.1) | copy-start | bytes 172804
  1.7 2.3 %collective-permute-start = (f32[8,128]{1,0:T(8,128)}, f32[8,128]{1,0:T(8,128)S(1)}, u32[]{:S(2)}, u32[]{:S(2)}) collective-permute-start(f32[8,128]{1,0:T(8,128)} %get-tuple-element.25), channel_id=1, source_target_pairs={{0,8},{8,0},{16,24},{24,16},{1,9},{9,1},{17,25},{25,17},{2,10},{10... | collective-permute-start | bytes 12296 | tf_op jit(solution)/shard_map/ppermute | solution.py:620
  1.7 3.3 %collective-permute-start.1 = (f32[8,128]{1,0:T(8,128)}, f32[8,128]{1,0:T(8,128)S(1)}, u32[]{:S(2)}, u32[]{:S(2)}) collective-permute-start(f32[8,128]{1,0:T(8,128)} %get-tuple-element.26), channel_id=1, source_target_pairs={{0,24},{8,16},{16,8},{24,0},{1,25},{9,17},{17,9},{25,1},{2,26},{10... | collective-permute-start | bytes 12296 | tf_op jit(solution)/shard_map/ppermute | solution.py:621
  3.9 1.1 %copy-start.4 = (s32[16]{0:T(128)S(1)}, s32[16]{0:T(128)}, u32[]{:S(2)}) copy-start(s32[16]{0:T(128)} %rows.11) | copy-start | bytes 196
  3.9 1.1 %copy-start.5 = (s32[16]{0:T(128)S(1)}, s32[16]{0:T(128)}, u32[]{:S(2)}) copy-start(s32[16]{0:T(128)} %keeps.7) | copy-start | bytes 196
  5.9 8.4 %collective-permute-start.2 = (f32[32,1920]{1,0:T(8,128)S(1)}, f32[32,1920]{1,0:T(8,128)S(1)}, u32[]{:S(2)}, u32[]{:S(2)}) collective-permute-start(f32[32,1920]{1,0:T(8,128)S(1)} %get-tuple-element.29), channel_id=1, source_target_pairs={{0,2},{2,0},{4,6},{6,4},{1,3},{3,1},{5,7},{7,5},{8,10},{10,8},{12,... | collective-permute-start | bytes 737288 | tf_op jit(solution)/shard_map/ppermute | solution.py:629
  6.2 11.0 %collective-permute-start.3 = (f32[32,1920]{1,0:T(8,128)S(1)}, f32[32,1920]{1,0:T(8,128)S(1)}, u32[]{:S(2)}, u32[]{:S(2)}) collective-permute-start(f32[32,1920]{1,0:T(8,128)S(1)} %get-tuple-element.30), channel_id=1, source_target_pairs={{2,4},{4,2},{3,5},{5,3},{10,12},{12,10},{11,13},{13,11},{18,20},{2... | collective-permute-start | bytes 737288 | tf_op jit(solution)/shard_map/ppermute | solution.py:630
  17.3 4.6 %copy-start = (bf16[1920,256]{1,0:T(8,128)(2,1)S(1)}, bf16[1920,256]{1,0:T(8,128)(2,1)}, u32[]{:S(2)}) copy-start(bf16[1920,256]{1,0:T(8,128)(2,1)} %constant.53.clone.wl) | copy-start | bytes 2949124
  17.3 4.6 %copy-start.1 = (bf16[1920,256]{1,0:T(8,128)(2,1)S(1)}, bf16[1920,256]{1,0:T(8,128)(2,1)}, u32[]{:S(2)}) copy-start(bf16[1920,256]{1,0:T(8,128)(2,1)} %constant.52.clone.wh) | copy-start | bytes 2949124
  17.4 4.5 %collective-permute-start.4 = (f32[8,2432]{1,0:T(8,128)S(1)}, f32[8,2432]{1,0:T(8,128)S(1)}, u32[]{:S(2)}, u32[]{:S(2)}) collective-permute-start(f32[8,2432]{1,0:T(8,128)S(1)} %get-tuple-element.35), channel_id=1, source_target_pairs={{0,1},{1,0},{2,3},{3,2},{4,5},{5,4},{6,7},{7,6},{8,9},{9,8},{10,11... | collective-permute-start | bytes 233480 | tf_op jit(solution)/shard_map/ppermute | solution.py:587
  23.3 1.4 %collective-permute-start.5 = (f32[88,256]{1,0:T(8,128)S(1)}, f32[88,256]{1,0:T(8,128)S(1)}, u32[]{:S(2)}, u32[]{:S(2)}) collective-permute-start(f32[88,256]{1,0:T(8,128)S(1)} %get-tuple-element.38), channel_id=1, source_target_pairs={{0,8},{8,0},{16,24},{24,16},{1,9},{9,1},{17,25},{25,17},{2,10},{10... | collective-permute-start | bytes 270344 | tf_op jit(solution)/shard_map/ppermute | solution.py:600
  24.6 4.7 %collective-permute-start.6 = (f32[88,256]{1,0:T(8,128)S(1)}, f32[88,256]{1,0:T(8,128)S(1)}, u32[]{:S(2)}, u32[]{:S(2)}) collective-permute-start(f32[88,256]{1,0:T(8,128)S(1)} %add.150.part), channel_id=1, source_target_pairs={{0,16},{8,24},{16,0},{24,8},{1,17},{9,25},{17,1},{25,9},{2,18},{10... | collective-permute-start | bytes 270344 | tf_op jit(solution)/shard_map/ppermute | solution.py:600
  30.9 4.5 %collective-permute-start.7 = (f32[8,2432]{1,0:T(8,128)S(1)}, f32[8,2432]{1,0:T(8,128)S(1)}, u32[]{:S(2)}, u32[]{:S(2)}) collective-permute-start(f32[8,2432]{1,0:T(8,128)S(1)} %get-tuple-element.42), channel_id=1, source_target_pairs={{0,1},{1,0},{2,3},{3,2},{4,5},{5,4},{6,7},{7,6},{8,9},{9,8},{10,11... | collective-permute-start | bytes 233480 | tf_op jit(solution)/shard_map/ppermute | solution.py:587
  36.7 1.3 %collective-permute-start.8 = (f32[64,256]{1,0:T(8,128)S(1)}, f32[64,256]{1,0:T(8,128)S(1)}, u32[]{:S(2)}, u32[]{:S(2)}) collective-permute-start(f32[64,256]{1,0:T(8,128)S(1)} %get-tuple-element.44), channel_id=1, source_target_pairs={{0,8},{8,0},{16,24},{24,16},{1,9},{9,1},{17,25},{25,17},{2,10},{10... | collective-permute-start | bytes 196616 | tf_op jit(solution)/shard_map/ppermute | solution.py:600
  38.0 4.3 %collective-permute-start.9 = (f32[64,256]{1,0:T(8,128)S(1)}, f32[64,256]{1,0:T(8,128)S(1)}, u32[]{:S(2)}, u32[]{:S(2)}) collective-permute-start(f32[64,256]{1,0:T(8,128)S(1)} %add.151.part), channel_id=1, source_target_pairs={{0,16},{8,24},{16,0},{24,8},{1,17},{9,25},{17,1},{25,9},{2,18},{10... | collective-permute-start | bytes 196616 | tf_op jit(solution)/shard_map/ppermute | solution.py:600

commit v3 on v2

--- a/solution.py
+++ b/solution.py
@@ -79,71 +79,67 @@
         if self.C - cuts[-1] <= LANES and len(cuts) > 1:
             cuts.pop()
         self.chunks = list(zip(cuts, cuts[1:] + [self.C]))
+        self.bits = (self.R - self.slots).bit_length()
+        assert self.R == 2 * self.slots and self.n_lon <= KMAX
         assert self.R == 2 * self.L and self.n_lon % 2 == 0
         assert 2 <= self.C - self.base <= LANES - 2 and 2 * self.planes <= LANES
 
 
-def pack_edges(z, fhead, ftail, shead, stail, m1, m2):
+def edge_tiles(z, count, head, tail, width):
     lane = lax.broadcasted_iota(jnp.int32, (z.R, LANES), 1)
     left = jnp.zeros((z.R, LANES), jnp.float32)
     right = left
-    first = z.C - 2 - z.base
+    first = z.C - width - z.base
+    for p in range(count):
+        here = (lane >= width * p) & (lane < width * (p + 1))
+        left = jnp.where(here, moved(head(p), width * p), left)
+        right = jnp.where(here, moved(tail(p), width * p - first), right)
+    return left, right
+
+
+def moved(x, shift):
+    shift = shift % x.shape[1]
+    return pltpu.roll(x, shift, 1) if shift else x
+
+
+def by_parity(axis, first, second, even, odd):
+    is_even = lax.axis_index(axis) % 2 == 0
+
+    @pl.when(is_even)
+    def _():
+        first[...] = even
+        second[...] = odd
+
+    @pl.when(jnp.logical_not(is_even))
+    def _():
+        first[...] = odd
+        second[...] = even
+
+
+def patch(z, ref, p, count, width, from_right, from_left):
+    lane = lax.broadcasted_iota(jnp.int32, (z.R, LANES), 1)
+    last = z.C - z.base
+    right = moved(from_right, last - width * p)
+    left = moved(from_left, LANES - width - width * p)
+    for start in sorted({z.base, z.W - LANES}):
+        tile = ref[:, start : start + LANES]
+        if start == z.base:
+            tile = jnp.where((lane >= last) & (lane < last + width), right, tile)
+        if start == z.W - LANES:
+            tile = jnp.where(lane >= LANES - width, left, tile)
+        ref[:, start : start + LANES] = tile
+
+
+def place_tiles(z, fields, surface, x, m1, m2, e1, e2):
+    lane = lax.broadcasted_iota(jnp.int32, (z.R, LANES), 1)
     for p in range(z.planes):
         f, l = divmod(p, z.L)
-        head = fhead[f, l] if p < 4 * z.L else shead[...]
-        tail = ftail[f, l] if p < 4 * z.L else stail[...]
-        here = (lane >= 2 * p) & (lane < 2 * p + 2)
-        left = jnp.where(here, pltpu.roll(head, 2 * p, 1) if p else head, left)
-        shift = (2 * p - first) % LANES
-        right = jnp.where(here, pltpu.roll(tail, shift, 1) if shift else tail, right)
-    even = lax.axis_index("lon") % 2 == 0
-
-    @pl.when(even)
-    def _():
-        m1[...] = right
-        m2[...] = left
-
-    @pl.when(jnp.logical_not(even))
-    def _():
-        m1[...] = left
-        m2[...] = right
-
-
-def widen(z, fields, surface, r1, r2, rows, keeps, x, m1, m2, sums, from_right, from_left):
-    lon_even = lax.axis_index("lon") % 2 == 0
-
-    @pl.when(lon_even)
-    def _():
-        from_right[...] = r1[...]
-        from_left[...] = r2[...]
-
-    @pl.when(jnp.logical_not(lon_even))
-    def _():
-        from_right[...] = r2[...]
-        from_left[...] = r1[...]
-
-    lane = lax.broadcasted_iota(jnp.int32, (z.R, LANES), 1)
-    last = z.C - z.base
-    fr, fl = from_right[...], from_left[...]
-    for p in range(z.planes):
-        f, l = divmod(p, z.L)
-        if p < 4 * z.L:
-            x[p, :, 0 : z.C] = fields[f, l]
-        else:
-            x[p, :, 0 : z.C] = surface[...]
-        for start in range(z.base, z.W, LANES):
-            if start == z.base:
-                tile = jnp.where(lane < last, x[p, :, start : start + LANES], 0.0)
-                shift = (last - 2 * p) % LANES
-                moved = pltpu.roll(fr, shift, 1) if shift else fr
-                tile = jnp.where((lane >= last) & (lane < last + 2), moved, tile)
-            else:
-                tile = jnp.zeros((z.R, LANES), jnp.float32)
-            if start == z.W - LANES:
-                moved = pltpu.roll(fl, LANES - 2 - 2 * p, 1)
-                tile = jnp.where(lane >= LANES - 2, moved, tile)
-            x[p, :, start : start + LANES] = tile
-
+        x[p, :, 0 : z.C] = fields[f, l] if p < 4 * z.L else surface[...]
+        x[p, :, z.base : z.base + LANES] = jnp.where(
+            lane < z.C - z.base, x[p, :, z.base : z.base + LANES], 0.0
+        )
+        if z.base + LANES < z.W:
+            x[p, :, z.base + LANES :] = jnp.zeros((z.R, z.W - z.base - LANES), jnp.float32)
     lat_even = lax.axis_index("lat") % 2 == 0
     near1 = jnp.where(lat_even, z.R - 1, 0)
     far1 = jnp.where(lat_even, z.R - 2, 1)
@@ -157,6 +153,22 @@
         msg[to : to + 1, :] = x[4 * z.L, pl.ds(near, 1), :]
         if z.lat_rows > to + 1:
             msg[to + 1 :, :] = jnp.zeros((z.lat_rows - to - 1, z.W), jnp.float32)
+    left, right = edge_tiles(
+        z,
+        z.planes,
+        lambda p: x[p, :, 0:LANES],
+        lambda p: x[p, :, z.base : z.base + LANES],
+        2,
+    )
+    by_parity("lon", e1, e2, right, left)
+
+
+def widen(z, x_in, r1, r2, x, sums, from_right, from_left):
+    del x_in
+    by_parity("lon", from_right, from_left, r1[...], r2[...])
+    right, left = from_right[...], from_left[...]
+    for p in range(z.planes):
+        patch(z, x.at[p], p, z.planes, 2, right, left)
     total = layer_weight(x[2 * z.L], x[3 * z.L])
     for l in range(1, z.L):
         total = total + layer_weight(x[2 * z.L + l], x[3 * z.L + l])
@@ -181,7 +193,7 @@
     return south, north
 
 
-def halo_rows(z, sums, r1, r2, ring, ring_surface, msg):
+def halo_rows(z, sums, r1, r2, ring, ring_surface, msg, c1, c2):
     lat_even = lax.axis_index("lat") % 2 == 0
 
     def place(d, source):
@@ -201,6 +213,11 @@
         place(0, r1)
         place(1, r2)
 
+    def row(k, lo):
+        return ring[k, :, lo : lo + LANES] if k < 4 else ring_surface[:, lo : lo + LANES]
+
+    left, right = edge_tiles(z, 5, lambda k: row(k, 0), lambda k: row(k, z.base), 1)
+    by_parity("lon", c1, c2, right, left)
     south, north = ring_sum(z, layer_weight(ring[2], ring[3]))
     put_column_sums(z, msg, sums[...], south, north)
 
@@ -270,8 +287,16 @@
             qput(l, q)
 
 
-def first_step(z, x, ring, geom, y, yring, inner, q_ring):
+def first_step(
+    z, x, ring_in, surface_in, r1, r2, geom, y, yring, ring_surface, ring, inner, q_ring, from_right, from_left
+):
     L = z.L
+    by_parity("lon", from_right, from_left, r1[...], r2[...])
+    right, left = from_right[...], from_left[...]
+    ring[...] = ring_in[...]
+    ring_surface[...] = surface_in[...]
+    for k in range(5):
+        patch(z, ring.at[k] if k < 4 else ring_surface, k, 5, 1, right, left)
     q_ring[...] = ring_geopot(z, ring[2], ring[3])
 
     def get(f, l):
@@ -315,7 +340,7 @@
     live = jnp.where(lax.axis_index("lev") < z.n_lev - 1, 1.0, 0.0)
     lat = lax.axis_index("lat")
     tile = surface + live * got[:, 0 : z.W]
-    rows = []
+    rows, beneath = [], []
     for d in range(2):
         there = jnp.where(lat > 0, 1.0, 0.0) if d == 0 else jnp.where(lat < z.n_lat - 1, 1.0, 0.0)
         parts = []
@@ -323,8 +348,10 @@
             at = z.W + (d * z.extra + t // z.R) * LANES
             parts.append(got[t % z.R : t % z.R + 1, at : at + LANES])
         sums = jnp.concatenate(parts, 1)
-        rows.append(there * (ring_surface[d * z.L : d * z.L + 1, :] + live * sums))
-    return tile, rows[0], rows[1]
+        sums = jnp.where(lax.broadcasted_iota(jnp.int32, sums.shape, 1) < z.C, sums, 0.0)
+        beneath.append(there * live * sums)
+        rows.append(there * ring_surface[d * z.L : d * z.L + 1, :] + beneath[d])
+    return tile, rows[0], rows[1], beneath[1]
 
 
 def split(x):
@@ -341,35 +368,52 @@
     return dot(high, wh[...], dims) + dot(low, wh[...], dims) + dot(high, wl[...], dims)
 
 
+def masked(z, x):
+    tail = x[:, z.base :]
+    lane = lax.broadcasted_iota(jnp.int32, tail.shape, 1)
+    tail = jnp.where(lane < z.C - z.base, tail, 0.0)
+    return jnp.concatenate([x[:, : z.base], tail], 1) if z.base else tail
+
+
 def spectra(z, x, wh, wl, phase):
-    lane = lax.broadcasted_iota(jnp.int32, (x.shape[0], z.W - z.base), 1)
-    tail = jnp.where(lane < z.C - z.base, x[:, z.base :], 0.0)
-    if z.base:
-        x = jnp.concatenate([x[:, : z.base], tail], 1)
-    else:
-        x = tail
     s = product(x, wh, wl, ((1,), (0,)))
     a, b = s[:, :KMAX], s[:, KMAX:]
     c, d = phase[0:1, :], phase[1:2, :]
     return jnp.concatenate([a * c - b * d, a * d + b * c], 1)
 
 
-def slot_row(z, rows, s):
-    lat = lax.axis_index("lat")
-    return rows[lat * z.slots + s] - lat * z.R
-
-
-def pick_spectra(z, full, rows, out):
-    for s in range(z.slots):
-        at = slot_row(z, rows, s)
-        for p in range(4 * z.L):
-            to = p * z.slots + s
-            out[to : to + 1, :] = full[pl.ds(p * z.R + at, 1), :]
-
-
-def first_spectra(z, y, yring, surface, ring_surface, got, geom, wh, wl, phase, rows, state, sring, out, full):
+def twice(x):
+    return jnp.concatenate([x, x], 1)
+
+
+def code_bit(code, k):
+    return twice((code >> k) & 1) == 1
+
+
+def compress(z, tile, code):
+    for b in range(z.bits):
+        tile = jnp.where(code_bit(code, b), pltpu.roll(tile, z.R - (1 << b), 0), tile)
+    return tile
+
+
+def expand(z, tile, code):
+    for b in reversed(range(z.bits)):
+        tile = jnp.where(code_bit(code, z.bits + b), pltpu.roll(tile, 1 << b, 0), tile)
+    return tile
+
+
+def pick_spectra(z, full, code, out):
+    code = code[0 : z.R, :]
+    row = lax.broadcasted_iota(jnp.int32, (z.R, 2 * KMAX), 0)
+    for i in range(2 * z.L):
+        a = compress(z, full[2 * i * z.R : (2 * i + 1) * z.R], code)
+        b = compress(z, full[(2 * i + 1) * z.R : (2 * i + 2) * z.R], code)
+        out[i * z.R : (i + 1) * z.R, :] = jnp.where(row < z.slots, a, pltpu.roll(b, z.slots, 0))
+
+
+def first_spectra(z, y, yring, surface, ring_surface, got, geom, wh, wl, phase, code, state, sring, out):
     L = z.L
-    g, gs, gn = level_part(z, surface[...], ring_surface, got)
+    g, gs, gn, beneath = level_part(z, surface[...], ring_surface, got)
     du = wide(geom, 0, 0, z.R, z.W) * (east(g) - g)
     dv = NORTH_COEF * (with_last(g, gn) - g)
     for l in range(L):
@@ -377,25 +421,47 @@
         state[L + l] = y[L + l] - dv
     for p in range(2 * L, 4 * L):
         state[p] = y[p]
-    south = lax.broadcasted_iota(jnp.int32, (2 * L, z.W), 0) < L
     shape = (2 * L, z.W)
-    du_north = wide(geom, 0, z.R, z.R + 2 * L, z.W) * jnp.broadcast_to(east(jnp.broadcast_to(gn, shape)) - gn, shape)
+    south = lax.broadcasted_iota(jnp.int32, shape, 0) < L
+    zonal = wide(geom, 0, z.R, z.R + 2 * L, z.W)
+    gn = jnp.broadcast_to(gn, shape)
+    du_north = zonal * (east(gn) - gn)
     dv_south = NORTH_COEF * jnp.broadcast_to(g[0:1] - gs, shape)
-    sring[0] = yring[0] - jnp.where(south, dv_south, du_north) * in_band(z, shape)
+    uv = yring[0] - jnp.where(south, dv_south, du_north) * in_band(z, shape)
+    sring[0] = uv
     sring[1] = yring[1]
     sring[2] = yring[2]
+    lane = lax.broadcasted_iota(jnp.int32, shape, 1)
+    corner = jnp.broadcast_to(beneath[:, 0:1], shape)
+    given = jnp.where((lane == z.W - 1) & jnp.logical_not(south), -zonal * corner, masked(z, uv))
     m = 4 * L * z.R
     everything = jnp.concatenate(
-        [state[...].reshape(m, z.W), sring[...].reshape(6 * L, z.W)], 0
-    )
-    full[...] = spectra(z, everything, wh, wl, phase)
-    pick_spectra(z, full, rows, out)
-    out[4 * L * z.slots :, :] = full[m:, :]
-
-
-def second_spectra(z, y, surface, ring_surface, got, geom, wh, wl, phase, rows, state, out, full):
+        [
+            masked(z, state[...].reshape(m, z.W)),
+            given,
+            masked(z, sring[1]),
+            masked(z, sring[2]),
+        ],
+        0,
+    )
+    full = spectra(z, everything, wh, wl, phase)
+    pick_spectra(z, full, code, out)
+    at = 4 * L * z.slots
+    out[at : at + 6 * L, :] = full[m:, :]
+    wide_shape = (2 * L, 2 * KMAX)
+    lane = lax.broadcasted_iota(jnp.int32, wide_shape, 1)
+    lon = lax.axis_index("lon")
+    ends = jnp.where(south[:, 0:1], uv[:, 0:1], uv[:, z.C - 1 : z.C])
+    out[at + 6 * L :, :] = jnp.where(
+        lane == lon,
+        jnp.broadcast_to(ends, wide_shape),
+        jnp.where(lane == KMAX + lon, jnp.broadcast_to(beneath[:, 0:1], wide_shape), 0.0),
+    )
+
+
+def second_spectra(z, y, surface, ring_surface, got, geom, wh, wl, phase, code, state, out):
     L = z.L
-    g, _, gn = level_part(z, surface[...], ring_surface, got)
+    g, _, gn, _ = level_part(z, surface[...], ring_surface, got)
     du = wide(geom, 0, 0, z.R, z.W) * (east(g) - g)
     dv = NORTH_COEF * (with_last(g, gn) - g)
     for l in range(L):
@@ -403,38 +469,26 @@
         state[L + l] = y[L + l] - dv
     for p in range(2 * L, 4 * L):
         state[p] = y[p]
-    full[...] = spectra(z, state[...].reshape(4 * L * z.R, z.W), wh, wl, phase)
-    pick_spectra(z, full, rows, out)
+    full = spectra(z, masked(z, state[...].reshape(4 * L * z.R, z.W)), wh, wl, phase)
+    pick_spectra(z, full, code, out)
 
 
 def mode_weight(z, keep):
+    keep = twice(keep)
     k = lax.broadcasted_iota(jnp.int32, keep.shape, 1)
     k = jnp.where(k < KMAX, k, k - KMAX)
     scale = jnp.where(k == 0, 1.0 / z.N, 2.0 / z.N)
     return jnp.where(k < keep, scale, 0.0)
 
 
-def tile_keep(z, rows, keeps, width):
-    lat = lax.axis_index("lat")
-    r = lax.broadcasted_iota(jnp.int32, (z.R, width), 0)
-    keep = jnp.zeros((z.R, width), jnp.int32)
-    for s in range(z.slots):
-        keep = jnp.where(r == slot_row(z, rows, s), keeps[lat * z.slots + s], keep)
-    return keep
-
-
-def ring_keep(z, rows, keeps, width):
-    lat = lax.axis_index("lat")
-    before = jnp.maximum(lat * z.slots - 1, 0)
-    after = jnp.minimum((lat + 1) * z.slots, z.filters - 1)
-    south = jnp.where((lat > 0) & (rows[before] == lat * z.R - 1), keeps[before], 0)
-    north = jnp.where((lat < z.n_lat - 1) & (rows[after] == (lat + 1) * z.R), keeps[after], 0)
-    r = lax.broadcasted_iota(jnp.int32, (2 * z.L, width), 0)
-    return jnp.where(r < z.L, south, north)
-
-
-def damping(keep):
-    return jnp.where(keep > 0, 1.0 - DAMPING, 0.0)
+def keeps(z, code):
+    keep = code[...] >> (2 * z.bits)
+    return keep[0 : z.R], keep[z.R :]
+
+
+def damping(z, keep, width):
+    value = jnp.where(keep > 0, 1.0 - DAMPING, 0.0)
+    return jnp.concatenate([value] * (width // LANES), 1)
 
 
 def local_modes(total, phase):
@@ -443,15 +497,13 @@
     return jnp.concatenate([a * c + b * d, b * c - a * d], 1)
 
 
-def tile_modes(z, modes, rows, weight, planes):
-    r = lax.broadcasted_iota(jnp.int32, (z.R, 2 * KMAX), 0)
+def tile_modes(z, modes, code, weight):
+    code = code[0 : z.R, :]
     out = []
-    for p in planes:
-        tile = jnp.zeros((z.R, 2 * KMAX), jnp.float32)
-        for s in range(z.slots):
-            row = modes[p * z.slots + s : p * z.slots + s + 1, :]
-            tile = jnp.where(r == slot_row(z, rows, s), jnp.broadcast_to(row, tile.shape), tile)
-        out.append(tile * weight)
+    for i in range(2 * z.L):
+        pair = modes[i * z.R : (i + 1) * z.R]
+        out.append(expand(z, pair, code) * weight)
+        out.append(expand(z, pltpu.roll(pair, z.R - z.slots, 0), code) * weight)
     return out
 
 
@@ -459,18 +511,17 @@
     return product(modes, wh, wl, ((1,), (1,)))
 
 
-def filter_mass(z, state, sring, part, got, wh, wl, phase, rows, keeps, ht, htring, uvmodes, msg):
+def filter_mass(z, state, sring, part, got, wh, wl, phase, code, ht, htring, uvmodes, msg):
     L, m = z.L, 4 * z.L * z.slots
-    modes = local_modes(part[...] + got[...], phase)
-    keep = tile_keep(z, rows, keeps, 2 * KMAX)
-    rkeep = ring_keep(z, rows, keeps, 2 * KMAX)
+    total = part[...] + got[...]
+    modes = local_modes(total, phase)
+    keep, rkeep = keeps(z, code)
     weight, rweight = mode_weight(z, keep), mode_weight(z, rkeep)
     ring = [modes[m + k * 2 * L : m + (k + 1) * 2 * L] * rweight for k in range(3)]
-    tiles = tile_modes(z, modes, rows, weight, range(4 * L))
-    uvmodes[...] = jnp.concatenate(tiles[: 2 * L] + [ring[0]], 0)
+    tiles = tile_modes(z, modes, code, weight)
+    uvmodes[...] = jnp.concatenate(tiles[: 2 * L] + [ring[0], total[m + 6 * L :]], 0)
     s = smooth(jnp.concatenate(tiles[2 * L :] + ring[1:], 0), wh, wl)
-    damp = jnp.broadcast_to(damping(keep[:, 0:1]), (z.R, z.W))
-    rdamp = jnp.broadcast_to(damping(rkeep[:, 0:1]), (2 * L, z.W))
+    damp, rdamp = damping(z, keep, z.W), damping(z, rkeep, z.W)
     for p in range(2 * L):
         x = state[2 * L + p]
         ht[p] = x + damp * (s[p * z.R : (p + 1) * z.R] - x)
@@ -485,16 +536,41 @@
     put_column_sums(z, msg, total, south, north)
 
 
-def second_step(z, state, sring, uvmodes, ht, htring, geom, wh, wl, rows, keeps, y, uv, uvring, q_ring):
+def ring_corners(z, uv, gathered, geom):
+    shape = uv.shape
+    lon = lax.axis_index("lon")
+    right = jnp.where(lon == z.n_lon - 1, 0, lon + 1)
+    left = jnp.where(lon == 0, z.n_lon - 1, lon - 1)
+    place = lax.broadcasted_iota(jnp.int32, gathered.shape, 1)
+
+    def of(lane):
+        value = jnp.sum(jnp.where(place == lane, gathered, 0.0), 1, keepdims=True)
+        return jnp.broadcast_to(value, shape)
+
+    south = lax.broadcasted_iota(jnp.int32, shape, 0) < z.L
+    north = jnp.logical_not(south)
+    lane = lax.broadcasted_iota(jnp.int32, shape, 1)
+    zonal = wide(geom, 0, z.R, z.R + 2 * z.L, z.W)
+    uv = jnp.where((lane == z.C) & south, of(right), uv)
+    uv = jnp.where((lane == z.W - 1) & north, of(left) - zonal * of(KMAX + lon), uv)
+    corner = of(KMAX + right)
+    uv = jnp.where((lane == z.C - 1) & north, uv - zonal * corner, uv)
+    row = lax.broadcasted_iota(jnp.int32, shape, 0)
+    above = jnp.where((lane == z.C) & (row == z.R - 1), NORTH_COEF * corner, 0.0)
+    return uv, above
+
+
+def second_step(z, state, sring, uvmodes, ht, htring, geom, wh, wl, code, y, uv, uvring, q_ring):
     L = z.L
-    s = smooth(uvmodes[...], wh, wl)
-    damp = jnp.broadcast_to(damping(tile_keep(z, rows, keeps, LANES)[:, 0:1]), (z.R, z.W))
-    rdamp = jnp.broadcast_to(damping(ring_keep(z, rows, keeps, LANES)[:, 0:1]), (2 * L, z.W))
+    m = 2 * L * z.R
+    s = smooth(uvmodes[0 : m + 2 * L, :], wh, wl)
+    keep, rkeep = keeps(z, code)
+    damp, rdamp = damping(z, keep, z.W), damping(z, rkeep, z.W)
+    x, above = ring_corners(z, sring[0], uvmodes[m + 2 * L :, :], geom)
     for p in range(2 * L):
-        x = state[p]
-        uv[p] = x + damp * (s[p * z.R : (p + 1) * z.R] - x)
-    x = sring[0]
-    uvring[...] = x + rdamp * (s[2 * L * z.R :] - x)
+        old = state[p] if p < L else state[p] - above
+        uv[p] = old + damp * (s[p * z.R : (p + 1) * z.R] - old)
+    uvring[...] = x + rdamp * (s[m:] - x)
     q_ring[...] = ring_geopot(z, htring[0], htring[1])
 
     def get(f, l):
@@ -510,20 +586,18 @@
     )
 
 
-def filter_all(z, state, part, got, wh, wl, phase, rows, keeps, out, held, sem):
+def filter_all(z, state, part, got, wh, wl, phase, code, out, held, sem):
     L = z.L
     modes = local_modes(part[...] + got[...], phase)
-    keep = tile_keep(z, rows, keeps, 2 * KMAX)
-    tiles = tile_modes(z, modes, rows, mode_weight(z, keep), range(4 * L))
-    high, low = split(jnp.concatenate(tiles, 0))
-    damp = damping(keep[:, 0:1])
+    keep, _ = keeps(z, code)
+    high, low = split(jnp.concatenate(tile_modes(z, modes, code, mode_weight(z, keep)), 0))
     across = ((1,), (1,))
     copies = []
     for i, (lo, hi) in enumerate(z.chunks):
         top = min(-(-hi // LANES) * LANES, z.W)
         w, v = wh[lo:top, :], wl[lo:top, :]
         s = dot(high, w, across) + dot(low, w, across) + dot(high, v, across)
-        d = jnp.broadcast_to(damp, (z.R, top - lo))
+        d = damping(z, keep, top - lo)
         for p in range(4 * L):
             x = state[p, :, lo:top]
             new = x + d * (s[p * z.R : (p + 1) * z.R] - x)
@@ -540,16 +614,16 @@
     L, R, W = z.L, z.R, z.W
     f32 = jnp.float32
     vmem = pl.BlockSpec(memory_space=pltpu.VMEM)
-    smem = pl.BlockSpec(memory_space=pltpu.SMEM)
-
-    def call(kernel, outs, ins, scratch=(), flops=1_000_000):
+
+    def call(kernel, outs, ins, scratch=(), flops=1_000_000, aliases={}):
         size = sum(int(np.prod(s)) for s in outs) * 4 + sum(i.size * i.dtype.itemsize for i in ins)
         return pl.pallas_call(
             functools.partial(kernel, z),
             out_shape=[jax.ShapeDtypeStruct(s, f32) for s in outs],
-            in_specs=[smem if i.dtype == jnp.int32 else vmem for i in ins],
+            in_specs=[vmem] * len(ins),
             out_specs=[vmem] * len(outs),
             scratch_shapes=[pltpu.VMEM(s, f32) for s in scratch],
+            input_output_aliases=aliases,
             compiler_params=pltpu.CompilerParams(vmem_limit_bytes=VMEM_LIMIT),
             cost_estimate=pl.CostEstimate(flops=flops, bytes_accessed=size, transcendentals=0),
             name=kernel.__name__,
@@ -577,6 +651,8 @@
     angle = turn.astype(f32) * (2.0 * jnp.pi / z.N)
     phase = jnp.stack([jnp.cos(angle), jnp.sin(angle)])
 
+    code = row_code(z, lat, filter_rows, keep_counts)
+
     lon_one = [(i, i ^ 1) for i in range(z.n_lon)]
     lon_two = [(i, (((i + 1) % z.n_lon ^ 1) - 1) % z.n_lon) for i in range(z.n_lon)]
     lat_one = [(i, i ^ 1) for i in range(z.n_lat) if i ^ 1 < z.n_lat]
@@ -601,79 +677,64 @@
             step *= 2
         return part, got
 
-    head = lambda i: (0, 0, 0, 0)
-    tail = lambda i: (0, 0, 0, z.base // LANES)
-    edge = pl.BlockSpec((R, LANES), lambda i: (0, 0))
-    e1, e2 = pl.pallas_call(
-        functools.partial(pack_edges, z),
-        grid=(1,),
-        out_shape=[jax.ShapeDtypeStruct((R, LANES), f32)] * 2,
-        in_specs=[
-            pl.BlockSpec((4, L, R, LANES), head),
-            pl.BlockSpec((4, L, R, LANES), tail),
-            edge,
-            pl.BlockSpec((R, LANES), lambda i: (0, z.base // LANES)),
-        ],
-        out_specs=[edge] * 2,
-        name="pack_edges",
-    )(fields, fields, surface, surface)
+    tile = (R, LANES)
+    x, m1, m2, e1, e2 = call(
+        place_tiles,
+        [(z.planes, R, W), (z.lat_rows, W), (z.lat_rows, W), tile, tile],
+        [fields, surface],
+    )
+    m1 = lax.ppermute(m1, "lat", lat_one)
+    m2 = lax.ppermute(m2, "lat", lat_two)
     e1 = lax.ppermute(e1, "lon", lon_one)
     e2 = lax.ppermute(e2, "lon", lon_two)
-
-    x, m1, m2, sums = call(
-        widen,
-        [(z.planes, R, W), (z.lat_rows, W), (z.lat_rows, W), (R, W)],
-        [fields, surface, e1, e2, filter_rows, keep_counts],
-        [(R, LANES)] * 2,
-    )
-    m1 = lax.ppermute(m1, "lat", lat_one)
-    m2 = lax.ppermute(m2, "lat", lat_two)
+    x, sums = call(
+        widen, [(z.planes, R, W), (R, W)], [x, e1, e2], [tile] * 2, aliases={0: 0}
+    )
 
     sent = (R, W + 2 * z.extra * LANES)
-    ring, ring_surface, msg = call(
-        halo_rows, [(7, 2 * L, W), (2 * L, W), sent], [sums, m1, m2]
-    )
+    ring, ring_surface, msg, c1, c2 = call(
+        halo_rows, [(7, 2 * L, W), (2 * L, W), sent, tile, tile], [sums, m1, m2]
+    )
+    c1 = lax.ppermute(c1, "lon", lon_one)
+    c2 = lax.ppermute(c2, "lon", lon_two)
     got = from_below(msg)
-    y, yring = call(
+    y, yring, ring_surface = call(
         first_step,
-        [(4 * L, R, W), (3, 2 * L, W)],
-        [x, ring, geom],
-        [(4, 2 * L, W), (2 * L, W)],
+        [(4 * L, R, W), (3, 2 * L, W), (2 * L, W)],
+        [x, ring, ring_surface, c1, c2, geom],
+        [(7, 2 * L, W), (4, 2 * L, W), (2 * L, W), tile, tile],
         flops=10_000_000,
     )
-    m = 4 * L * R
     surface_tile = x[4 * L]
     state, sring, part = call(
         first_spectra,
-        [(4 * L, R, W), (3, 2 * L, W), (4 * L * z.slots + 6 * L, 2 * KMAX)],
-        [y, yring, surface_tile, ring_surface, got, geom, wave_high, wave_low, phase, filter_rows],
-        [(m + 6 * L, 2 * KMAX)],
+        [(4 * L, R, W), (3, 2 * L, W), (4 * L * z.slots + 8 * L, 2 * KMAX)],
+        [y, yring, surface_tile, ring_surface, got, geom, wave_high, wave_low, phase, code],
     )
     part, got = over_lon(part)
     ht, htring, uvmodes, msg = call(
         filter_mass,
-        [(2 * L, R, W), (2, 2 * L, W), (2 * L * R + 2 * L, 2 * KMAX), sent],
-        [state, sring, part, got, wave_high, wave_low, phase, filter_rows, keep_counts],
+        [(2 * L, R, W), (2, 2 * L, W), (2 * L * R + 4 * L, 2 * KMAX), sent],
+        [state, sring, part, got, wave_high, wave_low, phase, code],
     )
     got = from_below(msg)
     (y,) = call(
         second_step,
         [(4 * L, R, W)],
-        [state, sring, uvmodes, ht, htring, geom, wave_high, wave_low, filter_rows, keep_counts],
+        [state, sring, uvmodes, ht, htring, geom, wave_high, wave_low, code],
         [(2 * L, R, W), (2 * L, W), (2 * L, W)],
         flops=10_000_000,
     )
     state, part = call(
         second_spectra,
         [(4 * L, R, W), (4 * L * z.slots, 2 * KMAX)],
-        [y, surface_tile, ring_surface, got, geom, wave_high, wave_low, phase, filter_rows],
-        [(m, 2 * KMAX)],
+        [y, surface_tile, ring_surface, got, geom, wave_high, wave_low, phase, code],
     )
     part, got = over_lon(part)
     return pl.pallas_call(
         functools.partial(filter_all, z),
         out_shape=jax.ShapeDtypeStruct((4, L, R, z.C), f32),
-        in_specs=[vmem] * 6 + [smem] * 2,
+        in_specs=[vmem] * 7,
         out_specs=pl.BlockSpec(memory_space=pl.ANY),
         scratch_shapes=[
             pltpu.VMEM((4, L, R, z.C), f32),
@@ -681,7 +742,31 @@
         ],
         compiler_params=pltpu.CompilerParams(vmem_limit_bytes=VMEM_LIMIT),
         name="filter_all",
-    )(state, part, got, wave_high, wave_low, phase, filter_rows, keep_counts)
+    )(state, part, got, wave_high, wave_low, phase, code)
+
+
+def row_code(z, lat, filter_rows, keep_counts):
+    row = lax.broadcasted_iota(jnp.int32, (z.R + 2 * z.L, LANES), 0)
+    own = lax.dynamic_slice_in_dim(filter_rows, lat * z.slots, z.slots) - lat * z.R
+    kept = lax.dynamic_slice_in_dim(keep_counts, lat * z.slots, z.slots)
+    code = jnp.zeros(row.shape, jnp.int32)
+    for s in range(z.slots):
+        at = own[s]
+        code = code + jnp.where(row == at, kept[s] << (2 * z.bits), 0)
+        for b in range(z.bits):
+            bit = ((own[s] - s) >> b) & 1
+            to = at - (bit << b)
+            code = code + jnp.where((row == to) & (bit == 1), 1 << b, 0)
+            code = code + jnp.where((row == at) & (bit == 1), 1 << (z.bits + b), 0)
+            at = to
+    before = jnp.maximum(lat * z.slots - 1, 0)
+    after = jnp.minimum((lat + 1) * z.slots, z.filters - 1)
+    south = jnp.where((lat > 0) & (filter_rows[before] == lat * z.R - 1), keep_counts[before], 0)
+    north = jnp.where(
+        (lat < z.n_lat - 1) & (filter_rows[after] == (lat + 1) * z.R), keep_counts[after], 0
+    )
+    ring = jnp.where(row < z.R + z.L, south, north) << (2 * z.bits)
+    return jnp.where(row < z.R, code, ring)
 
 
 def wave_tables(z):

time: 45 us -> 54.7 us (1.22)
  between operations: 0.16 us -> 12 us
  waiting for transfers between devices: 18.2 us -> 11.8 us
  local copies, waits for them, and re-layouts: 0.03 us -> 5.41 us
  Pallas kernels: 12.3 us -> 7.71 us
  other arithmetic: 0.77 us -> 3.58 us
  starting transfers between devices: 13.2 us -> 13.8 us
    unnamed x12, local copies, waits for them, and re-layouts: 0.03 us -> 3.34 us
    ppermute x1, waiting for transfers between devices: 3.08 us -> 0.01 us  [local(): m1 = lax.ppermute(m1, 'lat', lat_one)]
    ppermute x1, waiting for transfers between devices: 3.02 us -> 0.01 us  [local(): m2 = lax.ppermute(m2, 'lat', lat_two)]
    add x0 -> x1, other arithmetic: none -> 2.66 us  [row_code(): code = code + jnp.where((row == at) & (bit == 1), 1 << z.bits + b, 0)]
    pallas_call x7 -> x8, Pallas kernels: 8.33 us -> 5.85 us  [call(): pl.pallas_call(functools.partial(kernel, z), out_shape=[jax.ShapeDtypeStr...]
    pallas_call x1 -> x0, Pallas kernels: 1.66 us -> none  [local(): pl.pallas_call(functools.partial(pack_edges, z), grid=(1,), out_shape=[ja...]
    slice x0 -> x2, local copies, waits for them, and re-layouts: none -> 1.33 us  [the longest x1 0.67 us: row_code(): at = own[s]]
    ppermute x1, waiting for transfers between devices: 1.03 us -> 0.01 us  [local(): e2 = lax.ppermute(e2, 'lon', lon_two)]
  transfers between devices with their start and end apart: 10 -> 12, of which waited for: 9 -> 7; matrix products, arithmetic and copies ran while one was open for 2% -> 10% of each run, Pallas kernels for 7% -> 5%
where the time goes in v3:
time: 54.7 us; the launch traced here: 54.2 us
  starting transfers between devices  13.8 us (25%)
  between operations  12 us (22%)
  waiting for transfers between devices  11.8 us (22%)
  Pallas kernels  7.71 us (14%)
  local copies, waits for them, and re-layouts  5.41 us (10%)
  other arithmetic  3.58 us (7%)
    ppermute x4, waiting for transfers between devices, over_lon(): got = lax.ppermute(part, 'lon', [(i, i ^ step) for i in range(z.n_lon)])  8.61 us
    pallas_call x8, Pallas kernels, call(): pl.pallas_call(functools.partial(kernel, z), out_shape=[jax.ShapeDtypeStr...  5.85 us
    ppermute x1, starting transfers between devices, local(): m2 = lax.ppermute(m2, 'lat', lat_two)  4.6 us
    unnamed x12, local copies, waits for them, and re-layouts  3.34 us
    ppermute x4, starting transfers between devices, over_lon(): got = lax.ppermute(part, 'lon', [(i, i ^ step) for i in range(z.n_lon)])  3.31 us
    ppermute x2, starting transfers between devices, from_below(): return lax.ppermute(column, 'lev', [(0, 1), (1, 0)])  3.05 us
    add x1, other arithmetic, row_code(): code = code + jnp.where((row == at) & (bit == 1), 1 << z.bits + b, 0)  2.66 us
    ppermute x2, waiting for transfers between devices, from_below(): return lax.ppermute(column, 'lev', [(0, 1), (1, 0)])  2.2 us
  transfers between devices with their start and end apart: 12, of which 7 were waited for; matrix products, arithmetic and copies ran while one was open for 10% of the time, Pallas kernels for 5%

profile of v3, /device:TPU:8, one launch (start us, length us, event | category | flops | bytes accessed | tf_op | source)
XLA Modules:
  0.0 54.2 jit_solution(4532175463241264954)
XLA Ops:
  0.0 1.2 %copy-done.2 = f32[4,4,8,1800]{3,2,1,0:T(8,128)S(1)} copy-done((f32[4,4,8,1800]{3,2,1,0:T(8,128)S(1)}, f32[4,4,8,1800]{3,2,1,0:T(8,128)}, u32[]{:S(2)}) %copy-start.2) | copy-done | bytes 921624
  1.2 0.8 %copy-done.3 = f32[8,1800]{1,0:T(8,128)S(1)} copy-done((f32[8,1800]{1,0:T(8,128)S(1)}, f32[8,1800]{1,0:T(8,128)}, u32[]{:S(2)}) %copy-start.3) | copy-done | bytes 57624
  2.4 1.6 %collective-permute-start.1 = (f32[8,128]{1,0:T(8,128)S(1)}, f32[8,128]{1,0:T(8,128)S(1)}, u32[]{:S(2)}, u32[]{:S(2)}) collective-permute-start(f32[8,128]{1,0:T(8,128)S(1)} %get-tuple-element.31), channel_id=1, source_target_pairs={{0,24},{8,16},{16,8},{24,0},{1,25},{9,17},{17,9},{25,1},{2,26},{10... | collective-permute-start | bytes 12296 | tf_op jit(solution)/shard_map/ppermute | solution.py:689
  4.5 4.6 %collective-permute-start.3 = (f32[32,1920]{1,0:T(8,128)S(1)}, f32[32,1920]{1,0:T(8,128)S(1)}, u32[]{:S(2)}, u32[]{:S(2)}) collective-permute-start(f32[32,1920]{1,0:T(8,128)S(1)} %get-tuple-element.35), channel_id=1, source_target_pairs={{2,4},{4,2},{3,5},{5,3},{10,12},{12,10},{11,13},{13,11},{18,20},{2... | collective-permute-start | bytes 737288 | tf_op jit(solution)/shard_map/ppermute | solution.py:687
  9.9 0.7 %fusion.34 = (s32[1]{0:T(128)}, s32[1]{0:T(128)}, s32[1]{0:T(128)}, s32[1]{0:T(128)}) fusion(s32[4]{0:T(128)S(1)} %dynamic-slice_subtract_fusion), kind=kLoop, calls=%fused_computation.78 | loop fusion | bytes 32 | tf_op jit(solution)/shard_map/slice | solution.py:754
  21.6 0.7 %fusion.35 = (s32[1]{0:T(128)}, s32[1]{0:T(128)}, s32[1]{0:T(128)}, s32[1]{0:T(128)}) fusion(s32[16]{0:T(128)S(1)} %copy-done.5, s32[]{:T(128)S(6)} %max.3, s32[]{:T(128)S(6)} %select_n.222, s32[16]{0:T(128)S(1)} %copy-done.4), kind=kLoop, calls=%fused_computation.79 | loop fusion | bytes 40 | tf_op jit(solution)/shard_map/dynamic_slice | solution.py:764
  24.9 2.7 %fusion.24 = s32[16]{0:T(128)S(1)} fusion(pred[]{:T(512)S(6)} %eq.235, pred[]{:T(512)S(6)} %eq.232, pred[]{:T(512)S(6)} %eq.229, pred[]{:T(512)S(6)} %eq.224, pred[]{:T(512)S(6)} %eq.221, pred[]{:T(512)S(6)} %eq.218, pred[]{:T(512)S(6)} %eq.213, pred[]{:T(512)S(6)} %eq.210, pred[]{:T(512)S(6)} %eq.207, pred[]{:T(512)S(6)} %eq.202, pred[]{:T(512)S(6)} %eq.199, ...), kind=kLoop, calls=%fused_computation.67 | loop fusion | flops 1520 | bytes 156 | tf_op jit(solution)/shard_map/add | solution.py:760
  29.0 1.5 %collective-permute-start.6 = (f32[8,2432]{1,0:T(8,128)S(1)}, f32[8,2432]{1,0:T(8,128)S(1)}, u32[]{:S(2)}, u32[]{:S(2)}) collective-permute-start(f32[8,2432]{1,0:T(8,128)S(1)} %get-tuple-element.43), channel_id=1, source_target_pairs={{0,1},{1,0},{2,3},{3,2},{4,5},{5,4},{6,7},{7,6},{8,9},{9,8},{10,11... | collective-permute-start | bytes 233480 | tf_op jit(solution)/shard_map/ppermute | solution.py:663
  30.5 1.0 %collective-permute-done.5.r2 = f32[8,128]{1,0:T(8,128)S(1)} collective-permute-done((f32[8,128]{1,0:T(8,128)S(1)}, f32[8,128]{1,0:T(8,128)S(1)}, u32[]{:S(2)}, u32[]{:S(2)}) %collective-permute-start.5) | collective-permute-done | bytes 4128 | tf_op jit(solution)/shard_map/ppermute | solution.py:699
  31.5 1.1 %first_step.1 = (f32[16,8,1920]{2,1,0:T(8,128)S(1)}, f32[3,8,1920]{2,1,0:T(8,128)S(1)}, f32[8,1920]{1,0:T(8,128)S(1)}) custom-call(f32[17,8,1920]{2,1,0:T(8,128)S(1)} %get-tuple-element.32.x, f32[7,8,1920]{2,1,0:T(8,128)S(1)} %get-tuple-element.36.ring_in, f32[8,1920]{1,0:T(8,128)S(1)} %get-tuple-element.37.surface_in, ...), custom_call_target="tpu_custom_call" | custom-call | flops 10000000 | bytes 2813952 | tf_op jit(solution)/shard_map/first_step/pallas_call | solution.py:620
  32.6 0.8 %collective-permute-done.6.got = f32[8,2432]{1,0:T(8,128)S(1)} collective-permute-done((f32[8,2432]{1,0:T(8,128)S(1)}, f32[8,2432]{1,0:T(8,128)S(1)}, u32[]{:S(2)}, u32[]{:S(2)}) %collective-permute-start.6) | collective-permute-done | bytes 77856 | tf_op jit(solution)/shard_map/ppermute | solution.py:663
  33.4 0.8 %first_spectra.1 = (f32[16,8,1920]{2,1,0:T(8,128)S(1)}, f32[3,8,1920]{2,1,0:T(8,128)S(1)}, f32[96,256]{1,0:T(8,128)S(1)}) custom-call(f32[16,8,1920]{2,1,0:T(8,128)S(1)} %get-tuple-element.40.y, f32[3,8,1920]{2,1,0:T(8,128)S(1)} %get-tuple-element.41.yring, f32[8,1920]{1,0:T(8,128)S(1)} %slice_bitcast_fusion.surface, ...), custom_call_target="tpu_custom_call" | custom-call | flops 1000000 | bytes 4649984 | tf_op jit(solution)/shard_map/first_spectra/pallas_call | solution.py:620
  34.3 1.3 %collective-permute-done.7 = f32[96,256]{1,0:T(8,128)S(1)} collective-permute-done((f32[96,256]{1,0:T(8,128)S(1)}, f32[96,256]{1,0:T(8,128)S(1)}, u32[]{:S(2)}, u32[]{:S(2)}) %collective-permute-start.7) | collective-permute-done | bytes 98336 | tf_op jit(solution)/shard_map/ppermute | solution.py:676
  35.6 1.6 %collective-permute-start.8 = (f32[96,256]{1,0:T(8,128)S(1)}, f32[96,256]{1,0:T(8,128)S(1)}, u32[]{:S(2)}, u32[]{:S(2)}) collective-permute-start(f32[96,256]{1,0:T(8,128)S(1)} %add.307.part), channel_id=1, source_target_pairs={{0,16},{8,24},{16,0},{24,8},{1,17},{9,25},{17,1},{25,9},{2,18},{10... | collective-permute-start | bytes 294920 | tf_op jit(solution)/shard_map/ppermute | solution.py:676
  37.2 3.3 %collective-permute-done.8.got = f32[96,256]{1,0:T(8,128)S(1)} collective-permute-done((f32[96,256]{1,0:T(8,128)S(1)}, f32[96,256]{1,0:T(8,128)S(1)}, u32[]{:S(2)}, u32[]{:S(2)}) %collective-permute-start.8) | collective-permute-done | bytes 98336 | tf_op jit(solution)/shard_map/ppermute | solution.py:676
  40.5 1.0 %filter_mass.1 = (f32[8,8,1920]{2,1,0:T(8,128)S(1)}, f32[2,8,1920]{2,1,0:T(8,128)S(1)}, f32[80,256]{1,0:T(8,128)S(1)}, f32[8,2432]{1,0:T(8,128)S(1)}) custom-call(f32[16,8,1920]{2,1,0:T(8,128)S(1)} %get-tuple-element.44.state, f32[3,8,1920]{2,1,0:T(8,128)S(1)} %get-tuple-element.45.sring, f32[96,256]{1,0:T(8,128)S(1)} %add.307.part, ...), custom_call_target="tpu_custom_call" | custom-call | flops 1000000 | bytes 4113408 | tf_op jit(solution)/shard_map/filter_mass/pallas_call | solution.py:620
  41.5 1.6 %collective-permute-start.9 = (f32[8,2432]{1,0:T(8,128)S(1)}, f32[8,2432]{1,0:T(8,128)S(1)}, u32[]{:S(2)}, u32[]{:S(2)}) collective-permute-start(f32[8,2432]{1,0:T(8,128)S(1)} %get-tuple-element.50), channel_id=1, source_target_pairs={{0,1},{1,0},{2,3},{3,2},{4,5},{5,4},{6,7},{7,6},{8,9},{9,8},{10,11... | collective-permute-start | bytes 233480 | tf_op jit(solution)/shard_map/ppermute | solution.py:663
  43.1 1.5 %second_step.1.y = f32[16,8,1920]{2,1,0:T(8,128)S(1)} custom-call(f32[16,8,1920]{2,1,0:T(8,128)S(1)} %get-tuple-element.44.state, f32[3,8,1920]{2,1,0:T(8,128)S(1)} %get-tuple-element.45.sring, f32[80,256]{1,0:T(8,128)S(1)} %get-tuple-element.47.uvmodes, f32[8,8,1920]{2,1,0:T(8,128)S(1)} %get-tuple-element.48.ht, ...), custom_call_target="tpu_custom_call" | custom-call | flops 10000000 | bytes 4861952 | tf_op jit(solution)/shard_map/second_step/pallas_call | solution.py:620
  44.6 1.4 %collective-permute-done.9.got = f32[8,2432]{1,0:T(8,128)S(1)} collective-permute-done((f32[8,2432]{1,0:T(8,128)S(1)}, f32[8,2432]{1,0:T(8,128)S(1)}, u32[]{:S(2)}, u32[]{:S(2)}) %collective-permute-start.9) | collective-permute-done | bytes 77856 | tf_op jit(solution)/shard_map/ppermute | solution.py:663
  46.0 0.7 %second_spectra.1 = (f32[16,8,1920]{2,1,0:T(8,128)S(1)}, f32[64,256]{1,0:T(8,128)S(1)}) custom-call(f32[16,8,1920]{2,1,0:T(8,128)S(1)} %second_step.1.y, f32[8,1920]{1,0:T(8,128)S(1)} %slice_bitcast_fusion.surface, f32[8,1920]{1,0:T(8,128)S(1)} %get-tuple-element.42.ring_surface, f32[8,2432]{1,0:T(8,128)S(1)} %collective-permute-done.9.got, ...), custom_call_target="tpu_custom_call" | custom-call | flops 1000000 | bytes 4248576 | tf_op jit(solution)/shard_map/second_spectra/pallas_call | solution.py:620
  46.8 1.2 %collective-permute-done.10 = f32[64,256]{1,0:T(8,128)S(1)} collective-permute-done((f32[64,256]{1,0:T(8,128)S(1)}, f32[64,256]{1,0:T(8,128)S(1)}, u32[]{:S(2)}, u32[]{:S(2)}) %collective-permute-start.10) | collective-permute-done | bytes 65568 | tf_op jit(solution)/shard_map/ppermute | solution.py:676
  48.1 1.6 %collective-permute-start.11 = (f32[64,256]{1,0:T(8,128)S(1)}, f32[64,256]{1,0:T(8,128)S(1)}, u32[]{:S(2)}, u32[]{:S(2)}) collective-permute-start(f32[64,256]{1,0:T(8,128)S(1)} %add.308.part), channel_id=1, source_target_pairs={{0,16},{8,24},{16,0},{24,8},{1,17},{9,25},{17,1},{25,9},{2,18},{10... | collective-permute-start | bytes 196616 | tf_op jit(solution)/shard_map/ppermute | solution.py:676
  49.6 2.7 %collective-permute-done.11.got = f32[64,256]{1,0:T(8,128)S(1)} collective-permute-done((f32[64,256]{1,0:T(8,128)S(1)}, f32[64,256]{1,0:T(8,128)S(1)}, u32[]{:S(2)}, u32[]{:S(2)}) %collective-permute-start.11) | collective-permute-done | bytes 65568 | tf_op jit(solution)/shard_map/ppermute | solution.py:676
  52.4 1.9 %filter_all.1 = f32[4,4,8,1800]{3,2,1,0:T(8,128)} custom-call(f32[16,8,1920]{2,1,0:T(8,128)S(1)} %get-tuple-element.51.state, f32[64,256]{1,0:T(8,128)S(1)} %add.308.part, f32[64,256]{1,0:T(8,128)S(1)} %collective-permute-done.11.got, bf16[1920,256]{1,0:T(8,128)(2,1)S(1)} %copy-done.1, bf16[1920,256]{1,0:T(8,128)(2,1)S(1)} %copy-done, ...), custom_call_target="tpu_custom_call" | custom-call | tf_op jit(solution)/shard_map/filter_all/pallas_call | solution.py:734
  (41 shorter events, 5.0 us)
Async XLA Ops:
  0.0 1.2 %copy-start.2 = (f32[4,4,8,1800]{3,2,1,0:T(8,128)S(1)}, f32[4,4,8,1800]{3,2,1,0:T(8,128)}, u32[]{:S(2)}) copy-start(f32[4,4,8,1800]{3,2,1,0:T(8,128)} %fields.1) | copy-start | bytes 2764804
  1.2 0.8 %copy-start.3 = (f32[8,1800]{1,0:T(8,128)S(1)}, f32[8,1800]{1,0:T(8,128)}, u32[]{:S(2)}) copy-start(f32[8,1800]{1,0:T(8,128)} %surface.1) | copy-start | bytes 172804
  2.4 25.5 %collective-permute-start = (f32[8,128]{1,0:T(8,128)S(1)}, f32[8,128]{1,0:T(8,128)S(1)}, u32[]{:S(2)}, u32[]{:S(2)}) collective-permute-start(f32[8,128]{1,0:T(8,128)S(1)} %get-tuple-element.30), channel_id=1, source_target_pairs={{0,8},{8,0},{16,24},{24,16},{1,9},{9,1},{17,25},{25,17},{2,10},{10... | collective-permute-start | bytes 12296 | tf_op jit(solution)/shard_map/ppermute | solution.py:688
  2.4 25.4 %collective-permute-start.1 = (f32[8,128]{1,0:T(8,128)S(1)}, f32[8,128]{1,0:T(8,128)S(1)}, u32[]{:S(2)}, u32[]{:S(2)}) collective-permute-start(f32[8,128]{1,0:T(8,128)S(1)} %get-tuple-element.31), channel_id=1, source_target_pairs={{0,24},{8,16},{16,8},{24,0},{1,25},{9,17},{17,9},{25,1},{2,26},{10... | collective-permute-start | bytes 12296 | tf_op jit(solution)/shard_map/ppermute | solution.py:689
  4.1 23.9 %collective-permute-start.2 = (f32[32,1920]{1,0:T(8,128)S(1)}, f32[32,1920]{1,0:T(8,128)S(1)}, u32[]{:S(2)}, u32[]{:S(2)}) collective-permute-start(f32[32,1920]{1,0:T(8,128)S(1)} %get-tuple-element.34), channel_id=1, source_target_pairs={{0,2},{2,0},{4,6},{6,4},{1,3},{3,1},{5,7},{7,5},{8,10},{10,8},{12,... | collective-permute-start | bytes 737288 | tf_op jit(solution)/shard_map/ppermute | solution.py:686
  4.5 23.5 %collective-permute-start.3 = (f32[32,1920]{1,0:T(8,128)S(1)}, f32[32,1920]{1,0:T(8,128)S(1)}, u32[]{:S(2)}, u32[]{:S(2)}) collective-permute-start(f32[32,1920]{1,0:T(8,128)S(1)} %get-tuple-element.35), channel_id=1, source_target_pairs={{2,4},{4,2},{3,5},{5,3},{10,12},{12,10},{11,13},{13,11},{18,20},{2... | collective-permute-start | bytes 737288 | tf_op jit(solution)/shard_map/ppermute | solution.py:687
  9.2 0.7 %copy-start.4 = (s32[16]{0:T(128)S(1)}, s32[16]{0:T(128)}, u32[]{:S(2)}) copy-start(s32[16]{0:T(128)} %param.8) | copy-start | bytes 196
  14.6 0.7 %copy-start.5 = (s32[16]{0:T(128)S(1)}, s32[16]{0:T(128)}, u32[]{:S(2)}) copy-start(s32[16]{0:T(128)} %param.9) | copy-start | bytes 196
  28.0 5.4 %copy-start.1 = (bf16[1920,256]{1,0:T(8,128)(2,1)S(1)}, bf16[1920,256]{1,0:T(8,128)(2,1)}, u32[]{:S(2)}) copy-start(bf16[1920,256]{1,0:T(8,128)(2,1)} %constant.83.clone.wh) | copy-start | bytes 2949124
  28.3 5.1 %copy-start = (bf16[1920,256]{1,0:T(8,128)(2,1)S(1)}, bf16[1920,256]{1,0:T(8,128)(2,1)}, u32[]{:S(2)}) copy-start(bf16[1920,256]{1,0:T(8,128)(2,1)} %constant.84.clone.wl) | copy-start | bytes 2949124
  28.3 2.2 %collective-permute-start.4 = (f32[8,128]{1,0:T(8,128)S(1)}, f32[8,128]{1,0:T(8,128)S(1)}, u32[]{:S(2)}, u32[]{:S(2)}) collective-permute-start(f32[8,128]{1,0:T(8,128)S(1)} %get-tuple-element.38), channel_id=1, source_target_pairs={{0,8},{8,0},{16,24},{24,16},{1,9},{9,1},{17,25},{25,17},{2,10},{10... | collective-permute-start | bytes 12296 | tf_op jit(solution)/shard_map/ppermute | solution.py:698
  28.4 3.1 %collective-permute-start.5 = (f32[8,128]{1,0:T(8,128)S(1)}, f32[8,128]{1,0:T(8,128)S(1)}, u32[]{:S(2)}, u32[]{:S(2)}) collective-permute-start(f32[8,128]{1,0:T(8,128)S(1)} %get-tuple-element.39), channel_id=1, source_target_pairs={{0,24},{8,16},{16,8},{24,0},{1,25},{9,17},{17,9},{25,1},{2,26},{10... | collective-permute-start | bytes 12296 | tf_op jit(solution)/shard_map/ppermute | solution.py:699
  29.0 4.4 %collective-permute-start.6 = (f32[8,2432]{1,0:T(8,128)S(1)}, f32[8,2432]{1,0:T(8,128)S(1)}, u32[]{:S(2)}, u32[]{:S(2)}) collective-permute-start(f32[8,2432]{1,0:T(8,128)S(1)} %get-tuple-element.43), channel_id=1, source_target_pairs={{0,1},{1,0},{2,3},{3,2},{4,5},{5,4},{6,7},{7,6},{8,9},{9,8},{10,11... | collective-permute-start | bytes 233480 | tf_op jit(solution)/shard_map/ppermute | solution.py:663
  34.2 1.4 %collective-permute-start.7 = (f32[96,256]{1,0:T(8,128)S(1)}, f32[96,256]{1,0:T(8,128)S(1)}, u32[]{:S(2)}, u32[]{:S(2)}) collective-permute-start(f32[96,256]{1,0:T(8,128)S(1)} %get-tuple-element.46), channel_id=1, source_target_pairs={{0,8},{8,0},{16,24},{24,16},{1,9},{9,1},{17,25},{25,17},{2,10},{10... | collective-permute-start | bytes 294920 | tf_op jit(solution)/shard_map/ppermute | solution.py:676
  35.6 4.9 %collective-permute-start.8 = (f32[96,256]{1,0:T(8,128)S(1)}, f32[96,256]{1,0:T(8,128)S(1)}, u32[]{:S(2)}, u32[]{:S(2)}) collective-permute-start(f32[96,256]{1,0:T(8,128)S(1)} %add.307.part), channel_id=1, source_target_pairs={{0,16},{8,24},{16,0},{24,8},{1,17},{9,25},{17,1},{25,9},{2,18},{10... | collective-permute-start | bytes 294920 | tf_op jit(solution)/shard_map/ppermute | solution.py:676
  41.5 4.5 %collective-permute-start.9 = (f32[8,2432]{1,0:T(8,128)S(1)}, f32[8,2432]{1,0:T(8,128)S(1)}, u32[]{:S(2)}, u32[]{:S(2)}) collective-permute-start(f32[8,2432]{1,0:T(8,128)S(1)} %get-tuple-element.50), channel_id=1, source_target_pairs={{0,1},{1,0},{2,3},{3,2},{4,5},{5,4},{6,7},{7,6},{8,9},{9,8},{10,11... | collective-permute-start | bytes 233480 | tf_op jit(solution)/shard_map/ppermute | solution.py:663
  46.7 1.3 %collective-permute-start.10 = (f32[64,256]{1,0:T(8,128)S(1)}, f32[64,256]{1,0:T(8,128)S(1)}, u32[]{:S(2)}, u32[]{:S(2)}) collective-permute-start(f32[64,256]{1,0:T(8,128)S(1)} %get-tuple-element.52), channel_id=1, source_target_pairs={{0,8},{8,0},{16,24},{24,16},{1,9},{9,1},{17,25},{25,17},{2,10},{10... | collective-permute-start | bytes 196616 | tf_op jit(solution)/shard_map/ppermute | solution.py:676
  48.1 4.3 %collective-permute-start.11 = (f32[64,256]{1,0:T(8,128)S(1)}, f32[64,256]{1,0:T(8,128)S(1)}, u32[]{:S(2)}, u32[]{:S(2)}) collective-permute-start(f32[64,256]{1,0:T(8,128)S(1)} %add.308.part), channel_id=1, source_target_pairs={{0,16},{8,24},{16,0},{24,8},{1,17},{9,25},{17,1},{25,9},{2,18},{10... | collective-permute-start | bytes 196616 | tf_op jit(solution)/shard_map/ppermute | solution.py:676

commit v4 on v3

--- a/solution.py
+++ b/solution.py
@@ -130,11 +130,16 @@
         ref[:, start : start + LANES] = tile
 
 
-def place_tiles(z, fields, surface, x, m1, m2, e1, e2):
+def place_tiles(z, fields, surface, x, m1, m2, e1, e2, held, held_surface, sem):
     lane = lax.broadcasted_iota(jnp.int32, (z.R, LANES), 1)
+    copies = [pltpu.make_async_copy(fields.at[f], held.at[f], sem.at[f]) for f in range(4)]
+    copies.append(pltpu.make_async_copy(surface, held_surface, sem.at[4]))
+    for copy in copies:
+        copy.start()
     for p in range(z.planes):
-        f, l = divmod(p, z.L)
-        x[p, :, 0 : z.C] = fields[f, l] if p < 4 * z.L else surface[...]
+        if p % z.L == 0:
+            copies[p // z.L].wait()
+        x[p, :, 0 : z.C] = held[p // z.L, p % z.L] if p < 4 * z.L else held_surface[...]
         x[p, :, z.base : z.base + LANES] = jnp.where(
             lane < z.C - z.base, x[p, :, z.base : z.base + LANES], 0.0
         )
@@ -610,6 +615,30 @@
         copy.wait()
 
 
+def row_code(z, rows, counts, out):
+    row = lax.broadcasted_iota(jnp.int32, (z.R + 2 * z.L, LANES), 0)
+    lat = lax.axis_index("lat")
+    code = jnp.zeros(row.shape, jnp.int32)
+    for s in range(z.slots):
+        at = rows[lat * z.slots + s] - lat * z.R
+        far = at - s
+        code = code + jnp.where(row == at, counts[lat * z.slots + s] << (2 * z.bits), 0)
+        for b in range(z.bits):
+            bit = (far >> b) & 1
+            to = at - (bit << b)
+            code = code + jnp.where((row == to) & (bit == 1), 1 << b, 0)
+            code = code + jnp.where((row == at) & (bit == 1), 1 << (z.bits + b), 0)
+            at = to
+    before = jnp.maximum(lat * z.slots - 1, 0)
+    after = jnp.minimum((lat + 1) * z.slots, z.filters - 1)
+    south = jnp.where((lat > 0) & (rows[before] == lat * z.R - 1), counts[before], 0)
+    north = jnp.where(
+        (lat < z.n_lat - 1) & (rows[after] == (lat + 1) * z.R), counts[after], 0
+    )
+    ring = jnp.where(row < z.R + z.L, south, north) << (2 * z.bits)
+    out[...] = jnp.where(row < z.R, code, ring)
+
+
 def local(z, wave_high, wave_low, fields, surface, filter_rows, keep_counts):
     L, R, W = z.L, z.R, z.W
     f32 = jnp.float32
@@ -651,7 +680,14 @@
     angle = turn.astype(f32) * (2.0 * jnp.pi / z.N)
     phase = jnp.stack([jnp.cos(angle), jnp.sin(angle)])
 
-    code = row_code(z, lat, filter_rows, keep_counts)
+    smem = pl.BlockSpec(memory_space=pltpu.SMEM)
+    code = pl.pallas_call(
+        functools.partial(row_code, z),
+        out_shape=jax.ShapeDtypeStruct((R + 2 * L, LANES), jnp.int32),
+        in_specs=[smem] * 2,
+        out_specs=vmem,
+        name="row_code",
+    )(filter_rows, keep_counts)
 
     lon_one = [(i, i ^ 1) for i in range(z.n_lon)]
     lon_two = [(i, (((i + 1) % z.n_lon ^ 1) - 1) % z.n_lon) for i in range(z.n_lon)]
@@ -678,11 +714,20 @@
         return part, got
 
     tile = (R, LANES)
-    x, m1, m2, e1, e2 = call(
-        place_tiles,
-        [(z.planes, R, W), (z.lat_rows, W), (z.lat_rows, W), tile, tile],
-        [fields, surface],
-    )
+    outs = [(z.planes, R, W), (z.lat_rows, W), (z.lat_rows, W), tile, tile]
+    x, m1, m2, e1, e2 = pl.pallas_call(
+        functools.partial(place_tiles, z),
+        out_shape=[jax.ShapeDtypeStruct(s, f32) for s in outs],
+        in_specs=[pl.BlockSpec(memory_space=pltpu.HBM)] * 2,
+        out_specs=[vmem] * 5,
+        scratch_shapes=[
+            pltpu.VMEM((4, L, R, z.C), f32),
+            pltpu.VMEM((R, z.C), f32),
+            pltpu.SemaphoreType.DMA((5,)),
+        ],
+        compiler_params=pltpu.CompilerParams(vmem_limit_bytes=VMEM_LIMIT),
+        name="place_tiles",
+    )(fields, surface)
     m1 = lax.ppermute(m1, "lat", lat_one)
     m2 = lax.ppermute(m2, "lat", lat_two)
     e1 = lax.ppermute(e1, "lon", lon_one)
@@ -745,30 +790,6 @@
     )(state, part, got, wave_high, wave_low, phase, code)
 
 
-def row_code(z, lat, filter_rows, keep_counts):
-    row = lax.broadcasted_iota(jnp.int32, (z.R + 2 * z.L, LANES), 0)
-    own = lax.dynamic_slice_in_dim(filter_rows, lat * z.slots, z.slots) - lat * z.R
-    kept = lax.dynamic_slice_in_dim(keep_counts, lat * z.slots, z.slots)
-    code = jnp.zeros(row.shape, jnp.int32)
-    for s in range(z.slots):
-        at = own[s]
-        code = code + jnp.where(row == at, kept[s] << (2 * z.bits), 0)
-        for b in range(z.bits):
-            bit = ((own[s] - s) >> b) & 1
-            to = at - (bit << b)
-            code = code + jnp.where((row == to) & (bit == 1), 1 << b, 0)
-            code = code + jnp.where((row == at) & (bit == 1), 1 << (z.bits + b), 0)
-            at = to
-    before = jnp.maximum(lat * z.slots - 1, 0)
-    after = jnp.minimum((lat + 1) * z.slots, z.filters - 1)
-    south = jnp.where((lat > 0) & (filter_rows[before] == lat * z.R - 1), keep_counts[before], 0)
-    north = jnp.where(
-        (lat < z.n_lat - 1) & (filter_rows[after] == (lat + 1) * z.R), keep_counts[after], 0
-    )
-    ring = jnp.where(row < z.R + z.L, south, north) << (2 * z.bits)
-    return jnp.where(row < z.R, code, ring)
-
-
 def wave_tables(z):
     lane = np.arange(z.W)
     j = np.where(lane >= z.W - 2, lane - z.W, lane)

time: 54.7 us -> 42.9 us (0.78)
  between operations: 12 us -> 0.19 us
  waiting for transfers between devices: 11.8 us -> 15.4 us
  local copies, waits for them, and re-layouts: 5.41 us -> 2.05 us
  other arithmetic: 3.58 us -> 0.77 us
  Pallas kernels: 7.71 us -> 10.3 us
    ppermute x1, waiting for transfers between devices: 0.01 us -> 3.02 us  [local(): m2 = lax.ppermute(m2, 'lat', lat_two)]
    pallas_call x0 -> x2, Pallas kernels: none -> 2.95 us  [the longest x1 1.63 us: local(): pl.pallas_call(functools.partial(place_tiles, z), out_shape=[jax.ShapeDty...]
    add x1 -> x0, other arithmetic: 2.66 us -> none  [row_code(): code = code + jnp.where((row == at) & (bit == 1), 1 << z.bits + b, 0)]
    slice x2 -> x0, local copies, waits for them, and re-layouts: 1.33 us -> none  [the longest x1 0.67 us: row_code(): at = own[s]]
    unnamed x12 -> x10, local copies, waits for them, and re-layouts: 3.34 us -> 2.04 us
    dynamic_slice x2 -> x0, local copies, waits for them, and re-layouts: 0.74 us -> none  [the longest x1 0.66 us: row_code(): keep_counts[before]]
    ppermute x1, waiting for transfers between devices: 0.01 us -> 0.62 us  [local(): m1 = lax.ppermute(m1, 'lat', lat_one)]
    pallas_call x8 -> x7, Pallas kernels: 5.85 us -> 5.48 us  [call(): pl.pallas_call(functools.partial(kernel, z), out_shape=[jax.ShapeDtypeStr...]
  transfers between devices with their start and end apart: 12 -> 12, of which waited for: 7 -> 9; matrix products, arithmetic and copies ran while one was open for 10% -> 2% of each run, Pallas kernels for 5% -> 10%
where the time goes in v4:
time: 42.9 us; the launch traced here: 42.5 us
  waiting for transfers between devices  15.4 us (36%)
  starting transfers between devices  13.8 us (32%)
  Pallas kernels  10.3 us (24%)
  local copies, waits for them, and re-layouts  2.05 us (5%)
  other arithmetic  0.77 us (2%)
    ppermute x4, waiting for transfers between devices, over_lon(): got = lax.ppermute(part, 'lon', [(i, i ^ step) for i in range(z.n_lon)])  8.6 us
    pallas_call x7, Pallas kernels, call(): pl.pallas_call(functools.partial(kernel, z), out_shape=[jax.ShapeDtypeStr...  5.48 us
    ppermute x1, starting transfers between devices, local(): m2 = lax.ppermute(m2, 'lat', lat_two)  4.6 us
    ppermute x4, starting transfers between devices, over_lon(): got = lax.ppermute(part, 'lon', [(i, i ^ step) for i in range(z.n_lon)])  3.32 us
    ppermute x2, starting transfers between devices, from_below(): return lax.ppermute(column, 'lev', [(0, 1), (1, 0)])  3.05 us
    ppermute x1, waiting for transfers between devices, local(): m2 = lax.ppermute(m2, 'lat', lat_two)  3.02 us
    ppermute x2, waiting for transfers between devices, from_below(): return lax.ppermute(column, 'lev', [(0, 1), (1, 0)])  2.2 us
    unnamed x10, local copies, waits for them, and re-layouts  2.04 us
  transfers between devices with their start and end apart: 12, of which 9 were waited for; matrix products, arithmetic and copies ran while one was open for 2% of the time, Pallas kernels for 10%

profile of v4, /device:TPU:8, one launch (start us, length us, event | category | flops | bytes accessed | tf_op | source)
XLA Modules:
  0.0 42.5 jit_solution(17075211860771884356)
XLA Ops:
  0.0 1.2 %copy-done.2 = f32[4,4,8,1800]{3,2,1,0:T(8,128)S(1)} copy-done((f32[4,4,8,1800]{3,2,1,0:T(8,128)S(1)}, f32[4,4,8,1800]{3,2,1,0:T(8,128)}, u32[]{:S(2)}) %copy-start.2) | copy-done | bytes 921624
  1.2 0.8 %copy-done.4 = f32[8,1800]{1,0:T(8,128)S(1)} copy-done((f32[8,1800]{1,0:T(8,128)S(1)}, f32[8,1800]{1,0:T(8,128)}, u32[]{:S(2)}) %copy-start.4) | copy-done | bytes 57624
  2.0 1.6 %place_tiles.1 = (f32[17,8,1920]{2,1,0:T(8,128)S(1)}, f32[32,1920]{1,0:T(8,128)S(1)}, f32[32,1920]{1,0:T(8,128)S(1)}, f32[8,128]{1,0:T(8,128)S(1)}, f32[8,128]{1,0:T(8,128)S(1)}) custom-call(f32[4,4,8,1800]{3,2,1,0:T(8,128)S(1)} %copy-done.2, f32[8,1800]{1,0:T(8,128)S(1)} %copy-done.4), custom_call_target="tpu_custom_call" | custom-call | tf_op jit(solution)/shard_map/place_tiles/pallas_call | solution.py:718
  3.8 1.6 %collective-permute-start.1 = (f32[8,128]{1,0:T(8,128)S(1)}, f32[8,128]{1,0:T(8,128)S(1)}, u32[]{:S(2)}, u32[]{:S(2)}) collective-permute-start(f32[8,128]{1,0:T(8,128)S(1)} %get-tuple-element.31), channel_id=1, source_target_pairs={{0,24},{8,16},{16,8},{24,0},{1,25},{9,17},{17,9},{25,1},{2,26},{10... | collective-permute-start | bytes 12296 | tf_op jit(solution)/shard_map/ppermute | solution.py:734
  5.8 4.6 %collective-permute-start.3 = (f32[32,1920]{1,0:T(8,128)S(1)}, f32[32,1920]{1,0:T(8,128)S(1)}, u32[]{:S(2)}, u32[]{:S(2)}) collective-permute-start(f32[32,1920]{1,0:T(8,128)S(1)} %get-tuple-element.35), channel_id=1, source_target_pairs={{2,4},{4,2},{3,5},{5,3},{10,12},{12,10},{11,13},{13,11},{18,20},{2... | collective-permute-start | bytes 737288 | tf_op jit(solution)/shard_map/ppermute | solution.py:732
  11.3 1.3 %row_code.1.code = s32[16,128]{1,0:T(8,128)} custom-call(s32[16]{0:T(128)} %rows.1, s32[16]{0:T(128)} %counts.1), custom_call_target="tpu_custom_call" | custom-call | tf_op jit(solution)/shard_map/row_code/pallas_call | solution.py:684
  13.3 3.0 %collective-permute-done.3.r2 = f32[32,1920]{1,0:T(8,128)S(1)} collective-permute-done((f32[32,1920]{1,0:T(8,128)S(1)}, f32[32,1920]{1,0:T(8,128)S(1)}, u32[]{:S(2)}, u32[]{:S(2)}) %collective-permute-start.3) | collective-permute-done | bytes 245792 | tf_op jit(solution)/shard_map/ppermute | solution.py:732
  17.3 1.5 %collective-permute-start.6 = (f32[8,2432]{1,0:T(8,128)S(1)}, f32[8,2432]{1,0:T(8,128)S(1)}, u32[]{:S(2)}, u32[]{:S(2)}) collective-permute-start(f32[8,2432]{1,0:T(8,128)S(1)} %get-tuple-element.43), channel_id=1, source_target_pairs={{0,1},{1,0},{2,3},{3,2},{4,5},{5,4},{6,7},{7,6},{8,9},{9,8},{10,11... | collective-permute-start | bytes 233480 | tf_op jit(solution)/shard_map/ppermute | solution.py:699
  18.8 1.0 %collective-permute-done.5.r2 = f32[8,128]{1,0:T(8,128)S(1)} collective-permute-done((f32[8,128]{1,0:T(8,128)S(1)}, f32[8,128]{1,0:T(8,128)S(1)}, u32[]{:S(2)}, u32[]{:S(2)}) %collective-permute-start.5) | collective-permute-done | bytes 4128 | tf_op jit(solution)/shard_map/ppermute | solution.py:744
  19.7 1.1 %first_step.1 = (f32[16,8,1920]{2,1,0:T(8,128)S(1)}, f32[3,8,1920]{2,1,0:T(8,128)S(1)}, f32[8,1920]{1,0:T(8,128)S(1)}) custom-call(f32[17,8,1920]{2,1,0:T(8,128)S(1)} %get-tuple-element.32.x, f32[7,8,1920]{2,1,0:T(8,128)S(1)} %get-tuple-element.36.ring_in, f32[8,1920]{1,0:T(8,128)S(1)} %get-tuple-element.37.surface_in, ...), custom_call_target="tpu_custom_call" | custom-call | flops 10000000 | bytes 2813952 | tf_op jit(solution)/shard_map/first_step/pallas_call | solution.py:649
  20.8 0.8 %collective-permute-done.6.got = f32[8,2432]{1,0:T(8,128)S(1)} collective-permute-done((f32[8,2432]{1,0:T(8,128)S(1)}, f32[8,2432]{1,0:T(8,128)S(1)}, u32[]{:S(2)}, u32[]{:S(2)}) %collective-permute-start.6) | collective-permute-done | bytes 77856 | tf_op jit(solution)/shard_map/ppermute | solution.py:699
  21.7 0.8 %first_spectra.1 = (f32[16,8,1920]{2,1,0:T(8,128)S(1)}, f32[3,8,1920]{2,1,0:T(8,128)S(1)}, f32[96,256]{1,0:T(8,128)S(1)}) custom-call(f32[16,8,1920]{2,1,0:T(8,128)S(1)} %get-tuple-element.40.y, f32[3,8,1920]{2,1,0:T(8,128)S(1)} %get-tuple-element.41.yring, f32[8,1920]{1,0:T(8,128)S(1)} %slice_bitcast_fusion.surface, ...), custom_call_target="tpu_custom_call" | custom-call | flops 1000000 | bytes 4649984 | tf_op jit(solution)/shard_map/first_spectra/pallas_call | solution.py:649
  22.6 1.3 %collective-permute-done.7 = f32[96,256]{1,0:T(8,128)S(1)} collective-permute-done((f32[96,256]{1,0:T(8,128)S(1)}, f32[96,256]{1,0:T(8,128)S(1)}, u32[]{:S(2)}, u32[]{:S(2)}) %collective-permute-start.7) | collective-permute-done | bytes 98336 | tf_op jit(solution)/shard_map/ppermute | solution.py:712
  23.9 1.6 %collective-permute-start.8 = (f32[96,256]{1,0:T(8,128)S(1)}, f32[96,256]{1,0:T(8,128)S(1)}, u32[]{:S(2)}, u32[]{:S(2)}) collective-permute-start(f32[96,256]{1,0:T(8,128)S(1)} %add.150.part), channel_id=1, source_target_pairs={{0,16},{8,24},{16,0},{24,8},{1,17},{9,25},{17,1},{25,9},{2,18},{10... | collective-permute-start | bytes 294920 | tf_op jit(solution)/shard_map/ppermute | solution.py:712
  25.5 3.3 %collective-permute-done.8.got = f32[96,256]{1,0:T(8,128)S(1)} collective-permute-done((f32[96,256]{1,0:T(8,128)S(1)}, f32[96,256]{1,0:T(8,128)S(1)}, u32[]{:S(2)}, u32[]{:S(2)}) %collective-permute-start.8) | collective-permute-done | bytes 98336 | tf_op jit(solution)/shard_map/ppermute | solution.py:712
  28.8 1.0 %filter_mass.1 = (f32[8,8,1920]{2,1,0:T(8,128)S(1)}, f32[2,8,1920]{2,1,0:T(8,128)S(1)}, f32[80,256]{1,0:T(8,128)S(1)}, f32[8,2432]{1,0:T(8,128)S(1)}) custom-call(f32[16,8,1920]{2,1,0:T(8,128)S(1)} %get-tuple-element.44.state, f32[3,8,1920]{2,1,0:T(8,128)S(1)} %get-tuple-element.45.sring, f32[96,256]{1,0:T(8,128)S(1)} %add.150.part, ...), custom_call_target="tpu_custom_call" | custom-call | flops 1000000 | bytes 4113408 | tf_op jit(solution)/shard_map/filter_mass/pallas_call | solution.py:649
  29.8 1.6 %collective-permute-start.9 = (f32[8,2432]{1,0:T(8,128)S(1)}, f32[8,2432]{1,0:T(8,128)S(1)}, u32[]{:S(2)}, u32[]{:S(2)}) collective-permute-start(f32[8,2432]{1,0:T(8,128)S(1)} %get-tuple-element.50), channel_id=1, source_target_pairs={{0,1},{1,0},{2,3},{3,2},{4,5},{5,4},{6,7},{7,6},{8,9},{9,8},{10,11... | collective-permute-start | bytes 233480 | tf_op jit(solution)/shard_map/ppermute | solution.py:699
  31.4 1.5 %second_step.1.y = f32[16,8,1920]{2,1,0:T(8,128)S(1)} custom-call(f32[16,8,1920]{2,1,0:T(8,128)S(1)} %get-tuple-element.44.state, f32[3,8,1920]{2,1,0:T(8,128)S(1)} %get-tuple-element.45.sring, f32[80,256]{1,0:T(8,128)S(1)} %get-tuple-element.47.uvmodes, f32[8,8,1920]{2,1,0:T(8,128)S(1)} %get-tuple-element.48.ht, ...), custom_call_target="tpu_custom_call" | custom-call | flops 10000000 | bytes 4861952 | tf_op jit(solution)/shard_map/second_step/pallas_call | solution.py:649
  32.9 1.4 %collective-permute-done.9.got = f32[8,2432]{1,0:T(8,128)S(1)} collective-permute-done((f32[8,2432]{1,0:T(8,128)S(1)}, f32[8,2432]{1,0:T(8,128)S(1)}, u32[]{:S(2)}, u32[]{:S(2)}) %collective-permute-start.9) | collective-permute-done | bytes 77856 | tf_op jit(solution)/shard_map/ppermute | solution.py:699
  34.3 0.7 %second_spectra.1 = (f32[16,8,1920]{2,1,0:T(8,128)S(1)}, f32[64,256]{1,0:T(8,128)S(1)}) custom-call(f32[16,8,1920]{2,1,0:T(8,128)S(1)} %second_step.1.y, f32[8,1920]{1,0:T(8,128)S(1)} %slice_bitcast_fusion.surface, f32[8,1920]{1,0:T(8,128)S(1)} %get-tuple-element.42.ring_surface, f32[8,2432]{1,0:T(8,128)S(1)} %collective-permute-done.9.got, ...), custom_call_target="tpu_custom_call" | custom-call | flops 1000000 | bytes 4248576 | tf_op jit(solution)/shard_map/second_spectra/pallas_call | solution.py:649
  35.1 1.2 %collective-permute-done.10 = f32[64,256]{1,0:T(8,128)S(1)} collective-permute-done((f32[64,256]{1,0:T(8,128)S(1)}, f32[64,256]{1,0:T(8,128)S(1)}, u32[]{:S(2)}, u32[]{:S(2)}) %collective-permute-start.10) | collective-permute-done | bytes 65568 | tf_op jit(solution)/shard_map/ppermute | solution.py:712
  36.3 1.6 %collective-permute-start.11 = (f32[64,256]{1,0:T(8,128)S(1)}, f32[64,256]{1,0:T(8,128)S(1)}, u32[]{:S(2)}, u32[]{:S(2)}) collective-permute-start(f32[64,256]{1,0:T(8,128)S(1)} %add.151.part), channel_id=1, source_target_pairs={{0,16},{8,24},{16,0},{24,8},{1,17},{9,25},{17,1},{25,9},{2,18},{10... | collective-permute-start | bytes 196616 | tf_op jit(solution)/shard_map/ppermute | solution.py:712
  37.9 2.7 %collective-permute-done.11.got = f32[64,256]{1,0:T(8,128)S(1)} collective-permute-done((f32[64,256]{1,0:T(8,128)S(1)}, f32[64,256]{1,0:T(8,128)S(1)}, u32[]{:S(2)}, u32[]{:S(2)}) %collective-permute-start.11) | collective-permute-done | bytes 65568 | tf_op jit(solution)/shard_map/ppermute | solution.py:712
  40.7 1.9 %filter_all.1 = f32[4,4,8,1800]{3,2,1,0:T(8,128)} custom-call(f32[16,8,1920]{2,1,0:T(8,128)S(1)} %get-tuple-element.51.state, f32[64,256]{1,0:T(8,128)S(1)} %add.151.part, f32[64,256]{1,0:T(8,128)S(1)} %collective-permute-done.11.got, bf16[1920,256]{1,0:T(8,128)(2,1)S(1)} %copy-done.1, bf16[1920,256]{1,0:T(8,128)(2,1)S(1)} %copy-done, ...), custom_call_target="tpu_custom_call" | custom-call | tf_op jit(solution)/shard_map/filter_all/pallas_call | solution.py:779
  (32 shorter events, 3.1 us)
Async XLA Ops:
  0.0 1.2 %copy-start.2 = (f32[4,4,8,1800]{3,2,1,0:T(8,128)S(1)}, f32[4,4,8,1800]{3,2,1,0:T(8,128)}, u32[]{:S(2)}) copy-start(f32[4,4,8,1800]{3,2,1,0:T(8,128)} %fields.1) | copy-start | bytes 2764804
  1.2 0.8 %copy-start.4 = (f32[8,1800]{1,0:T(8,128)S(1)}, f32[8,1800]{1,0:T(8,128)}, u32[]{:S(2)}) copy-start(f32[8,1800]{1,0:T(8,128)} %surface.1) | copy-start | bytes 172804
  3.7 8.9 %collective-permute-start = (f32[8,128]{1,0:T(8,128)S(1)}, f32[8,128]{1,0:T(8,128)S(1)}, u32[]{:S(2)}, u32[]{:S(2)}) collective-permute-start(f32[8,128]{1,0:T(8,128)S(1)} %get-tuple-element.30), channel_id=1, source_target_pairs={{0,8},{8,0},{16,24},{24,16},{1,9},{9,1},{17,25},{25,17},{2,10},{10... | collective-permute-start | bytes 12296 | tf_op jit(solution)/shard_map/ppermute | solution.py:733
  3.8 8.8 %collective-permute-start.1 = (f32[8,128]{1,0:T(8,128)S(1)}, f32[8,128]{1,0:T(8,128)S(1)}, u32[]{:S(2)}, u32[]{:S(2)}) collective-permute-start(f32[8,128]{1,0:T(8,128)S(1)} %get-tuple-element.31), channel_id=1, source_target_pairs={{0,24},{8,16},{16,8},{24,0},{1,25},{9,17},{17,9},{25,1},{2,26},{10... | collective-permute-start | bytes 12296 | tf_op jit(solution)/shard_map/ppermute | solution.py:734
  5.4 7.9 %collective-permute-start.2 = (f32[32,1920]{1,0:T(8,128)S(1)}, f32[32,1920]{1,0:T(8,128)S(1)}, u32[]{:S(2)}, u32[]{:S(2)}) collective-permute-start(f32[32,1920]{1,0:T(8,128)S(1)} %get-tuple-element.34), channel_id=1, source_target_pairs={{0,2},{2,0},{4,6},{6,4},{1,3},{3,1},{5,7},{7,5},{8,10},{10,8},{12,... | collective-permute-start | bytes 737288 | tf_op jit(solution)/shard_map/ppermute | solution.py:731
  5.8 10.5 %collective-permute-start.3 = (f32[32,1920]{1,0:T(8,128)S(1)}, f32[32,1920]{1,0:T(8,128)S(1)}, u32[]{:S(2)}, u32[]{:S(2)}) collective-permute-start(f32[32,1920]{1,0:T(8,128)S(1)} %get-tuple-element.35), channel_id=1, source_target_pairs={{2,4},{4,2},{3,5},{5,3},{10,12},{12,10},{11,13},{13,11},{18,20},{2... | collective-permute-start | bytes 737288 | tf_op jit(solution)/shard_map/ppermute | solution.py:732
  16.3 5.3 %copy-start.1 = (bf16[1920,256]{1,0:T(8,128)(2,1)S(1)}, bf16[1920,256]{1,0:T(8,128)(2,1)}, u32[]{:S(2)}) copy-start(bf16[1920,256]{1,0:T(8,128)(2,1)} %constant.52.clone.wh) | copy-start | bytes 2949124
  16.5 5.1 %copy-start = (bf16[1920,256]{1,0:T(8,128)(2,1)S(1)}, bf16[1920,256]{1,0:T(8,128)(2,1)}, u32[]{:S(2)}) copy-start(bf16[1920,256]{1,0:T(8,128)(2,1)} %constant.53.clone.wl) | copy-start | bytes 2949124
  16.6 2.2 %collective-permute-start.4 = (f32[8,128]{1,0:T(8,128)S(1)}, f32[8,128]{1,0:T(8,128)S(1)}, u32[]{:S(2)}, u32[]{:S(2)}) collective-permute-start(f32[8,128]{1,0:T(8,128)S(1)} %get-tuple-element.38), channel_id=1, source_target_pairs={{0,8},{8,0},{16,24},{24,16},{1,9},{9,1},{17,25},{25,17},{2,10},{10... | collective-permute-start | bytes 12296 | tf_op jit(solution)/shard_map/ppermute | solution.py:743
  16.6 3.1 %collective-permute-start.5 = (f32[8,128]{1,0:T(8,128)S(1)}, f32[8,128]{1,0:T(8,128)S(1)}, u32[]{:S(2)}, u32[]{:S(2)}) collective-permute-start(f32[8,128]{1,0:T(8,128)S(1)} %get-tuple-element.39), channel_id=1, source_target_pairs={{0,24},{8,16},{16,8},{24,0},{1,25},{9,17},{17,9},{25,1},{2,26},{10... | collective-permute-start | bytes 12296 | tf_op jit(solution)/shard_map/ppermute | solution.py:744
  17.3 4.4 %collective-permute-start.6 = (f32[8,2432]{1,0:T(8,128)S(1)}, f32[8,2432]{1,0:T(8,128)S(1)}, u32[]{:S(2)}, u32[]{:S(2)}) collective-permute-start(f32[8,2432]{1,0:T(8,128)S(1)} %get-tuple-element.43), channel_id=1, source_target_pairs={{0,1},{1,0},{2,3},{3,2},{4,5},{5,4},{6,7},{7,6},{8,9},{9,8},{10,11... | collective-permute-start | bytes 233480 | tf_op jit(solution)/shard_map/ppermute | solution.py:699
  19.7 1.9 %copy-start.3 = (s32[16,128]{1,0:T(8,128)S(1)}, s32[16,128]{1,0:T(8,128)}, u32[]{:S(2)}) copy-start(s32[16,128]{1,0:T(8,128)} %row_code.1.code) | copy-start | bytes 24580
  22.5 1.4 %collective-permute-start.7 = (f32[96,256]{1,0:T(8,128)S(1)}, f32[96,256]{1,0:T(8,128)S(1)}, u32[]{:S(2)}, u32[]{:S(2)}) collective-permute-start(f32[96,256]{1,0:T(8,128)S(1)} %get-tuple-element.46), channel_id=1, source_target_pairs={{0,8},{8,0},{16,24},{24,16},{1,9},{9,1},{17,25},{25,17},{2,10},{10... | collective-permute-start | bytes 294920 | tf_op jit(solution)/shard_map/ppermute | solution.py:712
  23.9 4.9 %collective-permute-start.8 = (f32[96,256]{1,0:T(8,128)S(1)}, f32[96,256]{1,0:T(8,128)S(1)}, u32[]{:S(2)}, u32[]{:S(2)}) collective-permute-start(f32[96,256]{1,0:T(8,128)S(1)} %add.150.part), channel_id=1, source_target_pairs={{0,16},{8,24},{16,0},{24,8},{1,17},{9,25},{17,1},{25,9},{2,18},{10... | collective-permute-start | bytes 294920 | tf_op jit(solution)/shard_map/ppermute | solution.py:712
  29.8 4.5 %collective-permute-start.9 = (f32[8,2432]{1,0:T(8,128)S(1)}, f32[8,2432]{1,0:T(8,128)S(1)}, u32[]{:S(2)}, u32[]{:S(2)}) collective-permute-start(f32[8,2432]{1,0:T(8,128)S(1)} %get-tuple-element.50), channel_id=1, source_target_pairs={{0,1},{1,0},{2,3},{3,2},{4,5},{5,4},{6,7},{7,6},{8,9},{9,8},{10,11... | collective-permute-start | bytes 233480 | tf_op jit(solution)/shard_map/ppermute | solution.py:699
  35.0 1.3 %collective-permute-start.10 = (f32[64,256]{1,0:T(8,128)S(1)}, f32[64,256]{1,0:T(8,128)S(1)}, u32[]{:S(2)}, u32[]{:S(2)}) collective-permute-start(f32[64,256]{1,0:T(8,128)S(1)} %get-tuple-element.52), channel_id=1, source_target_pairs={{0,8},{8,0},{16,24},{24,16},{1,9},{9,1},{17,25},{25,17},{2,10},{10... | collective-permute-start | bytes 196616 | tf_op jit(solution)/shard_map/ppermute | solution.py:712
  36.3 4.3 %collective-permute-start.11 = (f32[64,256]{1,0:T(8,128)S(1)}, f32[64,256]{1,0:T(8,128)S(1)}, u32[]{:S(2)}, u32[]{:S(2)}) collective-permute-start(f32[64,256]{1,0:T(8,128)S(1)} %add.151.part), channel_id=1, source_target_pairs={{0,16},{8,24},{16,0},{24,8},{1,17},{9,25},{17,1},{25,9},{2,18},{10... | collective-permute-start | bytes 196616 | tf_op jit(solution)/shard_map/ppermute | solution.py:712

commit v5 on v4

--- a/solution.py
+++ b/solution.py
@@ -73,7 +73,8 @@
         self.base = (self.C - 1) // LANES * LANES
         self.tiles = self.W // LANES
         self.extra = -(-self.tiles // self.R)
-        self.lat_rows = -(-(7 * self.L + 1) // 8) * 8
+        self.fold = -(-self.tiles // 2)
+        self.lat_lanes = 3 * self.W + (self.fold + self.extra) * LANES
         width = -(-self.base // LANES // 3) * LANES if self.base else self.W
         cuts = [c for c in range(0, self.base + 1, width)] if self.base else [0]
         if self.C - cuts[-1] <= LANES and len(cuts) > 1:
@@ -130,34 +131,33 @@
         ref[:, start : start + LANES] = tile
 
 
-def place_tiles(z, fields, surface, x, m1, m2, e1, e2, held, held_surface, sem):
-    lane = lax.broadcasted_iota(jnp.int32, (z.R, LANES), 1)
-    copies = [pltpu.make_async_copy(fields.at[f], held.at[f], sem.at[f]) for f in range(4)]
-    copies.append(pltpu.make_async_copy(surface, held_surface, sem.at[4]))
-    for copy in copies:
-        copy.start()
-    for p in range(z.planes):
-        if p % z.L == 0:
-            copies[p // z.L].wait()
-        x[p, :, 0 : z.C] = held[p // z.L, p % z.L] if p < 4 * z.L else held_surface[...]
-        x[p, :, z.base : z.base + LANES] = jnp.where(
-            lane < z.C - z.base, x[p, :, z.base : z.base + LANES], 0.0
-        )
-        if z.base + LANES < z.W:
-            x[p, :, z.base + LANES :] = jnp.zeros((z.R, z.W - z.base - LANES), jnp.float32)
+def edge_rows(z, x, m1, m2, after):
+    L, W = z.L, z.W
+    fold = z.fold * LANES
+    after[...] = jnp.zeros(after.shape, jnp.float32)
     lat_even = lax.axis_index("lat") % 2 == 0
     near1 = jnp.where(lat_even, z.R - 1, 0)
     far1 = jnp.where(lat_even, z.R - 2, 1)
     for msg, near, far in ((m1, near1, far1), (m2, z.R - 1 - near1, z.R - 1 - far1)):
-        for p in range(4 * z.L):
-            msg[p : p + 1, :] = x[p, pl.ds(near, 1), :]
-        for p in range(z.L, 4 * z.L):
-            to = 3 * z.L + p
-            msg[to : to + 1, :] = x[p, pl.ds(far, 1), :]
-        to = 7 * z.L
-        msg[to : to + 1, :] = x[4 * z.L, pl.ds(near, 1), :]
-        if z.lat_rows > to + 1:
-            msg[to + 1 :, :] = jnp.zeros((z.lat_rows - to - 1, z.W), jnp.float32)
+        msg[:, 3 * W :] = jnp.zeros((z.R, z.lat_lanes - 3 * W), jnp.float32)
+        for k in range(7):
+            f, at = (k, near) if k < 4 else (k - 3, far)
+            for l in range(L):
+                row = x[f * L + l, pl.ds(at, 1), :]
+                to = (k % 2) * L + l
+                if k < 6:
+                    msg[to : to + 1, k // 2 * W : (k // 2 + 1) * W] = row
+                else:
+                    msg[l : l + 1, 3 * W : 3 * W + fold] = row[:, 0:fold]
+                    msg[L + l : L + l + 1, 3 * W : 4 * W - fold] = row[:, fold:]
+        row = x[4 * L, pl.ds(near, 1), :]
+        for t in range(z.tiles):
+            at = 3 * W + fold + t // z.R * LANES
+            msg[t % z.R : t % z.R + 1, at : at + LANES] = row[:, t * LANES : (t + 1) * LANES]
+
+
+def edge_columns(z, x, after, e1, e2):
+    del after
     left, right = edge_tiles(
         z,
         z.planes,
@@ -202,11 +202,18 @@
     lat_even = lax.axis_index("lat") % 2 == 0
 
     def place(d, source):
-        for k in range(7):
-            ring[k, d * z.L : (d + 1) * z.L, :] = source[k * z.L : (k + 1) * z.L, :]
-        ring_surface[d * z.L : (d + 1) * z.L, :] = jnp.broadcast_to(
-            source[7 * z.L : 7 * z.L + 1, :], (z.L, z.W)
-        )
+        L, W = z.L, z.W
+        fold = z.fold * LANES
+        here = slice(d * L, (d + 1) * L)
+        for k in range(6):
+            at = (k % 2) * L
+            ring[k, here, :] = source[at : at + L, k // 2 * W : (k // 2 + 1) * W]
+        ring[6, here, 0:fold] = source[0:L, 3 * W : 3 * W + fold]
+        ring[6, here, fold:] = source[L : 2 * L, 3 * W : 3 * W + W - fold]
+        for t in range(z.tiles):
+            at = 3 * W + fold + t // z.R * LANES
+            part = source[t % z.R : t % z.R + 1, at : at + LANES]
+            ring_surface[here, t * LANES : (t + 1) * LANES] = jnp.broadcast_to(part, (L, LANES))
 
     @pl.when(lat_even)
     def _():
@@ -714,22 +721,12 @@
         return part, got
 
     tile = (R, LANES)
-    outs = [(z.planes, R, W), (z.lat_rows, W), (z.lat_rows, W), tile, tile]
-    x, m1, m2, e1, e2 = pl.pallas_call(
-        functools.partial(place_tiles, z),
-        out_shape=[jax.ShapeDtypeStruct(s, f32) for s in outs],
-        in_specs=[pl.BlockSpec(memory_space=pltpu.HBM)] * 2,
-        out_specs=[vmem] * 5,
-        scratch_shapes=[
-            pltpu.VMEM((4, L, R, z.C), f32),
-            pltpu.VMEM((R, z.C), f32),
-            pltpu.SemaphoreType.DMA((5,)),
-        ],
-        compiler_params=pltpu.CompilerParams(vmem_limit_bytes=VMEM_LIMIT),
-        name="place_tiles",
-    )(fields, surface)
+    x = jnp.concatenate([fields.reshape(4 * L, R, z.C), surface[None]], 0)
+    x = jnp.pad(x, ((0, 0), (0, 0), (0, W - z.C)))
+    m1, m2, after = call(edge_rows, [(R, z.lat_lanes)] * 2 + [tile], [x])
     m1 = lax.ppermute(m1, "lat", lat_one)
     m2 = lax.ppermute(m2, "lat", lat_two)
+    e1, e2 = call(edge_columns, [tile, tile], [x, after])
     e1 = lax.ppermute(e1, "lon", lon_one)
     e2 = lax.ppermute(e2, "lon", lon_two)
     x, sums = call(

time: 42.9 us -> 40.3 us (0.939)
  local copies, waits for them, and re-layouts: 2.05 us -> 0.02 us
  Pallas kernels: 10.3 us -> 8.91 us
  other arithmetic: 0.77 us -> 2.08 us
    unnamed x10 -> x6, local copies, waits for them, and re-layouts: 2.04 us -> 0.01 us
    pallas_call x1 -> x0, Pallas kernels: 1.63 us -> none  [local(): pl.pallas_call(functools.partial(place_tiles, z), out_shape=[jax.ShapeDty...]
    concatenate x0 -> x1, other arithmetic: none -> 1.31 us  [local(): x = jnp.concatenate([fields.reshape(4 * L, R, z.C), surface[None]], 0)]
    ppermute x1, waiting for transfers between devices: 0.62 us -> 0.18 us  [local(): m1 = lax.ppermute(m1, 'lat', lat_one)]
    pallas_call x7 -> x9, Pallas kernels: 5.48 us -> 5.73 us  [call(): pl.pallas_call(functools.partial(kernel, z), out_shape=[jax.ShapeDtypeStr...]
where the time goes in v5:
time: 40.3 us; the launch traced here: 40 us
  waiting for transfers between devices  15 us (37%)
  starting transfers between devices  13.8 us (34%)
  Pallas kernels  8.91 us (22%)
  other arithmetic  2.08 us (5%)
    ppermute x4, waiting for transfers between devices, over_lon(): got = lax.ppermute(part, 'lon', [(i, i ^ step) for i in range(z.n_lon)])  8.61 us
    pallas_call x9, Pallas kernels, call(): pl.pallas_call(functools.partial(kernel, z), out_shape=[jax.ShapeDtypeStr...  5.73 us
    ppermute x1, starting transfers between devices, local(): m2 = lax.ppermute(m2, 'lat', lat_two)  4.6 us
    ppermute x4, starting transfers between devices, over_lon(): got = lax.ppermute(part, 'lon', [(i, i ^ step) for i in range(z.n_lon)])  3.31 us
    ppermute x2, starting transfers between devices, from_below(): return lax.ppermute(column, 'lev', [(0, 1), (1, 0)])  3.05 us
    ppermute x1, waiting for transfers between devices, local(): m2 = lax.ppermute(m2, 'lat', lat_two)  3.02 us
    ppermute x2, waiting for transfers between devices, from_below(): return lax.ppermute(column, 'lev', [(0, 1), (1, 0)])  2.2 us
    pallas_call x1, Pallas kernels, local(): pl.pallas_call(functools.partial(filter_all, z), out_shape=jax.ShapeDtype...  1.86 us
  transfers between devices with their start and end apart: 12, of which 9 were waited for; matrix products, arithmetic and copies ran while one was open for 2% of the time, Pallas kernels for 10%

profile of v5, /device:TPU:8, one launch (start us, length us, event | category | flops | bytes accessed | tf_op | source)
XLA Modules:
  0.0 40.0 jit_solution(9687389466359850056)
XLA Ops:
  0.0 1.3 %select_maximum_fusion.x.x_in = f32[17,8,1920]{2,1,0:T(8,128)S(1)} fusion(f32[1,8,1800]{2,1,0:T(8,128)} %bitcast.5, f32[16,8,1800]{2,1,0:T(8,128)} %bitcast.4), kind=kLoop, calls=%fused_computation | loop fusion | flops 1044480 | bytes 2023680 | tf_op jit(solution)/shard_map/concatenate | solution.py:724
  1.7 1.6 %collective-permute-start.1 = (f32[8,128]{1,0:T(8,128)S(1)}, f32[8,128]{1,0:T(8,128)S(1)}, u32[]{:S(2)}, u32[]{:S(2)}) collective-permute-start(f32[8,128]{1,0:T(8,128)S(1)} %get-tuple-element.31), channel_id=1, source_target_pairs={{0,24},{8,16},{16,8},{24,0},{1,25},{9,17},{17,9},{25,1},{2,26},{10... | collective-permute-start | bytes 12296 | tf_op jit(solution)/shard_map/ppermute | solution.py:731
  3.3 0.4 %collective-permute-start.2 = (f32[8,7040]{1,0:T(8,128)S(1)}, f32[8,7040]{1,0:T(8,128)S(1)}, u32[]{:S(2)}, u32[]{:S(2)}) collective-permute-start(f32[8,7040]{1,0:T(8,128)S(1)} %get-tuple-element.34), channel_id=1, source_target_pairs={{0,2},{2,0},{4,6},{6,4},{1,3},{3,1},{5,7},{7,5},{8,10},{10,8},{12,... | collective-permute-start | bytes 675848 | tf_op jit(solution)/shard_map/ppermute | solution.py:727
  3.7 4.6 %collective-permute-start.3 = (f32[8,7040]{1,0:T(8,128)S(1)}, f32[8,7040]{1,0:T(8,128)S(1)}, u32[]{:S(2)}, u32[]{:S(2)}) collective-permute-start(f32[8,7040]{1,0:T(8,128)S(1)} %get-tuple-element.35), channel_id=1, source_target_pairs={{2,4},{4,2},{3,5},{5,3},{10,12},{12,10},{11,13},{13,11},{18,20},{2... | collective-permute-start | bytes 675848 | tf_op jit(solution)/shard_map/ppermute | solution.py:728
  9.2 1.3 %row_code.1.code = s32[16,128]{1,0:T(8,128)} custom-call(s32[16]{0:T(128)} %rows.1, s32[16]{0:T(128)} %counts.1), custom_call_target="tpu_custom_call" | custom-call | tf_op jit(solution)/shard_map/row_code/pallas_call | solution.py:691
  10.8 3.0 %collective-permute-done.3.r2 = f32[8,7040]{1,0:T(8,128)S(1)} collective-permute-done((f32[8,7040]{1,0:T(8,128)S(1)}, f32[8,7040]{1,0:T(8,128)S(1)}, u32[]{:S(2)}, u32[]{:S(2)}) %collective-permute-start.3) | collective-permute-done | bytes 225312 | tf_op jit(solution)/shard_map/ppermute | solution.py:728
  14.1 0.6 %collective-permute-start.5 = (f32[8,128]{1,0:T(8,128)S(1)}, f32[8,128]{1,0:T(8,128)S(1)}, u32[]{:S(2)}, u32[]{:S(2)}) collective-permute-start(f32[8,128]{1,0:T(8,128)S(1)} %get-tuple-element.39), channel_id=1, source_target_pairs={{0,24},{8,16},{16,8},{24,0},{1,25},{9,17},{17,9},{25,1},{2,26},{10... | collective-permute-start | bytes 12296 | tf_op jit(solution)/shard_map/ppermute | solution.py:741
  14.7 1.5 %collective-permute-start.6 = (f32[8,2432]{1,0:T(8,128)S(1)}, f32[8,2432]{1,0:T(8,128)S(1)}, u32[]{:S(2)}, u32[]{:S(2)}) collective-permute-start(f32[8,2432]{1,0:T(8,128)S(1)} %get-tuple-element.43), channel_id=1, source_target_pairs={{0,1},{1,0},{2,3},{3,2},{4,5},{5,4},{6,7},{7,6},{8,9},{9,8},{10,11... | collective-permute-start | bytes 233480 | tf_op jit(solution)/shard_map/ppermute | solution.py:706
  16.2 1.0 %collective-permute-done.5.r2 = f32[8,128]{1,0:T(8,128)S(1)} collective-permute-done((f32[8,128]{1,0:T(8,128)S(1)}, f32[8,128]{1,0:T(8,128)S(1)}, u32[]{:S(2)}, u32[]{:S(2)}) %collective-permute-start.5) | collective-permute-done | bytes 4128 | tf_op jit(solution)/shard_map/ppermute | solution.py:741
  17.2 1.1 %first_step.1 = (f32[16,8,1920]{2,1,0:T(8,128)S(1)}, f32[3,8,1920]{2,1,0:T(8,128)S(1)}, f32[8,1920]{1,0:T(8,128)S(1)}) custom-call(f32[17,8,1920]{2,1,0:T(8,128)S(1)} %get-tuple-element.32.x, f32[7,8,1920]{2,1,0:T(8,128)S(1)} %get-tuple-element.36.ring_in, f32[8,1920]{1,0:T(8,128)S(1)} %get-tuple-element.37.surface_in, ...), custom_call_target="tpu_custom_call" | custom-call | flops 10000000 | bytes 2813952 | tf_op jit(solution)/shard_map/first_step/pallas_call | solution.py:656
  18.3 0.8 %collective-permute-done.6.got = f32[8,2432]{1,0:T(8,128)S(1)} collective-permute-done((f32[8,2432]{1,0:T(8,128)S(1)}, f32[8,2432]{1,0:T(8,128)S(1)}, u32[]{:S(2)}, u32[]{:S(2)}) %collective-permute-start.6) | collective-permute-done | bytes 77856 | tf_op jit(solution)/shard_map/ppermute | solution.py:706
  19.1 0.8 %first_spectra.1 = (f32[16,8,1920]{2,1,0:T(8,128)S(1)}, f32[3,8,1920]{2,1,0:T(8,128)S(1)}, f32[96,256]{1,0:T(8,128)S(1)}) custom-call(f32[16,8,1920]{2,1,0:T(8,128)S(1)} %get-tuple-element.40.y, f32[3,8,1920]{2,1,0:T(8,128)S(1)} %get-tuple-element.41.yring, f32[8,1920]{1,0:T(8,128)S(1)} %slice_bitcast_fusion.surface, ...), custom_call_target="tpu_custom_call" | custom-call | flops 1000000 | bytes 4649984 | tf_op jit(solution)/shard_map/first_spectra/pallas_call | solution.py:656
  20.1 1.3 %collective-permute-done.7 = f32[96,256]{1,0:T(8,128)S(1)} collective-permute-done((f32[96,256]{1,0:T(8,128)S(1)}, f32[96,256]{1,0:T(8,128)S(1)}, u32[]{:S(2)}, u32[]{:S(2)}) %collective-permute-start.7) | collective-permute-done | bytes 98336 | tf_op jit(solution)/shard_map/ppermute | solution.py:719
  21.4 1.6 %collective-permute-start.8 = (f32[96,256]{1,0:T(8,128)S(1)}, f32[96,256]{1,0:T(8,128)S(1)}, u32[]{:S(2)}, u32[]{:S(2)}) collective-permute-start(f32[96,256]{1,0:T(8,128)S(1)} %add.152.part), channel_id=1, source_target_pairs={{0,16},{8,24},{16,0},{24,8},{1,17},{9,25},{17,1},{25,9},{2,18},{10... | collective-permute-start | bytes 294920 | tf_op jit(solution)/shard_map/ppermute | solution.py:719
  22.9 3.3 %collective-permute-done.8.got = f32[96,256]{1,0:T(8,128)S(1)} collective-permute-done((f32[96,256]{1,0:T(8,128)S(1)}, f32[96,256]{1,0:T(8,128)S(1)}, u32[]{:S(2)}, u32[]{:S(2)}) %collective-permute-start.8) | collective-permute-done | bytes 98336 | tf_op jit(solution)/shard_map/ppermute | solution.py:719
  26.3 1.0 %filter_mass.1 = (f32[8,8,1920]{2,1,0:T(8,128)S(1)}, f32[2,8,1920]{2,1,0:T(8,128)S(1)}, f32[80,256]{1,0:T(8,128)S(1)}, f32[8,2432]{1,0:T(8,128)S(1)}) custom-call(f32[16,8,1920]{2,1,0:T(8,128)S(1)} %get-tuple-element.44.state, f32[3,8,1920]{2,1,0:T(8,128)S(1)} %get-tuple-element.45.sring, f32[96,256]{1,0:T(8,128)S(1)} %add.152.part, ...), custom_call_target="tpu_custom_call" | custom-call | flops 1000000 | bytes 4113408 | tf_op jit(solution)/shard_map/filter_mass/pallas_call | solution.py:656
  27.3 1.6 %collective-permute-start.9 = (f32[8,2432]{1,0:T(8,128)S(1)}, f32[8,2432]{1,0:T(8,128)S(1)}, u32[]{:S(2)}, u32[]{:S(2)}) collective-permute-start(f32[8,2432]{1,0:T(8,128)S(1)} %get-tuple-element.50), channel_id=1, source_target_pairs={{0,1},{1,0},{2,3},{3,2},{4,5},{5,4},{6,7},{7,6},{8,9},{9,8},{10,11... | collective-permute-start | bytes 233480 | tf_op jit(solution)/shard_map/ppermute | solution.py:706
  28.8 1.5 %second_step.1.y = f32[16,8,1920]{2,1,0:T(8,128)S(1)} custom-call(f32[16,8,1920]{2,1,0:T(8,128)S(1)} %get-tuple-element.44.state, f32[3,8,1920]{2,1,0:T(8,128)S(1)} %get-tuple-element.45.sring, f32[80,256]{1,0:T(8,128)S(1)} %get-tuple-element.47.uvmodes, f32[8,8,1920]{2,1,0:T(8,128)S(1)} %get-tuple-element.48.ht, ...), custom_call_target="tpu_custom_call" | custom-call | flops 10000000 | bytes 4861952 | tf_op jit(solution)/shard_map/second_step/pallas_call | solution.py:656
  30.4 1.4 %collective-permute-done.9.got = f32[8,2432]{1,0:T(8,128)S(1)} collective-permute-done((f32[8,2432]{1,0:T(8,128)S(1)}, f32[8,2432]{1,0:T(8,128)S(1)}, u32[]{:S(2)}, u32[]{:S(2)}) %collective-permute-start.9) | collective-permute-done | bytes 77856 | tf_op jit(solution)/shard_map/ppermute | solution.py:706
  31.7 0.7 %second_spectra.1 = (f32[16,8,1920]{2,1,0:T(8,128)S(1)}, f32[64,256]{1,0:T(8,128)S(1)}) custom-call(f32[16,8,1920]{2,1,0:T(8,128)S(1)} %second_step.1.y, f32[8,1920]{1,0:T(8,128)S(1)} %slice_bitcast_fusion.surface, f32[8,1920]{1,0:T(8,128)S(1)} %get-tuple-element.42.ring_surface, f32[8,2432]{1,0:T(8,128)S(1)} %collective-permute-done.9.got, ...), custom_call_target="tpu_custom_call" | custom-call | flops 1000000 | bytes 4248576 | tf_op jit(solution)/shard_map/second_spectra/pallas_call | solution.py:656
  32.5 1.2 %collective-permute-done.10 = f32[64,256]{1,0:T(8,128)S(1)} collective-permute-done((f32[64,256]{1,0:T(8,128)S(1)}, f32[64,256]{1,0:T(8,128)S(1)}, u32[]{:S(2)}, u32[]{:S(2)}) %collective-permute-start.10) | collective-permute-done | bytes 65568 | tf_op jit(solution)/shard_map/ppermute | solution.py:719
  33.8 1.6 %collective-permute-start.11 = (f32[64,256]{1,0:T(8,128)S(1)}, f32[64,256]{1,0:T(8,128)S(1)}, u32[]{:S(2)}, u32[]{:S(2)}) collective-permute-start(f32[64,256]{1,0:T(8,128)S(1)} %add.153.part), channel_id=1, source_target_pairs={{0,16},{8,24},{16,0},{24,8},{1,17},{9,25},{17,1},{25,9},{2,18},{10... | collective-permute-start | bytes 196616 | tf_op jit(solution)/shard_map/ppermute | solution.py:719
  35.4 2.7 %collective-permute-done.11.got = f32[64,256]{1,0:T(8,128)S(1)} collective-permute-done((f32[64,256]{1,0:T(8,128)S(1)}, f32[64,256]{1,0:T(8,128)S(1)}, u32[]{:S(2)}, u32[]{:S(2)}) %collective-permute-start.11) | collective-permute-done | bytes 65568 | tf_op jit(solution)/shard_map/ppermute | solution.py:719
  38.1 1.9 %filter_all.1 = f32[4,4,8,1800]{3,2,1,0:T(8,128)} custom-call(f32[16,8,1920]{2,1,0:T(8,128)S(1)} %get-tuple-element.51.state, f32[64,256]{1,0:T(8,128)S(1)} %add.153.part, f32[64,256]{1,0:T(8,128)S(1)} %collective-permute-done.11.got, bf16[1920,256]{1,0:T(8,128)(2,1)S(1)} %copy-done.1, bf16[1920,256]{1,0:T(8,128)(2,1)S(1)} %copy-done, ...), custom_call_target="tpu_custom_call" | custom-call | tf_op jit(solution)/shard_map/filter_all/pallas_call | solution.py:776
  (30 shorter events, 1.8 us)
Async XLA Ops:
  1.6 8.9 %collective-permute-start = (f32[8,128]{1,0:T(8,128)S(1)}, f32[8,128]{1,0:T(8,128)S(1)}, u32[]{:S(2)}, u32[]{:S(2)}) collective-permute-start(f32[8,128]{1,0:T(8,128)S(1)} %get-tuple-element.30), channel_id=1, source_target_pairs={{0,8},{8,0},{16,24},{24,16},{1,9},{9,1},{17,25},{25,17},{2,10},{10... | collective-permute-start | bytes 12296 | tf_op jit(solution)/shard_map/ppermute | solution.py:730
  1.7 8.8 %collective-permute-start.1 = (f32[8,128]{1,0:T(8,128)S(1)}, f32[8,128]{1,0:T(8,128)S(1)}, u32[]{:S(2)}, u32[]{:S(2)}) collective-permute-start(f32[8,128]{1,0:T(8,128)S(1)} %get-tuple-element.31), channel_id=1, source_target_pairs={{0,24},{8,16},{16,8},{24,0},{1,25},{9,17},{17,9},{25,1},{2,26},{10... | collective-permute-start | bytes 12296 | tf_op jit(solution)/shard_map/ppermute | solution.py:731
  3.3 7.5 %collective-permute-start.2 = (f32[8,7040]{1,0:T(8,128)S(1)}, f32[8,7040]{1,0:T(8,128)S(1)}, u32[]{:S(2)}, u32[]{:S(2)}) collective-permute-start(f32[8,7040]{1,0:T(8,128)S(1)} %get-tuple-element.34), channel_id=1, source_target_pairs={{0,2},{2,0},{4,6},{6,4},{1,3},{3,1},{5,7},{7,5},{8,10},{10,8},{12,... | collective-permute-start | bytes 675848 | tf_op jit(solution)/shard_map/ppermute | solution.py:727
  3.7 10.1 %collective-permute-start.3 = (f32[8,7040]{1,0:T(8,128)S(1)}, f32[8,7040]{1,0:T(8,128)S(1)}, u32[]{:S(2)}, u32[]{:S(2)}) collective-permute-start(f32[8,7040]{1,0:T(8,128)S(1)} %get-tuple-element.35), channel_id=1, source_target_pairs={{2,4},{4,2},{3,5},{5,3},{10,12},{12,10},{11,13},{13,11},{18,20},{2... | collective-permute-start | bytes 675848 | tf_op jit(solution)/shard_map/ppermute | solution.py:728
  13.8 5.3 %copy-start.1 = (bf16[1920,256]{1,0:T(8,128)(2,1)S(1)}, bf16[1920,256]{1,0:T(8,128)(2,1)}, u32[]{:S(2)}) copy-start(bf16[1920,256]{1,0:T(8,128)(2,1)} %constant.55.clone.wh) | copy-start | bytes 2949124
  14.0 5.1 %copy-start = (bf16[1920,256]{1,0:T(8,128)(2,1)S(1)}, bf16[1920,256]{1,0:T(8,128)(2,1)}, u32[]{:S(2)}) copy-start(bf16[1920,256]{1,0:T(8,128)(2,1)} %constant.56.clone.wl) | copy-start | bytes 2949124
  14.0 2.2 %collective-permute-start.4 = (f32[8,128]{1,0:T(8,128)S(1)}, f32[8,128]{1,0:T(8,128)S(1)}, u32[]{:S(2)}, u32[]{:S(2)}) collective-permute-start(f32[8,128]{1,0:T(8,128)S(1)} %get-tuple-element.38), channel_id=1, source_target_pairs={{0,8},{8,0},{16,24},{24,16},{1,9},{9,1},{17,25},{25,17},{2,10},{10... | collective-permute-start | bytes 12296 | tf_op jit(solution)/shard_map/ppermute | solution.py:740
  14.1 3.1 %collective-permute-start.5 = (f32[8,128]{1,0:T(8,128)S(1)}, f32[8,128]{1,0:T(8,128)S(1)}, u32[]{:S(2)}, u32[]{:S(2)}) collective-permute-start(f32[8,128]{1,0:T(8,128)S(1)} %get-tuple-element.39), channel_id=1, source_target_pairs={{0,24},{8,16},{16,8},{24,0},{1,25},{9,17},{17,9},{25,1},{2,26},{10... | collective-permute-start | bytes 12296 | tf_op jit(solution)/shard_map/ppermute | solution.py:741
  14.7 4.4 %collective-permute-start.6 = (f32[8,2432]{1,0:T(8,128)S(1)}, f32[8,2432]{1,0:T(8,128)S(1)}, u32[]{:S(2)}, u32[]{:S(2)}) collective-permute-start(f32[8,2432]{1,0:T(8,128)S(1)} %get-tuple-element.43), channel_id=1, source_target_pairs={{0,1},{1,0},{2,3},{3,2},{4,5},{5,4},{6,7},{7,6},{8,9},{9,8},{10,11... | collective-permute-start | bytes 233480 | tf_op jit(solution)/shard_map/ppermute | solution.py:706
  17.2 1.9 %copy-start.2 = (s32[16,128]{1,0:T(8,128)S(1)}, s32[16,128]{1,0:T(8,128)}, u32[]{:S(2)}) copy-start(s32[16,128]{1,0:T(8,128)} %row_code.1.code) | copy-start | bytes 24580
  20.0 1.4 %collective-permute-start.7 = (f32[96,256]{1,0:T(8,128)S(1)}, f32[96,256]{1,0:T(8,128)S(1)}, u32[]{:S(2)}, u32[]{:S(2)}) collective-permute-start(f32[96,256]{1,0:T(8,128)S(1)} %get-tuple-element.46), channel_id=1, source_target_pairs={{0,8},{8,0},{16,24},{24,16},{1,9},{9,1},{17,25},{25,17},{2,10},{10... | collective-permute-start | bytes 294920 | tf_op jit(solution)/shard_map/ppermute | solution.py:719
  21.4 4.9 %collective-permute-start.8 = (f32[96,256]{1,0:T(8,128)S(1)}, f32[96,256]{1,0:T(8,128)S(1)}, u32[]{:S(2)}, u32[]{:S(2)}) collective-permute-start(f32[96,256]{1,0:T(8,128)S(1)} %add.152.part), channel_id=1, source_target_pairs={{0,16},{8,24},{16,0},{24,8},{1,17},{9,25},{17,1},{25,9},{2,18},{10... | collective-permute-start | bytes 294920 | tf_op jit(solution)/shard_map/ppermute | solution.py:719
  27.3 4.5 %collective-permute-start.9 = (f32[8,2432]{1,0:T(8,128)S(1)}, f32[8,2432]{1,0:T(8,128)S(1)}, u32[]{:S(2)}, u32[]{:S(2)}) collective-permute-start(f32[8,2432]{1,0:T(8,128)S(1)} %get-tuple-element.50), channel_id=1, source_target_pairs={{0,1},{1,0},{2,3},{3,2},{4,5},{5,4},{6,7},{7,6},{8,9},{9,8},{10,11... | collective-permute-start | bytes 233480 | tf_op jit(solution)/shard_map/ppermute | solution.py:706
  32.5 1.3 %collective-permute-start.10 = (f32[64,256]{1,0:T(8,128)S(1)}, f32[64,256]{1,0:T(8,128)S(1)}, u32[]{:S(2)}, u32[]{:S(2)}) collective-permute-start(f32[64,256]{1,0:T(8,128)S(1)} %get-tuple-element.52), channel_id=1, source_target_pairs={{0,8},{8,0},{16,24},{24,16},{1,9},{9,1},{17,25},{25,17},{2,10},{10... | collective-permute-start | bytes 196616 | tf_op jit(solution)/shard_map/ppermute | solution.py:719
  33.8 4.3 %collective-permute-start.11 = (f32[64,256]{1,0:T(8,128)S(1)}, f32[64,256]{1,0:T(8,128)S(1)}, u32[]{:S(2)}, u32[]{:S(2)}) collective-permute-start(f32[64,256]{1,0:T(8,128)S(1)} %add.153.part), channel_id=1, source_target_pairs={{0,16},{8,24},{16,0},{24,8},{1,17},{9,25},{17,1},{25,9},{2,18},{10... | collective-permute-start | bytes 196616 | tf_op jit(solution)/shard_map/ppermute | solution.py:719

commit v6 on v5

--- a/solution.py
+++ b/solution.py
@@ -73,16 +73,17 @@
         self.base = (self.C - 1) // LANES * LANES
         self.tiles = self.W // LANES
         self.extra = -(-self.tiles // self.R)
-        self.fold = -(-self.tiles // 2)
-        self.lat_lanes = 3 * self.W + (self.fold + self.extra) * LANES
+        whole = self.base // LANES
+        self.fold = -(-whole // 2)
+        self.lat_lanes = 3 * self.base + (self.fold + -(-whole // self.R)) * LANES
         width = -(-self.base // LANES // 3) * LANES if self.base else self.W
         cuts = [c for c in range(0, self.base + 1, width)] if self.base else [0]
         if self.C - cuts[-1] <= LANES and len(cuts) > 1:
             cuts.pop()
         self.chunks = list(zip(cuts, cuts[1:] + [self.C]))
         self.bits = (self.R - self.slots).bit_length()
-        assert self.R == 2 * self.slots and self.n_lon <= KMAX
-        assert self.R == 2 * self.L and self.n_lon % 2 == 0
+        assert self.R == 2 * self.slots and self.base > 0
+        assert self.R == 2 * self.L and self.n_lon % 4 == 0 and self.L % 2 == 0
         assert 2 <= self.C - self.base <= LANES - 2 and 2 * self.planes <= LANES
 
 
@@ -131,28 +132,32 @@
         ref[:, start : start + LANES] = tile
 
 
+def near_and_far(z):
+    lat_even = lax.axis_index("lat") % 2 == 0
+    near = jnp.where(lat_even, z.R - 1, 0)
+    far = jnp.where(lat_even, z.R - 2, 1)
+    return (near, far), (z.R - 1 - near, z.R - 1 - far)
+
+
 def edge_rows(z, x, m1, m2, after):
-    L, W = z.L, z.W
+    L, B = z.L, z.base
     fold = z.fold * LANES
     after[...] = jnp.zeros(after.shape, jnp.float32)
-    lat_even = lax.axis_index("lat") % 2 == 0
-    near1 = jnp.where(lat_even, z.R - 1, 0)
-    far1 = jnp.where(lat_even, z.R - 2, 1)
-    for msg, near, far in ((m1, near1, far1), (m2, z.R - 1 - near1, z.R - 1 - far1)):
-        msg[:, 3 * W :] = jnp.zeros((z.R, z.lat_lanes - 3 * W), jnp.float32)
+    for msg, (near, far) in zip((m1, m2), near_and_far(z)):
+        msg[:, 3 * B :] = jnp.zeros((z.R, z.lat_lanes - 3 * B), jnp.float32)
         for k in range(7):
             f, at = (k, near) if k < 4 else (k - 3, far)
             for l in range(L):
-                row = x[f * L + l, pl.ds(at, 1), :]
+                row = x[f * L + l, pl.ds(at, 1), 0:B]
                 to = (k % 2) * L + l
                 if k < 6:
-                    msg[to : to + 1, k // 2 * W : (k // 2 + 1) * W] = row
+                    msg[to : to + 1, k // 2 * B : (k // 2 + 1) * B] = row
                 else:
-                    msg[l : l + 1, 3 * W : 3 * W + fold] = row[:, 0:fold]
-                    msg[L + l : L + l + 1, 3 * W : 4 * W - fold] = row[:, fold:]
-        row = x[4 * L, pl.ds(near, 1), :]
-        for t in range(z.tiles):
-            at = 3 * W + fold + t // z.R * LANES
+                    msg[l : l + 1, 3 * B : 3 * B + fold] = row[:, 0:fold]
+                    msg[L + l : L + l + 1, 3 * B : 4 * B - fold] = row[:, fold:]
+        row = x[4 * L, pl.ds(near, 1), 0:B]
+        for t in range(B // LANES):
+            at = 3 * B + fold + t // z.R * LANES
             msg[t % z.R : t % z.R + 1, at : at + LANES] = row[:, t * LANES : (t + 1) * LANES]
 
 
@@ -168,24 +173,30 @@
     by_parity("lon", e1, e2, right, left)
 
 
-def widen(z, x_in, r1, r2, x, sums, from_right, from_left):
+def widen(z, x_in, r1, r2, x, sums, k1, k2, from_right, from_left):
     del x_in
+    L, T = z.L, z.W - z.base
     by_parity("lon", from_right, from_left, r1[...], r2[...])
     right, left = from_right[...], from_left[...]
     for p in range(z.planes):
         patch(z, x.at[p], p, z.planes, 2, right, left)
-    total = layer_weight(x[2 * z.L], x[3 * z.L])
-    for l in range(1, z.L):
-        total = total + layer_weight(x[2 * z.L + l], x[3 * z.L + l])
+    total = layer_weight(x[2 * L], x[3 * L])
+    for l in range(1, L):
+        total = total + layer_weight(x[2 * L + l], x[3 * L + l])
     sums[...] = total
-
-
-def put_column_sums(z, msg, total, south, north):
-    if total is not None:
-        msg[:, 0 : z.W] = total
+    for msg, (near, far) in zip((k1, k2), near_and_far(z)):
+        for k in range(8):
+            f, at = (k, near) if k < 4 else (k - 3, far) if k < 7 else (4, near)
+            for l in range(L):
+                p = f * L + l if k < 7 else 4 * L
+                to = (k % 2) * L + l
+                msg[to : to + 1, k // 2 * T : (k // 2 + 1) * T] = x[p, pl.ds(at, 1), :][:, z.base :]
+
+
+def put_ring_sums(z, msg, south, north):
     for d, row in enumerate((south, north)):
         for t in range(z.tiles):
-            at = z.W + (d * z.extra + t // z.R) * LANES
+            at = (d * z.extra + t // z.R) * LANES
             msg[t % z.R : t % z.R + 1, at : at + LANES] = row[:, t * LANES : (t + 1) * LANES]
 
 
@@ -198,40 +209,40 @@
     return south, north
 
 
-def halo_rows(z, sums, r1, r2, ring, ring_surface, msg, c1, c2):
+def halo_rows(z, sums, r1, r2, t1, t2, ring, ring_surface, msg):
     lat_even = lax.axis_index("lat") % 2 == 0
-
-    def place(d, source):
-        L, W = z.L, z.W
-        fold = z.fold * LANES
+    L, B, T = z.L, z.base, z.W - z.base
+    fold = z.fold * LANES
+    msg[:, 0 : z.W] = sums[...]
+    msg[:, z.W :] = jnp.zeros((z.R, 2 * z.extra * LANES), jnp.float32)
+
+    def place(d, source, tail):
         here = slice(d * L, (d + 1) * L)
-        for k in range(6):
+        for k in range(7):
             at = (k % 2) * L
-            ring[k, here, :] = source[at : at + L, k // 2 * W : (k // 2 + 1) * W]
-        ring[6, here, 0:fold] = source[0:L, 3 * W : 3 * W + fold]
-        ring[6, here, fold:] = source[L : 2 * L, 3 * W : 3 * W + W - fold]
-        for t in range(z.tiles):
-            at = 3 * W + fold + t // z.R * LANES
+            if k < 6:
+                ring[k, here, 0:B] = source[at : at + L, k // 2 * B : (k // 2 + 1) * B]
+            ring[k, here, B:] = tail[at : at + L, k // 2 * T : (k // 2 + 1) * T]
+        ring[6, here, 0:fold] = source[0:L, 3 * B : 3 * B + fold]
+        ring[6, here, fold:B] = source[L : 2 * L, 3 * B : 4 * B - fold]
+        for t in range(B // LANES):
+            at = 3 * B + fold + t // z.R * LANES
             part = source[t % z.R : t % z.R + 1, at : at + LANES]
             ring_surface[here, t * LANES : (t + 1) * LANES] = jnp.broadcast_to(part, (L, LANES))
+        ring_surface[here, B:] = tail[L : 2 * L, 3 * T :]
 
     @pl.when(lat_even)
     def _():
-        place(0, r2)
-        place(1, r1)
+        place(0, r2, t2)
+        place(1, r1, t1)
 
     @pl.when(jnp.logical_not(lat_even))
     def _():
-        place(0, r1)
-        place(1, r2)
-
-    def row(k, lo):
-        return ring[k, :, lo : lo + LANES] if k < 4 else ring_surface[:, lo : lo + LANES]
-
-    left, right = edge_tiles(z, 5, lambda k: row(k, 0), lambda k: row(k, z.base), 1)
-    by_parity("lon", c1, c2, right, left)
+        place(0, r1, t1)
+        place(1, r2, t2)
+
     south, north = ring_sum(z, layer_weight(ring[2], ring[3]))
-    put_column_sums(z, msg, sums[...], south, north)
+    put_ring_sums(z, msg.at[:, z.W :], south, north)
 
 
 def in_band(z, shape):
@@ -299,16 +310,8 @@
             qput(l, q)
 
 
-def first_step(
-    z, x, ring_in, surface_in, r1, r2, geom, y, yring, ring_surface, ring, inner, q_ring, from_right, from_left
-):
+def first_step(z, x, ring, geom, y, yring, inner, q_ring):
     L = z.L
-    by_parity("lon", from_right, from_left, r1[...], r2[...])
-    right, left = from_right[...], from_left[...]
-    ring[...] = ring_in[...]
-    ring_surface[...] = surface_in[...]
-    for k in range(5):
-        patch(z, ring.at[k] if k < 4 else ring_surface, k, 5, 1, right, left)
     q_ring[...] = ring_geopot(z, ring[2], ring[3])
 
     def get(f, l):
@@ -348,22 +351,19 @@
     yring[2] = new["t"] * mask
 
 
-def level_part(z, surface, ring_surface, got):
+def level_part(z, surface, ring_surface, below, ring_below):
     live = jnp.where(lax.axis_index("lev") < z.n_lev - 1, 1.0, 0.0)
     lat = lax.axis_index("lat")
-    tile = surface + live * got[:, 0 : z.W]
-    rows, beneath = [], []
+    rows = []
     for d in range(2):
         there = jnp.where(lat > 0, 1.0, 0.0) if d == 0 else jnp.where(lat < z.n_lat - 1, 1.0, 0.0)
         parts = []
         for t in range(z.tiles):
-            at = z.W + (d * z.extra + t // z.R) * LANES
-            parts.append(got[t % z.R : t % z.R + 1, at : at + LANES])
+            at = (d * z.extra + t // z.R) * LANES
+            parts.append(ring_below[t % z.R : t % z.R + 1, at : at + LANES])
         sums = jnp.concatenate(parts, 1)
-        sums = jnp.where(lax.broadcasted_iota(jnp.int32, sums.shape, 1) < z.C, sums, 0.0)
-        beneath.append(there * live * sums)
-        rows.append(there * ring_surface[d * z.L : d * z.L + 1, :] + beneath[d])
-    return tile, rows[0], rows[1], beneath[1]
+        rows.append(there * (ring_surface[d * z.L : d * z.L + 1, :] + live * sums))
+    return surface + live * below, rows[0], rows[1]
 
 
 def split(x):
@@ -423,66 +423,89 @@
         out[i * z.R : (i + 1) * z.R, :] = jnp.where(row < z.slots, a, pltpu.roll(b, z.slots, 0))
 
 
-def first_spectra(z, y, yring, surface, ring_surface, got, geom, wh, wl, phase, code, state, sring, out):
+def tile_spectra(z, y, wh, wl, phase, code, out):
+    x = masked(z, y[...].reshape(4 * z.L * z.R, z.W))
+    pick_spectra(z, spectra(z, x, wh, wl, phase), code, out)
+
+
+def tile_and_ring_spectra(z, y, yring, wh, wl, phase, code, out):
+    m = 4 * z.L * z.R
+    x = jnp.concatenate([y[...].reshape(m, z.W), yring[...].reshape(6 * z.L, z.W)], 0)
+    full = spectra(z, masked(z, x), wh, wl, phase)
+    pick_spectra(z, full, code, out)
+    out[4 * z.L * z.slots :, :] = full[m:, :]
+
+
+def pick_level_part(z, full, code):
+    code = code[0 : z.R, :]
+    row = lax.broadcasted_iota(jnp.int32, (z.R, 2 * KMAX), 0)
+    a = compress(z, full[0 : z.R], code)
+    b = compress(z, full[z.R : 2 * z.R], code)
+    return jnp.where(row < z.slots, a, pltpu.roll(b, z.slots, 0))
+
+
+def first_level_spectra(
+    z, surface, ring_surface, got, part, part_got, geom, wh, wl, phase, code, sent, own, change, ring_change
+):
     L = z.L
-    g, gs, gn, beneath = level_part(z, surface[...], ring_surface, got)
+    g, gs, gn = level_part(z, surface[...], ring_surface, got[:, 0 : z.W], got[:, z.W :])
     du = wide(geom, 0, 0, z.R, z.W) * (east(g) - g)
     dv = NORTH_COEF * (with_last(g, gn) - g)
-    for l in range(L):
-        state[l] = y[l] - du
-        state[L + l] = y[L + l] - dv
-    for p in range(2 * L, 4 * L):
-        state[p] = y[p]
     shape = (2 * L, z.W)
     south = lax.broadcasted_iota(jnp.int32, shape, 0) < L
-    zonal = wide(geom, 0, z.R, z.R + 2 * L, z.W)
     gn = jnp.broadcast_to(gn, shape)
-    du_north = zonal * (east(gn) - gn)
+    du_north = wide(geom, 0, z.R, z.R + 2 * L, z.W) * (east(gn) - gn)
     dv_south = NORTH_COEF * jnp.broadcast_to(g[0:1] - gs, shape)
-    uv = yring[0] - jnp.where(south, dv_south, du_north) * in_band(z, shape)
-    sring[0] = uv
-    sring[1] = yring[1]
-    sring[2] = yring[2]
-    lane = lax.broadcasted_iota(jnp.int32, shape, 1)
-    corner = jnp.broadcast_to(beneath[:, 0:1], shape)
-    given = jnp.where((lane == z.W - 1) & jnp.logical_not(south), -zonal * corner, masked(z, uv))
-    m = 4 * L * z.R
-    everything = jnp.concatenate(
-        [
-            masked(z, state[...].reshape(m, z.W)),
-            given,
-            masked(z, sring[1]),
-            masked(z, sring[2]),
-        ],
-        0,
-    )
-    full = spectra(z, everything, wh, wl, phase)
-    pick_spectra(z, full, code, out)
-    at = 4 * L * z.slots
-    out[at : at + 6 * L, :] = full[m:, :]
-    wide_shape = (2 * L, 2 * KMAX)
-    lane = lax.broadcasted_iota(jnp.int32, wide_shape, 1)
-    lon = lax.axis_index("lon")
-    ends = jnp.where(south[:, 0:1], uv[:, 0:1], uv[:, z.C - 1 : z.C])
-    out[at + 6 * L :, :] = jnp.where(
-        lane == lon,
-        jnp.broadcast_to(ends, wide_shape),
-        jnp.where(lane == KMAX + lon, jnp.broadcast_to(beneath[:, 0:1], wide_shape), 0.0),
-    )
-
-
-def second_spectra(z, y, surface, ring_surface, got, geom, wh, wl, phase, code, state, out):
-    L = z.L
-    g, _, gn, _ = level_part(z, surface[...], ring_surface, got)
+    ring = jnp.where(south, dv_south, du_north) * in_band(z, shape)
+    change[0] = du
+    change[1] = dv
+    ring_change[...] = ring
+    full = spectra(z, masked(z, jnp.concatenate([du, dv, ring], 0)), wh, wl, phase)
+    own[0 : z.R, :] = pick_level_part(z, full, code)
+    own[z.R :, :] = full[2 * z.R :]
+    n = part.shape[0]
+    sent[0:n, :] = part[...] + part_got[...]
+    sent[n:, :] = own[...]
+
+
+def second_level_spectra(
+    z, surface, ring_surface, got, part, part_got, geom, wh, wl, phase, code, sent, own, change
+):
+    g, _, gn = level_part(z, surface[...], ring_surface, got[:, 0 : z.W], got[:, z.W :])
     du = wide(geom, 0, 0, z.R, z.W) * (east(g) - g)
     dv = NORTH_COEF * (with_last(g, gn) - g)
-    for l in range(L):
-        state[l] = y[l] - du
-        state[L + l] = y[L + l] - dv
-    for p in range(2 * L, 4 * L):
-        state[p] = y[p]
-    full = spectra(z, masked(z, state[...].reshape(4 * L * z.R, z.W)), wh, wl, phase)
-    pick_spectra(z, full, code, out)
+    change[0] = du
+    change[1] = dv
+    full = spectra(z, masked(z, jnp.concatenate([du, dv], 0)), wh, wl, phase)
+    own[...] = pick_level_part(z, full, code)
+    n = part.shape[0]
+    sent[0:n, :] = part[...] + part_got[...]
+    sent[n:, :] = own[...]
+
+
+def total_modes(z, parts):
+    if len(parts) == 2:
+        return parts[0][...] + parts[1][...]
+    mine, got, core, across = parts
+    n = mine.shape[0] - core.shape[0]
+    total = mine[0:n, :] + got[0:n, :]
+    level = (mine[n:, :] + core[...]) + (got[n:, :] + across[...])
+    both = level[0 : z.R]
+    row = lax.broadcasted_iota(jnp.int32, both.shape, 0)
+    other = pltpu.roll(both, z.slots, 0)
+    du = jnp.where(row < z.slots, both, other)
+    dv = jnp.where(row < z.slots, other, both)
+    pairs = z.L // 2
+    m = 4 * z.L * z.slots
+    tiles = [total[i * z.R : (i + 1) * z.R] - (du if i < pairs else dv) for i in range(z.L)]
+    tiles.append(total[z.L * z.R : m])
+    if n > m:
+        tiles += [total[m : m + 2 * z.L] - level[z.R :], total[m + 2 * z.L :]]
+    return jnp.concatenate(tiles, 0)
+
+
+def join(z, mine, got, core, across, out):
+    out[...] = total_modes(z, (mine, got, core, across))
 
 
 def mode_weight(z, keep):
@@ -523,15 +546,16 @@
     return product(modes, wh, wl, ((1,), (1,)))
 
 
-def filter_mass(z, state, sring, part, got, wh, wl, phase, code, ht, htring, uvmodes, msg):
+def filter_mass(z, *refs):
+    parts, refs = refs[:-10], refs[-10:]
+    state, sring, wh, wl, phase, code, ht, htring, uvmodes, msg = refs
     L, m = z.L, 4 * z.L * z.slots
-    total = part[...] + got[...]
-    modes = local_modes(total, phase)
+    modes = local_modes(total_modes(z, parts), phase)
     keep, rkeep = keeps(z, code)
     weight, rweight = mode_weight(z, keep), mode_weight(z, rkeep)
     ring = [modes[m + k * 2 * L : m + (k + 1) * 2 * L] * rweight for k in range(3)]
     tiles = tile_modes(z, modes, code, weight)
-    uvmodes[...] = jnp.concatenate(tiles[: 2 * L] + [ring[0], total[m + 6 * L :]], 0)
+    uvmodes[...] = jnp.concatenate(tiles[: 2 * L] + [ring[0]], 0)
     s = smooth(jnp.concatenate(tiles[2 * L :] + ring[1:], 0), wh, wl)
     damp, rdamp = damping(z, keep, z.W), damping(z, rkeep, z.W)
     for p in range(2 * L):
@@ -545,43 +569,21 @@
     for l in range(1, L):
         total = total + layer_weight(ht[l], ht[L + l])
     south, north = ring_sum(z, layer_weight(htring[0], htring[1]))
-    put_column_sums(z, msg, total, south, north)
-
-
-def ring_corners(z, uv, gathered, geom):
-    shape = uv.shape
-    lon = lax.axis_index("lon")
-    right = jnp.where(lon == z.n_lon - 1, 0, lon + 1)
-    left = jnp.where(lon == 0, z.n_lon - 1, lon - 1)
-    place = lax.broadcasted_iota(jnp.int32, gathered.shape, 1)
-
-    def of(lane):
-        value = jnp.sum(jnp.where(place == lane, gathered, 0.0), 1, keepdims=True)
-        return jnp.broadcast_to(value, shape)
-
-    south = lax.broadcasted_iota(jnp.int32, shape, 0) < z.L
-    north = jnp.logical_not(south)
-    lane = lax.broadcasted_iota(jnp.int32, shape, 1)
-    zonal = wide(geom, 0, z.R, z.R + 2 * z.L, z.W)
-    uv = jnp.where((lane == z.C) & south, of(right), uv)
-    uv = jnp.where((lane == z.W - 1) & north, of(left) - zonal * of(KMAX + lon), uv)
-    corner = of(KMAX + right)
-    uv = jnp.where((lane == z.C - 1) & north, uv - zonal * corner, uv)
-    row = lax.broadcasted_iota(jnp.int32, shape, 0)
-    above = jnp.where((lane == z.C) & (row == z.R - 1), NORTH_COEF * corner, 0.0)
-    return uv, above
-
-
-def second_step(z, state, sring, uvmodes, ht, htring, geom, wh, wl, code, y, uv, uvring, q_ring):
+    msg[:, 0 : z.W] = total
+    msg[:, z.W :] = jnp.zeros((z.R, 2 * z.extra * LANES), jnp.float32)
+    put_ring_sums(z, msg.at[:, z.W :], south, north)
+
+
+def second_step(z, state, sring, change, ring_change, uvmodes, ht, htring, geom, wh, wl, code, y, uv, uvring, q_ring):
     L = z.L
     m = 2 * L * z.R
-    s = smooth(uvmodes[0 : m + 2 * L, :], wh, wl)
+    s = smooth(uvmodes[...], wh, wl)
     keep, rkeep = keeps(z, code)
     damp, rdamp = damping(z, keep, z.W), damping(z, rkeep, z.W)
-    x, above = ring_corners(z, sring[0], uvmodes[m + 2 * L :, :], geom)
     for p in range(2 * L):
-        old = state[p] if p < L else state[p] - above
-        uv[p] = old + damp * (s[p * z.R : (p + 1) * z.R] - old)
+        x = state[p] - change[p // L]
+        uv[p] = x + damp * (s[p * z.R : (p + 1) * z.R] - x)
+    x = sring[0] - ring_change[...]
     uvring[...] = x + rdamp * (s[m:] - x)
     q_ring[...] = ring_geopot(z, htring[0], htring[1])
 
@@ -598,9 +600,11 @@
     )
 
 
-def filter_all(z, state, part, got, wh, wl, phase, code, out, held, sem):
+def filter_all(z, *refs):
+    parts, refs = refs[:-9], refs[-9:]
+    state, change, wh, wl, phase, code, out, held, sem = refs
     L = z.L
-    modes = local_modes(part[...] + got[...], phase)
+    modes = local_modes(total_modes(z, parts), phase)
     keep, _ = keeps(z, code)
     high, low = split(jnp.concatenate(tile_modes(z, modes, code, mode_weight(z, keep)), 0))
     across = ((1,), (1,))
@@ -612,6 +616,8 @@
         d = damping(z, keep, top - lo)
         for p in range(4 * L):
             x = state[p, :, lo:top]
+            if p < 2 * L:
+                x = x - change[p // L, :, lo:top]
             new = x + d * (s[p * z.R : (p + 1) * z.R] - x)
             held[p // L, p % L, :, lo:hi] = new[:, : hi - lo]
         copies.append(
@@ -711,14 +717,19 @@
             total = total + jnp.where(place + s < z.n_lev, got, 0.0)
         return total
 
-    def over_lon(part):
-        got, step = None, 1
+    def lon_swap(value, step):
+        return lax.ppermute(value, "lon", [(i, i ^ step) for i in range(z.n_lon)])
+
+    def over_lon(sent, own, rows):
+        parts = [sent, lon_swap(sent, 2), lon_swap(own, 1), lon_swap(own, 3)]
+        if z.n_lon == 4:
+            return parts
+        (part,) = call(join, [(rows, 2 * KMAX)], parts)
+        got, step = lon_swap(part, 4), 8
         while step < z.n_lon:
-            if got is not None:
-                part = part + got
-            got = lax.ppermute(part, "lon", [(i, i ^ step) for i in range(z.n_lon)])
-            step *= 2
-        return part, got
+            part = part + got
+            got, step = lon_swap(part, step), step * 2
+        return [part, got]
 
     tile = (R, LANES)
     x = jnp.concatenate([fields.reshape(4 * L, R, z.C), surface[None]], 0)
@@ -729,54 +740,62 @@
     e1, e2 = call(edge_columns, [tile, tile], [x, after])
     e1 = lax.ppermute(e1, "lon", lon_one)
     e2 = lax.ppermute(e2, "lon", lon_two)
-    x, sums = call(
-        widen, [(z.planes, R, W), (R, W)], [x, e1, e2], [tile] * 2, aliases={0: 0}
-    )
-
-    sent = (R, W + 2 * z.extra * LANES)
-    ring, ring_surface, msg, c1, c2 = call(
-        halo_rows, [(7, 2 * L, W), (2 * L, W), sent, tile, tile], [sums, m1, m2]
-    )
-    c1 = lax.ppermute(c1, "lon", lon_one)
-    c2 = lax.ppermute(c2, "lon", lon_two)
+    tails = (R, 4 * (W - z.base))
+    x, sums, t1, t2 = call(
+        widen,
+        [(z.planes, R, W), (R, W), tails, tails],
+        [x, e1, e2],
+        [tile] * 2,
+        aliases={0: 0},
+    )
+    t1 = lax.ppermute(t1, "lat", lat_one)
+    t2 = lax.ppermute(t2, "lat", lat_two)
+    ring_lanes = 2 * z.extra * LANES
+    ring, ring_surface, msg = call(
+        halo_rows, [(7, 2 * L, W), (2 * L, W), (R, W + ring_lanes)], [sums, m1, m2, t1, t2]
+    )
     got = from_below(msg)
-    y, yring, ring_surface = call(
+    y, yring = call(
         first_step,
-        [(4 * L, R, W), (3, 2 * L, W), (2 * L, W)],
-        [x, ring, ring_surface, c1, c2, geom],
-        [(7, 2 * L, W), (4, 2 * L, W), (2 * L, W), tile, tile],
+        [(4 * L, R, W), (3, 2 * L, W)],
+        [x, ring, geom],
+        [(4, 2 * L, W), (2 * L, W)],
         flops=10_000_000,
     )
+    waves = [wave_high, wave_low, phase, code]
+    rows = 4 * L * z.slots
+    (part,) = call(tile_and_ring_spectra, [(rows + 6 * L, 2 * KMAX)], [y, yring, *waves])
     surface_tile = x[4 * L]
-    state, sring, part = call(
-        first_spectra,
-        [(4 * L, R, W), (3, 2 * L, W), (4 * L * z.slots + 8 * L, 2 * KMAX)],
-        [y, yring, surface_tile, ring_surface, got, geom, wave_high, wave_low, phase, code],
-    )
-    part, got = over_lon(part)
+    sent, own, change, ring_change = call(
+        first_level_spectra,
+        [(rows + 8 * L + R, 2 * KMAX), (2 * L + R, 2 * KMAX), (2, R, W), (2 * L, W)],
+        [surface_tile, ring_surface, got, part, lon_swap(part, 1), geom, *waves],
+    )
+    parts = over_lon(sent, own, rows + 6 * L)
     ht, htring, uvmodes, msg = call(
         filter_mass,
-        [(2 * L, R, W), (2, 2 * L, W), (2 * L * R + 4 * L, 2 * KMAX), sent],
-        [state, sring, part, got, wave_high, wave_low, phase, code],
+        [(2 * L, R, W), (2, 2 * L, W), (2 * L * R + 2 * L, 2 * KMAX), (R, W + ring_lanes)],
+        [*parts, y, yring, *waves],
     )
     got = from_below(msg)
     (y,) = call(
         second_step,
         [(4 * L, R, W)],
-        [state, sring, uvmodes, ht, htring, geom, wave_high, wave_low, code],
+        [y, yring, change, ring_change, uvmodes, ht, htring, geom, wave_high, wave_low, code],
         [(2 * L, R, W), (2 * L, W), (2 * L, W)],
         flops=10_000_000,
     )
-    state, part = call(
-        second_spectra,
-        [(4 * L, R, W), (4 * L * z.slots, 2 * KMAX)],
-        [y, surface_tile, ring_surface, got, geom, wave_high, wave_low, phase, code],
-    )
-    part, got = over_lon(part)
+    (part,) = call(tile_spectra, [(rows, 2 * KMAX)], [y, *waves])
+    sent, own, change = call(
+        second_level_spectra,
+        [(rows + R, 2 * KMAX), (R, 2 * KMAX), (2, R, W)],
+        [surface_tile, ring_surface, got, part, lon_swap(part, 1), geom, *waves],
+    )
+    parts = over_lon(sent, own, rows)
     return pl.pallas_call(
         functools.partial(filter_all, z),
         out_shape=jax.ShapeDtypeStruct((4, L, R, z.C), f32),
-        in_specs=[vmem] * 7,
+        in_specs=[vmem] * (len(parts) + 6),
         out_specs=pl.BlockSpec(memory_space=pl.ANY),
         scratch_shapes=[
             pltpu.VMEM((4, L, R, z.C), f32),
@@ -784,7 +803,7 @@
         ],
         compiler_params=pltpu.CompilerParams(vmem_limit_bytes=VMEM_LIMIT),
         name="filter_all",
-    )(state, part, got, wave_high, wave_low, phase, code)
+    )(*parts, y, change, *waves)
 
 
 def wave_tables(z):

time: 40.3 us -> 38.7 us (0.960)
  waiting for transfers between devices: 15 us -> 10.2 us
  starting transfers between devices: 13.8 us -> 15.8 us
  Pallas kernels: 8.91 us -> 9.86 us
    ppermute x1, waiting for transfers between devices: 3.02 us -> 0.01 us  [local(): m2 = lax.ppermute(m2, 'lat', lat_two)]
    ppermute x6 -> x10, starting transfers between devices: 4.01 us -> 6.55 us  [the longest x8 4.55 us: lon_swap(): return lax.ppermute(value, 'lon', [(i, i ^ step) for i in range(z.n_lon)])]
    ppermute x2, waiting for transfers between devices: 2.2 us -> 1.06 us  [from_below(): return lax.ppermute(column, 'lev', [(0, 1), (1, 0)])]
    pallas_call x9 -> x11, Pallas kernels: 5.73 us -> 6.72 us  [call(): pl.pallas_call(functools.partial(kernel, z), out_shape=[jax.ShapeDtypeStr...]
    ppermute x2, starting transfers between devices: 3.05 us -> 2.46 us  [from_below(): return lax.ppermute(column, 'lev', [(0, 1), (1, 0)])]
    ppermute x6 -> x10, waiting for transfers between devices: 9.58 us -> 9.18 us  [the longest x8 6.81 us: lon_swap(): return lax.ppermute(value, 'lon', [(i, i ^ step) for i in range(z.n_lon)])]
  transfers between devices with their start and end apart: 12 -> 16, of which waited for: 9 -> 10; matrix products, arithmetic and copies ran while one was open for 2% -> 2% of each run, Pallas kernels for 10% -> 14%
where the time goes in v6:
time: 38.7 us; the launch traced here: 38.2 us
  starting transfers between devices  15.8 us (41%)
  waiting for transfers between devices  10.2 us (26%)
  Pallas kernels  9.86 us (25%)
  other arithmetic  2.06 us (5%)
    ppermute x8, waiting for transfers between devices, lon_swap(): return lax.ppermute(value, 'lon', [(i, i ^ step) for i in range(z.n_lon)])  6.81 us
    pallas_call x11, Pallas kernels, call(): pl.pallas_call(functools.partial(kernel, z), out_shape=[jax.ShapeDtypeStr...  6.72 us
    ppermute x1, starting transfers between devices, local(): m2 = lax.ppermute(m2, 'lat', lat_two)  4.6 us
    ppermute x8, starting transfers between devices, lon_swap(): return lax.ppermute(value, 'lon', [(i, i ^ step) for i in range(z.n_lon)])  4.55 us
    ppermute x2, starting transfers between devices, from_below(): return lax.ppermute(column, 'lev', [(0, 1), (1, 0)])  2.46 us
    ppermute x1, starting transfers between devices, local(): t2 = lax.ppermute(t2, 'lat', lat_two)  1.92 us
    ppermute x1, waiting for transfers between devices, local(): t2 = lax.ppermute(t2, 'lat', lat_two)  1.91 us
    pallas_call x1, Pallas kernels, local(): pl.pallas_call(functools.partial(filter_all, z), out_shape=jax.ShapeDtype...  1.83 us
  transfers between devices with their start and end apart: 16, of which 10 were waited for; matrix products, arithmetic and copies ran while one was open for 2% of the time, Pallas kernels for 14%

profile of v6, /device:TPU:8, one launch (start us, length us, event | category | flops | bytes accessed | tf_op | source)
XLA Modules:
  0.0 38.2 jit_solution(16615882955710600128)
XLA Ops:
  0.0 1.3 %select_maximum_fusion.x.x_in = f32[17,8,1920]{2,1,0:T(8,128)S(1)} fusion(f32[1,8,1800]{2,1,0:T(8,128)} %bitcast.5, f32[16,8,1800]{2,1,0:T(8,128)} %bitcast.4), kind=kLoop, calls=%fused_computation | loop fusion | flops 1044480 | bytes 2023680 | tf_op jit(solution)/shard_map/concatenate | solution.py:735
  1.7 1.6 %collective-permute-start.1 = (f32[8,128]{1,0:T(8,128)S(1)}, f32[8,128]{1,0:T(8,128)S(1)}, u32[]{:S(2)}, u32[]{:S(2)}) collective-permute-start(f32[8,128]{1,0:T(8,128)S(1)} %get-tuple-element.32), channel_id=1, source_target_pairs={{0,24},{8,16},{16,8},{24,0},{1,25},{9,17},{17,9},{25,1},{2,26},{10... | collective-permute-start | bytes 12296 | tf_op jit(solution)/shard_map/ppermute | solution.py:742
  3.7 4.6 %collective-permute-start.3 = (f32[8,6528]{1,0:T(8,128)S(1)}, f32[8,6528]{1,0:T(8,128)S(1)}, u32[]{:S(2)}, u32[]{:S(2)}) collective-permute-start(f32[8,6528]{1,0:T(8,128)S(1)} %get-tuple-element.36), channel_id=1, source_target_pairs={{2,4},{4,2},{3,5},{5,3},{10,12},{12,10},{11,13},{13,11},{18,20},{2... | collective-permute-start | bytes 626696 | tf_op jit(solution)/shard_map/ppermute | solution.py:739
  9.4 1.9 %collective-permute-start.5 = (f32[8,512]{1,0:T(8,128)S(1)}, f32[8,512]{1,0:T(8,128)S(1)}, u32[]{:S(2)}, u32[]{:S(2)}) collective-permute-start(f32[8,512]{1,0:T(8,128)S(1)} %get-tuple-element.38), channel_id=1, source_target_pairs={{2,4},{4,2},{3,5},{5,3},{10,12},{12,10},{11,13},{13,11},{18,20},{2... | collective-permute-start | bytes 49160 | tf_op jit(solution)/shard_map/ppermute | solution.py:752
  11.4 1.3 %row_code.1.code.refs_9_ = s32[16,128]{1,0:T(8,128)} custom-call(s32[16]{0:T(128)} %rows.1, s32[16]{0:T(128)} %counts.1), custom_call_target="tpu_custom_call" | custom-call | tf_op jit(solution)/shard_map/row_code/pallas_call | solution.py:697
  13.2 1.9 %collective-permute-done.5.t2 = f32[8,512]{1,0:T(8,128)S(1)} collective-permute-done((f32[8,512]{1,0:T(8,128)S(1)}, f32[8,512]{1,0:T(8,128)S(1)}, u32[]{:S(2)}, u32[]{:S(2)}) %collective-permute-start.5) | collective-permute-done | bytes 16416 | tf_op jit(solution)/shard_map/ppermute | solution.py:752
  15.3 1.6 %collective-permute-start.6 = (f32[8,2432]{1,0:T(8,128)S(1)}, f32[8,2432]{1,0:T(8,128)S(1)}, u32[]{:S(2)}, u32[]{:S(2)}) collective-permute-start(f32[8,2432]{1,0:T(8,128)S(1)} %get-tuple-element.40), channel_id=1, source_target_pairs={{0,1},{1,0},{2,3},{3,2},{4,5},{5,4},{6,7},{7,6},{8,9},{9,8},{10,11... | collective-permute-start | bytes 233480 | tf_op jit(solution)/shard_map/ppermute | solution.py:712
  16.8 1.0 %first_step.1 = (f32[16,8,1920]{2,1,0:T(8,128)S(1)}, f32[3,8,1920]{2,1,0:T(8,128)S(1)}) custom-call(f32[17,8,1920]{2,1,0:T(8,128)S(1)} %get-tuple-element.33.x, f32[7,8,1920]{2,1,0:T(8,128)S(1)} %get-tuple-element.41.ring, f32[5,16,128]{2,1,0:T(8,128)S(1)} %constant_dynamic-update-slice_fusion.geom), custom_call_target="tpu_custom_call" | custom-call | flops 10000000 | bytes 2682880 | tf_op jit(solution)/shard_map/first_step/pallas_call | solution.py:662
  17.9 0.7 %tile_and_ring_spectra.1.part = f32[88,256]{1,0:T(8,128)S(1)} custom-call(f32[16,8,1920]{2,1,0:T(8,128)S(1)} %get-tuple-element.42.y.refs_4_.state, f32[3,8,1920]{2,1,0:T(8,128)S(1)} %get-tuple-element.43.yring.refs_5_.sring, bf16[1920,256]{1,0:T(8,128)(2,1)S(1)} %copy-done, bf16[1920,256]{1,0:T(8,128)(2,1)S(1)} %copy-done.1, ...), custom_call_target="tpu_custom_call" | custom-call | flops 1000000 | bytes 3232768 | tf_op jit(solution)/shard_map/tile_and_ring_spectra/pallas_call | solution.py:662
  18.7 1.0 %collective-permute-done.6.got = f32[8,2432]{1,0:T(8,128)S(1)} collective-permute-done((f32[8,2432]{1,0:T(8,128)S(1)}, f32[8,2432]{1,0:T(8,128)S(1)}, u32[]{:S(2)}, u32[]{:S(2)}) %collective-permute-start.6) | collective-permute-done | bytes 77856 | tf_op jit(solution)/shard_map/ppermute | solution.py:712
  20.0 0.6 %first_level_spectra.1 = (f32[104,256]{1,0:T(8,128)S(1)}, f32[16,256]{1,0:T(8,128)S(1)}, f32[2,8,1920]{2,1,0:T(8,128)S(1)}, f32[8,1920]{1,0:T(8,128)S(1)}) custom-call(f32[8,1920]{1,0:T(8,128)S(1)} %slice_bitcast_fusion.surface, f32[8,1920]{1,0:T(8,128)S(1)} %get-tuple-element.39.ring_surface, f32[8,2432]{1,0:T(8,128)S(1)} %collective-permute-done.6.got, ...), custom_call_target="tpu_custom_call" | custom-call | flops 1000000 | bytes 2704384 | tf_op jit(solution)/shard_map/first_level_spectra/pallas_call | solution.py:662
  21.2 1.6 %collective-permute-start.10 = (f32[16,256]{1,0:T(8,128)S(1)}, f32[16,256]{1,0:T(8,128)S(1)}, u32[]{:S(2)}, u32[]{:S(2)}) collective-permute-start(f32[16,256]{1,0:T(8,128)S(1)} %get-tuple-element.45), channel_id=1, source_target_pairs={{0,24},{8,16},{16,8},{24,0},{1,25},{9,17},{17,9},{25,1},{2,26},{10... | collective-permute-start | bytes 49160 | tf_op jit(solution)/shard_map/ppermute | solution.py:721
  22.8 2.4 %collective-permute-done.10.refs_3_ = f32[16,256]{1,0:T(8,128)S(1)} collective-permute-done((f32[16,256]{1,0:T(8,128)S(1)}, f32[16,256]{1,0:T(8,128)S(1)}, u32[]{:S(2)}, u32[]{:S(2)}) %collective-permute-start.10) | collective-permute-done | bytes 16416 | tf_op jit(solution)/shard_map/ppermute | solution.py:721
  25.3 0.6 %collective-permute-done.8.refs_1_ = f32[104,256]{1,0:T(8,128)S(1)} collective-permute-done((f32[104,256]{1,0:T(8,128)S(1)}, f32[104,256]{1,0:T(8,128)S(1)}, u32[]{:S(2)}, u32[]{:S(2)}) %collective-permute-start.8) | collective-permute-done | bytes 106528 | tf_op jit(solution)/shard_map/ppermute | solution.py:721
  25.9 1.0 %filter_mass.1 = (f32[8,8,1920]{2,1,0:T(8,128)S(1)}, f32[2,8,1920]{2,1,0:T(8,128)S(1)}, f32[72,256]{1,0:T(8,128)S(1)}, f32[8,2432]{1,0:T(8,128)S(1)}) custom-call(f32[104,256]{1,0:T(8,128)S(1)} %get-tuple-element.44.refs_0_, f32[104,256]{1,0:T(8,128)S(1)} %collective-permute-done.8.refs_1_, f32[16,256]{1,0:T(8,128)S(1)} %collective-permute-done.9.refs_2_, ...), custom_call_target="tpu_custom_call" | custom-call | flops 1000000 | bytes 4154368 | tf_op jit(solution)/shard_map/filter_mass/pallas_call | solution.py:662
  26.9 0.9 %collective-permute-start.11 = (f32[8,2432]{1,0:T(8,128)S(1)}, f32[8,2432]{1,0:T(8,128)S(1)}, u32[]{:S(2)}, u32[]{:S(2)}) collective-permute-start(f32[8,2432]{1,0:T(8,128)S(1)} %get-tuple-element.46), channel_id=1, source_target_pairs={{0,1},{1,0},{2,3},{3,2},{4,5},{5,4},{6,7},{7,6},{8,9},{9,8},{10,11... | collective-permute-start | bytes 233480 | tf_op jit(solution)/shard_map/ppermute | solution.py:712
  27.8 1.5 %second_step.1.y.refs_4_ = f32[16,8,1920]{2,1,0:T(8,128)S(1)} custom-call(f32[16,8,1920]{2,1,0:T(8,128)S(1)} %get-tuple-element.42.y.refs_4_.state, f32[3,8,1920]{2,1,0:T(8,128)S(1)} %get-tuple-element.43.yring.refs_5_.sring, f32[2,8,1920]{2,1,0:T(8,128)S(1)} %get-tuple-element.47.change, f32[8,1920]{1,0:T(8,128)S(1)} %get-tuple-element.48.ring_change, ...), custom_call_target="tpu_custom_call" | custom-call | flops 10000000 | bytes 5038080 | tf_op jit(solution)/shard_map/second_step/pallas_call | solution.py:662
  29.3 0.6 %tile_spectra.1.part = f32[64,256]{1,0:T(8,128)S(1)} custom-call(f32[16,8,1920]{2,1,0:T(8,128)S(1)} %second_step.1.y.refs_4_, bf16[1920,256]{1,0:T(8,128)(2,1)S(1)} %copy-done, bf16[1920,256]{1,0:T(8,128)(2,1)S(1)} %copy-done.1, f32[2,128]{1,0:T(2,128)S(1)} %pad_maximum_fusion.phase.refs_8_, s32[16,128]{1,0:T(8,128)S(1)} %copy-done.2), custom_call_target="tpu_custom_call" | custom-call | flops 1000000 | bytes 3023872 | tf_op jit(solution)/shard_map/tile_spectra/pallas_call | solution.py:662
  30.0 1.2 %collective-permute-done.12.part_got = f32[64,256]{1,0:T(8,128)S(1)} collective-permute-done((f32[64,256]{1,0:T(8,128)S(1)}, f32[64,256]{1,0:T(8,128)S(1)}, u32[]{:S(2)}, u32[]{:S(2)}) %collective-permute-start.12) | collective-permute-done | bytes 65568 | tf_op jit(solution)/shard_map/ppermute | solution.py:721
  31.4 0.6 %second_level_spectra.1 = (f32[72,256]{1,0:T(8,128)S(1)}, f32[8,256]{1,0:T(8,128)S(1)}, f32[2,8,1920]{2,1,0:T(8,128)S(1)}) custom-call(f32[8,1920]{1,0:T(8,128)S(1)} %slice_bitcast_fusion.surface, f32[8,1920]{1,0:T(8,128)S(1)} %get-tuple-element.39.ring_surface, f32[8,2432]{1,0:T(8,128)S(1)} %collective-permute-done.11.got, f32[64,256]{1,0:T(8,128)S(1)} %tile_spectra.1.part, ...), custom_call_target="tpu_custom_call" | custom-call | flops 1000000 | bytes 2552832 | tf_op jit(solution)/shard_map/second_level_spectra/pallas_call | solution.py:662
  32.5 1.6 %collective-permute-start.15 = (f32[8,256]{1,0:T(8,128)S(1)}, f32[8,256]{1,0:T(8,128)S(1)}, u32[]{:S(2)}, u32[]{:S(2)}) collective-permute-start(f32[8,256]{1,0:T(8,128)S(1)} %get-tuple-element.53), channel_id=1, source_target_pairs={{0,24},{8,16},{16,8},{24,0},{1,25},{9,17},{17,9},{25,1},{2,26},{10... | collective-permute-start | bytes 24584 | tf_op jit(solution)/shard_map/ppermute | solution.py:721
  34.2 1.5 %collective-permute-done.15.refs_3_ = f32[8,256]{1,0:T(8,128)S(1)} collective-permute-done((f32[8,256]{1,0:T(8,128)S(1)}, f32[8,256]{1,0:T(8,128)S(1)}, u32[]{:S(2)}, u32[]{:S(2)}) %collective-permute-start.15) | collective-permute-done | bytes 8224 | tf_op jit(solution)/shard_map/ppermute | solution.py:721
  35.6 0.8 %collective-permute-done.13.refs_1_ = f32[72,256]{1,0:T(8,128)S(1)} collective-permute-done((f32[72,256]{1,0:T(8,128)S(1)}, f32[72,256]{1,0:T(8,128)S(1)}, u32[]{:S(2)}, u32[]{:S(2)}) %collective-permute-start.13) | collective-permute-done | bytes 73760 | tf_op jit(solution)/shard_map/ppermute | solution.py:721
  36.4 1.8 %filter_all.1 = f32[4,4,8,1800]{3,2,1,0:T(8,128)} custom-call(f32[72,256]{1,0:T(8,128)S(1)} %get-tuple-element.52.refs_0_, f32[72,256]{1,0:T(8,128)S(1)} %collective-permute-done.13.refs_1_, f32[8,256]{1,0:T(8,128)S(1)} %collective-permute-done.14.refs_2_, f32[8,256]{1,0:T(8,128)S(1)} %collective-permute-done.15.refs_3_, ...), custom_call_target="tpu_custom_call" | custom-call | tf_op jit(solution)/shard_map/filter_all/pallas_call | solution.py:795
  (38 shorter events, 4.1 us)
Async XLA Ops:
  1.6 7.6 %collective-permute-start = (f32[8,128]{1,0:T(8,128)S(1)}, f32[8,128]{1,0:T(8,128)S(1)}, u32[]{:S(2)}, u32[]{:S(2)}) collective-permute-start(f32[8,128]{1,0:T(8,128)S(1)} %get-tuple-element.31), channel_id=1, source_target_pairs={{0,8},{8,0},{16,24},{24,16},{1,9},{9,1},{17,25},{25,17},{2,10},{10... | collective-permute-start | bytes 12296 | tf_op jit(solution)/shard_map/ppermute | solution.py:741
  1.7 7.5 %collective-permute-start.1 = (f32[8,128]{1,0:T(8,128)S(1)}, f32[8,128]{1,0:T(8,128)S(1)}, u32[]{:S(2)}, u32[]{:S(2)}) collective-permute-start(f32[8,128]{1,0:T(8,128)S(1)} %get-tuple-element.32), channel_id=1, source_target_pairs={{0,24},{8,16},{16,8},{24,0},{1,25},{9,17},{17,9},{25,1},{2,26},{10... | collective-permute-start | bytes 12296 | tf_op jit(solution)/shard_map/ppermute | solution.py:742
  3.3 11.8 %collective-permute-start.2 = (f32[8,6528]{1,0:T(8,128)S(1)}, f32[8,6528]{1,0:T(8,128)S(1)}, u32[]{:S(2)}, u32[]{:S(2)}) collective-permute-start(f32[8,6528]{1,0:T(8,128)S(1)} %get-tuple-element.35), channel_id=1, source_target_pairs={{0,2},{2,0},{4,6},{6,4},{1,3},{3,1},{5,7},{7,5},{8,10},{10,8},{12,... | collective-permute-start | bytes 626696 | tf_op jit(solution)/shard_map/ppermute | solution.py:738
  3.7 11.3 %collective-permute-start.3 = (f32[8,6528]{1,0:T(8,128)S(1)}, f32[8,6528]{1,0:T(8,128)S(1)}, u32[]{:S(2)}, u32[]{:S(2)}) collective-permute-start(f32[8,6528]{1,0:T(8,128)S(1)} %get-tuple-element.36), channel_id=1, source_target_pairs={{2,4},{4,2},{3,5},{5,3},{10,12},{12,10},{11,13},{13,11},{18,20},{2... | collective-permute-start | bytes 626696 | tf_op jit(solution)/shard_map/ppermute | solution.py:739
  9.4 3.8 %collective-permute-start.4 = (f32[8,512]{1,0:T(8,128)S(1)}, f32[8,512]{1,0:T(8,128)S(1)}, u32[]{:S(2)}, u32[]{:S(2)}) collective-permute-start(f32[8,512]{1,0:T(8,128)S(1)} %get-tuple-element.37), channel_id=1, source_target_pairs={{0,2},{2,0},{4,6},{6,4},{1,3},{3,1},{5,7},{7,5},{8,10},{10,8},{12,... | collective-permute-start | bytes 49160 | tf_op jit(solution)/shard_map/ppermute | solution.py:751
  9.4 5.6 %collective-permute-start.5 = (f32[8,512]{1,0:T(8,128)S(1)}, f32[8,512]{1,0:T(8,128)S(1)}, u32[]{:S(2)}, u32[]{:S(2)}) collective-permute-start(f32[8,512]{1,0:T(8,128)S(1)} %get-tuple-element.38), channel_id=1, source_target_pairs={{2,4},{4,2},{3,5},{5,3},{10,12},{12,10},{11,13},{13,11},{18,20},{2... | collective-permute-start | bytes 49160 | tf_op jit(solution)/shard_map/ppermute | solution.py:752
  15.1 2.8 %copy-start = (bf16[1920,256]{1,0:T(8,128)(2,1)S(1)}, bf16[1920,256]{1,0:T(8,128)(2,1)}, u32[]{:S(2)}) copy-start(bf16[1920,256]{1,0:T(8,128)(2,1)} %constant.55.clone.wh.refs_6_) | copy-start | bytes 2949124
  15.1 2.8 %copy-start.1 = (bf16[1920,256]{1,0:T(8,128)(2,1)S(1)}, bf16[1920,256]{1,0:T(8,128)(2,1)}, u32[]{:S(2)}) copy-start(bf16[1920,256]{1,0:T(8,128)(2,1)} %constant.56.clone.wl.refs_7_) | copy-start | bytes 2949124
  15.3 4.5 %collective-permute-start.6 = (f32[8,2432]{1,0:T(8,128)S(1)}, f32[8,2432]{1,0:T(8,128)S(1)}, u32[]{:S(2)}, u32[]{:S(2)}) collective-permute-start(f32[8,2432]{1,0:T(8,128)S(1)} %get-tuple-element.40), channel_id=1, source_target_pairs={{0,1},{1,0},{2,3},{3,2},{4,5},{5,4},{6,7},{7,6},{8,9},{9,8},{10,11... | collective-permute-start | bytes 233480 | tf_op jit(solution)/shard_map/ppermute | solution.py:712
  16.8 1.1 %copy-start.2 = (s32[16,128]{1,0:T(8,128)S(1)}, s32[16,128]{1,0:T(8,128)}, u32[]{:S(2)}) copy-start(s32[16,128]{1,0:T(8,128)} %row_code.1.code.refs_9_) | copy-start | bytes 24580
  18.6 1.4 %collective-permute-start.7 = (f32[88,256]{1,0:T(8,128)S(1)}, f32[88,256]{1,0:T(8,128)S(1)}, u32[]{:S(2)}, u32[]{:S(2)}) collective-permute-start(f32[88,256]{1,0:T(8,128)S(1)} %tile_and_ring_spectra.1.part), channel_id=1, source_target_pairs={{0,8},{8,0},{16,24},{24,16},{1,9},{9,1},{17,25},{25,17},{2,10},{10... | collective-permute-start | bytes 270344 | tf_op jit(solution)/shard_map/ppermute | solution.py:721
  20.6 5.3 %collective-permute-start.8 = (f32[104,256]{1,0:T(8,128)S(1)}, f32[104,256]{1,0:T(8,128)S(1)}, u32[]{:S(2)}, u32[]{:S(2)}) collective-permute-start(f32[104,256]{1,0:T(8,128)S(1)} %get-tuple-element.44.refs_0_), channel_id=1, source_target_pairs={{0,16},{8,24},{16,0},{24,8},{1,17},{9,25},{17,1},{25,9},{2,18},{10... | collective-permute-start | bytes 319496 | tf_op jit(solution)/shard_map/ppermute | solution.py:721
  21.2 1.6 %collective-permute-start.9 = (f32[16,256]{1,0:T(8,128)S(1)}, f32[16,256]{1,0:T(8,128)S(1)}, u32[]{:S(2)}, u32[]{:S(2)}) collective-permute-start(f32[16,256]{1,0:T(8,128)S(1)} %get-tuple-element.45), channel_id=1, source_target_pairs={{0,8},{8,0},{16,24},{24,16},{1,9},{9,1},{17,25},{25,17},{2,10},{10... | collective-permute-start | bytes 49160 | tf_op jit(solution)/shard_map/ppermute | solution.py:721
  21.2 4.1 %collective-permute-start.10 = (f32[16,256]{1,0:T(8,128)S(1)}, f32[16,256]{1,0:T(8,128)S(1)}, u32[]{:S(2)}, u32[]{:S(2)}) collective-permute-start(f32[16,256]{1,0:T(8,128)S(1)} %get-tuple-element.45), channel_id=1, source_target_pairs={{0,24},{8,16},{16,8},{24,0},{1,25},{9,17},{17,9},{25,1},{2,26},{10... | collective-permute-start | bytes 49160 | tf_op jit(solution)/shard_map/ppermute | solution.py:721
  26.9 4.5 %collective-permute-start.11 = (f32[8,2432]{1,0:T(8,128)S(1)}, f32[8,2432]{1,0:T(8,128)S(1)}, u32[]{:S(2)}, u32[]{:S(2)}) collective-permute-start(f32[8,2432]{1,0:T(8,128)S(1)} %get-tuple-element.46), channel_id=1, source_target_pairs={{0,1},{1,0},{2,3},{3,2},{4,5},{5,4},{6,7},{7,6},{8,9},{9,8},{10,11... | collective-permute-start | bytes 233480 | tf_op jit(solution)/shard_map/ppermute | solution.py:712
  30.0 1.3 %collective-permute-start.12 = (f32[64,256]{1,0:T(8,128)S(1)}, f32[64,256]{1,0:T(8,128)S(1)}, u32[]{:S(2)}, u32[]{:S(2)}) collective-permute-start(f32[64,256]{1,0:T(8,128)S(1)} %tile_spectra.1.part), channel_id=1, source_target_pairs={{0,8},{8,0},{16,24},{24,16},{1,9},{9,1},{17,25},{25,17},{2,10},{10... | collective-permute-start | bytes 196616 | tf_op jit(solution)/shard_map/ppermute | solution.py:721
  31.9 4.4 %collective-permute-start.13 = (f32[72,256]{1,0:T(8,128)S(1)}, f32[72,256]{1,0:T(8,128)S(1)}, u32[]{:S(2)}, u32[]{:S(2)}) collective-permute-start(f32[72,256]{1,0:T(8,128)S(1)} %get-tuple-element.52.refs_0_), channel_id=1, source_target_pairs={{0,16},{8,24},{16,0},{24,8},{1,17},{9,25},{17,1},{25,9},{2,18},{10... | collective-permute-start | bytes 221192 | tf_op jit(solution)/shard_map/ppermute | solution.py:721
  32.5 1.6 %collective-permute-start.14 = (f32[8,256]{1,0:T(8,128)S(1)}, f32[8,256]{1,0:T(8,128)S(1)}, u32[]{:S(2)}, u32[]{:S(2)}) collective-permute-start(f32[8,256]{1,0:T(8,128)S(1)} %get-tuple-element.53), channel_id=1, source_target_pairs={{0,8},{8,0},{16,24},{24,16},{1,9},{9,1},{17,25},{25,17},{2,10},{10... | collective-permute-start | bytes 24584 | tf_op jit(solution)/shard_map/ppermute | solution.py:721
  32.5 3.1 %collective-permute-start.15 = (f32[8,256]{1,0:T(8,128)S(1)}, f32[8,256]{1,0:T(8,128)S(1)}, u32[]{:S(2)}, u32[]{:S(2)}) collective-permute-start(f32[8,256]{1,0:T(8,128)S(1)} %get-tuple-element.53), channel_id=1, source_target_pairs={{0,24},{8,16},{16,8},{24,0},{1,25},{9,17},{17,9},{25,1},{2,26},{10... | collective-permute-start | bytes 24584 | tf_op jit(solution)/shard_map/ppermute | solution.py:721

commit v7 on v6

--- a/solution.py
+++ b/solution.py
@@ -543,7 +543,7 @@
 
 
 def smooth(modes, wh, wl):
-    return product(modes, wh, wl, ((1,), (1,)))
+    return product(modes, wh, wl, ((1,), (0,)))
 
 
 def filter_mass(z, *refs):
@@ -607,11 +607,11 @@
     modes = local_modes(total_modes(z, parts), phase)
     keep, _ = keeps(z, code)
     high, low = split(jnp.concatenate(tile_modes(z, modes, code, mode_weight(z, keep)), 0))
-    across = ((1,), (1,))
+    across = ((1,), (0,))
     copies = []
     for i, (lo, hi) in enumerate(z.chunks):
         top = min(-(-hi // LANES) * LANES, z.W)
-        w, v = wh[lo:top, :], wl[lo:top, :]
+        w, v = wh[:, lo:top], wl[:, lo:top]
         s = dot(high, w, across) + dot(low, w, across) + dot(high, v, across)
         d = damping(z, keep, top - lo)
         for p in range(4 * L):
@@ -652,9 +652,10 @@
     out[...] = jnp.where(row < z.R, code, ring)
 
 
-def local(z, wave_high, wave_low, fields, surface, filter_rows, keep_counts):
+def local(z, tables, fields, surface, filter_rows, keep_counts):
     L, R, W = z.L, z.R, z.W
     f32 = jnp.float32
+    wave_high, wave_low, back_high, back_low = tables
     vmem = pl.BlockSpec(memory_space=pltpu.VMEM)
 
     def call(kernel, outs, ins, scratch=(), flops=1_000_000, aliases={}):
@@ -763,6 +764,7 @@
         flops=10_000_000,
     )
     waves = [wave_high, wave_low, phase, code]
+    back = [back_high, back_low, phase, code]
     rows = 4 * L * z.slots
     (part,) = call(tile_and_ring_spectra, [(rows + 6 * L, 2 * KMAX)], [y, yring, *waves])
     surface_tile = x[4 * L]
@@ -775,13 +777,13 @@
     ht, htring, uvmodes, msg = call(
         filter_mass,
         [(2 * L, R, W), (2, 2 * L, W), (2 * L * R + 2 * L, 2 * KMAX), (R, W + ring_lanes)],
-        [*parts, y, yring, *waves],
+        [*parts, y, yring, *back],
     )
     got = from_below(msg)
     (y,) = call(
         second_step,
         [(4 * L, R, W)],
-        [y, yring, change, ring_change, uvmodes, ht, htring, geom, wave_high, wave_low, code],
+        [y, yring, change, ring_change, uvmodes, ht, htring, geom, back_high, back_low, code],
         [(2 * L, R, W), (2 * L, W), (2 * L, W)],
         flops=10_000_000,
     )
@@ -803,7 +805,7 @@
         ],
         compiler_params=pltpu.CompilerParams(vmem_limit_bytes=VMEM_LIMIT),
         name="filter_all",
-    )(*parts, y, change, *waves)
+    )(*parts, y, change, *back)
 
 
 def wave_tables(z):
@@ -820,10 +822,11 @@
     def run(fields, surface, filter_rows, keep_counts):
         z = Sizes(mesh, fields.shape, filter_rows.shape[0])
         high, low = wave_tables(z)
+        tables = [high, low, np.ascontiguousarray(high.T), np.ascontiguousarray(low.T)]
 
         def body(fields, surface, filter_rows, keep_counts):
             return local(
-                z, jnp.asarray(high), jnp.asarray(low), fields, surface, filter_rows, keep_counts
+                z, [jnp.asarray(t) for t in tables], fields, surface, filter_rows, keep_counts
             )
 
         spec = P(None, "lev", "lat", "lon")

time: 38.7 us -> 37.9 us (0.979)
  Pallas kernels: 9.86 us -> 8.82 us
    pallas_call x11, Pallas kernels: 6.72 us -> 6.07 us  [call(): pl.pallas_call(functools.partial(kernel, z), out_shape=[jax.ShapeDtypeStr...]
    pallas_call x1, Pallas kernels: 1.83 us -> 1.43 us  [local(): pl.pallas_call(functools.partial(filter_all, z), out_shape=jax.ShapeDtype...]
where the time goes in v7:
time: 37.9 us; the launch traced here: 37.5 us
  starting transfers between devices  15.8 us (42%)
  waiting for transfers between devices  10.5 us (28%)
  Pallas kernels  8.82 us (23%)
  other arithmetic  2.06 us (5%)
    ppermute x8, waiting for transfers between devices, lon_swap(): return lax.ppermute(value, 'lon', [(i, i ^ step) for i in range(z.n_lon)])  6.81 us
    pallas_call x11, Pallas kernels, call(): pl.pallas_call(functools.partial(kernel, z), out_shape=[jax.ShapeDtypeStr...  6.07 us
    ppermute x1, starting transfers between devices, local(): m2 = lax.ppermute(m2, 'lat', lat_two)  4.6 us
    ppermute x8, starting transfers between devices, lon_swap(): return lax.ppermute(value, 'lon', [(i, i ^ step) for i in range(z.n_lon)])  4.55 us
    ppermute x2, starting transfers between devices, from_below(): return lax.ppermute(column, 'lev', [(0, 1), (1, 0)])  2.46 us
    ppermute x1, starting transfers between devices, local(): t2 = lax.ppermute(t2, 'lat', lat_two)  1.92 us
    ppermute x1, waiting for transfers between devices, local(): t2 = lax.ppermute(t2, 'lat', lat_two)  1.91 us
    ppermute x1, starting transfers between devices, local(): e2 = lax.ppermute(e2, 'lon', lon_two)  1.64 us
  transfers between devices with their start and end apart: 16, of which 10 were waited for; matrix products, arithmetic and copies ran while one was open for 2% of the time, Pallas kernels for 14%

profile of v7, /device:TPU:8, one launch (start us, length us, event | category | flops | bytes accessed | tf_op | source)
XLA Modules:
  0.0 37.5 jit_solution(753763313429487638)
XLA Ops:
  0.0 1.3 %select_maximum_fusion.x.x_in = f32[17,8,1920]{2,1,0:T(8,128)S(1)} fusion(f32[1,8,1800]{2,1,0:T(8,128)} %bitcast.5, f32[16,8,1800]{2,1,0:T(8,128)} %bitcast.4), kind=kLoop, calls=%fused_computation | loop fusion | flops 1044480 | bytes 2023680 | tf_op jit(solution)/shard_map/concatenate | solution.py:736
  1.7 1.6 %collective-permute-start.1 = (f32[8,128]{1,0:T(8,128)S(1)}, f32[8,128]{1,0:T(8,128)S(1)}, u32[]{:S(2)}, u32[]{:S(2)}) collective-permute-start(f32[8,128]{1,0:T(8,128)S(1)} %get-tuple-element.32), channel_id=1, source_target_pairs={{0,24},{8,16},{16,8},{24,0},{1,25},{9,17},{17,9},{25,1},{2,26},{10... | collective-permute-start | bytes 12296 | tf_op jit(solution)/shard_map/ppermute | solution.py:743
  3.7 4.6 %collective-permute-start.3 = (f32[8,6528]{1,0:T(8,128)S(1)}, f32[8,6528]{1,0:T(8,128)S(1)}, u32[]{:S(2)}, u32[]{:S(2)}) collective-permute-start(f32[8,6528]{1,0:T(8,128)S(1)} %get-tuple-element.36), channel_id=1, source_target_pairs={{2,4},{4,2},{3,5},{5,3},{10,12},{12,10},{11,13},{13,11},{18,20},{2... | collective-permute-start | bytes 626696 | tf_op jit(solution)/shard_map/ppermute | solution.py:740
  9.4 1.9 %collective-permute-start.5 = (f32[8,512]{1,0:T(8,128)S(1)}, f32[8,512]{1,0:T(8,128)S(1)}, u32[]{:S(2)}, u32[]{:S(2)}) collective-permute-start(f32[8,512]{1,0:T(8,128)S(1)} %get-tuple-element.38), channel_id=1, source_target_pairs={{2,4},{4,2},{3,5},{5,3},{10,12},{12,10},{11,13},{13,11},{18,20},{2... | collective-permute-start | bytes 49160 | tf_op jit(solution)/shard_map/ppermute | solution.py:753
  11.4 1.3 %row_code.1.code.refs_9_ = s32[16,128]{1,0:T(8,128)} custom-call(s32[16]{0:T(128)} %rows.1, s32[16]{0:T(128)} %counts.1), custom_call_target="tpu_custom_call" | custom-call | tf_op jit(solution)/shard_map/row_code/pallas_call | solution.py:698
  13.2 1.9 %collective-permute-done.5.t2 = f32[8,512]{1,0:T(8,128)S(1)} collective-permute-done((f32[8,512]{1,0:T(8,128)S(1)}, f32[8,512]{1,0:T(8,128)S(1)}, u32[]{:S(2)}, u32[]{:S(2)}) %collective-permute-start.5) | collective-permute-done | bytes 16416 | tf_op jit(solution)/shard_map/ppermute | solution.py:753
  15.3 1.6 %collective-permute-start.6 = (f32[8,2432]{1,0:T(8,128)S(1)}, f32[8,2432]{1,0:T(8,128)S(1)}, u32[]{:S(2)}, u32[]{:S(2)}) collective-permute-start(f32[8,2432]{1,0:T(8,128)S(1)} %get-tuple-element.40), channel_id=1, source_target_pairs={{0,1},{1,0},{2,3},{3,2},{4,5},{5,4},{6,7},{7,6},{8,9},{9,8},{10,11... | collective-permute-start | bytes 233480 | tf_op jit(solution)/shard_map/ppermute | solution.py:713
  16.8 1.0 %first_step.1 = (f32[16,8,1920]{2,1,0:T(8,128)S(1)}, f32[3,8,1920]{2,1,0:T(8,128)S(1)}) custom-call(f32[17,8,1920]{2,1,0:T(8,128)S(1)} %get-tuple-element.33.x, f32[7,8,1920]{2,1,0:T(8,128)S(1)} %get-tuple-element.41.ring, f32[5,16,128]{2,1,0:T(8,128)S(1)} %constant_dynamic-update-slice_fusion.geom), custom_call_target="tpu_custom_call" | custom-call | flops 10000000 | bytes 2682880 | tf_op jit(solution)/shard_map/first_step/pallas_call | solution.py:663
  17.9 0.7 %tile_and_ring_spectra.1.part = f32[88,256]{1,0:T(8,128)S(1)} custom-call(f32[16,8,1920]{2,1,0:T(8,128)S(1)} %get-tuple-element.42.y.refs_4_.state, f32[3,8,1920]{2,1,0:T(8,128)S(1)} %get-tuple-element.43.yring.refs_5_.sring, bf16[1920,256]{1,0:T(8,128)(2,1)S(1)} %copy-done, bf16[1920,256]{1,0:T(8,128)(2,1)S(1)} %copy-done.1, ...), custom_call_target="tpu_custom_call" | custom-call | flops 1000000 | bytes 3232768 | tf_op jit(solution)/shard_map/tile_and_ring_spectra/pallas_call | solution.py:663
  18.7 1.0 %collective-permute-done.6.got = f32[8,2432]{1,0:T(8,128)S(1)} collective-permute-done((f32[8,2432]{1,0:T(8,128)S(1)}, f32[8,2432]{1,0:T(8,128)S(1)}, u32[]{:S(2)}, u32[]{:S(2)}) %collective-permute-start.6) | collective-permute-done | bytes 77856 | tf_op jit(solution)/shard_map/ppermute | solution.py:713
  20.0 0.6 %first_level_spectra.1 = (f32[104,256]{1,0:T(8,128)S(1)}, f32[16,256]{1,0:T(8,128)S(1)}, f32[2,8,1920]{2,1,0:T(8,128)S(1)}, f32[8,1920]{1,0:T(8,128)S(1)}) custom-call(f32[8,1920]{1,0:T(8,128)S(1)} %slice_bitcast_fusion.surface, f32[8,1920]{1,0:T(8,128)S(1)} %get-tuple-element.39.ring_surface, f32[8,2432]{1,0:T(8,128)S(1)} %collective-permute-done.6.got, ...), custom_call_target="tpu_custom_call" | custom-call | flops 1000000 | bytes 2704384 | tf_op jit(solution)/shard_map/first_level_spectra/pallas_call | solution.py:663
  21.2 1.6 %collective-permute-start.10 = (f32[16,256]{1,0:T(8,128)S(1)}, f32[16,256]{1,0:T(8,128)S(1)}, u32[]{:S(2)}, u32[]{:S(2)}) collective-permute-start(f32[16,256]{1,0:T(8,128)S(1)} %get-tuple-element.45), channel_id=1, source_target_pairs={{0,24},{8,16},{16,8},{24,0},{1,25},{9,17},{17,9},{25,1},{2,26},{10... | collective-permute-start | bytes 49160 | tf_op jit(solution)/shard_map/ppermute | solution.py:722
  22.8 2.4 %collective-permute-done.10.refs_3_ = f32[16,256]{1,0:T(8,128)S(1)} collective-permute-done((f32[16,256]{1,0:T(8,128)S(1)}, f32[16,256]{1,0:T(8,128)S(1)}, u32[]{:S(2)}, u32[]{:S(2)}) %collective-permute-start.10) | collective-permute-done | bytes 16416 | tf_op jit(solution)/shard_map/ppermute | solution.py:722
  25.3 0.6 %collective-permute-done.8.refs_1_ = f32[104,256]{1,0:T(8,128)S(1)} collective-permute-done((f32[104,256]{1,0:T(8,128)S(1)}, f32[104,256]{1,0:T(8,128)S(1)}, u32[]{:S(2)}, u32[]{:S(2)}) %collective-permute-start.8) | collective-permute-done | bytes 106528 | tf_op jit(solution)/shard_map/ppermute | solution.py:722
  25.9 0.6 %filter_mass.1 = (f32[8,8,1920]{2,1,0:T(8,128)S(1)}, f32[2,8,1920]{2,1,0:T(8,128)S(1)}, f32[72,256]{1,0:T(8,128)S(1)}, f32[8,2432]{1,0:T(8,128)S(1)}) custom-call(f32[104,256]{1,0:T(8,128)S(1)} %get-tuple-element.44.refs_0_, f32[104,256]{1,0:T(8,128)S(1)} %collective-permute-done.8.refs_1_, f32[16,256]{1,0:T(8,128)S(1)} %collective-permute-done.9.refs_2_, ...), custom_call_target="tpu_custom_call" | custom-call | flops 1000000 | bytes 4154368 | tf_op jit(solution)/shard_map/filter_mass/pallas_call | solution.py:663
  26.5 0.9 %collective-permute-start.11 = (f32[8,2432]{1,0:T(8,128)S(1)}, f32[8,2432]{1,0:T(8,128)S(1)}, u32[]{:S(2)}, u32[]{:S(2)}) collective-permute-start(f32[8,2432]{1,0:T(8,128)S(1)} %get-tuple-element.46), channel_id=1, source_target_pairs={{0,1},{1,0},{2,3},{3,2},{4,5},{5,4},{6,7},{7,6},{8,9},{9,8},{10,11... | collective-permute-start | bytes 233480 | tf_op jit(solution)/shard_map/ppermute | solution.py:713
  27.4 1.3 %second_step.1.y.refs_4_ = f32[16,8,1920]{2,1,0:T(8,128)S(1)} custom-call(f32[16,8,1920]{2,1,0:T(8,128)S(1)} %get-tuple-element.42.y.refs_4_.state, f32[3,8,1920]{2,1,0:T(8,128)S(1)} %get-tuple-element.43.yring.refs_5_.sring, f32[2,8,1920]{2,1,0:T(8,128)S(1)} %get-tuple-element.47.change, f32[8,1920]{1,0:T(8,128)S(1)} %get-tuple-element.48.ring_change, ...), custom_call_target="tpu_custom_call" | custom-call | flops 10000000 | bytes 5038080 | tf_op jit(solution)/shard_map/second_step/pallas_call | solution.py:663
  28.7 0.6 %tile_spectra.1.part = f32[64,256]{1,0:T(8,128)S(1)} custom-call(f32[16,8,1920]{2,1,0:T(8,128)S(1)} %second_step.1.y.refs_4_, bf16[1920,256]{1,0:T(8,128)(2,1)S(1)} %copy-done, bf16[1920,256]{1,0:T(8,128)(2,1)S(1)} %copy-done.1, f32[2,128]{1,0:T(2,128)S(1)} %pad_maximum_fusion.phase.refs_8_, s32[16,128]{1,0:T(8,128)S(1)} %copy-done.4), custom_call_target="tpu_custom_call" | custom-call | flops 1000000 | bytes 3023872 | tf_op jit(solution)/shard_map/tile_spectra/pallas_call | solution.py:663
  29.4 1.2 %collective-permute-done.12.part_got = f32[64,256]{1,0:T(8,128)S(1)} collective-permute-done((f32[64,256]{1,0:T(8,128)S(1)}, f32[64,256]{1,0:T(8,128)S(1)}, u32[]{:S(2)}, u32[]{:S(2)}) %collective-permute-start.12) | collective-permute-done | bytes 65568 | tf_op jit(solution)/shard_map/ppermute | solution.py:722
  31.0 0.6 %second_level_spectra.1 = (f32[72,256]{1,0:T(8,128)S(1)}, f32[8,256]{1,0:T(8,128)S(1)}, f32[2,8,1920]{2,1,0:T(8,128)S(1)}) custom-call(f32[8,1920]{1,0:T(8,128)S(1)} %slice_bitcast_fusion.surface, f32[8,1920]{1,0:T(8,128)S(1)} %get-tuple-element.39.ring_surface, f32[8,2432]{1,0:T(8,128)S(1)} %collective-permute-done.11.got, f32[64,256]{1,0:T(8,128)S(1)} %tile_spectra.1.part, ...), custom_call_target="tpu_custom_call" | custom-call | flops 1000000 | bytes 2552832 | tf_op jit(solution)/shard_map/second_level_spectra/pallas_call | solution.py:663
  32.2 1.6 %collective-permute-start.15 = (f32[8,256]{1,0:T(8,128)S(1)}, f32[8,256]{1,0:T(8,128)S(1)}, u32[]{:S(2)}, u32[]{:S(2)}) collective-permute-start(f32[8,256]{1,0:T(8,128)S(1)} %get-tuple-element.53), channel_id=1, source_target_pairs={{0,24},{8,16},{16,8},{24,0},{1,25},{9,17},{17,9},{25,1},{2,26},{10... | collective-permute-start | bytes 24584 | tf_op jit(solution)/shard_map/ppermute | solution.py:722
  33.8 1.5 %collective-permute-done.15.refs_3_ = f32[8,256]{1,0:T(8,128)S(1)} collective-permute-done((f32[8,256]{1,0:T(8,128)S(1)}, f32[8,256]{1,0:T(8,128)S(1)}, u32[]{:S(2)}, u32[]{:S(2)}) %collective-permute-start.15) | collective-permute-done | bytes 8224 | tf_op jit(solution)/shard_map/ppermute | solution.py:722
  35.3 0.8 %collective-permute-done.13.refs_1_ = f32[72,256]{1,0:T(8,128)S(1)} collective-permute-done((f32[72,256]{1,0:T(8,128)S(1)}, f32[72,256]{1,0:T(8,128)S(1)}, u32[]{:S(2)}, u32[]{:S(2)}) %collective-permute-start.13) | collective-permute-done | bytes 73760 | tf_op jit(solution)/shard_map/ppermute | solution.py:722
  36.0 1.4 %filter_all.1 = f32[4,4,8,1800]{3,2,1,0:T(8,128)} custom-call(f32[72,256]{1,0:T(8,128)S(1)} %get-tuple-element.52.refs_0_, f32[72,256]{1,0:T(8,128)S(1)} %collective-permute-done.13.refs_1_, f32[8,256]{1,0:T(8,128)S(1)} %collective-permute-done.14.refs_2_, f32[8,256]{1,0:T(8,128)S(1)} %collective-permute-done.15.refs_3_, ...), custom_call_target="tpu_custom_call" | custom-call | tf_op jit(solution)/shard_map/filter_all/pallas_call | solution.py:797
  (42 shorter events, 4.4 us)
Async XLA Ops:
  1.6 7.6 %collective-permute-start = (f32[8,128]{1,0:T(8,128)S(1)}, f32[8,128]{1,0:T(8,128)S(1)}, u32[]{:S(2)}, u32[]{:S(2)}) collective-permute-start(f32[8,128]{1,0:T(8,128)S(1)} %get-tuple-element.31), channel_id=1, source_target_pairs={{0,8},{8,0},{16,24},{24,16},{1,9},{9,1},{17,25},{25,17},{2,10},{10... | collective-permute-start | bytes 12296 | tf_op jit(solution)/shard_map/ppermute | solution.py:742
  1.7 7.5 %collective-permute-start.1 = (f32[8,128]{1,0:T(8,128)S(1)}, f32[8,128]{1,0:T(8,128)S(1)}, u32[]{:S(2)}, u32[]{:S(2)}) collective-permute-start(f32[8,128]{1,0:T(8,128)S(1)} %get-tuple-element.32), channel_id=1, source_target_pairs={{0,24},{8,16},{16,8},{24,0},{1,25},{9,17},{17,9},{25,1},{2,26},{10... | collective-permute-start | bytes 12296 | tf_op jit(solution)/shard_map/ppermute | solution.py:743
  3.3 11.8 %collective-permute-start.2 = (f32[8,6528]{1,0:T(8,128)S(1)}, f32[8,6528]{1,0:T(8,128)S(1)}, u32[]{:S(2)}, u32[]{:S(2)}) collective-permute-start(f32[8,6528]{1,0:T(8,128)S(1)} %get-tuple-element.35), channel_id=1, source_target_pairs={{0,2},{2,0},{4,6},{6,4},{1,3},{3,1},{5,7},{7,5},{8,10},{10,8},{12,... | collective-permute-start | bytes 626696 | tf_op jit(solution)/shard_map/ppermute | solution.py:739
  3.7 11.3 %collective-permute-start.3 = (f32[8,6528]{1,0:T(8,128)S(1)}, f32[8,6528]{1,0:T(8,128)S(1)}, u32[]{:S(2)}, u32[]{:S(2)}) collective-permute-start(f32[8,6528]{1,0:T(8,128)S(1)} %get-tuple-element.36), channel_id=1, source_target_pairs={{2,4},{4,2},{3,5},{5,3},{10,12},{12,10},{11,13},{13,11},{18,20},{2... | collective-permute-start | bytes 626696 | tf_op jit(solution)/shard_map/ppermute | solution.py:740
  9.4 3.8 %collective-permute-start.4 = (f32[8,512]{1,0:T(8,128)S(1)}, f32[8,512]{1,0:T(8,128)S(1)}, u32[]{:S(2)}, u32[]{:S(2)}) collective-permute-start(f32[8,512]{1,0:T(8,128)S(1)} %get-tuple-element.37), channel_id=1, source_target_pairs={{0,2},{2,0},{4,6},{6,4},{1,3},{3,1},{5,7},{7,5},{8,10},{10,8},{12,... | collective-permute-start | bytes 49160 | tf_op jit(solution)/shard_map/ppermute | solution.py:752
  9.4 5.6 %collective-permute-start.5 = (f32[8,512]{1,0:T(8,128)S(1)}, f32[8,512]{1,0:T(8,128)S(1)}, u32[]{:S(2)}, u32[]{:S(2)}) collective-permute-start(f32[8,512]{1,0:T(8,128)S(1)} %get-tuple-element.38), channel_id=1, source_target_pairs={{2,4},{4,2},{3,5},{5,3},{10,12},{12,10},{11,13},{13,11},{18,20},{2... | collective-permute-start | bytes 49160 | tf_op jit(solution)/shard_map/ppermute | solution.py:753
  15.1 2.8 %copy-start = (bf16[1920,256]{1,0:T(8,128)(2,1)S(1)}, bf16[1920,256]{1,0:T(8,128)(2,1)}, u32[]{:S(2)}) copy-start(bf16[1920,256]{1,0:T(8,128)(2,1)} %constant.59.clone.wh) | copy-start | bytes 2949124
  15.1 2.8 %copy-start.1 = (bf16[1920,256]{1,0:T(8,128)(2,1)S(1)}, bf16[1920,256]{1,0:T(8,128)(2,1)}, u32[]{:S(2)}) copy-start(bf16[1920,256]{1,0:T(8,128)(2,1)} %constant.60.clone.wl) | copy-start | bytes 2949124
  15.3 4.5 %collective-permute-start.6 = (f32[8,2432]{1,0:T(8,128)S(1)}, f32[8,2432]{1,0:T(8,128)S(1)}, u32[]{:S(2)}, u32[]{:S(2)}) collective-permute-start(f32[8,2432]{1,0:T(8,128)S(1)} %get-tuple-element.40), channel_id=1, source_target_pairs={{0,1},{1,0},{2,3},{3,2},{4,5},{5,4},{6,7},{7,6},{8,9},{9,8},{10,11... | collective-permute-start | bytes 233480 | tf_op jit(solution)/shard_map/ppermute | solution.py:713
  16.8 1.1 %copy-start.4 = (s32[16,128]{1,0:T(8,128)S(1)}, s32[16,128]{1,0:T(8,128)}, u32[]{:S(2)}) copy-start(s32[16,128]{1,0:T(8,128)} %row_code.1.code.refs_9_) | copy-start | bytes 24580
  18.6 1.4 %collective-permute-start.7 = (f32[88,256]{1,0:T(8,128)S(1)}, f32[88,256]{1,0:T(8,128)S(1)}, u32[]{:S(2)}, u32[]{:S(2)}) collective-permute-start(f32[88,256]{1,0:T(8,128)S(1)} %tile_and_ring_spectra.1.part), channel_id=1, source_target_pairs={{0,8},{8,0},{16,24},{24,16},{1,9},{9,1},{17,25},{25,17},{2,10},{10... | collective-permute-start | bytes 270344 | tf_op jit(solution)/shard_map/ppermute | solution.py:722
  20.0 5.9 %copy-start.2 = (bf16[256,1920]{1,0:T(8,128)(2,1)S(1)}, bf16[256,1920]{1,0:T(8,128)(2,1)}, u32[]{:S(2)}) copy-start(bf16[256,1920]{1,0:T(8,128)(2,1)} %constant.61.clone.refs_6_.wh) | copy-start | bytes 2949124
  20.0 5.9 %copy-start.3 = (bf16[256,1920]{1,0:T(8,128)(2,1)S(1)}, bf16[256,1920]{1,0:T(8,128)(2,1)}, u32[]{:S(2)}) copy-start(bf16[256,1920]{1,0:T(8,128)(2,1)} %constant.62.clone.refs_7_.wl) | copy-start | bytes 2949124
  20.6 5.3 %collective-permute-start.8 = (f32[104,256]{1,0:T(8,128)S(1)}, f32[104,256]{1,0:T(8,128)S(1)}, u32[]{:S(2)}, u32[]{:S(2)}) collective-permute-start(f32[104,256]{1,0:T(8,128)S(1)} %get-tuple-element.44.refs_0_), channel_id=1, source_target_pairs={{0,16},{8,24},{16,0},{24,8},{1,17},{9,25},{17,1},{25,9},{2,18},{10... | collective-permute-start | bytes 319496 | tf_op jit(solution)/shard_map/ppermute | solution.py:722
  21.2 1.6 %collective-permute-start.9 = (f32[16,256]{1,0:T(8,128)S(1)}, f32[16,256]{1,0:T(8,128)S(1)}, u32[]{:S(2)}, u32[]{:S(2)}) collective-permute-start(f32[16,256]{1,0:T(8,128)S(1)} %get-tuple-element.45), channel_id=1, source_target_pairs={{0,8},{8,0},{16,24},{24,16},{1,9},{9,1},{17,25},{25,17},{2,10},{10... | collective-permute-start | bytes 49160 | tf_op jit(solution)/shard_map/ppermute | solution.py:722
  21.2 4.1 %collective-permute-start.10 = (f32[16,256]{1,0:T(8,128)S(1)}, f32[16,256]{1,0:T(8,128)S(1)}, u32[]{:S(2)}, u32[]{:S(2)}) collective-permute-start(f32[16,256]{1,0:T(8,128)S(1)} %get-tuple-element.45), channel_id=1, source_target_pairs={{0,24},{8,16},{16,8},{24,0},{1,25},{9,17},{17,9},{25,1},{2,26},{10... | collective-permute-start | bytes 49160 | tf_op jit(solution)/shard_map/ppermute | solution.py:722
  26.5 4.5 %collective-permute-start.11 = (f32[8,2432]{1,0:T(8,128)S(1)}, f32[8,2432]{1,0:T(8,128)S(1)}, u32[]{:S(2)}, u32[]{:S(2)}) collective-permute-start(f32[8,2432]{1,0:T(8,128)S(1)} %get-tuple-element.46), channel_id=1, source_target_pairs={{0,1},{1,0},{2,3},{3,2},{4,5},{5,4},{6,7},{7,6},{8,9},{9,8},{10,11... | collective-permute-start | bytes 233480 | tf_op jit(solution)/shard_map/ppermute | solution.py:713
  29.3 1.3 %collective-permute-start.12 = (f32[64,256]{1,0:T(8,128)S(1)}, f32[64,256]{1,0:T(8,128)S(1)}, u32[]{:S(2)}, u32[]{:S(2)}) collective-permute-start(f32[64,256]{1,0:T(8,128)S(1)} %tile_spectra.1.part), channel_id=1, source_target_pairs={{0,8},{8,0},{16,24},{24,16},{1,9},{9,1},{17,25},{25,17},{2,10},{10... | collective-permute-start | bytes 196616 | tf_op jit(solution)/shard_map/ppermute | solution.py:722
  31.6 4.4 %collective-permute-start.13 = (f32[72,256]{1,0:T(8,128)S(1)}, f32[72,256]{1,0:T(8,128)S(1)}, u32[]{:S(2)}, u32[]{:S(2)}) collective-permute-start(f32[72,256]{1,0:T(8,128)S(1)} %get-tuple-element.52.refs_0_), channel_id=1, source_target_pairs={{0,16},{8,24},{16,0},{24,8},{1,17},{9,25},{17,1},{25,9},{2,18},{10... | collective-permute-start | bytes 221192 | tf_op jit(solution)/shard_map/ppermute | solution.py:722
  32.2 1.6 %collective-permute-start.14 = (f32[8,256]{1,0:T(8,128)S(1)}, f32[8,256]{1,0:T(8,128)S(1)}, u32[]{:S(2)}, u32[]{:S(2)}) collective-permute-start(f32[8,256]{1,0:T(8,128)S(1)} %get-tuple-element.53), channel_id=1, source_target_pairs={{0,8},{8,0},{16,24},{24,16},{1,9},{9,1},{17,25},{25,17},{2,10},{10... | collective-permute-start | bytes 24584 | tf_op jit(solution)/shard_map/ppermute | solution.py:722
  32.2 3.1 %collective-permute-start.15 = (f32[8,256]{1,0:T(8,128)S(1)}, f32[8,256]{1,0:T(8,128)S(1)}, u32[]{:S(2)}, u32[]{:S(2)}) collective-permute-start(f32[8,256]{1,0:T(8,128)S(1)} %get-tuple-element.53), channel_id=1, source_target_pairs={{0,24},{8,16},{16,8},{24,0},{1,25},{9,17},{17,9},{25,1},{2,26},{10... | collective-permute-start | bytes 24584 | tf_op jit(solution)/shard_map/ppermute | solution.py:722

commit v8 on v7

--- a/solution.py
+++ b/solution.py
@@ -76,7 +76,7 @@
         whole = self.base // LANES
         self.fold = -(-whole // 2)
         self.lat_lanes = 3 * self.base + (self.fold + -(-whole // self.R)) * LANES
-        width = -(-self.base // LANES // 3) * LANES if self.base else self.W
+        width = -(-self.base // LANES // 4) * LANES if self.base else self.W
         cuts = [c for c in range(0, self.base + 1, width)] if self.base else [0]
         if self.C - cuts[-1] <= LANES and len(cuts) > 1:
             cuts.pop()
@@ -209,37 +209,57 @@
     return south, north
 
 
-def halo_rows(z, sums, r1, r2, t1, t2, ring, ring_surface, msg):
+def unfold(z, r1, r2, ring, ring_surface):
     lat_even = lax.axis_index("lat") % 2 == 0
-    L, B, T = z.L, z.base, z.W - z.base
+    L, B = z.L, z.base
     fold = z.fold * LANES
-    msg[:, 0 : z.W] = sums[...]
-    msg[:, z.W :] = jnp.zeros((z.R, 2 * z.extra * LANES), jnp.float32)
-
-    def place(d, source, tail):
+
+    def place(d, source):
         here = slice(d * L, (d + 1) * L)
-        for k in range(7):
+        for k in range(6):
             at = (k % 2) * L
-            if k < 6:
-                ring[k, here, 0:B] = source[at : at + L, k // 2 * B : (k // 2 + 1) * B]
-            ring[k, here, B:] = tail[at : at + L, k // 2 * T : (k // 2 + 1) * T]
+            ring[k, here, 0:B] = source[at : at + L, k // 2 * B : (k // 2 + 1) * B]
         ring[6, here, 0:fold] = source[0:L, 3 * B : 3 * B + fold]
         ring[6, here, fold:B] = source[L : 2 * L, 3 * B : 4 * B - fold]
         for t in range(B // LANES):
             at = 3 * B + fold + t // z.R * LANES
             part = source[t % z.R : t % z.R + 1, at : at + LANES]
             ring_surface[here, t * LANES : (t + 1) * LANES] = jnp.broadcast_to(part, (L, LANES))
-        ring_surface[here, B:] = tail[L : 2 * L, 3 * T :]
 
     @pl.when(lat_even)
     def _():
-        place(0, r2, t2)
-        place(1, r1, t1)
+        place(0, r2)
+        place(1, r1)
 
     @pl.when(jnp.logical_not(lat_even))
     def _():
-        place(0, r1, t1)
-        place(1, r2, t2)
+        place(0, r1)
+        place(1, r2)
+
+
+def halo_rows(z, ring_in, surface_in, sums, t1, t2, ring, ring_surface, msg):
+    del ring_in, surface_in
+    lat_even = lax.axis_index("lat") % 2 == 0
+    L, B, T = z.L, z.base, z.W - z.base
+    msg[:, 0 : z.W] = sums[...]
+    msg[:, z.W :] = jnp.zeros((z.R, 2 * z.extra * LANES), jnp.float32)
+
+    def place(d, tail):
+        here = slice(d * L, (d + 1) * L)
+        for k in range(7):
+            at = (k % 2) * L
+            ring[k, here, B:] = tail[at : at + L, k // 2 * T : (k // 2 + 1) * T]
+        ring_surface[here, B:] = tail[L : 2 * L, 3 * T :]
+
+    @pl.when(lat_even)
+    def _():
+        place(0, t2)
+        place(1, t1)
+
+    @pl.when(jnp.logical_not(lat_even))
+    def _():
+        place(0, t1)
+        place(1, t2)
 
     south, north = ring_sum(z, layer_weight(ring[2], ring[3]))
     put_ring_sums(z, msg.at[:, z.W :], south, north)
@@ -366,18 +386,16 @@
     return surface + live * below, rows[0], rows[1]
 
 
-def split(x):
-    high = x.astype(jnp.bfloat16)
-    return high, (x - high.astype(jnp.float32)).astype(jnp.bfloat16)
-
-
 def dot(a, b, dims):
     return lax.dot_general(a, b, (dims, ((), ())), preferred_element_type=jnp.float32)
 
 
 def product(x, wh, wl, dims):
-    high, low = split(x)
-    return dot(high, wh[...], dims) + dot(low, wh[...], dims) + dot(high, wl[...], dims)
+    high = x.astype(jnp.bfloat16)
+    wide = high.astype(jnp.float32)
+    both = dot(jnp.concatenate([wide, x - wide], 0).astype(jnp.bfloat16), wh[...], dims)
+    m = x.shape[0]
+    return both[0:m] + both[m:] + dot(high, wl[...], dims)
 
 
 def masked(z, x):
@@ -606,13 +624,18 @@
     L = z.L
     modes = local_modes(total_modes(z, parts), phase)
     keep, _ = keeps(z, code)
-    high, low = split(jnp.concatenate(tile_modes(z, modes, code, mode_weight(z, keep)), 0))
+    modes = jnp.concatenate(tile_modes(z, modes, code, mode_weight(z, keep)), 0)
+    high = modes.astype(jnp.bfloat16)
+    wide_high = high.astype(jnp.float32)
+    both = jnp.concatenate([wide_high, modes - wide_high], 0).astype(jnp.bfloat16)
+    m = modes.shape[0]
     across = ((1,), (0,))
     copies = []
     for i, (lo, hi) in enumerate(z.chunks):
         top = min(-(-hi // LANES) * LANES, z.W)
         w, v = wh[:, lo:top], wl[:, lo:top]
-        s = dot(high, w, across) + dot(low, w, across) + dot(high, v, across)
+        s = dot(both, w, across)
+        s = s[0:m] + s[m:] + dot(high, v, across)
         d = damping(z, keep, top - lo)
         for p in range(4 * L):
             x = state[p, :, lo:top]
@@ -752,8 +775,12 @@
     t1 = lax.ppermute(t1, "lat", lat_one)
     t2 = lax.ppermute(t2, "lat", lat_two)
     ring_lanes = 2 * z.extra * LANES
+    ring, ring_surface = call(unfold, [(7, 2 * L, W), (2 * L, W)], [m1, m2], flops=2_000_000)
     ring, ring_surface, msg = call(
-        halo_rows, [(7, 2 * L, W), (2 * L, W), (R, W + ring_lanes)], [sums, m1, m2, t1, t2]
+        halo_rows,
+        [(7, 2 * L, W), (2 * L, W), (R, W + ring_lanes)],
+        [ring, ring_surface, sums, t1, t2],
+        aliases={0: 0, 1: 1},
     )
     got = from_below(msg)
     y, yring = call(

time: 37.9 us -> 37.4 us (0.987)
  Pallas kernels: 8.82 us -> 8.36 us
    ppermute x1, waiting for transfers between devices: 0.01 us -> 0.74 us  [local(): m2 = lax.ppermute(m2, 'lat', lat_two)]
    ppermute x1, waiting for transfers between devices: 0.46 us -> 0.01 us  [local(): t1 = lax.ppermute(t1, 'lat', lat_one)]
    ppermute x1, waiting for transfers between devices: 1.91 us -> 1.52 us  [local(): t2 = lax.ppermute(t2, 'lat', lat_two)]
    pallas_call x11 -> x12, Pallas kernels: 6.07 us -> 5.73 us  [call(): pl.pallas_call(functools.partial(kernel, z), out_shape=[jax.ShapeDtypeStr...]
where the time goes in v8:
time: 37.4 us; the launch traced here: 36.9 us
  starting transfers between devices  15.8 us (42%)
  waiting for transfers between devices  10.4 us (28%)
  Pallas kernels  8.36 us (22%)
  other arithmetic  2.06 us (6%)
    ppermute x8, waiting for transfers between devices, lon_swap(): return lax.ppermute(value, 'lon', [(i, i ^ step) for i in range(z.n_lon)])  6.8 us
    pallas_call x12, Pallas kernels, call(): pl.pallas_call(functools.partial(kernel, z), out_shape=[jax.ShapeDtypeStr...  5.73 us
    ppermute x1, starting transfers between devices, local(): m2 = lax.ppermute(m2, 'lat', lat_two)  4.6 us
    ppermute x8, starting transfers between devices, lon_swap(): return lax.ppermute(value, 'lon', [(i, i ^ step) for i in range(z.n_lon)])  4.55 us
    ppermute x2, starting transfers between devices, from_below(): return lax.ppermute(column, 'lev', [(0, 1), (1, 0)])  2.46 us
    ppermute x1, starting transfers between devices, local(): t2 = lax.ppermute(t2, 'lat', lat_two)  1.92 us
    ppermute x1, starting transfers between devices, local(): e2 = lax.ppermute(e2, 'lon', lon_two)  1.64 us
    ppermute x1, waiting for transfers between devices, local(): t2 = lax.ppermute(t2, 'lat', lat_two)  1.52 us
  transfers between devices with their start and end apart: 16, of which 10 were waited for; matrix products, arithmetic and copies ran while one was open for 2% of the time, Pallas kernels for 14%

profile of v8, /device:TPU:8, one launch (start us, length us, event | category | flops | bytes accessed | tf_op | source)
XLA Modules:
  0.0 36.9 jit_solution(17859972793573137855)
XLA Ops:
  0.0 1.3 %select_maximum_fusion.x.x_in = f32[17,8,1920]{2,1,0:T(8,128)S(1)} fusion(f32[1,8,1800]{2,1,0:T(8,128)} %bitcast.5, f32[16,8,1800]{2,1,0:T(8,128)} %bitcast.4), kind=kLoop, calls=%fused_computation | loop fusion | flops 1044480 | bytes 2023680 | tf_op jit(solution)/shard_map/concatenate | solution.py:759
  1.7 1.6 %collective-permute-start.1 = (f32[8,128]{1,0:T(8,128)S(1)}, f32[8,128]{1,0:T(8,128)S(1)}, u32[]{:S(2)}, u32[]{:S(2)}) collective-permute-start(f32[8,128]{1,0:T(8,128)S(1)} %get-tuple-element.34), channel_id=1, source_target_pairs={{0,24},{8,16},{16,8},{24,0},{1,25},{9,17},{17,9},{25,1},{2,26},{10... | collective-permute-start | bytes 12296 | tf_op jit(solution)/shard_map/ppermute | solution.py:766
  3.7 4.6 %collective-permute-start.3 = (f32[8,6528]{1,0:T(8,128)S(1)}, f32[8,6528]{1,0:T(8,128)S(1)}, u32[]{:S(2)}, u32[]{:S(2)}) collective-permute-start(f32[8,6528]{1,0:T(8,128)S(1)} %get-tuple-element.37), channel_id=1, source_target_pairs={{2,4},{4,2},{3,5},{5,3},{10,12},{12,10},{11,13},{13,11},{18,20},{2... | collective-permute-start | bytes 626696 | tf_op jit(solution)/shard_map/ppermute | solution.py:763
  9.4 1.9 %collective-permute-start.5 = (f32[8,512]{1,0:T(8,128)S(1)}, f32[8,512]{1,0:T(8,128)S(1)}, u32[]{:S(2)}, u32[]{:S(2)}) collective-permute-start(f32[8,512]{1,0:T(8,128)S(1)} %get-tuple-element.42), channel_id=1, source_target_pairs={{2,4},{4,2},{3,5},{5,3},{10,12},{12,10},{11,13},{13,11},{18,20},{2... | collective-permute-start | bytes 49160 | tf_op jit(solution)/shard_map/ppermute | solution.py:776
  11.4 1.3 %row_code.1.code.refs_9_ = s32[16,128]{1,0:T(8,128)} custom-call(s32[16]{0:T(128)} %rows.1, s32[16]{0:T(128)} %counts.1), custom_call_target="tpu_custom_call" | custom-call | tf_op jit(solution)/shard_map/row_code/pallas_call | solution.py:721
  12.7 0.7 %collective-permute-done.3.r2 = f32[8,6528]{1,0:T(8,128)S(1)} collective-permute-done((f32[8,6528]{1,0:T(8,128)S(1)}, f32[8,6528]{1,0:T(8,128)S(1)}, u32[]{:S(2)}, u32[]{:S(2)}) %collective-permute-start.3) | collective-permute-done | bytes 208928 | tf_op jit(solution)/shard_map/ppermute | solution.py:763
  13.6 1.5 %collective-permute-done.5.t2 = f32[8,512]{1,0:T(8,128)S(1)} collective-permute-done((f32[8,512]{1,0:T(8,128)S(1)}, f32[8,512]{1,0:T(8,128)S(1)}, u32[]{:S(2)}, u32[]{:S(2)}) %collective-permute-start.5) | collective-permute-done | bytes 16416 | tf_op jit(solution)/shard_map/ppermute | solution.py:776
  15.1 1.6 %collective-permute-start.6 = (f32[8,2432]{1,0:T(8,128)S(1)}, f32[8,2432]{1,0:T(8,128)S(1)}, u32[]{:S(2)}, u32[]{:S(2)}) collective-permute-start(f32[8,2432]{1,0:T(8,128)S(1)} %get-tuple-element.44), channel_id=1, source_target_pairs={{0,1},{1,0},{2,3},{3,2},{4,5},{5,4},{6,7},{7,6},{8,9},{9,8},{10,11... | collective-permute-start | bytes 233480 | tf_op jit(solution)/shard_map/ppermute | solution.py:736
  16.7 1.0 %first_step.1 = (f32[16,8,1920]{2,1,0:T(8,128)S(1)}, f32[3,8,1920]{2,1,0:T(8,128)S(1)}) custom-call(f32[17,8,1920]{2,1,0:T(8,128)S(1)} %get-tuple-element.35.x, f32[7,8,1920]{2,1,0:T(8,128)S(1)} %get-tuple-element.45.ring, f32[5,16,128]{2,1,0:T(8,128)S(1)} %constant_dynamic-update-slice_fusion.geom), custom_call_target="tpu_custom_call" | custom-call | flops 10000000 | bytes 2682880 | tf_op jit(solution)/shard_map/first_step/pallas_call | solution.py:686
  17.8 0.7 %tile_and_ring_spectra.1.part = f32[88,256]{1,0:T(8,128)S(1)} custom-call(f32[16,8,1920]{2,1,0:T(8,128)S(1)} %get-tuple-element.46.y.refs_4_.state, f32[3,8,1920]{2,1,0:T(8,128)S(1)} %get-tuple-element.47.yring.refs_5_.sring, bf16[1920,256]{1,0:T(8,128)(2,1)S(1)} %copy-done, bf16[1920,256]{1,0:T(8,128)(2,1)S(1)} %copy-done.1, ...), custom_call_target="tpu_custom_call" | custom-call | flops 1000000 | bytes 3232768 | tf_op jit(solution)/shard_map/tile_and_ring_spectra/pallas_call | solution.py:686
  18.6 1.0 %collective-permute-done.6.got = f32[8,2432]{1,0:T(8,128)S(1)} collective-permute-done((f32[8,2432]{1,0:T(8,128)S(1)}, f32[8,2432]{1,0:T(8,128)S(1)}, u32[]{:S(2)}, u32[]{:S(2)}) %collective-permute-start.6) | collective-permute-done | bytes 77856 | tf_op jit(solution)/shard_map/ppermute | solution.py:736
  20.4 0.6 %collective-permute-start.8 = (f32[104,256]{1,0:T(8,128)S(1)}, f32[104,256]{1,0:T(8,128)S(1)}, u32[]{:S(2)}, u32[]{:S(2)}) collective-permute-start(f32[104,256]{1,0:T(8,128)S(1)} %get-tuple-element.48.refs_0_), channel_id=1, source_target_pairs={{0,16},{8,24},{16,0},{24,8},{1,17},{9,25},{17,1},{25,9},{2,18},{10... | collective-permute-start | bytes 319496 | tf_op jit(solution)/shard_map/ppermute | solution.py:745
  21.0 1.6 %collective-permute-start.10 = (f32[16,256]{1,0:T(8,128)S(1)}, f32[16,256]{1,0:T(8,128)S(1)}, u32[]{:S(2)}, u32[]{:S(2)}) collective-permute-start(f32[16,256]{1,0:T(8,128)S(1)} %get-tuple-element.49), channel_id=1, source_target_pairs={{0,24},{8,16},{16,8},{24,0},{1,25},{9,17},{17,9},{25,1},{2,26},{10... | collective-permute-start | bytes 49160 | tf_op jit(solution)/shard_map/ppermute | solution.py:745
  22.6 2.4 %collective-permute-done.10.refs_3_ = f32[16,256]{1,0:T(8,128)S(1)} collective-permute-done((f32[16,256]{1,0:T(8,128)S(1)}, f32[16,256]{1,0:T(8,128)S(1)}, u32[]{:S(2)}, u32[]{:S(2)}) %collective-permute-start.10) | collective-permute-done | bytes 16416 | tf_op jit(solution)/shard_map/ppermute | solution.py:745
  25.1 0.6 %collective-permute-done.8.refs_1_ = f32[104,256]{1,0:T(8,128)S(1)} collective-permute-done((f32[104,256]{1,0:T(8,128)S(1)}, f32[104,256]{1,0:T(8,128)S(1)}, u32[]{:S(2)}, u32[]{:S(2)}) %collective-permute-start.8) | collective-permute-done | bytes 106528 | tf_op jit(solution)/shard_map/ppermute | solution.py:745
  26.2 0.9 %collective-permute-start.11 = (f32[8,2432]{1,0:T(8,128)S(1)}, f32[8,2432]{1,0:T(8,128)S(1)}, u32[]{:S(2)}, u32[]{:S(2)}) collective-permute-start(f32[8,2432]{1,0:T(8,128)S(1)} %get-tuple-element.50), channel_id=1, source_target_pairs={{0,1},{1,0},{2,3},{3,2},{4,5},{5,4},{6,7},{7,6},{8,9},{9,8},{10,11... | collective-permute-start | bytes 233480 | tf_op jit(solution)/shard_map/ppermute | solution.py:736
  27.1 1.3 %second_step.1.y.refs_4_ = f32[16,8,1920]{2,1,0:T(8,128)S(1)} custom-call(f32[16,8,1920]{2,1,0:T(8,128)S(1)} %get-tuple-element.46.y.refs_4_.state, f32[3,8,1920]{2,1,0:T(8,128)S(1)} %get-tuple-element.47.yring.refs_5_.sring, f32[2,8,1920]{2,1,0:T(8,128)S(1)} %get-tuple-element.51.change, f32[8,1920]{1,0:T(8,128)S(1)} %get-tuple-element.52.ring_change, ...), custom_call_target="tpu_custom_call" | custom-call | flops 10000000 | bytes 5038080 | tf_op jit(solution)/shard_map/second_step/pallas_call | solution.py:686
  28.4 0.6 %tile_spectra.1.part = f32[64,256]{1,0:T(8,128)S(1)} custom-call(f32[16,8,1920]{2,1,0:T(8,128)S(1)} %second_step.1.y.refs_4_, bf16[1920,256]{1,0:T(8,128)(2,1)S(1)} %copy-done, bf16[1920,256]{1,0:T(8,128)(2,1)S(1)} %copy-done.1, f32[2,128]{1,0:T(2,128)S(1)} %pad_maximum_fusion.phase.refs_8_, s32[16,128]{1,0:T(8,128)S(1)} %copy-done.4), custom_call_target="tpu_custom_call" | custom-call | flops 1000000 | bytes 3023872 | tf_op jit(solution)/shard_map/tile_spectra/pallas_call | solution.py:686
  29.1 1.2 %collective-permute-done.12.part_got = f32[64,256]{1,0:T(8,128)S(1)} collective-permute-done((f32[64,256]{1,0:T(8,128)S(1)}, f32[64,256]{1,0:T(8,128)S(1)}, u32[]{:S(2)}, u32[]{:S(2)}) %collective-permute-start.12) | collective-permute-done | bytes 65568 | tf_op jit(solution)/shard_map/ppermute | solution.py:745
  31.1 0.6 %collective-permute-start.13 = (f32[72,256]{1,0:T(8,128)S(1)}, f32[72,256]{1,0:T(8,128)S(1)}, u32[]{:S(2)}, u32[]{:S(2)}) collective-permute-start(f32[72,256]{1,0:T(8,128)S(1)} %get-tuple-element.56.refs_0_), channel_id=1, source_target_pairs={{0,16},{8,24},{16,0},{24,8},{1,17},{9,25},{17,1},{25,9},{2,18},{10... | collective-permute-start | bytes 221192 | tf_op jit(solution)/shard_map/ppermute | solution.py:745
  31.7 1.6 %collective-permute-start.15 = (f32[8,256]{1,0:T(8,128)S(1)}, f32[8,256]{1,0:T(8,128)S(1)}, u32[]{:S(2)}, u32[]{:S(2)}) collective-permute-start(f32[8,256]{1,0:T(8,128)S(1)} %get-tuple-element.57), channel_id=1, source_target_pairs={{0,24},{8,16},{16,8},{24,0},{1,25},{9,17},{17,9},{25,1},{2,26},{10... | collective-permute-start | bytes 24584 | tf_op jit(solution)/shard_map/ppermute | solution.py:745
  33.3 1.5 %collective-permute-done.15.refs_3_ = f32[8,256]{1,0:T(8,128)S(1)} collective-permute-done((f32[8,256]{1,0:T(8,128)S(1)}, f32[8,256]{1,0:T(8,128)S(1)}, u32[]{:S(2)}, u32[]{:S(2)}) %collective-permute-start.15) | collective-permute-done | bytes 8224 | tf_op jit(solution)/shard_map/ppermute | solution.py:745
  34.8 0.8 %collective-permute-done.13.refs_1_ = f32[72,256]{1,0:T(8,128)S(1)} collective-permute-done((f32[72,256]{1,0:T(8,128)S(1)}, f32[72,256]{1,0:T(8,128)S(1)}, u32[]{:S(2)}, u32[]{:S(2)}) %collective-permute-start.13) | collective-permute-done | bytes 73760 | tf_op jit(solution)/shard_map/ppermute | solution.py:745
  35.6 1.3 %filter_all.1 = f32[4,4,8,1800]{3,2,1,0:T(8,128)} custom-call(f32[72,256]{1,0:T(8,128)S(1)} %get-tuple-element.56.refs_0_, f32[72,256]{1,0:T(8,128)S(1)} %collective-permute-done.13.refs_1_, f32[8,256]{1,0:T(8,128)S(1)} %collective-permute-done.14.refs_2_, f32[8,256]{1,0:T(8,128)S(1)} %collective-permute-done.15.refs_3_, ...), custom_call_target="tpu_custom_call" | custom-call | tf_op jit(solution)/shard_map/filter_all/pallas_call | solution.py:824
  (43 shorter events, 4.2 us)
Async XLA Ops:
  1.6 7.6 %collective-permute-start = (f32[8,128]{1,0:T(8,128)S(1)}, f32[8,128]{1,0:T(8,128)S(1)}, u32[]{:S(2)}, u32[]{:S(2)}) collective-permute-start(f32[8,128]{1,0:T(8,128)S(1)} %get-tuple-element.33), channel_id=1, source_target_pairs={{0,8},{8,0},{16,24},{24,16},{1,9},{9,1},{17,25},{25,17},{2,10},{10... | collective-permute-start | bytes 12296 | tf_op jit(solution)/shard_map/ppermute | solution.py:765
  1.7 7.5 %collective-permute-start.1 = (f32[8,128]{1,0:T(8,128)S(1)}, f32[8,128]{1,0:T(8,128)S(1)}, u32[]{:S(2)}, u32[]{:S(2)}) collective-permute-start(f32[8,128]{1,0:T(8,128)S(1)} %get-tuple-element.34), channel_id=1, source_target_pairs={{0,24},{8,16},{16,8},{24,0},{1,25},{9,17},{17,9},{25,1},{2,26},{10... | collective-permute-start | bytes 12296 | tf_op jit(solution)/shard_map/ppermute | solution.py:766
  3.3 9.4 %collective-permute-start.2 = (f32[8,6528]{1,0:T(8,128)S(1)}, f32[8,6528]{1,0:T(8,128)S(1)}, u32[]{:S(2)}, u32[]{:S(2)}) collective-permute-start(f32[8,6528]{1,0:T(8,128)S(1)} %get-tuple-element.36), channel_id=1, source_target_pairs={{0,2},{2,0},{4,6},{6,4},{1,3},{3,1},{5,7},{7,5},{8,10},{10,8},{12,... | collective-permute-start | bytes 626696 | tf_op jit(solution)/shard_map/ppermute | solution.py:762
  3.7 9.7 %collective-permute-start.3 = (f32[8,6528]{1,0:T(8,128)S(1)}, f32[8,6528]{1,0:T(8,128)S(1)}, u32[]{:S(2)}, u32[]{:S(2)}) collective-permute-start(f32[8,6528]{1,0:T(8,128)S(1)} %get-tuple-element.37), channel_id=1, source_target_pairs={{2,4},{4,2},{3,5},{5,3},{10,12},{12,10},{11,13},{13,11},{18,20},{2... | collective-permute-start | bytes 626696 | tf_op jit(solution)/shard_map/ppermute | solution.py:763
  9.4 4.2 %collective-permute-start.4 = (f32[8,512]{1,0:T(8,128)S(1)}, f32[8,512]{1,0:T(8,128)S(1)}, u32[]{:S(2)}, u32[]{:S(2)}) collective-permute-start(f32[8,512]{1,0:T(8,128)S(1)} %get-tuple-element.41), channel_id=1, source_target_pairs={{0,2},{2,0},{4,6},{6,4},{1,3},{3,1},{5,7},{7,5},{8,10},{10,8},{12,... | collective-permute-start | bytes 49160 | tf_op jit(solution)/shard_map/ppermute | solution.py:775
  9.4 5.6 %collective-permute-start.5 = (f32[8,512]{1,0:T(8,128)S(1)}, f32[8,512]{1,0:T(8,128)S(1)}, u32[]{:S(2)}, u32[]{:S(2)}) collective-permute-start(f32[8,512]{1,0:T(8,128)S(1)} %get-tuple-element.42), channel_id=1, source_target_pairs={{2,4},{4,2},{3,5},{5,3},{10,12},{12,10},{11,13},{13,11},{18,20},{2... | collective-permute-start | bytes 49160 | tf_op jit(solution)/shard_map/ppermute | solution.py:776
  15.1 2.7 %copy-start = (bf16[1920,256]{1,0:T(8,128)(2,1)S(1)}, bf16[1920,256]{1,0:T(8,128)(2,1)}, u32[]{:S(2)}) copy-start(bf16[1920,256]{1,0:T(8,128)(2,1)} %constant.59.clone.wh) | copy-start | bytes 2949124
  15.1 2.7 %copy-start.1 = (bf16[1920,256]{1,0:T(8,128)(2,1)S(1)}, bf16[1920,256]{1,0:T(8,128)(2,1)}, u32[]{:S(2)}) copy-start(bf16[1920,256]{1,0:T(8,128)(2,1)} %constant.60.clone.wl) | copy-start | bytes 2949124
  15.1 4.5 %collective-permute-start.6 = (f32[8,2432]{1,0:T(8,128)S(1)}, f32[8,2432]{1,0:T(8,128)S(1)}, u32[]{:S(2)}, u32[]{:S(2)}) collective-permute-start(f32[8,2432]{1,0:T(8,128)S(1)} %get-tuple-element.44), channel_id=1, source_target_pairs={{0,1},{1,0},{2,3},{3,2},{4,5},{5,4},{6,7},{7,6},{8,9},{9,8},{10,11... | collective-permute-start | bytes 233480 | tf_op jit(solution)/shard_map/ppermute | solution.py:736
  16.7 1.1 %copy-start.4 = (s32[16,128]{1,0:T(8,128)S(1)}, s32[16,128]{1,0:T(8,128)}, u32[]{:S(2)}) copy-start(s32[16,128]{1,0:T(8,128)} %row_code.1.code.refs_9_) | copy-start | bytes 24580
  18.5 1.4 %collective-permute-start.7 = (f32[88,256]{1,0:T(8,128)S(1)}, f32[88,256]{1,0:T(8,128)S(1)}, u32[]{:S(2)}, u32[]{:S(2)}) collective-permute-start(f32[88,256]{1,0:T(8,128)S(1)} %tile_and_ring_spectra.1.part), channel_id=1, source_target_pairs={{0,8},{8,0},{16,24},{24,16},{1,9},{9,1},{17,25},{25,17},{2,10},{10... | collective-permute-start | bytes 270344 | tf_op jit(solution)/shard_map/ppermute | solution.py:745
  19.9 5.8 %copy-start.2 = (bf16[256,1920]{1,0:T(8,128)(2,1)S(1)}, bf16[256,1920]{1,0:T(8,128)(2,1)}, u32[]{:S(2)}) copy-start(bf16[256,1920]{1,0:T(8,128)(2,1)} %constant.61.clone.refs_6_.wh) | copy-start | bytes 2949124
  19.9 5.8 %copy-start.3 = (bf16[256,1920]{1,0:T(8,128)(2,1)S(1)}, bf16[256,1920]{1,0:T(8,128)(2,1)}, u32[]{:S(2)}) copy-start(bf16[256,1920]{1,0:T(8,128)(2,1)} %constant.62.clone.refs_7_.wl) | copy-start | bytes 2949124
  20.4 5.3 %collective-permute-start.8 = (f32[104,256]{1,0:T(8,128)S(1)}, f32[104,256]{1,0:T(8,128)S(1)}, u32[]{:S(2)}, u32[]{:S(2)}) collective-permute-start(f32[104,256]{1,0:T(8,128)S(1)} %get-tuple-element.48.refs_0_), channel_id=1, source_target_pairs={{0,16},{8,24},{16,0},{24,8},{1,17},{9,25},{17,1},{25,9},{2,18},{10... | collective-permute-start | bytes 319496 | tf_op jit(solution)/shard_map/ppermute | solution.py:745
  21.0 1.6 %collective-permute-start.9 = (f32[16,256]{1,0:T(8,128)S(1)}, f32[16,256]{1,0:T(8,128)S(1)}, u32[]{:S(2)}, u32[]{:S(2)}) collective-permute-start(f32[16,256]{1,0:T(8,128)S(1)} %get-tuple-element.49), channel_id=1, source_target_pairs={{0,8},{8,0},{16,24},{24,16},{1,9},{9,1},{17,25},{25,17},{2,10},{10... | collective-permute-start | bytes 49160 | tf_op jit(solution)/shard_map/ppermute | solution.py:745
  21.0 4.1 %collective-permute-start.10 = (f32[16,256]{1,0:T(8,128)S(1)}, f32[16,256]{1,0:T(8,128)S(1)}, u32[]{:S(2)}, u32[]{:S(2)}) collective-permute-start(f32[16,256]{1,0:T(8,128)S(1)} %get-tuple-element.49), channel_id=1, source_target_pairs={{0,24},{8,16},{16,8},{24,0},{1,25},{9,17},{17,9},{25,1},{2,26},{10... | collective-permute-start | bytes 49160 | tf_op jit(solution)/shard_map/ppermute | solution.py:745
  26.2 4.5 %collective-permute-start.11 = (f32[8,2432]{1,0:T(8,128)S(1)}, f32[8,2432]{1,0:T(8,128)S(1)}, u32[]{:S(2)}, u32[]{:S(2)}) collective-permute-start(f32[8,2432]{1,0:T(8,128)S(1)} %get-tuple-element.50), channel_id=1, source_target_pairs={{0,1},{1,0},{2,3},{3,2},{4,5},{5,4},{6,7},{7,6},{8,9},{9,8},{10,11... | collective-permute-start | bytes 233480 | tf_op jit(solution)/shard_map/ppermute | solution.py:736
  29.0 1.3 %collective-permute-start.12 = (f32[64,256]{1,0:T(8,128)S(1)}, f32[64,256]{1,0:T(8,128)S(1)}, u32[]{:S(2)}, u32[]{:S(2)}) collective-permute-start(f32[64,256]{1,0:T(8,128)S(1)} %tile_spectra.1.part), channel_id=1, source_target_pairs={{0,8},{8,0},{16,24},{24,16},{1,9},{9,1},{17,25},{25,17},{2,10},{10... | collective-permute-start | bytes 196616 | tf_op jit(solution)/shard_map/ppermute | solution.py:745
  31.1 4.4 %collective-permute-start.13 = (f32[72,256]{1,0:T(8,128)S(1)}, f32[72,256]{1,0:T(8,128)S(1)}, u32[]{:S(2)}, u32[]{:S(2)}) collective-permute-start(f32[72,256]{1,0:T(8,128)S(1)} %get-tuple-element.56.refs_0_), channel_id=1, source_target_pairs={{0,16},{8,24},{16,0},{24,8},{1,17},{9,25},{17,1},{25,9},{2,18},{10... | collective-permute-start | bytes 221192 | tf_op jit(solution)/shard_map/ppermute | solution.py:745
  31.7 1.6 %collective-permute-start.14 = (f32[8,256]{1,0:T(8,128)S(1)}, f32[8,256]{1,0:T(8,128)S(1)}, u32[]{:S(2)}, u32[]{:S(2)}) collective-permute-start(f32[8,256]{1,0:T(8,128)S(1)} %get-tuple-element.57), channel_id=1, source_target_pairs={{0,8},{8,0},{16,24},{24,16},{1,9},{9,1},{17,25},{25,17},{2,10},{10... | collective-permute-start | bytes 24584 | tf_op jit(solution)/shard_map/ppermute | solution.py:745
  31.7 3.1 %collective-permute-start.15 = (f32[8,256]{1,0:T(8,128)S(1)}, f32[8,256]{1,0:T(8,128)S(1)}, u32[]{:S(2)}, u32[]{:S(2)}) collective-permute-start(f32[8,256]{1,0:T(8,128)S(1)} %get-tuple-element.57), channel_id=1, source_target_pairs={{0,24},{8,16},{16,8},{24,0},{1,25},{9,17},{17,9},{25,1},{2,26},{10... | collective-permute-start | bytes 24584 | tf_op jit(solution)/shard_map/ppermute | solution.py:745

commit v9 on v8

--- a/solution.py
+++ b/solution.py
@@ -133,9 +133,9 @@
 
 
 def near_and_far(z):
-    lat_even = lax.axis_index("lat") % 2 == 0
-    near = jnp.where(lat_even, z.R - 1, 0)
-    far = jnp.where(lat_even, z.R - 2, 1)
+    lat_odd = lax.axis_index("lat") % 2 == 1
+    near = jnp.where(lat_odd, z.R - 1, 0)
+    far = jnp.where(lat_odd, z.R - 2, 1)
     return (near, far), (z.R - 1 - near, z.R - 1 - far)
 
 
@@ -193,8 +193,8 @@
                 msg[to : to + 1, k // 2 * T : (k // 2 + 1) * T] = x[p, pl.ds(at, 1), :][:, z.base :]
 
 
-def put_ring_sums(z, msg, south, north):
-    for d, row in enumerate((south, north)):
+def put_ring_sums(z, msg, *rows):
+    for d, row in enumerate(rows):
         for t in range(z.tiles):
             at = (d * z.extra + t // z.R) * LANES
             msg[t % z.R : t % z.R + 1, at : at + LANES] = row[:, t * LANES : (t + 1) * LANES]
@@ -210,7 +210,7 @@
 
 
 def unfold(z, r1, r2, ring, ring_surface):
-    lat_even = lax.axis_index("lat") % 2 == 0
+    lat_odd = lax.axis_index("lat") % 2 == 1
     L, B = z.L, z.base
     fold = z.fold * LANES
 
@@ -226,12 +226,12 @@
             part = source[t % z.R : t % z.R + 1, at : at + LANES]
             ring_surface[here, t * LANES : (t + 1) * LANES] = jnp.broadcast_to(part, (L, LANES))
 
-    @pl.when(lat_even)
+    @pl.when(lat_odd)
     def _():
         place(0, r2)
         place(1, r1)
 
-    @pl.when(jnp.logical_not(lat_even))
+    @pl.when(jnp.logical_not(lat_odd))
     def _():
         place(0, r1)
         place(1, r2)
@@ -239,7 +239,7 @@
 
 def halo_rows(z, ring_in, surface_in, sums, t1, t2, ring, ring_surface, msg):
     del ring_in, surface_in
-    lat_even = lax.axis_index("lat") % 2 == 0
+    lat_odd = lax.axis_index("lat") % 2 == 1
     L, B, T = z.L, z.base, z.W - z.base
     msg[:, 0 : z.W] = sums[...]
     msg[:, z.W :] = jnp.zeros((z.R, 2 * z.extra * LANES), jnp.float32)
@@ -251,18 +251,18 @@
             ring[k, here, B:] = tail[at : at + L, k // 2 * T : (k // 2 + 1) * T]
         ring_surface[here, B:] = tail[L : 2 * L, 3 * T :]
 
-    @pl.when(lat_even)
+    @pl.when(lat_odd)
     def _():
         place(0, t2)
         place(1, t1)
 
-    @pl.when(jnp.logical_not(lat_even))
+    @pl.when(jnp.logical_not(lat_odd))
     def _():
         place(0, t1)
         place(1, t2)
 
     south, north = ring_sum(z, layer_weight(ring[2], ring[3]))
-    put_ring_sums(z, msg.at[:, z.W :], south, north)
+    put_ring_sums(z, msg.at[:, z.W :], north, south)
 
 
 def in_band(z, shape):
@@ -371,19 +371,20 @@
     yring[2] = new["t"] * mask
 
 
-def level_part(z, surface, ring_surface, below, ring_below):
+def level_part(z, surface, ring_surface, got):
     live = jnp.where(lax.axis_index("lev") < z.n_lev - 1, 1.0, 0.0)
     lat = lax.axis_index("lat")
-    rows = []
-    for d in range(2):
-        there = jnp.where(lat > 0, 1.0, 0.0) if d == 0 else jnp.where(lat < z.n_lat - 1, 1.0, 0.0)
+    out = [surface + live * got[:, 0 : z.W]]
+    for d in range((got.shape[1] - z.W) // (z.extra * LANES)):
+        inside = lat < z.n_lat - 1 if d == 0 else lat > 0
         parts = []
         for t in range(z.tiles):
-            at = (d * z.extra + t // z.R) * LANES
-            parts.append(ring_below[t % z.R : t % z.R + 1, at : at + LANES])
+            at = z.W + (d * z.extra + t // z.R) * LANES
+            parts.append(got[t % z.R : t % z.R + 1, at : at + LANES])
         sums = jnp.concatenate(parts, 1)
-        rows.append(there * (ring_surface[d * z.L : d * z.L + 1, :] + live * sums))
-    return surface + live * below, rows[0], rows[1]
+        row = (1 - d) * z.L
+        out.append(jnp.where(inside, 1.0, 0.0) * (ring_surface[row : row + 1, :] + live * sums))
+    return out
 
 
 def dot(a, b, dims):
@@ -466,7 +467,7 @@
     z, surface, ring_surface, got, part, part_got, geom, wh, wl, phase, code, sent, own, change, ring_change
 ):
     L = z.L
-    g, gs, gn = level_part(z, surface[...], ring_surface, got[:, 0 : z.W], got[:, z.W :])
+    g, gn, gs = level_part(z, surface[...], ring_surface, got)
     du = wide(geom, 0, 0, z.R, z.W) * (east(g) - g)
     dv = NORTH_COEF * (with_last(g, gn) - g)
     shape = (2 * L, z.W)
@@ -489,7 +490,7 @@
 def second_level_spectra(
     z, surface, ring_surface, got, part, part_got, geom, wh, wl, phase, code, sent, own, change
 ):
-    g, _, gn = level_part(z, surface[...], ring_surface, got[:, 0 : z.W], got[:, z.W :])
+    g, gn = level_part(z, surface[...], ring_surface, got)
     du = wide(geom, 0, 0, z.R, z.W) * (east(g) - g)
     dv = NORTH_COEF * (with_last(g, gn) - g)
     change[0] = du
@@ -586,10 +587,10 @@
     total = layer_weight(ht[0], ht[L])
     for l in range(1, L):
         total = total + layer_weight(ht[l], ht[L + l])
-    south, north = ring_sum(z, layer_weight(htring[0], htring[1]))
+    _, north = ring_sum(z, layer_weight(htring[0], htring[1]))
     msg[:, 0 : z.W] = total
-    msg[:, z.W :] = jnp.zeros((z.R, 2 * z.extra * LANES), jnp.float32)
-    put_ring_sums(z, msg.at[:, z.W :], south, north)
+    msg[:, z.W :] = jnp.zeros((z.R, z.extra * LANES), jnp.float32)
+    put_ring_sums(z, msg.at[:, z.W :], north)
 
 
 def second_step(z, state, sring, change, ring_change, uvmodes, ht, htring, geom, wh, wl, code, y, uv, uvring, q_ring):
@@ -728,8 +729,8 @@
 
     lon_one = [(i, i ^ 1) for i in range(z.n_lon)]
     lon_two = [(i, (((i + 1) % z.n_lon ^ 1) - 1) % z.n_lon) for i in range(z.n_lon)]
-    lat_one = [(i, i ^ 1) for i in range(z.n_lat) if i ^ 1 < z.n_lat]
-    lat_two = [(i, ((i + 1) ^ 1) - 1) for i in range(1, z.n_lat) if ((i + 1) ^ 1) - 1 < z.n_lat]
+    lat_two = [(i, i ^ 1) for i in range(z.n_lat) if i ^ 1 < z.n_lat]
+    lat_one = [(i, ((i + 1) ^ 1) - 1) for i in range(1, z.n_lat) if ((i + 1) ^ 1) - 1 < z.n_lat]
 
     def from_below(column):
         if z.n_lev == 2:
@@ -803,7 +804,7 @@
     parts = over_lon(sent, own, rows + 6 * L)
     ht, htring, uvmodes, msg = call(
         filter_mass,
-        [(2 * L, R, W), (2, 2 * L, W), (2 * L * R + 2 * L, 2 * KMAX), (R, W + ring_lanes)],
+        [(2 * L, R, W), (2, 2 * L, W), (2 * L * R + 2 * L, 2 * KMAX), (R, W + ring_lanes // 2)],
         [*parts, y, yring, *back],
     )
     got = from_below(msg)

time: 37.4 us -> 37.2 us (level)
  the two profiles are of different devices: /device:TPU:8 before, /device:TPU:0 now
where the time goes in v9:
time: 37.2 us; the launch traced here: 37.1 us
  starting transfers between devices  17.7 us (48%)
  waiting for transfers between devices  8.65 us (23%)
  Pallas kernels  8.35 us (22%)
  other arithmetic  2.06 us (6%)
    ppermute x8, waiting for transfers between devices, lon_swap(): return lax.ppermute(value, 'lon', [(i, i ^ step) for i in range(z.n_lon)])  6.8 us
    pallas_call x12, Pallas kernels, call(): pl.pallas_call(functools.partial(kernel, z), out_shape=[jax.ShapeDtypeStr...  5.73 us
    ppermute x8, starting transfers between devices, lon_swap(): return lax.ppermute(value, 'lon', [(i, i ^ step) for i in range(z.n_lon)])  4.55 us
    ppermute x1, starting transfers between devices, local(): m2 = lax.ppermute(m2, 'lat', lat_two)  4.45 us
    ppermute x1, starting transfers between devices, local(): e2 = lax.ppermute(e2, 'lon', lon_two)  2.64 us
    ppermute x2, starting transfers between devices, from_below(): return lax.ppermute(column, 'lev', [(0, 1), (1, 0)])  2.46 us
    ppermute x1, starting transfers between devices, local(): t2 = lax.ppermute(t2, 'lat', lat_two)  1.8 us
    pallas_call x1, Pallas kernels, local(): pl.pallas_call(functools.partial(row_code, z), out_shape=jax.ShapeDtypeSt...  1.31 us
  transfers between devices with their start and end apart: 16, of which 10 were waited for; matrix products, arithmetic and copies ran while one was open for 2% of the time, Pallas kernels for 14%

profile of v9, /device:TPU:0, one launch (start us, length us, event | category | flops | bytes accessed | tf_op | source)
XLA Modules:
  0.0 37.1 jit_solution(3014647718555824855)
XLA Ops:
  0.0 1.3 %select_maximum_fusion.x.x_in = f32[17,8,1920]{2,1,0:T(8,128)S(1)} fusion(f32[1,8,1800]{2,1,0:T(8,128)} %bitcast.5, f32[16,8,1800]{2,1,0:T(8,128)} %bitcast.4), kind=kLoop, calls=%fused_computation | loop fusion | flops 1044480 | bytes 2023680 | tf_op jit(solution)/shard_map/concatenate | solution.py:760
  2.1 2.6 %collective-permute-start.1 = (f32[8,128]{1,0:T(8,128)S(1)}, f32[8,128]{1,0:T(8,128)S(1)}, u32[]{:S(2)}, u32[]{:S(2)}) collective-permute-start(f32[8,128]{1,0:T(8,128)S(1)} %get-tuple-element.34), channel_id=1, source_target_pairs={{0,24},{8,16},{16,8},{24,0},{1,25},{9,17},{17,9},{25,1},{2,26},{10... | collective-permute-start | bytes 12296 | tf_op jit(solution)/shard_map/ppermute | solution.py:767
  4.7 0.7 %collective-permute-start.2 = (f32[8,6528]{1,0:T(8,128)S(1)}, f32[8,6528]{1,0:T(8,128)S(1)}, u32[]{:S(2)}, u32[]{:S(2)}) collective-permute-start(f32[8,6528]{1,0:T(8,128)S(1)} %get-tuple-element.36), channel_id=1, source_target_pairs={{2,4},{4,2},{3,5},{5,3},{10,12},{12,10},{11,13},{13,11},{18,20},{2... | collective-permute-start | bytes 626696 | tf_op jit(solution)/shard_map/ppermute | solution.py:763
  5.4 4.5 %collective-permute-start.3 = (f32[8,6528]{1,0:T(8,128)S(1)}, f32[8,6528]{1,0:T(8,128)S(1)}, u32[]{:S(2)}, u32[]{:S(2)}) collective-permute-start(f32[8,6528]{1,0:T(8,128)S(1)} %get-tuple-element.37), channel_id=1, source_target_pairs={{0,2},{2,0},{4,6},{6,4},{1,3},{3,1},{5,7},{7,5},{8,10},{10,8},{12,... | collective-permute-start | bytes 626696 | tf_op jit(solution)/shard_map/ppermute | solution.py:764
  10.9 0.7 %collective-permute-start.4 = (f32[8,512]{1,0:T(8,128)S(1)}, f32[8,512]{1,0:T(8,128)S(1)}, u32[]{:S(2)}, u32[]{:S(2)}) collective-permute-start(f32[8,512]{1,0:T(8,128)S(1)} %get-tuple-element.41), channel_id=1, source_target_pairs={{2,4},{4,2},{3,5},{5,3},{10,12},{12,10},{11,13},{13,11},{18,20},{2... | collective-permute-start | bytes 49160 | tf_op jit(solution)/shard_map/ppermute | solution.py:776
  11.5 1.8 %collective-permute-start.5 = (f32[8,512]{1,0:T(8,128)S(1)}, f32[8,512]{1,0:T(8,128)S(1)}, u32[]{:S(2)}, u32[]{:S(2)}) collective-permute-start(f32[8,512]{1,0:T(8,128)S(1)} %get-tuple-element.42), channel_id=1, source_target_pairs={{0,2},{2,0},{4,6},{6,4},{1,3},{3,1},{5,7},{7,5},{8,10},{10,8},{12,... | collective-permute-start | bytes 49160 | tf_op jit(solution)/shard_map/ppermute | solution.py:777
  13.3 1.3 %row_code.1.code.refs_9_ = s32[16,128]{1,0:T(8,128)} custom-call(s32[16]{0:T(128)} %rows.1, s32[16]{0:T(128)} %counts.1), custom_call_target="tpu_custom_call" | custom-call | tf_op jit(solution)/shard_map/row_code/pallas_call | solution.py:722
  15.4 1.6 %collective-permute-start.6 = (f32[8,2432]{1,0:T(8,128)S(1)}, f32[8,2432]{1,0:T(8,128)S(1)}, u32[]{:S(2)}, u32[]{:S(2)}) collective-permute-start(f32[8,2432]{1,0:T(8,128)S(1)} %get-tuple-element.44), channel_id=1, source_target_pairs={{0,1},{1,0},{2,3},{3,2},{4,5},{5,4},{6,7},{7,6},{8,9},{9,8},{10,11... | collective-permute-start | bytes 233480 | tf_op jit(solution)/shard_map/ppermute | solution.py:737
  17.0 1.0 %first_step.1 = (f32[16,8,1920]{2,1,0:T(8,128)S(1)}, f32[3,8,1920]{2,1,0:T(8,128)S(1)}) custom-call(f32[17,8,1920]{2,1,0:T(8,128)S(1)} %get-tuple-element.35.x, f32[7,8,1920]{2,1,0:T(8,128)S(1)} %get-tuple-element.45.ring, f32[5,16,128]{2,1,0:T(8,128)S(1)} %constant_dynamic-update-slice_fusion.geom), custom_call_target="tpu_custom_call" | custom-call | flops 10000000 | bytes 2682880 | tf_op jit(solution)/shard_map/first_step/pallas_call | solution.py:687
  18.0 0.7 %tile_and_ring_spectra.1.part = f32[88,256]{1,0:T(8,128)S(1)} custom-call(f32[16,8,1920]{2,1,0:T(8,128)S(1)} %get-tuple-element.46.y.refs_4_.state, f32[3,8,1920]{2,1,0:T(8,128)S(1)} %get-tuple-element.47.yring.refs_5_.sring, bf16[1920,256]{1,0:T(8,128)(2,1)S(1)} %copy-done, bf16[1920,256]{1,0:T(8,128)(2,1)S(1)} %copy-done.1, ...), custom_call_target="tpu_custom_call" | custom-call | flops 1000000 | bytes 3232768 | tf_op jit(solution)/shard_map/tile_and_ring_spectra/pallas_call | solution.py:687
  18.9 1.0 %collective-permute-done.6.got = f32[8,2432]{1,0:T(8,128)S(1)} collective-permute-done((f32[8,2432]{1,0:T(8,128)S(1)}, f32[8,2432]{1,0:T(8,128)S(1)}, u32[]{:S(2)}, u32[]{:S(2)}) %collective-permute-start.6) | collective-permute-done | bytes 77856 | tf_op jit(solution)/shard_map/ppermute | solution.py:737
  20.7 0.6 %collective-permute-start.8 = (f32[104,256]{1,0:T(8,128)S(1)}, f32[104,256]{1,0:T(8,128)S(1)}, u32[]{:S(2)}, u32[]{:S(2)}) collective-permute-start(f32[104,256]{1,0:T(8,128)S(1)} %get-tuple-element.48.refs_0_), channel_id=1, source_target_pairs={{0,16},{8,24},{16,0},{24,8},{1,17},{9,25},{17,1},{25,9},{2,18},{10... | collective-permute-start | bytes 319496 | tf_op jit(solution)/shard_map/ppermute | solution.py:746
  21.2 1.6 %collective-permute-start.10 = (f32[16,256]{1,0:T(8,128)S(1)}, f32[16,256]{1,0:T(8,128)S(1)}, u32[]{:S(2)}, u32[]{:S(2)}) collective-permute-start(f32[16,256]{1,0:T(8,128)S(1)} %get-tuple-element.49), channel_id=1, source_target_pairs={{0,24},{8,16},{16,8},{24,0},{1,25},{9,17},{17,9},{25,1},{2,26},{10... | collective-permute-start | bytes 49160 | tf_op jit(solution)/shard_map/ppermute | solution.py:746
  22.9 2.4 %collective-permute-done.10.refs_3_ = f32[16,256]{1,0:T(8,128)S(1)} collective-permute-done((f32[16,256]{1,0:T(8,128)S(1)}, f32[16,256]{1,0:T(8,128)S(1)}, u32[]{:S(2)}, u32[]{:S(2)}) %collective-permute-start.10) | collective-permute-done | bytes 16416 | tf_op jit(solution)/shard_map/ppermute | solution.py:746
  25.3 0.6 %collective-permute-done.8.refs_1_ = f32[104,256]{1,0:T(8,128)S(1)} collective-permute-done((f32[104,256]{1,0:T(8,128)S(1)}, f32[104,256]{1,0:T(8,128)S(1)}, u32[]{:S(2)}, u32[]{:S(2)}) %collective-permute-start.8) | collective-permute-done | bytes 106528 | tf_op jit(solution)/shard_map/ppermute | solution.py:746
  26.5 0.9 %collective-permute-start.11 = (f32[8,2176]{1,0:T(8,128)S(1)}, f32[8,2176]{1,0:T(8,128)S(1)}, u32[]{:S(2)}, u32[]{:S(2)}) collective-permute-start(f32[8,2176]{1,0:T(8,128)S(1)} %get-tuple-element.50), channel_id=1, source_target_pairs={{0,1},{1,0},{2,3},{3,2},{4,5},{5,4},{6,7},{7,6},{8,9},{9,8},{10,11... | collective-permute-start | bytes 208904 | tf_op jit(solution)/shard_map/ppermute | solution.py:737
  27.4 1.3 %second_step.1.y.refs_4_ = f32[16,8,1920]{2,1,0:T(8,128)S(1)} custom-call(f32[16,8,1920]{2,1,0:T(8,128)S(1)} %get-tuple-element.46.y.refs_4_.state, f32[3,8,1920]{2,1,0:T(8,128)S(1)} %get-tuple-element.47.yring.refs_5_.sring, f32[2,8,1920]{2,1,0:T(8,128)S(1)} %get-tuple-element.51.change, f32[8,1920]{1,0:T(8,128)S(1)} %get-tuple-element.52.ring_change, ...), custom_call_target="tpu_custom_call" | custom-call | flops 10000000 | bytes 5038080 | tf_op jit(solution)/shard_map/second_step/pallas_call | solution.py:687
  28.7 0.6 %tile_spectra.1.part = f32[64,256]{1,0:T(8,128)S(1)} custom-call(f32[16,8,1920]{2,1,0:T(8,128)S(1)} %second_step.1.y.refs_4_, bf16[1920,256]{1,0:T(8,128)(2,1)S(1)} %copy-done, bf16[1920,256]{1,0:T(8,128)(2,1)S(1)} %copy-done.1, f32[2,128]{1,0:T(2,128)S(1)} %pad_maximum_fusion.phase.refs_8_, s32[16,128]{1,0:T(8,128)S(1)} %copy-done.4), custom_call_target="tpu_custom_call" | custom-call | flops 1000000 | bytes 3023872 | tf_op jit(solution)/shard_map/tile_spectra/pallas_call | solution.py:687
  29.3 1.2 %collective-permute-done.12.part_got = f32[64,256]{1,0:T(8,128)S(1)} collective-permute-done((f32[64,256]{1,0:T(8,128)S(1)}, f32[64,256]{1,0:T(8,128)S(1)}, u32[]{:S(2)}, u32[]{:S(2)}) %collective-permute-start.12) | collective-permute-done | bytes 65568 | tf_op jit(solution)/shard_map/ppermute | solution.py:746
  31.3 0.6 %collective-permute-start.13 = (f32[72,256]{1,0:T(8,128)S(1)}, f32[72,256]{1,0:T(8,128)S(1)}, u32[]{:S(2)}, u32[]{:S(2)}) collective-permute-start(f32[72,256]{1,0:T(8,128)S(1)} %get-tuple-element.56.refs_0_), channel_id=1, source_target_pairs={{0,16},{8,24},{16,0},{24,8},{1,17},{9,25},{17,1},{25,9},{2,18},{10... | collective-permute-start | bytes 221192 | tf_op jit(solution)/shard_map/ppermute | solution.py:746
  31.9 1.6 %collective-permute-start.15 = (f32[8,256]{1,0:T(8,128)S(1)}, f32[8,256]{1,0:T(8,128)S(1)}, u32[]{:S(2)}, u32[]{:S(2)}) collective-permute-start(f32[8,256]{1,0:T(8,128)S(1)} %get-tuple-element.57), channel_id=1, source_target_pairs={{0,24},{8,16},{16,8},{24,0},{1,25},{9,17},{17,9},{25,1},{2,26},{10... | collective-permute-start | bytes 24584 | tf_op jit(solution)/shard_map/ppermute | solution.py:746
  33.5 1.5 %collective-permute-done.15.refs_3_ = f32[8,256]{1,0:T(8,128)S(1)} collective-permute-done((f32[8,256]{1,0:T(8,128)S(1)}, f32[8,256]{1,0:T(8,128)S(1)}, u32[]{:S(2)}, u32[]{:S(2)}) %collective-permute-start.15) | collective-permute-done | bytes 8224 | tf_op jit(solution)/shard_map/ppermute | solution.py:746
  35.0 0.8 %collective-permute-done.13.refs_1_ = f32[72,256]{1,0:T(8,128)S(1)} collective-permute-done((f32[72,256]{1,0:T(8,128)S(1)}, f32[72,256]{1,0:T(8,128)S(1)}, u32[]{:S(2)}, u32[]{:S(2)}) %collective-permute-start.13) | collective-permute-done | bytes 73760 | tf_op jit(solution)/shard_map/ppermute | solution.py:746
  35.7 1.3 %filter_all.1 = f32[4,4,8,1800]{3,2,1,0:T(8,128)} custom-call(f32[72,256]{1,0:T(8,128)S(1)} %get-tuple-element.56.refs_0_, f32[72,256]{1,0:T(8,128)S(1)} %collective-permute-done.13.refs_1_, f32[8,256]{1,0:T(8,128)S(1)} %collective-permute-done.14.refs_2_, f32[8,256]{1,0:T(8,128)S(1)} %collective-permute-done.15.refs_3_, ...), custom_call_target="tpu_custom_call" | custom-call | tf_op jit(solution)/shard_map/filter_all/pallas_call | solution.py:825
  (43 shorter events, 4.6 us)
Async XLA Ops:
  1.6 9.1 %collective-permute-start = (f32[8,128]{1,0:T(8,128)S(1)}, f32[8,128]{1,0:T(8,128)S(1)}, u32[]{:S(2)}, u32[]{:S(2)}) collective-permute-start(f32[8,128]{1,0:T(8,128)S(1)} %get-tuple-element.33), channel_id=1, source_target_pairs={{0,8},{8,0},{16,24},{24,16},{1,9},{9,1},{17,25},{25,17},{2,10},{10... | collective-permute-start | bytes 12296 | tf_op jit(solution)/shard_map/ppermute | solution.py:766
  2.1 8.6 %collective-permute-start.1 = (f32[8,128]{1,0:T(8,128)S(1)}, f32[8,128]{1,0:T(8,128)S(1)}, u32[]{:S(2)}, u32[]{:S(2)}) collective-permute-start(f32[8,128]{1,0:T(8,128)S(1)} %get-tuple-element.34), channel_id=1, source_target_pairs={{0,24},{8,16},{16,8},{24,0},{1,25},{9,17},{17,9},{25,1},{2,26},{10... | collective-permute-start | bytes 12296 | tf_op jit(solution)/shard_map/ppermute | solution.py:767
  4.7 9.9 %collective-permute-start.2 = (f32[8,6528]{1,0:T(8,128)S(1)}, f32[8,6528]{1,0:T(8,128)S(1)}, u32[]{:S(2)}, u32[]{:S(2)}) collective-permute-start(f32[8,6528]{1,0:T(8,128)S(1)} %get-tuple-element.36), channel_id=1, source_target_pairs={{2,4},{4,2},{3,5},{5,3},{10,12},{12,10},{11,13},{13,11},{18,20},{2... | collective-permute-start | bytes 626696 | tf_op jit(solution)/shard_map/ppermute | solution.py:763
  5.4 9.7 %collective-permute-start.3 = (f32[8,6528]{1,0:T(8,128)S(1)}, f32[8,6528]{1,0:T(8,128)S(1)}, u32[]{:S(2)}, u32[]{:S(2)}) collective-permute-start(f32[8,6528]{1,0:T(8,128)S(1)} %get-tuple-element.37), channel_id=1, source_target_pairs={{0,2},{2,0},{4,6},{6,4},{1,3},{3,1},{5,7},{7,5},{8,10},{10,8},{12,... | collective-permute-start | bytes 626696 | tf_op jit(solution)/shard_map/ppermute | solution.py:764
  10.9 4.4 %collective-permute-start.4 = (f32[8,512]{1,0:T(8,128)S(1)}, f32[8,512]{1,0:T(8,128)S(1)}, u32[]{:S(2)}, u32[]{:S(2)}) collective-permute-start(f32[8,512]{1,0:T(8,128)S(1)} %get-tuple-element.41), channel_id=1, source_target_pairs={{2,4},{4,2},{3,5},{5,3},{10,12},{12,10},{11,13},{13,11},{18,20},{2... | collective-permute-start | bytes 49160 | tf_op jit(solution)/shard_map/ppermute | solution.py:776
  11.5 3.8 %collective-permute-start.5 = (f32[8,512]{1,0:T(8,128)S(1)}, f32[8,512]{1,0:T(8,128)S(1)}, u32[]{:S(2)}, u32[]{:S(2)}) collective-permute-start(f32[8,512]{1,0:T(8,128)S(1)} %get-tuple-element.42), channel_id=1, source_target_pairs={{0,2},{2,0},{4,6},{6,4},{1,3},{3,1},{5,7},{7,5},{8,10},{10,8},{12,... | collective-permute-start | bytes 49160 | tf_op jit(solution)/shard_map/ppermute | solution.py:777
  15.3 2.7 %copy-start = (bf16[1920,256]{1,0:T(8,128)(2,1)S(1)}, bf16[1920,256]{1,0:T(8,128)(2,1)}, u32[]{:S(2)}) copy-start(bf16[1920,256]{1,0:T(8,128)(2,1)} %constant.59.clone.wh) | copy-start | bytes 2949124
  15.3 2.7 %copy-start.1 = (bf16[1920,256]{1,0:T(8,128)(2,1)S(1)}, bf16[1920,256]{1,0:T(8,128)(2,1)}, u32[]{:S(2)}) copy-start(bf16[1920,256]{1,0:T(8,128)(2,1)} %constant.60.clone.wl) | copy-start | bytes 2949124
  15.4 4.5 %collective-permute-start.6 = (f32[8,2432]{1,0:T(8,128)S(1)}, f32[8,2432]{1,0:T(8,128)S(1)}, u32[]{:S(2)}, u32[]{:S(2)}) collective-permute-start(f32[8,2432]{1,0:T(8,128)S(1)} %get-tuple-element.44), channel_id=1, source_target_pairs={{0,1},{1,0},{2,3},{3,2},{4,5},{5,4},{6,7},{7,6},{8,9},{9,8},{10,11... | collective-permute-start | bytes 233480 | tf_op jit(solution)/shard_map/ppermute | solution.py:737
  17.0 1.1 %copy-start.4 = (s32[16,128]{1,0:T(8,128)S(1)}, s32[16,128]{1,0:T(8,128)}, u32[]{:S(2)}) copy-start(s32[16,128]{1,0:T(8,128)} %row_code.1.code.refs_9_) | copy-start | bytes 24580
  18.8 1.4 %collective-permute-start.7 = (f32[88,256]{1,0:T(8,128)S(1)}, f32[88,256]{1,0:T(8,128)S(1)}, u32[]{:S(2)}, u32[]{:S(2)}) collective-permute-start(f32[88,256]{1,0:T(8,128)S(1)} %tile_and_ring_spectra.1.part), channel_id=1, source_target_pairs={{0,8},{8,0},{16,24},{24,16},{1,9},{9,1},{17,25},{25,17},{2,10},{10... | collective-permute-start | bytes 270344 | tf_op jit(solution)/shard_map/ppermute | solution.py:746
  20.1 5.8 %copy-start.2 = (bf16[256,1920]{1,0:T(8,128)(2,1)S(1)}, bf16[256,1920]{1,0:T(8,128)(2,1)}, u32[]{:S(2)}) copy-start(bf16[256,1920]{1,0:T(8,128)(2,1)} %constant.61.clone.refs_6_.wh) | copy-start | bytes 2949124
  20.1 5.8 %copy-start.3 = (bf16[256,1920]{1,0:T(8,128)(2,1)S(1)}, bf16[256,1920]{1,0:T(8,128)(2,1)}, u32[]{:S(2)}) copy-start(bf16[256,1920]{1,0:T(8,128)(2,1)} %constant.62.clone.refs_7_.wl) | copy-start | bytes 2949124
  20.7 5.3 %collective-permute-start.8 = (f32[104,256]{1,0:T(8,128)S(1)}, f32[104,256]{1,0:T(8,128)S(1)}, u32[]{:S(2)}, u32[]{:S(2)}) collective-permute-start(f32[104,256]{1,0:T(8,128)S(1)} %get-tuple-element.48.refs_0_), channel_id=1, source_target_pairs={{0,16},{8,24},{16,0},{24,8},{1,17},{9,25},{17,1},{25,9},{2,18},{10... | collective-permute-start | bytes 319496 | tf_op jit(solution)/shard_map/ppermute | solution.py:746
  21.2 1.6 %collective-permute-start.9 = (f32[16,256]{1,0:T(8,128)S(1)}, f32[16,256]{1,0:T(8,128)S(1)}, u32[]{:S(2)}, u32[]{:S(2)}) collective-permute-start(f32[16,256]{1,0:T(8,128)S(1)} %get-tuple-element.49), channel_id=1, source_target_pairs={{0,8},{8,0},{16,24},{24,16},{1,9},{9,1},{17,25},{25,17},{2,10},{10... | collective-permute-start | bytes 49160 | tf_op jit(solution)/shard_map/ppermute | solution.py:746
  21.2 4.1 %collective-permute-start.10 = (f32[16,256]{1,0:T(8,128)S(1)}, f32[16,256]{1,0:T(8,128)S(1)}, u32[]{:S(2)}, u32[]{:S(2)}) collective-permute-start(f32[16,256]{1,0:T(8,128)S(1)} %get-tuple-element.49), channel_id=1, source_target_pairs={{0,24},{8,16},{16,8},{24,0},{1,25},{9,17},{17,9},{25,1},{2,26},{10... | collective-permute-start | bytes 49160 | tf_op jit(solution)/shard_map/ppermute | solution.py:746
  26.5 4.4 %collective-permute-start.11 = (f32[8,2176]{1,0:T(8,128)S(1)}, f32[8,2176]{1,0:T(8,128)S(1)}, u32[]{:S(2)}, u32[]{:S(2)}) collective-permute-start(f32[8,2176]{1,0:T(8,128)S(1)} %get-tuple-element.50), channel_id=1, source_target_pairs={{0,1},{1,0},{2,3},{3,2},{4,5},{5,4},{6,7},{7,6},{8,9},{9,8},{10,11... | collective-permute-start | bytes 208904 | tf_op jit(solution)/shard_map/ppermute | solution.py:737
  29.3 1.3 %collective-permute-start.12 = (f32[64,256]{1,0:T(8,128)S(1)}, f32[64,256]{1,0:T(8,128)S(1)}, u32[]{:S(2)}, u32[]{:S(2)}) collective-permute-start(f32[64,256]{1,0:T(8,128)S(1)} %tile_spectra.1.part), channel_id=1, source_target_pairs={{0,8},{8,0},{16,24},{24,16},{1,9},{9,1},{17,25},{25,17},{2,10},{10... | collective-permute-start | bytes 196616 | tf_op jit(solution)/shard_map/ppermute | solution.py:746
  31.3 4.4 %collective-permute-start.13 = (f32[72,256]{1,0:T(8,128)S(1)}, f32[72,256]{1,0:T(8,128)S(1)}, u32[]{:S(2)}, u32[]{:S(2)}) collective-permute-start(f32[72,256]{1,0:T(8,128)S(1)} %get-tuple-element.56.refs_0_), channel_id=1, source_target_pairs={{0,16},{8,24},{16,0},{24,8},{1,17},{9,25},{17,1},{25,9},{2,18},{10... | collective-permute-start | bytes 221192 | tf_op jit(solution)/shard_map/ppermute | solution.py:746
  31.9 1.6 %collective-permute-start.14 = (f32[8,256]{1,0:T(8,128)S(1)}, f32[8,256]{1,0:T(8,128)S(1)}, u32[]{:S(2)}, u32[]{:S(2)}) collective-permute-start(f32[8,256]{1,0:T(8,128)S(1)} %get-tuple-element.57), channel_id=1, source_target_pairs={{0,8},{8,0},{16,24},{24,16},{1,9},{9,1},{17,25},{25,17},{2,10},{10... | collective-permute-start | bytes 24584 | tf_op jit(solution)/shard_map/ppermute | solution.py:746
  31.9 3.1 %collective-permute-start.15 = (f32[8,256]{1,0:T(8,128)S(1)}, f32[8,256]{1,0:T(8,128)S(1)}, u32[]{:S(2)}, u32[]{:S(2)}) collective-permute-start(f32[8,256]{1,0:T(8,128)S(1)} %get-tuple-element.57), channel_id=1, source_target_pairs={{0,24},{8,16},{16,8},{24,0},{1,25},{9,17},{17,9},{25,1},{2,26},{10... | collective-permute-start | bytes 24584 | tf_op jit(solution)/shard_map/ppermute | solution.py:746

commit v10 on v9

--- a/solution.py
+++ b/solution.py
@@ -139,10 +139,9 @@
     return (near, far), (z.R - 1 - near, z.R - 1 - far)
 
 
-def edge_rows(z, x, m1, m2, after):
+def edges(z, x, m1, m2, e1, e2):
     L, B = z.L, z.base
     fold = z.fold * LANES
-    after[...] = jnp.zeros(after.shape, jnp.float32)
     for msg, (near, far) in zip((m1, m2), near_and_far(z)):
         msg[:, 3 * B :] = jnp.zeros((z.R, z.lat_lanes - 3 * B), jnp.float32)
         for k in range(7):
@@ -159,10 +158,6 @@
         for t in range(B // LANES):
             at = 3 * B + fold + t // z.R * LANES
             msg[t % z.R : t % z.R + 1, at : at + LANES] = row[:, t * LANES : (t + 1) * LANES]
-
-
-def edge_columns(z, x, after, e1, e2):
-    del after
     left, right = edge_tiles(
         z,
         z.planes,
@@ -759,10 +754,9 @@
     tile = (R, LANES)
     x = jnp.concatenate([fields.reshape(4 * L, R, z.C), surface[None]], 0)
     x = jnp.pad(x, ((0, 0), (0, 0), (0, W - z.C)))
-    m1, m2, after = call(edge_rows, [(R, z.lat_lanes)] * 2 + [tile], [x])
+    m1, m2, e1, e2 = call(edges, [(R, z.lat_lanes)] * 2 + [tile] * 2, [x])
     m1 = lax.ppermute(m1, "lat", lat_one)
     m2 = lax.ppermute(m2, "lat", lat_two)
-    e1, e2 = call(edge_columns, [tile, tile], [x, after])
     e1 = lax.ppermute(e1, "lon", lon_one)
     e2 = lax.ppermute(e2, "lon", lon_two)
     tails = (R, 4 * (W - z.base))

time: 37.2 us -> 37.1 us (level)
    pallas_call x12 -> x11, Pallas kernels: 5.73 us -> 5.64 us  [call(): pl.pallas_call(functools.partial(kernel, z), out_shape=[jax.ShapeDtypeStr...]
where the time goes in v10:
time: 37.1 us; the launch traced here: 37 us
  starting transfers between devices  17.7 us (48%)
  waiting for transfers between devices  8.65 us (23%)
  Pallas kernels  8.26 us (22%)
  other arithmetic  2.06 us (6%)
    ppermute x8, waiting for transfers between devices, lon_swap(): return lax.ppermute(value, 'lon', [(i, i ^ step) for i in range(z.n_lon)])  6.8 us
    pallas_call x11, Pallas kernels, call(): pl.pallas_call(functools.partial(kernel, z), out_shape=[jax.ShapeDtypeStr...  5.64 us
    ppermute x8, starting transfers between devices, lon_swap(): return lax.ppermute(value, 'lon', [(i, i ^ step) for i in range(z.n_lon)])  4.55 us
    ppermute x1, starting transfers between devices, local(): m2 = lax.ppermute(m2, 'lat', lat_two)  4.45 us
    ppermute x1, starting transfers between devices, local(): e2 = lax.ppermute(e2, 'lon', lon_two)  2.64 us
    ppermute x2, starting transfers between devices, from_below(): return lax.ppermute(column, 'lev', [(0, 1), (1, 0)])  2.46 us
    ppermute x1, starting transfers between devices, local(): t2 = lax.ppermute(t2, 'lat', lat_two)  1.8 us
    pallas_call x1, Pallas kernels, local(): pl.pallas_call(functools.partial(row_code, z), out_shape=jax.ShapeDtypeSt...  1.31 us
  transfers between devices with their start and end apart: 16, of which 10 were waited for; matrix products, arithmetic and copies ran while one was open for 2% of the time, Pallas kernels for 14%

profile of v10, /device:TPU:0, one launch (start us, length us, event | category | flops | bytes accessed | tf_op | source)
XLA Modules:
  0.0 37.0 jit_solution(7132188398470884125)
XLA Ops:
  0.0 1.3 %select_maximum_fusion.x.x_in = f32[17,8,1920]{2,1,0:T(8,128)S(1)} fusion(f32[1,8,1800]{2,1,0:T(8,128)} %bitcast.5, f32[16,8,1800]{2,1,0:T(8,128)} %bitcast.4), kind=kLoop, calls=%fused_computation | loop fusion | flops 1044480 | bytes 2023680 | tf_op jit(solution)/shard_map/concatenate | solution.py:755
  2.0 2.6 %collective-permute-start.1 = (f32[8,128]{1,0:T(8,128)S(1)}, f32[8,128]{1,0:T(8,128)S(1)}, u32[]{:S(2)}, u32[]{:S(2)}) collective-permute-start(f32[8,128]{1,0:T(8,128)S(1)} %get-tuple-element.32), channel_id=1, source_target_pairs={{0,24},{8,16},{16,8},{24,0},{1,25},{9,17},{17,9},{25,1},{2,26},{10... | collective-permute-start | bytes 12296 | tf_op jit(solution)/shard_map/ppermute | solution.py:761
  4.7 0.7 %collective-permute-start.2 = (f32[8,6528]{1,0:T(8,128)S(1)}, f32[8,6528]{1,0:T(8,128)S(1)}, u32[]{:S(2)}, u32[]{:S(2)}) collective-permute-start(f32[8,6528]{1,0:T(8,128)S(1)} %get-tuple-element.34), channel_id=1, source_target_pairs={{2,4},{4,2},{3,5},{5,3},{10,12},{12,10},{11,13},{13,11},{18,20},{2... | collective-permute-start | bytes 626696 | tf_op jit(solution)/shard_map/ppermute | solution.py:758
  5.3 4.5 %collective-permute-start.3 = (f32[8,6528]{1,0:T(8,128)S(1)}, f32[8,6528]{1,0:T(8,128)S(1)}, u32[]{:S(2)}, u32[]{:S(2)}) collective-permute-start(f32[8,6528]{1,0:T(8,128)S(1)} %get-tuple-element.35), channel_id=1, source_target_pairs={{0,2},{2,0},{4,6},{6,4},{1,3},{3,1},{5,7},{7,5},{8,10},{10,8},{12,... | collective-permute-start | bytes 626696 | tf_op jit(solution)/shard_map/ppermute | solution.py:759
  10.8 0.7 %collective-permute-start.4 = (f32[8,512]{1,0:T(8,128)S(1)}, f32[8,512]{1,0:T(8,128)S(1)}, u32[]{:S(2)}, u32[]{:S(2)}) collective-permute-start(f32[8,512]{1,0:T(8,128)S(1)} %get-tuple-element.39), channel_id=1, source_target_pairs={{2,4},{4,2},{3,5},{5,3},{10,12},{12,10},{11,13},{13,11},{18,20},{2... | collective-permute-start | bytes 49160 | tf_op jit(solution)/shard_map/ppermute | solution.py:770
  11.4 1.8 %collective-permute-start.5 = (f32[8,512]{1,0:T(8,128)S(1)}, f32[8,512]{1,0:T(8,128)S(1)}, u32[]{:S(2)}, u32[]{:S(2)}) collective-permute-start(f32[8,512]{1,0:T(8,128)S(1)} %get-tuple-element.40), channel_id=1, source_target_pairs={{0,2},{2,0},{4,6},{6,4},{1,3},{3,1},{5,7},{7,5},{8,10},{10,8},{12,... | collective-permute-start | bytes 49160 | tf_op jit(solution)/shard_map/ppermute | solution.py:771
  13.2 1.3 %row_code.1.code.refs_9_ = s32[16,128]{1,0:T(8,128)} custom-call(s32[16]{0:T(128)} %rows.1, s32[16]{0:T(128)} %counts.1), custom_call_target="tpu_custom_call" | custom-call | tf_op jit(solution)/shard_map/row_code/pallas_call | solution.py:717
  15.3 1.6 %collective-permute-start.6 = (f32[8,2432]{1,0:T(8,128)S(1)}, f32[8,2432]{1,0:T(8,128)S(1)}, u32[]{:S(2)}, u32[]{:S(2)}) collective-permute-start(f32[8,2432]{1,0:T(8,128)S(1)} %get-tuple-element.42), channel_id=1, source_target_pairs={{0,1},{1,0},{2,3},{3,2},{4,5},{5,4},{6,7},{7,6},{8,9},{9,8},{10,11... | collective-permute-start | bytes 233480 | tf_op jit(solution)/shard_map/ppermute | solution.py:732
  16.9 1.0 %first_step.1 = (f32[16,8,1920]{2,1,0:T(8,128)S(1)}, f32[3,8,1920]{2,1,0:T(8,128)S(1)}) custom-call(f32[17,8,1920]{2,1,0:T(8,128)S(1)} %get-tuple-element.33.x, f32[7,8,1920]{2,1,0:T(8,128)S(1)} %get-tuple-element.43.ring, f32[5,16,128]{2,1,0:T(8,128)S(1)} %constant_dynamic-update-slice_fusion.geom), custom_call_target="tpu_custom_call" | custom-call | flops 10000000 | bytes 2682880 | tf_op jit(solution)/shard_map/first_step/pallas_call | solution.py:682
  17.9 0.7 %tile_and_ring_spectra.1.part = f32[88,256]{1,0:T(8,128)S(1)} custom-call(f32[16,8,1920]{2,1,0:T(8,128)S(1)} %get-tuple-element.44.y.refs_4_.state, f32[3,8,1920]{2,1,0:T(8,128)S(1)} %get-tuple-element.45.yring.refs_5_.sring, bf16[1920,256]{1,0:T(8,128)(2,1)S(1)} %copy-done, bf16[1920,256]{1,0:T(8,128)(2,1)S(1)} %copy-done.1, ...), custom_call_target="tpu_custom_call" | custom-call | flops 1000000 | bytes 3232768 | tf_op jit(solution)/shard_map/tile_and_ring_spectra/pallas_call | solution.py:682
  18.8 1.0 %collective-permute-done.6.got = f32[8,2432]{1,0:T(8,128)S(1)} collective-permute-done((f32[8,2432]{1,0:T(8,128)S(1)}, f32[8,2432]{1,0:T(8,128)S(1)}, u32[]{:S(2)}, u32[]{:S(2)}) %collective-permute-start.6) | collective-permute-done | bytes 77856 | tf_op jit(solution)/shard_map/ppermute | solution.py:732
  20.6 0.6 %collective-permute-start.8 = (f32[104,256]{1,0:T(8,128)S(1)}, f32[104,256]{1,0:T(8,128)S(1)}, u32[]{:S(2)}, u32[]{:S(2)}) collective-permute-start(f32[104,256]{1,0:T(8,128)S(1)} %get-tuple-element.46.refs_0_), channel_id=1, source_target_pairs={{0,16},{8,24},{16,0},{24,8},{1,17},{9,25},{17,1},{25,9},{2,18},{10... | collective-permute-start | bytes 319496 | tf_op jit(solution)/shard_map/ppermute | solution.py:741
  21.1 1.6 %collective-permute-start.10 = (f32[16,256]{1,0:T(8,128)S(1)}, f32[16,256]{1,0:T(8,128)S(1)}, u32[]{:S(2)}, u32[]{:S(2)}) collective-permute-start(f32[16,256]{1,0:T(8,128)S(1)} %get-tuple-element.47), channel_id=1, source_target_pairs={{0,24},{8,16},{16,8},{24,0},{1,25},{9,17},{17,9},{25,1},{2,26},{10... | collective-permute-start | bytes 49160 | tf_op jit(solution)/shard_map/ppermute | solution.py:741
  22.8 2.4 %collective-permute-done.10.refs_3_ = f32[16,256]{1,0:T(8,128)S(1)} collective-permute-done((f32[16,256]{1,0:T(8,128)S(1)}, f32[16,256]{1,0:T(8,128)S(1)}, u32[]{:S(2)}, u32[]{:S(2)}) %collective-permute-start.10) | collective-permute-done | bytes 16416 | tf_op jit(solution)/shard_map/ppermute | solution.py:741
  25.2 0.6 %collective-permute-done.8.refs_1_ = f32[104,256]{1,0:T(8,128)S(1)} collective-permute-done((f32[104,256]{1,0:T(8,128)S(1)}, f32[104,256]{1,0:T(8,128)S(1)}, u32[]{:S(2)}, u32[]{:S(2)}) %collective-permute-start.8) | collective-permute-done | bytes 106528 | tf_op jit(solution)/shard_map/ppermute | solution.py:741
  26.4 0.9 %collective-permute-start.11 = (f32[8,2176]{1,0:T(8,128)S(1)}, f32[8,2176]{1,0:T(8,128)S(1)}, u32[]{:S(2)}, u32[]{:S(2)}) collective-permute-start(f32[8,2176]{1,0:T(8,128)S(1)} %get-tuple-element.48), channel_id=1, source_target_pairs={{0,1},{1,0},{2,3},{3,2},{4,5},{5,4},{6,7},{7,6},{8,9},{9,8},{10,11... | collective-permute-start | bytes 208904 | tf_op jit(solution)/shard_map/ppermute | solution.py:732
  27.3 1.3 %second_step.1.y.refs_4_ = f32[16,8,1920]{2,1,0:T(8,128)S(1)} custom-call(f32[16,8,1920]{2,1,0:T(8,128)S(1)} %get-tuple-element.44.y.refs_4_.state, f32[3,8,1920]{2,1,0:T(8,128)S(1)} %get-tuple-element.45.yring.refs_5_.sring, f32[2,8,1920]{2,1,0:T(8,128)S(1)} %get-tuple-element.49.change, f32[8,1920]{1,0:T(8,128)S(1)} %get-tuple-element.50.ring_change, ...), custom_call_target="tpu_custom_call" | custom-call | flops 10000000 | bytes 5038080 | tf_op jit(solution)/shard_map/second_step/pallas_call | solution.py:682
  28.6 0.6 %tile_spectra.1.part = f32[64,256]{1,0:T(8,128)S(1)} custom-call(f32[16,8,1920]{2,1,0:T(8,128)S(1)} %second_step.1.y.refs_4_, bf16[1920,256]{1,0:T(8,128)(2,1)S(1)} %copy-done, bf16[1920,256]{1,0:T(8,128)(2,1)S(1)} %copy-done.1, f32[2,128]{1,0:T(2,128)S(1)} %pad_maximum_fusion.phase.refs_8_, s32[16,128]{1,0:T(8,128)S(1)} %copy-done.4), custom_call_target="tpu_custom_call" | custom-call | flops 1000000 | bytes 3023872 | tf_op jit(solution)/shard_map/tile_spectra/pallas_call | solution.py:682
  29.2 1.2 %collective-permute-done.12.part_got = f32[64,256]{1,0:T(8,128)S(1)} collective-permute-done((f32[64,256]{1,0:T(8,128)S(1)}, f32[64,256]{1,0:T(8,128)S(1)}, u32[]{:S(2)}, u32[]{:S(2)}) %collective-permute-start.12) | collective-permute-done | bytes 65568 | tf_op jit(solution)/shard_map/ppermute | solution.py:741
  31.2 0.6 %collective-permute-start.13 = (f32[72,256]{1,0:T(8,128)S(1)}, f32[72,256]{1,0:T(8,128)S(1)}, u32[]{:S(2)}, u32[]{:S(2)}) collective-permute-start(f32[72,256]{1,0:T(8,128)S(1)} %get-tuple-element.54.refs_0_), channel_id=1, source_target_pairs={{0,16},{8,24},{16,0},{24,8},{1,17},{9,25},{17,1},{25,9},{2,18},{10... | collective-permute-start | bytes 221192 | tf_op jit(solution)/shard_map/ppermute | solution.py:741
  31.8 1.6 %collective-permute-start.15 = (f32[8,256]{1,0:T(8,128)S(1)}, f32[8,256]{1,0:T(8,128)S(1)}, u32[]{:S(2)}, u32[]{:S(2)}) collective-permute-start(f32[8,256]{1,0:T(8,128)S(1)} %get-tuple-element.55), channel_id=1, source_target_pairs={{0,24},{8,16},{16,8},{24,0},{1,25},{9,17},{17,9},{25,1},{2,26},{10... | collective-permute-start | bytes 24584 | tf_op jit(solution)/shard_map/ppermute | solution.py:741
  33.4 1.5 %collective-permute-done.15.refs_3_ = f32[8,256]{1,0:T(8,128)S(1)} collective-permute-done((f32[8,256]{1,0:T(8,128)S(1)}, f32[8,256]{1,0:T(8,128)S(1)}, u32[]{:S(2)}, u32[]{:S(2)}) %collective-permute-start.15) | collective-permute-done | bytes 8224 | tf_op jit(solution)/shard_map/ppermute | solution.py:741
  34.9 0.8 %collective-permute-done.13.refs_1_ = f32[72,256]{1,0:T(8,128)S(1)} collective-permute-done((f32[72,256]{1,0:T(8,128)S(1)}, f32[72,256]{1,0:T(8,128)S(1)}, u32[]{:S(2)}, u32[]{:S(2)}) %collective-permute-start.13) | collective-permute-done | bytes 73760 | tf_op jit(solution)/shard_map/ppermute | solution.py:741
  35.7 1.3 %filter_all.1 = f32[4,4,8,1800]{3,2,1,0:T(8,128)} custom-call(f32[72,256]{1,0:T(8,128)S(1)} %get-tuple-element.54.refs_0_, f32[72,256]{1,0:T(8,128)S(1)} %collective-permute-done.13.refs_1_, f32[8,256]{1,0:T(8,128)S(1)} %collective-permute-done.14.refs_2_, f32[8,256]{1,0:T(8,128)S(1)} %collective-permute-done.15.refs_3_, ...), custom_call_target="tpu_custom_call" | custom-call | tf_op jit(solution)/shard_map/filter_all/pallas_call | solution.py:819
  (42 shorter events, 4.6 us)
Async XLA Ops:
  1.5 9.1 %collective-permute-start = (f32[8,128]{1,0:T(8,128)S(1)}, f32[8,128]{1,0:T(8,128)S(1)}, u32[]{:S(2)}, u32[]{:S(2)}) collective-permute-start(f32[8,128]{1,0:T(8,128)S(1)} %get-tuple-element.31), channel_id=1, source_target_pairs={{0,8},{8,0},{16,24},{24,16},{1,9},{9,1},{17,25},{25,17},{2,10},{10... | collective-permute-start | bytes 12296 | tf_op jit(solution)/shard_map/ppermute | solution.py:760
  2.0 8.6 %collective-permute-start.1 = (f32[8,128]{1,0:T(8,128)S(1)}, f32[8,128]{1,0:T(8,128)S(1)}, u32[]{:S(2)}, u32[]{:S(2)}) collective-permute-start(f32[8,128]{1,0:T(8,128)S(1)} %get-tuple-element.32), channel_id=1, source_target_pairs={{0,24},{8,16},{16,8},{24,0},{1,25},{9,17},{17,9},{25,1},{2,26},{10... | collective-permute-start | bytes 12296 | tf_op jit(solution)/shard_map/ppermute | solution.py:761
  4.7 9.9 %collective-permute-start.2 = (f32[8,6528]{1,0:T(8,128)S(1)}, f32[8,6528]{1,0:T(8,128)S(1)}, u32[]{:S(2)}, u32[]{:S(2)}) collective-permute-start(f32[8,6528]{1,0:T(8,128)S(1)} %get-tuple-element.34), channel_id=1, source_target_pairs={{2,4},{4,2},{3,5},{5,3},{10,12},{12,10},{11,13},{13,11},{18,20},{2... | collective-permute-start | bytes 626696 | tf_op jit(solution)/shard_map/ppermute | solution.py:758
  5.3 9.7 %collective-permute-start.3 = (f32[8,6528]{1,0:T(8,128)S(1)}, f32[8,6528]{1,0:T(8,128)S(1)}, u32[]{:S(2)}, u32[]{:S(2)}) collective-permute-start(f32[8,6528]{1,0:T(8,128)S(1)} %get-tuple-element.35), channel_id=1, source_target_pairs={{0,2},{2,0},{4,6},{6,4},{1,3},{3,1},{5,7},{7,5},{8,10},{10,8},{12,... | collective-permute-start | bytes 626696 | tf_op jit(solution)/shard_map/ppermute | solution.py:759
  10.8 4.4 %collective-permute-start.4 = (f32[8,512]{1,0:T(8,128)S(1)}, f32[8,512]{1,0:T(8,128)S(1)}, u32[]{:S(2)}, u32[]{:S(2)}) collective-permute-start(f32[8,512]{1,0:T(8,128)S(1)} %get-tuple-element.39), channel_id=1, source_target_pairs={{2,4},{4,2},{3,5},{5,3},{10,12},{12,10},{11,13},{13,11},{18,20},{2... | collective-permute-start | bytes 49160 | tf_op jit(solution)/shard_map/ppermute | solution.py:770
  11.4 3.8 %collective-permute-start.5 = (f32[8,512]{1,0:T(8,128)S(1)}, f32[8,512]{1,0:T(8,128)S(1)}, u32[]{:S(2)}, u32[]{:S(2)}) collective-permute-start(f32[8,512]{1,0:T(8,128)S(1)} %get-tuple-element.40), channel_id=1, source_target_pairs={{0,2},{2,0},{4,6},{6,4},{1,3},{3,1},{5,7},{7,5},{8,10},{10,8},{12,... | collective-permute-start | bytes 49160 | tf_op jit(solution)/shard_map/ppermute | solution.py:771
  15.2 2.7 %copy-start = (bf16[1920,256]{1,0:T(8,128)(2,1)S(1)}, bf16[1920,256]{1,0:T(8,128)(2,1)}, u32[]{:S(2)}) copy-start(bf16[1920,256]{1,0:T(8,128)(2,1)} %constant.59.clone.wh) | copy-start | bytes 2949124
  15.2 2.7 %copy-start.1 = (bf16[1920,256]{1,0:T(8,128)(2,1)S(1)}, bf16[1920,256]{1,0:T(8,128)(2,1)}, u32[]{:S(2)}) copy-start(bf16[1920,256]{1,0:T(8,128)(2,1)} %constant.60.clone.wl) | copy-start | bytes 2949124
  15.3 4.5 %collective-permute-start.6 = (f32[8,2432]{1,0:T(8,128)S(1)}, f32[8,2432]{1,0:T(8,128)S(1)}, u32[]{:S(2)}, u32[]{:S(2)}) collective-permute-start(f32[8,2432]{1,0:T(8,128)S(1)} %get-tuple-element.42), channel_id=1, source_target_pairs={{0,1},{1,0},{2,3},{3,2},{4,5},{5,4},{6,7},{7,6},{8,9},{9,8},{10,11... | collective-permute-start | bytes 233480 | tf_op jit(solution)/shard_map/ppermute | solution.py:732
  16.9 1.1 %copy-start.4 = (s32[16,128]{1,0:T(8,128)S(1)}, s32[16,128]{1,0:T(8,128)}, u32[]{:S(2)}) copy-start(s32[16,128]{1,0:T(8,128)} %row_code.1.code.refs_9_) | copy-start | bytes 24580
  18.7 1.4 %collective-permute-start.7 = (f32[88,256]{1,0:T(8,128)S(1)}, f32[88,256]{1,0:T(8,128)S(1)}, u32[]{:S(2)}, u32[]{:S(2)}) collective-permute-start(f32[88,256]{1,0:T(8,128)S(1)} %tile_and_ring_spectra.1.part), channel_id=1, source_target_pairs={{0,8},{8,0},{16,24},{24,16},{1,9},{9,1},{17,25},{25,17},{2,10},{10... | collective-permute-start | bytes 270344 | tf_op jit(solution)/shard_map/ppermute | solution.py:741
  20.0 5.8 %copy-start.2 = (bf16[256,1920]{1,0:T(8,128)(2,1)S(1)}, bf16[256,1920]{1,0:T(8,128)(2,1)}, u32[]{:S(2)}) copy-start(bf16[256,1920]{1,0:T(8,128)(2,1)} %constant.61.clone.refs_6_.wh) | copy-start | bytes 2949124
  20.0 5.8 %copy-start.3 = (bf16[256,1920]{1,0:T(8,128)(2,1)S(1)}, bf16[256,1920]{1,0:T(8,128)(2,1)}, u32[]{:S(2)}) copy-start(bf16[256,1920]{1,0:T(8,128)(2,1)} %constant.62.clone.refs_7_.wl) | copy-start | bytes 2949124
  20.6 5.3 %collective-permute-start.8 = (f32[104,256]{1,0:T(8,128)S(1)}, f32[104,256]{1,0:T(8,128)S(1)}, u32[]{:S(2)}, u32[]{:S(2)}) collective-permute-start(f32[104,256]{1,0:T(8,128)S(1)} %get-tuple-element.46.refs_0_), channel_id=1, source_target_pairs={{0,16},{8,24},{16,0},{24,8},{1,17},{9,25},{17,1},{25,9},{2,18},{10... | collective-permute-start | bytes 319496 | tf_op jit(solution)/shard_map/ppermute | solution.py:741
  21.1 1.6 %collective-permute-start.9 = (f32[16,256]{1,0:T(8,128)S(1)}, f32[16,256]{1,0:T(8,128)S(1)}, u32[]{:S(2)}, u32[]{:S(2)}) collective-permute-start(f32[16,256]{1,0:T(8,128)S(1)} %get-tuple-element.47), channel_id=1, source_target_pairs={{0,8},{8,0},{16,24},{24,16},{1,9},{9,1},{17,25},{25,17},{2,10},{10... | collective-permute-start | bytes 49160 | tf_op jit(solution)/shard_map/ppermute | solution.py:741
  21.1 4.1 %collective-permute-start.10 = (f32[16,256]{1,0:T(8,128)S(1)}, f32[16,256]{1,0:T(8,128)S(1)}, u32[]{:S(2)}, u32[]{:S(2)}) collective-permute-start(f32[16,256]{1,0:T(8,128)S(1)} %get-tuple-element.47), channel_id=1, source_target_pairs={{0,24},{8,16},{16,8},{24,0},{1,25},{9,17},{17,9},{25,1},{2,26},{10... | collective-permute-start | bytes 49160 | tf_op jit(solution)/shard_map/ppermute | solution.py:741
  26.4 4.4 %collective-permute-start.11 = (f32[8,2176]{1,0:T(8,128)S(1)}, f32[8,2176]{1,0:T(8,128)S(1)}, u32[]{:S(2)}, u32[]{:S(2)}) collective-permute-start(f32[8,2176]{1,0:T(8,128)S(1)} %get-tuple-element.48), channel_id=1, source_target_pairs={{0,1},{1,0},{2,3},{3,2},{4,5},{5,4},{6,7},{7,6},{8,9},{9,8},{10,11... | collective-permute-start | bytes 208904 | tf_op jit(solution)/shard_map/ppermute | solution.py:732
  29.2 1.3 %collective-permute-start.12 = (f32[64,256]{1,0:T(8,128)S(1)}, f32[64,256]{1,0:T(8,128)S(1)}, u32[]{:S(2)}, u32[]{:S(2)}) collective-permute-start(f32[64,256]{1,0:T(8,128)S(1)} %tile_spectra.1.part), channel_id=1, source_target_pairs={{0,8},{8,0},{16,24},{24,16},{1,9},{9,1},{17,25},{25,17},{2,10},{10... | collective-permute-start | bytes 196616 | tf_op jit(solution)/shard_map/ppermute | solution.py:741
  31.2 4.4 %collective-permute-start.13 = (f32[72,256]{1,0:T(8,128)S(1)}, f32[72,256]{1,0:T(8,128)S(1)}, u32[]{:S(2)}, u32[]{:S(2)}) collective-permute-start(f32[72,256]{1,0:T(8,128)S(1)} %get-tuple-element.54.refs_0_), channel_id=1, source_target_pairs={{0,16},{8,24},{16,0},{24,8},{1,17},{9,25},{17,1},{25,9},{2,18},{10... | collective-permute-start | bytes 221192 | tf_op jit(solution)/shard_map/ppermute | solution.py:741
  31.8 1.6 %collective-permute-start.14 = (f32[8,256]{1,0:T(8,128)S(1)}, f32[8,256]{1,0:T(8,128)S(1)}, u32[]{:S(2)}, u32[]{:S(2)}) collective-permute-start(f32[8,256]{1,0:T(8,128)S(1)} %get-tuple-element.55), channel_id=1, source_target_pairs={{0,8},{8,0},{16,24},{24,16},{1,9},{9,1},{17,25},{25,17},{2,10},{10... | collective-permute-start | bytes 24584 | tf_op jit(solution)/shard_map/ppermute | solution.py:741
  31.8 3.1 %collective-permute-start.15 = (f32[8,256]{1,0:T(8,128)S(1)}, f32[8,256]{1,0:T(8,128)S(1)}, u32[]{:S(2)}, u32[]{:S(2)}) collective-permute-start(f32[8,256]{1,0:T(8,128)S(1)} %get-tuple-element.55), channel_id=1, source_target_pairs={{0,24},{8,16},{16,8},{24,0},{1,25},{9,17},{17,9},{25,1},{2,26},{10... | collective-permute-start | bytes 24584 | tf_op jit(solution)/shard_map/ppermute | solution.py:741

commit v11 on v10

--- a/solution.py
+++ b/solution.py
@@ -133,9 +133,9 @@
 
 
 def near_and_far(z):
-    lat_odd = lax.axis_index("lat") % 2 == 1
-    near = jnp.where(lat_odd, z.R - 1, 0)
-    far = jnp.where(lat_odd, z.R - 2, 1)
+    lat_even = lax.axis_index("lat") % 2 == 0
+    near = jnp.where(lat_even, z.R - 1, 0)
+    far = jnp.where(lat_even, z.R - 2, 1)
     return (near, far), (z.R - 1 - near, z.R - 1 - far)
 
 
@@ -205,7 +205,7 @@
 
 
 def unfold(z, r1, r2, ring, ring_surface):
-    lat_odd = lax.axis_index("lat") % 2 == 1
+    lat_even = lax.axis_index("lat") % 2 == 0
     L, B = z.L, z.base
     fold = z.fold * LANES
 
@@ -221,12 +221,12 @@
             part = source[t % z.R : t % z.R + 1, at : at + LANES]
             ring_surface[here, t * LANES : (t + 1) * LANES] = jnp.broadcast_to(part, (L, LANES))
 
-    @pl.when(lat_odd)
+    @pl.when(lat_even)
     def _():
         place(0, r2)
         place(1, r1)
 
-    @pl.when(jnp.logical_not(lat_odd))
+    @pl.when(jnp.logical_not(lat_even))
     def _():
         place(0, r1)
         place(1, r2)
@@ -234,7 +234,7 @@
 
 def halo_rows(z, ring_in, surface_in, sums, t1, t2, ring, ring_surface, msg):
     del ring_in, surface_in
-    lat_odd = lax.axis_index("lat") % 2 == 1
+    lat_even = lax.axis_index("lat") % 2 == 0
     L, B, T = z.L, z.base, z.W - z.base
     msg[:, 0 : z.W] = sums[...]
     msg[:, z.W :] = jnp.zeros((z.R, 2 * z.extra * LANES), jnp.float32)
@@ -246,12 +246,12 @@
             ring[k, here, B:] = tail[at : at + L, k // 2 * T : (k // 2 + 1) * T]
         ring_surface[here, B:] = tail[L : 2 * L, 3 * T :]
 
-    @pl.when(lat_odd)
+    @pl.when(lat_even)
     def _():
         place(0, t2)
         place(1, t1)
 
-    @pl.when(jnp.logical_not(lat_odd))
+    @pl.when(jnp.logical_not(lat_even))
     def _():
         place(0, t1)
         place(1, t2)
@@ -724,8 +724,8 @@
 
     lon_one = [(i, i ^ 1) for i in range(z.n_lon)]
     lon_two = [(i, (((i + 1) % z.n_lon ^ 1) - 1) % z.n_lon) for i in range(z.n_lon)]
-    lat_two = [(i, i ^ 1) for i in range(z.n_lat) if i ^ 1 < z.n_lat]
-    lat_one = [(i, ((i + 1) ^ 1) - 1) for i in range(1, z.n_lat) if ((i + 1) ^ 1) - 1 < z.n_lat]
+    lat_one = [(i, i ^ 1) for i in range(z.n_lat) if i ^ 1 < z.n_lat]
+    lat_two = [(i, ((i + 1) ^ 1) - 1) for i in range(1, z.n_lat) if ((i + 1) ^ 1) - 1 < z.n_lat]
 
     def from_below(column):
         if z.n_lev == 2:

time: 37.1 us -> 37.2 us (level)
  the two profiles are of different devices: /device:TPU:0 before, /device:TPU:8 now
where the time goes in v11:
time: 37.2 us; the launch traced here: 36.7 us
  starting transfers between devices  15.8 us (42%)
  waiting for transfers between devices  10.3 us (28%)
  Pallas kernels  8.27 us (22%)
  other arithmetic  2.06 us (6%)
    ppermute x8, waiting for transfers between devices, lon_swap(): return lax.ppermute(value, 'lon', [(i, i ^ step) for i in range(z.n_lon)])  6.8 us
    pallas_call x11, Pallas kernels, call(): pl.pallas_call(functools.partial(kernel, z), out_shape=[jax.ShapeDtypeStr...  5.65 us
    ppermute x1, starting transfers between devices, local(): m2 = lax.ppermute(m2, 'lat', lat_two)  4.6 us
    ppermute x8, starting transfers between devices, lon_swap(): return lax.ppermute(value, 'lon', [(i, i ^ step) for i in range(z.n_lon)])  4.55 us
    ppermute x2, starting transfers between devices, from_below(): return lax.ppermute(column, 'lev', [(0, 1), (1, 0)])  2.46 us
    ppermute x1, starting transfers between devices, local(): t2 = lax.ppermute(t2, 'lat', lat_two)  1.92 us
    ppermute x1, starting transfers between devices, local(): e2 = lax.ppermute(e2, 'lon', lon_two)  1.64 us
    ppermute x1, waiting for transfers between devices, local(): t2 = lax.ppermute(t2, 'lat', lat_two)  1.52 us
  transfers between devices with their start and end apart: 16, of which 10 were waited for; matrix products, arithmetic and copies ran while one was open for 2% of the time, Pallas kernels for 14%

profile of v11, /device:TPU:8, one launch (start us, length us, event | category | flops | bytes accessed | tf_op | source)
XLA Modules:
  0.0 36.7 jit_solution(5864863570645425867)
XLA Ops:
  0.0 1.3 %select_maximum_fusion.x.x_in = f32[17,8,1920]{2,1,0:T(8,128)S(1)} fusion(f32[1,8,1800]{2,1,0:T(8,128)} %bitcast.5, f32[16,8,1800]{2,1,0:T(8,128)} %bitcast.4), kind=kLoop, calls=%fused_computation | loop fusion | flops 1044480 | bytes 2023680 | tf_op jit(solution)/shard_map/concatenate | solution.py:755
  1.6 1.6 %collective-permute-start.1 = (f32[8,128]{1,0:T(8,128)S(1)}, f32[8,128]{1,0:T(8,128)S(1)}, u32[]{:S(2)}, u32[]{:S(2)}) collective-permute-start(f32[8,128]{1,0:T(8,128)S(1)} %get-tuple-element.32), channel_id=1, source_target_pairs={{0,24},{8,16},{16,8},{24,0},{1,25},{9,17},{17,9},{25,1},{2,26},{10... | collective-permute-start | bytes 12296 | tf_op jit(solution)/shard_map/ppermute | solution.py:761
  3.7 4.6 %collective-permute-start.3 = (f32[8,6528]{1,0:T(8,128)S(1)}, f32[8,6528]{1,0:T(8,128)S(1)}, u32[]{:S(2)}, u32[]{:S(2)}) collective-permute-start(f32[8,6528]{1,0:T(8,128)S(1)} %get-tuple-element.35), channel_id=1, source_target_pairs={{2,4},{4,2},{3,5},{5,3},{10,12},{12,10},{11,13},{13,11},{18,20},{2... | collective-permute-start | bytes 626696 | tf_op jit(solution)/shard_map/ppermute | solution.py:759
  9.4 1.9 %collective-permute-start.5 = (f32[8,512]{1,0:T(8,128)S(1)}, f32[8,512]{1,0:T(8,128)S(1)}, u32[]{:S(2)}, u32[]{:S(2)}) collective-permute-start(f32[8,512]{1,0:T(8,128)S(1)} %get-tuple-element.40), channel_id=1, source_target_pairs={{2,4},{4,2},{3,5},{5,3},{10,12},{12,10},{11,13},{13,11},{18,20},{2... | collective-permute-start | bytes 49160 | tf_op jit(solution)/shard_map/ppermute | solution.py:771
  11.3 1.3 %row_code.1.code.refs_9_ = s32[16,128]{1,0:T(8,128)} custom-call(s32[16]{0:T(128)} %rows.1, s32[16]{0:T(128)} %counts.1), custom_call_target="tpu_custom_call" | custom-call | tf_op jit(solution)/shard_map/row_code/pallas_call | solution.py:717
  12.6 0.7 %collective-permute-done.3.r2 = f32[8,6528]{1,0:T(8,128)S(1)} collective-permute-done((f32[8,6528]{1,0:T(8,128)S(1)}, f32[8,6528]{1,0:T(8,128)S(1)}, u32[]{:S(2)}, u32[]{:S(2)}) %collective-permute-start.3) | collective-permute-done | bytes 208928 | tf_op jit(solution)/shard_map/ppermute | solution.py:759
  13.5 1.5 %collective-permute-done.5.t2 = f32[8,512]{1,0:T(8,128)S(1)} collective-permute-done((f32[8,512]{1,0:T(8,128)S(1)}, f32[8,512]{1,0:T(8,128)S(1)}, u32[]{:S(2)}, u32[]{:S(2)}) %collective-permute-start.5) | collective-permute-done | bytes 16416 | tf_op jit(solution)/shard_map/ppermute | solution.py:771
  15.1 1.6 %collective-permute-start.6 = (f32[8,2432]{1,0:T(8,128)S(1)}, f32[8,2432]{1,0:T(8,128)S(1)}, u32[]{:S(2)}, u32[]{:S(2)}) collective-permute-start(f32[8,2432]{1,0:T(8,128)S(1)} %get-tuple-element.42), channel_id=1, source_target_pairs={{0,1},{1,0},{2,3},{3,2},{4,5},{5,4},{6,7},{7,6},{8,9},{9,8},{10,11... | collective-permute-start | bytes 233480 | tf_op jit(solution)/shard_map/ppermute | solution.py:732
  16.6 1.0 %first_step.1 = (f32[16,8,1920]{2,1,0:T(8,128)S(1)}, f32[3,8,1920]{2,1,0:T(8,128)S(1)}) custom-call(f32[17,8,1920]{2,1,0:T(8,128)S(1)} %get-tuple-element.33.x, f32[7,8,1920]{2,1,0:T(8,128)S(1)} %get-tuple-element.43.ring, f32[5,16,128]{2,1,0:T(8,128)S(1)} %constant_dynamic-update-slice_fusion.geom), custom_call_target="tpu_custom_call" | custom-call | flops 10000000 | bytes 2682880 | tf_op jit(solution)/shard_map/first_step/pallas_call | solution.py:682
  17.7 0.7 %tile_and_ring_spectra.1.part = f32[88,256]{1,0:T(8,128)S(1)} custom-call(f32[16,8,1920]{2,1,0:T(8,128)S(1)} %get-tuple-element.44.y.refs_4_.state, f32[3,8,1920]{2,1,0:T(8,128)S(1)} %get-tuple-element.45.yring.refs_5_.sring, bf16[1920,256]{1,0:T(8,128)(2,1)S(1)} %copy-done, bf16[1920,256]{1,0:T(8,128)(2,1)S(1)} %copy-done.1, ...), custom_call_target="tpu_custom_call" | custom-call | flops 1000000 | bytes 3232768 | tf_op jit(solution)/shard_map/tile_and_ring_spectra/pallas_call | solution.py:682
  18.5 1.0 %collective-permute-done.6.got = f32[8,2432]{1,0:T(8,128)S(1)} collective-permute-done((f32[8,2432]{1,0:T(8,128)S(1)}, f32[8,2432]{1,0:T(8,128)S(1)}, u32[]{:S(2)}, u32[]{:S(2)}) %collective-permute-start.6) | collective-permute-done | bytes 77856 | tf_op jit(solution)/shard_map/ppermute | solution.py:732
  20.3 0.6 %collective-permute-start.8 = (f32[104,256]{1,0:T(8,128)S(1)}, f32[104,256]{1,0:T(8,128)S(1)}, u32[]{:S(2)}, u32[]{:S(2)}) collective-permute-start(f32[104,256]{1,0:T(8,128)S(1)} %get-tuple-element.46.refs_0_), channel_id=1, source_target_pairs={{0,16},{8,24},{16,0},{24,8},{1,17},{9,25},{17,1},{25,9},{2,18},{10... | collective-permute-start | bytes 319496 | tf_op jit(solution)/shard_map/ppermute | solution.py:741
  20.9 1.6 %collective-permute-start.10 = (f32[16,256]{1,0:T(8,128)S(1)}, f32[16,256]{1,0:T(8,128)S(1)}, u32[]{:S(2)}, u32[]{:S(2)}) collective-permute-start(f32[16,256]{1,0:T(8,128)S(1)} %get-tuple-element.47), channel_id=1, source_target_pairs={{0,24},{8,16},{16,8},{24,0},{1,25},{9,17},{17,9},{25,1},{2,26},{10... | collective-permute-start | bytes 49160 | tf_op jit(solution)/shard_map/ppermute | solution.py:741
  22.5 2.4 %collective-permute-done.10.refs_3_ = f32[16,256]{1,0:T(8,128)S(1)} collective-permute-done((f32[16,256]{1,0:T(8,128)S(1)}, f32[16,256]{1,0:T(8,128)S(1)}, u32[]{:S(2)}, u32[]{:S(2)}) %collective-permute-start.10) | collective-permute-done | bytes 16416 | tf_op jit(solution)/shard_map/ppermute | solution.py:741
  25.0 0.6 %collective-permute-done.8.refs_1_ = f32[104,256]{1,0:T(8,128)S(1)} collective-permute-done((f32[104,256]{1,0:T(8,128)S(1)}, f32[104,256]{1,0:T(8,128)S(1)}, u32[]{:S(2)}, u32[]{:S(2)}) %collective-permute-start.8) | collective-permute-done | bytes 106528 | tf_op jit(solution)/shard_map/ppermute | solution.py:741
  26.1 0.9 %collective-permute-start.11 = (f32[8,2176]{1,0:T(8,128)S(1)}, f32[8,2176]{1,0:T(8,128)S(1)}, u32[]{:S(2)}, u32[]{:S(2)}) collective-permute-start(f32[8,2176]{1,0:T(8,128)S(1)} %get-tuple-element.48), channel_id=1, source_target_pairs={{0,1},{1,0},{2,3},{3,2},{4,5},{5,4},{6,7},{7,6},{8,9},{9,8},{10,11... | collective-permute-start | bytes 208904 | tf_op jit(solution)/shard_map/ppermute | solution.py:732
  27.0 1.3 %second_step.1.y.refs_4_ = f32[16,8,1920]{2,1,0:T(8,128)S(1)} custom-call(f32[16,8,1920]{2,1,0:T(8,128)S(1)} %get-tuple-element.44.y.refs_4_.state, f32[3,8,1920]{2,1,0:T(8,128)S(1)} %get-tuple-element.45.yring.refs_5_.sring, f32[2,8,1920]{2,1,0:T(8,128)S(1)} %get-tuple-element.49.change, f32[8,1920]{1,0:T(8,128)S(1)} %get-tuple-element.50.ring_change, ...), custom_call_target="tpu_custom_call" | custom-call | flops 10000000 | bytes 5038080 | tf_op jit(solution)/shard_map/second_step/pallas_call | solution.py:682
  28.3 0.6 %tile_spectra.1.part = f32[64,256]{1,0:T(8,128)S(1)} custom-call(f32[16,8,1920]{2,1,0:T(8,128)S(1)} %second_step.1.y.refs_4_, bf16[1920,256]{1,0:T(8,128)(2,1)S(1)} %copy-done, bf16[1920,256]{1,0:T(8,128)(2,1)S(1)} %copy-done.1, f32[2,128]{1,0:T(2,128)S(1)} %pad_maximum_fusion.phase.refs_8_, s32[16,128]{1,0:T(8,128)S(1)} %copy-done.4), custom_call_target="tpu_custom_call" | custom-call | flops 1000000 | bytes 3023872 | tf_op jit(solution)/shard_map/tile_spectra/pallas_call | solution.py:682
  29.0 1.2 %collective-permute-done.12.part_got = f32[64,256]{1,0:T(8,128)S(1)} collective-permute-done((f32[64,256]{1,0:T(8,128)S(1)}, f32[64,256]{1,0:T(8,128)S(1)}, u32[]{:S(2)}, u32[]{:S(2)}) %collective-permute-start.12) | collective-permute-done | bytes 65568 | tf_op jit(solution)/shard_map/ppermute | solution.py:741
  31.0 0.6 %collective-permute-start.13 = (f32[72,256]{1,0:T(8,128)S(1)}, f32[72,256]{1,0:T(8,128)S(1)}, u32[]{:S(2)}, u32[]{:S(2)}) collective-permute-start(f32[72,256]{1,0:T(8,128)S(1)} %get-tuple-element.54.refs_0_), channel_id=1, source_target_pairs={{0,16},{8,24},{16,0},{24,8},{1,17},{9,25},{17,1},{25,9},{2,18},{10... | collective-permute-start | bytes 221192 | tf_op jit(solution)/shard_map/ppermute | solution.py:741
  31.5 1.6 %collective-permute-start.15 = (f32[8,256]{1,0:T(8,128)S(1)}, f32[8,256]{1,0:T(8,128)S(1)}, u32[]{:S(2)}, u32[]{:S(2)}) collective-permute-start(f32[8,256]{1,0:T(8,128)S(1)} %get-tuple-element.55), channel_id=1, source_target_pairs={{0,24},{8,16},{16,8},{24,0},{1,25},{9,17},{17,9},{25,1},{2,26},{10... | collective-permute-start | bytes 24584 | tf_op jit(solution)/shard_map/ppermute | solution.py:741
  33.2 1.5 %collective-permute-done.15.refs_3_ = f32[8,256]{1,0:T(8,128)S(1)} collective-permute-done((f32[8,256]{1,0:T(8,128)S(1)}, f32[8,256]{1,0:T(8,128)S(1)}, u32[]{:S(2)}, u32[]{:S(2)}) %collective-permute-start.15) | collective-permute-done | bytes 8224 | tf_op jit(solution)/shard_map/ppermute | solution.py:741
  34.6 0.8 %collective-permute-done.13.refs_1_ = f32[72,256]{1,0:T(8,128)S(1)} collective-permute-done((f32[72,256]{1,0:T(8,128)S(1)}, f32[72,256]{1,0:T(8,128)S(1)}, u32[]{:S(2)}, u32[]{:S(2)}) %collective-permute-start.13) | collective-permute-done | bytes 73760 | tf_op jit(solution)/shard_map/ppermute | solution.py:741
  35.4 1.3 %filter_all.1 = f32[4,4,8,1800]{3,2,1,0:T(8,128)} custom-call(f32[72,256]{1,0:T(8,128)S(1)} %get-tuple-element.54.refs_0_, f32[72,256]{1,0:T(8,128)S(1)} %collective-permute-done.13.refs_1_, f32[8,256]{1,0:T(8,128)S(1)} %collective-permute-done.14.refs_2_, f32[8,256]{1,0:T(8,128)S(1)} %collective-permute-done.15.refs_3_, ...), custom_call_target="tpu_custom_call" | custom-call | tf_op jit(solution)/shard_map/filter_all/pallas_call | solution.py:819
  (42 shorter events, 4.1 us)
Async XLA Ops:
  1.5 7.6 %collective-permute-start = (f32[8,128]{1,0:T(8,128)S(1)}, f32[8,128]{1,0:T(8,128)S(1)}, u32[]{:S(2)}, u32[]{:S(2)}) collective-permute-start(f32[8,128]{1,0:T(8,128)S(1)} %get-tuple-element.31), channel_id=1, source_target_pairs={{0,8},{8,0},{16,24},{24,16},{1,9},{9,1},{17,25},{25,17},{2,10},{10... | collective-permute-start | bytes 12296 | tf_op jit(solution)/shard_map/ppermute | solution.py:760
  1.6 7.5 %collective-permute-start.1 = (f32[8,128]{1,0:T(8,128)S(1)}, f32[8,128]{1,0:T(8,128)S(1)}, u32[]{:S(2)}, u32[]{:S(2)}) collective-permute-start(f32[8,128]{1,0:T(8,128)S(1)} %get-tuple-element.32), channel_id=1, source_target_pairs={{0,24},{8,16},{16,8},{24,0},{1,25},{9,17},{17,9},{25,1},{2,26},{10... | collective-permute-start | bytes 12296 | tf_op jit(solution)/shard_map/ppermute | solution.py:761
  3.2 9.4 %collective-permute-start.2 = (f32[8,6528]{1,0:T(8,128)S(1)}, f32[8,6528]{1,0:T(8,128)S(1)}, u32[]{:S(2)}, u32[]{:S(2)}) collective-permute-start(f32[8,6528]{1,0:T(8,128)S(1)} %get-tuple-element.34), channel_id=1, source_target_pairs={{0,2},{2,0},{4,6},{6,4},{1,3},{3,1},{5,7},{7,5},{8,10},{10,8},{12,... | collective-permute-start | bytes 626696 | tf_op jit(solution)/shard_map/ppermute | solution.py:758
  3.7 9.7 %collective-permute-start.3 = (f32[8,6528]{1,0:T(8,128)S(1)}, f32[8,6528]{1,0:T(8,128)S(1)}, u32[]{:S(2)}, u32[]{:S(2)}) collective-permute-start(f32[8,6528]{1,0:T(8,128)S(1)} %get-tuple-element.35), channel_id=1, source_target_pairs={{2,4},{4,2},{3,5},{5,3},{10,12},{12,10},{11,13},{13,11},{18,20},{2... | collective-permute-start | bytes 626696 | tf_op jit(solution)/shard_map/ppermute | solution.py:759
  9.3 4.2 %collective-permute-start.4 = (f32[8,512]{1,0:T(8,128)S(1)}, f32[8,512]{1,0:T(8,128)S(1)}, u32[]{:S(2)}, u32[]{:S(2)}) collective-permute-start(f32[8,512]{1,0:T(8,128)S(1)} %get-tuple-element.39), channel_id=1, source_target_pairs={{0,2},{2,0},{4,6},{6,4},{1,3},{3,1},{5,7},{7,5},{8,10},{10,8},{12,... | collective-permute-start | bytes 49160 | tf_op jit(solution)/shard_map/ppermute | solution.py:770
  9.4 5.6 %collective-permute-start.5 = (f32[8,512]{1,0:T(8,128)S(1)}, f32[8,512]{1,0:T(8,128)S(1)}, u32[]{:S(2)}, u32[]{:S(2)}) collective-permute-start(f32[8,512]{1,0:T(8,128)S(1)} %get-tuple-element.40), channel_id=1, source_target_pairs={{2,4},{4,2},{3,5},{5,3},{10,12},{12,10},{11,13},{13,11},{18,20},{2... | collective-permute-start | bytes 49160 | tf_op jit(solution)/shard_map/ppermute | solution.py:771
  15.0 2.7 %copy-start = (bf16[1920,256]{1,0:T(8,128)(2,1)S(1)}, bf16[1920,256]{1,0:T(8,128)(2,1)}, u32[]{:S(2)}) copy-start(bf16[1920,256]{1,0:T(8,128)(2,1)} %constant.59.clone.wh) | copy-start | bytes 2949124
  15.0 2.7 %copy-start.1 = (bf16[1920,256]{1,0:T(8,128)(2,1)S(1)}, bf16[1920,256]{1,0:T(8,128)(2,1)}, u32[]{:S(2)}) copy-start(bf16[1920,256]{1,0:T(8,128)(2,1)} %constant.60.clone.wl) | copy-start | bytes 2949124
  15.1 4.5 %collective-permute-start.6 = (f32[8,2432]{1,0:T(8,128)S(1)}, f32[8,2432]{1,0:T(8,128)S(1)}, u32[]{:S(2)}, u32[]{:S(2)}) collective-permute-start(f32[8,2432]{1,0:T(8,128)S(1)} %get-tuple-element.42), channel_id=1, source_target_pairs={{0,1},{1,0},{2,3},{3,2},{4,5},{5,4},{6,7},{7,6},{8,9},{9,8},{10,11... | collective-permute-start | bytes 233480 | tf_op jit(solution)/shard_map/ppermute | solution.py:732
  16.6 1.1 %copy-start.4 = (s32[16,128]{1,0:T(8,128)S(1)}, s32[16,128]{1,0:T(8,128)}, u32[]{:S(2)}) copy-start(s32[16,128]{1,0:T(8,128)} %row_code.1.code.refs_9_) | copy-start | bytes 24580
  18.4 1.4 %collective-permute-start.7 = (f32[88,256]{1,0:T(8,128)S(1)}, f32[88,256]{1,0:T(8,128)S(1)}, u32[]{:S(2)}, u32[]{:S(2)}) collective-permute-start(f32[88,256]{1,0:T(8,128)S(1)} %tile_and_ring_spectra.1.part), channel_id=1, source_target_pairs={{0,8},{8,0},{16,24},{24,16},{1,9},{9,1},{17,25},{25,17},{2,10},{10... | collective-permute-start | bytes 270344 | tf_op jit(solution)/shard_map/ppermute | solution.py:741
  19.8 5.8 %copy-start.2 = (bf16[256,1920]{1,0:T(8,128)(2,1)S(1)}, bf16[256,1920]{1,0:T(8,128)(2,1)}, u32[]{:S(2)}) copy-start(bf16[256,1920]{1,0:T(8,128)(2,1)} %constant.61.clone.refs_6_.wh) | copy-start | bytes 2949124
  19.8 5.8 %copy-start.3 = (bf16[256,1920]{1,0:T(8,128)(2,1)S(1)}, bf16[256,1920]{1,0:T(8,128)(2,1)}, u32[]{:S(2)}) copy-start(bf16[256,1920]{1,0:T(8,128)(2,1)} %constant.62.clone.refs_7_.wl) | copy-start | bytes 2949124
  20.3 5.3 %collective-permute-start.8 = (f32[104,256]{1,0:T(8,128)S(1)}, f32[104,256]{1,0:T(8,128)S(1)}, u32[]{:S(2)}, u32[]{:S(2)}) collective-permute-start(f32[104,256]{1,0:T(8,128)S(1)} %get-tuple-element.46.refs_0_), channel_id=1, source_target_pairs={{0,16},{8,24},{16,0},{24,8},{1,17},{9,25},{17,1},{25,9},{2,18},{10... | collective-permute-start | bytes 319496 | tf_op jit(solution)/shard_map/ppermute | solution.py:741
  20.9 1.6 %collective-permute-start.9 = (f32[16,256]{1,0:T(8,128)S(1)}, f32[16,256]{1,0:T(8,128)S(1)}, u32[]{:S(2)}, u32[]{:S(2)}) collective-permute-start(f32[16,256]{1,0:T(8,128)S(1)} %get-tuple-element.47), channel_id=1, source_target_pairs={{0,8},{8,0},{16,24},{24,16},{1,9},{9,1},{17,25},{25,17},{2,10},{10... | collective-permute-start | bytes 49160 | tf_op jit(solution)/shard_map/ppermute | solution.py:741
  20.9 4.1 %collective-permute-start.10 = (f32[16,256]{1,0:T(8,128)S(1)}, f32[16,256]{1,0:T(8,128)S(1)}, u32[]{:S(2)}, u32[]{:S(2)}) collective-permute-start(f32[16,256]{1,0:T(8,128)S(1)} %get-tuple-element.47), channel_id=1, source_target_pairs={{0,24},{8,16},{16,8},{24,0},{1,25},{9,17},{17,9},{25,1},{2,26},{10... | collective-permute-start | bytes 49160 | tf_op jit(solution)/shard_map/ppermute | solution.py:741
  26.1 4.4 %collective-permute-start.11 = (f32[8,2176]{1,0:T(8,128)S(1)}, f32[8,2176]{1,0:T(8,128)S(1)}, u32[]{:S(2)}, u32[]{:S(2)}) collective-permute-start(f32[8,2176]{1,0:T(8,128)S(1)} %get-tuple-element.48), channel_id=1, source_target_pairs={{0,1},{1,0},{2,3},{3,2},{4,5},{5,4},{6,7},{7,6},{8,9},{9,8},{10,11... | collective-permute-start | bytes 208904 | tf_op jit(solution)/shard_map/ppermute | solution.py:732
  28.9 1.3 %collective-permute-start.12 = (f32[64,256]{1,0:T(8,128)S(1)}, f32[64,256]{1,0:T(8,128)S(1)}, u32[]{:S(2)}, u32[]{:S(2)}) collective-permute-start(f32[64,256]{1,0:T(8,128)S(1)} %tile_spectra.1.part), channel_id=1, source_target_pairs={{0,8},{8,0},{16,24},{24,16},{1,9},{9,1},{17,25},{25,17},{2,10},{10... | collective-permute-start | bytes 196616 | tf_op jit(solution)/shard_map/ppermute | solution.py:741
  31.0 4.4 %collective-permute-start.13 = (f32[72,256]{1,0:T(8,128)S(1)}, f32[72,256]{1,0:T(8,128)S(1)}, u32[]{:S(2)}, u32[]{:S(2)}) collective-permute-start(f32[72,256]{1,0:T(8,128)S(1)} %get-tuple-element.54.refs_0_), channel_id=1, source_target_pairs={{0,16},{8,24},{16,0},{24,8},{1,17},{9,25},{17,1},{25,9},{2,18},{10... | collective-permute-start | bytes 221192 | tf_op jit(solution)/shard_map/ppermute | solution.py:741
  31.5 1.6 %collective-permute-start.14 = (f32[8,256]{1,0:T(8,128)S(1)}, f32[8,256]{1,0:T(8,128)S(1)}, u32[]{:S(2)}, u32[]{:S(2)}) collective-permute-start(f32[8,256]{1,0:T(8,128)S(1)} %get-tuple-element.55), channel_id=1, source_target_pairs={{0,8},{8,0},{16,24},{24,16},{1,9},{9,1},{17,25},{25,17},{2,10},{10... | collective-permute-start | bytes 24584 | tf_op jit(solution)/shard_map/ppermute | solution.py:741
  31.5 3.1 %collective-permute-start.15 = (f32[8,256]{1,0:T(8,128)S(1)}, f32[8,256]{1,0:T(8,128)S(1)}, u32[]{:S(2)}, u32[]{:S(2)}) collective-permute-start(f32[8,256]{1,0:T(8,128)S(1)} %get-tuple-element.55), channel_id=1, source_target_pairs={{0,24},{8,16},{16,8},{24,0},{1,25},{9,17},{17,9},{25,1},{2,26},{10... | collective-permute-start | bytes 24584 | tf_op jit(solution)/shard_map/ppermute | solution.py:741
